TPU v7x, 512 devices: a whole 4x8x8 slice. The times are simulated.
512 devices in a mesh: gx: 16 (over y, x_lo), yz: 16 (over z, core), lvl: 2 (over x_hi).
Axes of the slice: x: 4 (x_hi: 2, x_lo: 2; x = x_hi * 2 + x_lo), y: 8, z: 8, core: 2. Of those that a mesh axis runs over, the one named last changes fastest.
Arguments:
- input_residual: float32 [64, 16, 128, 256], P(None, 'gx', 'yz', 'lvl'), may hold values from -6 to 6
- coefficient: float32 [16, 128, 256], P('gx', 'yz', 'lvl'), may hold values from 0.1 to 1.35
- element_block: float32 [64, 64], replicated, may hold values from -0.03125 to 3, as said below
- face_blocks: float32 [4, 16, 16], replicated, may hold values from -0.5 to 12, as said below
- face_block_kind: int32 [6, 16, 128, 256], P(None, 'gx', 'yz', 'lvl'), may hold values from 0 to 3, as said below
- face_wall_flag: int32 [6, 16, 128, 256], P(None, 'gx', 'yz', 'lvl'), may hold values from 0 to 1, as said below
Outputs:
- correction: float32 [64, 16, 128, 256], P(None, 'gx', 'yz', 'lvl')
- residual: float32 [64, 16, 128, 256], P(None, 'gx', 'yz', 'lvl')
Inputs may be any that keep to these rules, and one draw needn't show every extreme that they name: `element_block`: symmetric. `face_blocks`: each block symmetric. `face_block_kind`: the entry of an element for its + face along a direction equals the entry of its neighbour on that side for its - face. `face_wall_flag`: 1 marks a wall; the entry of an element for its + face along a direction equals the entry of its neighbour on that side for its - face.
All inputs are finite; a program needn't handle non-finite values.
Results may differ from a plain program's by a relative error of at most 0.00027.
Values sent between devices are 32-bit elements; how exact they have to be, the bound alone decides.
No kernel may reach another device: no remote copies, remote signals or barrier semaphores. Data moves between devices by JAX's collectives and lax.ppermute only.
A program may use at most 64 MiB of HBM per device.

v0:
```python
import math

import jax
import jax.numpy as jnp
from jax import lax
from jax.sharding import PartitionSpec as P

CHEB = 3
CITERS = 8


HIGHEST = lax.Precision.HIGHEST
LOW_EIG = 0.3
HIGH_EIG = 3.0


def with_halo(block, sides, width):
    for axis, dim in sides:
        count = lax.axis_size(axis)
        forward = [(i, i + 1) for i in range(count - 1)]
        backward = [(target, source) for source, target in forward]
        low = lax.ppermute(
            lax.slice_in_dim(block, block.shape[dim] - width, None, axis=dim), axis, forward
        )
        high = lax.ppermute(lax.slice_in_dim(block, 0, width, axis=dim), axis, backward)
        block = jnp.concatenate([low, block, high], axis=dim)
    return block


def prolong_tables():
    node_points = jnp.array(
        [-1.0, -1.0 / math.sqrt(5.0), 1.0 / math.sqrt(5.0), 1.0], dtype=jnp.float32
    )
    basis_table = jnp.stack([(1.0 - node_points) * 0.5, (1.0 + node_points) * 0.5], axis=1)
    volume = (
        basis_table[:, None, None, :, None, None]
        * basis_table[None, :, None, None, :, None]
        * basis_table[None, None, :, None, None, :]
    ).reshape(64, 8)
    surface = (basis_table[:, None, :, None] * basis_table[None, :, None, :]).reshape(16, 4)
    return (volume, surface)


def level_tables(element_block, face_blocks, volume, surface):
    elem_mid = jnp.dot(
        volume.T, jnp.dot(element_block, volume, precision=HIGHEST), precision=HIGHEST
    )
    face_mid = jnp.einsum("kij,jb->kib", face_blocks, surface, precision=HIGHEST)
    face_mid = jnp.einsum("ia,kib->kab", surface, face_mid, precision=HIGHEST)
    elem_coarse = jnp.sum(elem_mid).reshape(1, 1)
    face_coarse = jnp.sum(face_mid, axis=(1, 2)).reshape(-1, 1, 1)
    return (elem_mid, face_mid, elem_coarse, face_coarse)


def build_weights(face_block_kind, face_wall_flag, offsets, totals, kinds):
    shape = face_block_kind.shape[1:]
    places = [offsets[d] + lax.broadcasted_iota(jnp.int32, shape, d) for d in range(3)]
    has_next = [places[d] < totals[d] - 1 for d in range(3)]
    has_prev = [places[d] > 0 for d in range(3)]
    kind_ids = jnp.arange(kinds, dtype=jnp.int32).reshape(kinds, 1, 1, 1)

    def weigh_faces(row, allowed):
        chosen = (
            (face_block_kind[row][None] == kind_ids)
            & (face_wall_flag[row][None] == 0)
            & allowed[None]
        )
        return chosen.astype(jnp.float32)

    plus_side_weight = [weigh_faces(2 * d + 1, has_next[d]) for d in range(3)]
    minus_side_weight = [weigh_faces(2 * d, has_prev[d]) for d in range(3)]
    return (plus_side_weight, minus_side_weight)


def trace_of(values, points, direction, at):
    shaped = values.reshape((points, points, points) + values.shape[1:])
    picked = lax.index_in_dim(shaped, at, axis=direction, keepdims=False)
    return picked.reshape((points * points,) + values.shape[1:])


def add_to_trace(values, points, direction, at, addend):
    shaped = values.reshape((points, points, points) + values.shape[1:])
    face_piece = addend.reshape((points, points) + values.shape[1:])
    index_list = [slice(None)] * direction + [at]
    shaped = shaped.at[tuple(index_list)].add(face_piece)
    return shaped.reshape(values.shape)


def select(blocks, weights, jump_vals):
    running = jnp.zeros_like(jump_vals)
    for k in range(blocks.shape[0]):
        running = running + weights[k][None] * jnp.einsum(
            "ij,jxyz->ixyz", blocks[k], jump_vals, precision=HIGHEST
        )
    return running


def pick_diag(face_diag, weights):
    running = jnp.zeros((face_diag.shape[1],) + weights.shape[1:], jnp.float32)
    for k in range(face_diag.shape[0]):
        running = running + face_diag[k][:, None, None, None] * weights[k][None]
    return running


def diag_of(points, element, blocks, coefficient, plus_side_weight, minus_side_weight):
    result = coefficient[None] * jnp.diagonal(element)[:, None, None, None]
    face_diag = jnp.diagonal(blocks, axis1=1, axis2=2)
    for d in range(3):
        result = add_to_trace(
            result, points, d, points - 1, pick_diag(face_diag, plus_side_weight[d])
        )
        result = add_to_trace(result, points, d, 0, pick_diag(face_diag, minus_side_weight[d]))
    return result


def rims_of(values, points, halo_fns):
    found = []
    for d in range(3):
        axis = 1 + d
        count = values.shape[axis]
        upper = trace_of(values, points, d, points - 1)
        bottom = trace_of(values, points, d, 0)
        outgoing = jnp.concatenate(
            [
                lax.slice_in_dim(bottom, 0, 1, axis=axis),
                lax.slice_in_dim(upper, count - 1, count, axis=axis),
            ],
            axis=axis,
        )
        padded = halo_fns[d](outgoing)
        found.append(
            (lax.slice_in_dim(padded, 0, 1, axis=axis), lax.slice_in_dim(padded, 3, 4, axis=axis))
        )
    return found


def operate_split(
    values, points, element, blocks, coefficient, plus_side_weight, minus_side_weight, rim_list
):
    result = coefficient[None] * jnp.einsum("ij,jxyz->ixyz", element, values, precision=HIGHEST)
    for d in range(3):
        axis = 1 + d
        count = values.shape[axis]
        from_left, from_right = rim_list[d]
        upper = trace_of(values, points, d, points - 1)
        bottom = trace_of(values, points, d, 0)
        upcoming = jnp.concatenate(
            [lax.slice_in_dim(bottom, 1, count, axis=axis), from_right], axis=axis
        )
        face_flux = select(blocks, plus_side_weight[d], upper - upcoming)
        left_flux = select(
            blocks,
            lax.slice_in_dim(minus_side_weight[d], 0, 1, axis=axis),
            from_left - lax.slice_in_dim(bottom, 0, 1, axis=axis),
        )
        result = add_to_trace(result, points, d, points - 1, face_flux)
        behind = jnp.concatenate(
            [left_flux, lax.slice_in_dim(face_flux, 0, count - 1, axis=axis)], axis=axis
        )
        result = add_to_trace(result, points, d, 0, -behind)
    return result


def neighbour_of(padded, axis, offset):
    index_list = [slice(None), slice(1, -1), slice(1, -1), slice(1, -1)]
    index_list[axis] = slice(1 + offset, padded.shape[axis] - 1 + offset)
    return padded[tuple(index_list)]


def coarse_operate(values, coef_row, conductance, elem_value, padded):
    result = coef_row * (elem_value * values)
    for d in range(3):
        axis = 1 + d
        following = neighbour_of(padded, axis, 1)
        preceding = neighbour_of(padded, axis, -1)
        result = result + conductance[d : d + 1] * (values - following)
        result = result - conductance[3 + d : 4 + d] * (preceding - values)
    return result


def smooth(operate_fn, inverse, start_vec, residual, keep_last):
    middle = 0.5 * (HIGH_EIG + LOW_EIG)
    spread = 0.5 * (HIGH_EIG - LOW_EIG)
    scaled = middle / spread
    rho_now = 1.0 / scaled
    update = inverse * residual / middle
    solution = start_vec
    for k in range(CHEB):
        solution = solution + update
        is_last = k == CHEB - 1
        if keep_last or not is_last:
            residual = residual - operate_fn(update)
        if not is_last:
            rho_next = 1.0 / (2.0 * scaled - rho_now)
            update = rho_next * rho_now * update + 2.0 * rho_next / spread * (inverse * residual)
            rho_now = rho_next
    return (solution, residual)


def conjugate(operate_fn, rhs, total_fn):
    solution = jnp.zeros_like(rhs)
    residual = rhs
    search = rhs
    norm_now = total_fn(jnp.sum(residual * residual))
    for k in range(CITERS):
        image_vec = operate_fn(search)
        step_len = norm_now / total_fn(jnp.sum(search * image_vec))
        solution = solution + step_len * search
        residual = residual - step_len * image_vec
        if k + 1 < CITERS:
            norm_next = total_fn(jnp.sum(residual * residual))
            search = residual + norm_next / norm_now * search
            norm_now = norm_next
    return solution


def local(input_residual, coefficient, element_block, face_blocks, face_block_kind, face_wall_flag):
    block_x, block_y, block_z = coefficient.shape
    volume, surface = prolong_tables()
    elem_mid, face_mid, elem_coarse, face_coarse = level_tables(
        element_block, face_blocks, volume, surface
    )
    offsets = (
        lax.axis_index("gx") * block_x,
        lax.axis_index("yz") * block_y,
        lax.axis_index("lvl") * block_z,
    )
    totals = (
        lax.axis_size("gx") * block_x,
        lax.axis_size("yz") * block_y,
        lax.axis_size("lvl") * block_z,
    )
    plus_side_weight, minus_side_weight = build_weights(
        face_block_kind, face_wall_flag, offsets, totals, face_blocks.shape[0]
    )
    fine_halos = (
        lambda outgoing: with_halo(outgoing, (("gx", 1),), 1),
        lambda outgoing: with_halo(outgoing, (("yz", 2),), 1),
        lambda outgoing: with_halo(outgoing, (("lvl", 3),), 1),
    )
    mid_halos = (
        lambda outgoing: with_halo(outgoing, (("gx", 1),), 1),
        lambda outgoing: with_halo(outgoing, (("yz", 2),), 1),
        lambda outgoing: with_halo(outgoing, (("lvl", 3),), 1),
    )

    def fine_apply(values):
        return operate_split(
            values,
            4,
            element_block,
            face_blocks,
            coefficient,
            plus_side_weight,
            minus_side_weight,
            rims_of(values, 4, fine_halos),
        )

    def mid_apply(values):
        return operate_split(
            values,
            2,
            elem_mid,
            face_mid,
            coefficient,
            plus_side_weight,
            minus_side_weight,
            rims_of(values, 2, mid_halos),
        )

    fine_inverse = 1.0 / diag_of(
        4, element_block, face_blocks, coefficient, plus_side_weight, minus_side_weight
    )
    mid_inverse = 1.0 / diag_of(
        2, elem_mid, face_mid, coefficient, plus_side_weight, minus_side_weight
    )
    fine_pre, fine_res = smooth(
        fine_apply, fine_inverse, jnp.zeros_like(input_residual), input_residual, True
    )
    mid_rhs = jnp.einsum("ij,jxyz->ixyz", volume.T, fine_res, precision=HIGHEST)
    mid_pre, mid_res = smooth(mid_apply, mid_inverse, jnp.zeros_like(mid_rhs), mid_rhs, True)
    coarse_rhs = jnp.sum(mid_res, axis=0, keepdims=True)
    coarse_faces = face_coarse[:, 0, 0]

    def conduct(weights):
        running = jnp.zeros(weights.shape[1:], jnp.float32)
        for k in range(weights.shape[0]):
            running = running + coarse_faces[k] * weights[k]
        return running

    conductance = jnp.stack(
        [
            conduct(plus_side_weight[0]),
            conduct(plus_side_weight[1]),
            conduct(plus_side_weight[2]),
            conduct(minus_side_weight[0]),
            conduct(minus_side_weight[1]),
            conduct(minus_side_weight[2]),
        ]
    )
    elem_value = elem_coarse[0, 0]

    def coarse_total(scalar):
        return lax.psum(scalar, ("gx", "yz", "lvl"))

    def coarse_apply(values):
        padded = with_halo(values, (("gx", 1), ("yz", 2), ("lvl", 3)), 1)
        return coarse_operate(values, coefficient[None], conductance, elem_value, padded)

    coarse_sol = conjugate(coarse_apply, coarse_rhs, coarse_total)
    spread_sol = jnp.broadcast_to(coarse_sol, mid_pre.shape)
    mid_sol, unused = smooth(
        mid_apply, mid_inverse, mid_pre + spread_sol, mid_res - mid_apply(spread_sol), False
    )
    lifted = jnp.einsum("ij,jxyz->ixyz", volume, mid_sol, precision=HIGHEST)
    lifted_rims = rims_of(lifted, 4, fine_halos)
    lifted_image = operate_split(
        lifted,
        4,
        element_block,
        face_blocks,
        coefficient,
        plus_side_weight,
        minus_side_weight,
        lifted_rims,
    )
    correction, residual = smooth(
        fine_apply, fine_inverse, fine_pre + lifted, fine_res - lifted_image, True
    )
    return (correction, residual)


def solution(mesh):
    in_specs = (
        P(None, "gx", "yz", "lvl"),
        P("gx", "yz", "lvl"),
        P(),
        P(),
        P(None, "gx", "yz", "lvl"),
        P(None, "gx", "yz", "lvl"),
    )
    out_specs = (P(None, "gx", "yz", "lvl"), P(None, "gx", "yz", "lvl"))
    return jax.shard_map(local, mesh=mesh, in_specs=in_specs, out_specs=out_specs, check_vma=False)
```

profile of v0, /device:TPU:282, one launch (start us, length us, event | category | flops | bytes accessed | tf_op | source)
XLA Modules:
  0.0 2195.6 jit_solution(12593372092997465043)
XLA Ops:
  107.3 6.0 collective-permute-start.13
  250.4 6.0 collective-permute-start.41
  261.8 98.3 %all-reduce = (f32[]{:T(128)}, f32[]{:T(128)}) all-reduce(f32[]{:T(128)} %multiply_reduce_fusion.14, f32[]{:T(128)} %get-tuple-element.1135), channel_id=1, replica_groups=mesh['gx'=16,'yz'=16,'lvl'=2] {'gx','yz','lvl'}, use_global_device_ids=true, to_apply=%region_2.3 | all-reduce | flops 2 | bytes 16 | tf_op jit(solution)/shard_map/psum | solution.py:304
  362.0 95.2 %psum.114 = f32[]{:T(128)} all-reduce(f32[]{:T(128)} %multiply_reduce_fusion.12), channel_id=1, replica_groups=mesh['gx'=16,'yz'=16,'lvl'=2] {'gx','yz','lvl'}, use_global_device_ids=true, to_apply=%region_8.9 | all-reduce | flops 1 | bytes 8 | tf_op jit(solution)/shard_map/psum | solution.py:304
  477.2 6.0 collective-permute-start.47
  486.0 98.3 %psum.115 = f32[]{:T(128)} all-reduce(f32[]{:T(128)} %get-tuple-element.1133), channel_id=1, replica_groups=mesh['gx'=16,'yz'=16,'lvl'=2] {'gx','yz','lvl'}, use_global_device_ids=true, to_apply=%region_10.11 | all-reduce | flops 1 | bytes 8 | tf_op jit(solution)/shard_map/psum | solution.py:304
  586.2 95.3 %psum.116 = f32[]{:T(128)} all-reduce(f32[]{:T(128)} %get-tuple-element.1131), channel_id=1, replica_groups=mesh['gx'=16,'yz'=16,'lvl'=2] {'gx','yz','lvl'}, use_global_device_ids=true, to_apply=%region_12.13 | all-reduce | flops 1 | bytes 8 | tf_op jit(solution)/shard_map/psum | solution.py:304
  701.6 6.0 collective-permute-start.53
  710.5 98.2 %psum.117 = f32[]{:T(128)} all-reduce(f32[]{:T(128)} %get-tuple-element.1129), channel_id=1, replica_groups=mesh['gx'=16,'yz'=16,'lvl'=2] {'gx','yz','lvl'}, use_global_device_ids=true, to_apply=%region_14.15 | all-reduce | flops 1 | bytes 8 | tf_op jit(solution)/shard_map/psum | solution.py:304
  810.7 95.3 %psum.118 = f32[]{:T(128)} all-reduce(f32[]{:T(128)} %get-tuple-element.1127), channel_id=1, replica_groups=mesh['gx'=16,'yz'=16,'lvl'=2] {'gx','yz','lvl'}, use_global_device_ids=true, to_apply=%region_16.17 | all-reduce | flops 1 | bytes 8 | tf_op jit(solution)/shard_map/psum | solution.py:304
  926.1 6.0 collective-permute-start.59
  934.9 98.3 %psum.119 = f32[]{:T(128)} all-reduce(f32[]{:T(128)} %get-tuple-element.1125), channel_id=1, replica_groups=mesh['gx'=16,'yz'=16,'lvl'=2] {'gx','yz','lvl'}, use_global_device_ids=true, to_apply=%region_18.19 | all-reduce | flops 1 | bytes 8 | tf_op jit(solution)/shard_map/psum | solution.py:304
  1035.2 95.3 %psum.120 = f32[]{:T(128)} all-reduce(f32[]{:T(128)} %get-tuple-element.1123), channel_id=1, replica_groups=mesh['gx'=16,'yz'=16,'lvl'=2] {'gx','yz','lvl'}, use_global_device_ids=true, to_apply=%region_20.21 | all-reduce | flops 1 | bytes 8 | tf_op jit(solution)/shard_map/psum | solution.py:304
  1150.6 6.0 collective-permute-start.65
  1159.4 98.2 %psum.121 = f32[]{:T(128)} all-reduce(f32[]{:T(128)} %get-tuple-element.1121), channel_id=1, replica_groups=mesh['gx'=16,'yz'=16,'lvl'=2] {'gx','yz','lvl'}, use_global_device_ids=true, to_apply=%region_22.23 | all-reduce | flops 1 | bytes 8 | tf_op jit(solution)/shard_map/psum | solution.py:304
  1259.6 95.3 %psum.122 = f32[]{:T(128)} all-reduce(f32[]{:T(128)} %get-tuple-element.1119), channel_id=1, replica_groups=mesh['gx'=16,'yz'=16,'lvl'=2] {'gx','yz','lvl'}, use_global_device_ids=true, to_apply=%region_24.25 | all-reduce | flops 1 | bytes 8 | tf_op jit(solution)/shard_map/psum | solution.py:304
  1375.0 6.0 collective-permute-start.71
  1383.9 98.3 %psum.123 = f32[]{:T(128)} all-reduce(f32[]{:T(128)} %get-tuple-element.1117), channel_id=1, replica_groups=mesh['gx'=16,'yz'=16,'lvl'=2] {'gx','yz','lvl'}, use_global_device_ids=true, to_apply=%region_26.27 | all-reduce | flops 1 | bytes 8 | tf_op jit(solution)/shard_map/psum | solution.py:304
  1484.2 95.3 %psum.124 = f32[]{:T(128)} all-reduce(f32[]{:T(128)} %get-tuple-element.1115), channel_id=1, replica_groups=mesh['gx'=16,'yz'=16,'lvl'=2] {'gx','yz','lvl'}, use_global_device_ids=true, to_apply=%region_28.29 | all-reduce | flops 1 | bytes 8 | tf_op jit(solution)/shard_map/psum | solution.py:304
  1599.5 6.0 collective-permute-start.77
  1608.4 98.2 %psum.125 = f32[]{:T(128)} all-reduce(f32[]{:T(128)} %get-tuple-element.1113), channel_id=1, replica_groups=mesh['gx'=16,'yz'=16,'lvl'=2] {'gx','yz','lvl'}, use_global_device_ids=true, to_apply=%region_30.31 | all-reduce | flops 1 | bytes 8 | tf_op jit(solution)/shard_map/psum | solution.py:304
  1708.6 95.3 %psum.126 = f32[]{:T(128)} all-reduce(f32[]{:T(128)} %multiply_reduce_fusion), channel_id=1, replica_groups=mesh['gx'=16,'yz'=16,'lvl'=2] {'gx','yz','lvl'}, use_global_device_ids=true, to_apply=%region_32.33 | all-reduce | flops 1 | bytes 8 | tf_op jit(solution)/shard_map/psum | solution.py:304
  1823.8 6.0 collective-permute-start.83
  1832.7 98.3 %psum.127 = f32[]{:T(128)} all-reduce(f32[]{:T(128)} %fusion.727), channel_id=1, replica_groups=mesh['gx'=16,'yz'=16,'lvl'=2] {'gx','yz','lvl'}, use_global_device_ids=true, to_apply=%region_34.35 | all-reduce | flops 1 | bytes 8 | tf_op jit(solution)/shard_map/psum | solution.py:304
  (1175 shorter events, 661.1 us)
Async XLA Ops:
  12.7 24.6 %collective-permute-start.5 = (f32[16,1,8,1]{2,0,3,1:T(8,128)S(1)}, f32[16,1,8,1]{2,0,3,1:T(8,128)S(1)}, u32[]{:S(2)}, u32[]{:S(2)}) collective-permute-start(f32[16,1,8,1]{2,0,3,1:T(8,128)S(1)} %slice.5694), channel_id=1, source_target_pairs={{0,1},{2,3},{4,5},{6,7},{8,9},{10,11},{12,13},{14,15},{16,17},{18,... | collective-permute-start | bytes 1544 | tf_op jit(solution)/shard_map/ppermute | solution.py:22
  16.7 29.4 %collective-permute-start.2 = (f32[16,1,1,128]{3,0,2,1:T(8,128)S(1)}, f32[16,1,1,128]{3,0,2,1:T(8,128)S(1)}, u32[]{:S(2)}, u32[]{:S(2)}) collective-permute-start(f32[16,1,1,128]{3,0,2,1:T(8,128)S(1)} %slice.5679), channel_id=1, source_target_pairs={{2,0},{4,2},{6,4},{8,6},{10,8},{12,10},{14,12},{16,14},{18,16},{20... | collective-permute-start | bytes 24584 | tf_op jit(solution)/shard_map/ppermute | solution.py:25
  18.7 34.3 %collective-permute-start = (f32[16,1,8,128]{3,0,2,1:T(8,128)S(1)}, f32[16,1,8,128]{3,0,2,1:T(8,128)S(1)}, u32[]{:S(2)}, u32[]{:S(2)}) collective-permute-start(f32[16,1,8,128]{3,0,2,1:T(8,128)S(1)} %get-tuple-element.1224), channel_id=1, source_target_pairs={{32,0},{64,32},{96,64},{128,96},{160,128},{192,160},{224,192},{256... | collective-permute-start | bytes 196616 | tf_op jit(solution)/shard_map/ppermute | solution.py:25
  22.0 30.9 %collective-permute-start.1 = (f32[16,1,8,128]{3,0,2,1:T(8,128)S(1)}, f32[16,1,8,128]{3,0,2,1:T(8,128)S(1)}, u32[]{:S(2)}, u32[]{:S(2)}) collective-permute-start(f32[16,1,8,128]{3,0,2,1:T(8,128)S(1)} %get-tuple-element.1223), channel_id=1, source_target_pairs={{0,32},{32,64},{64,96},{96,128},{128,160},{160,192},{192,224},{224... | collective-permute-start | bytes 196616 | tf_op jit(solution)/shard_map/ppermute | solution.py:22
  66.4 23.7 %collective-permute-start.6 = (f32[16,1,8,128]{3,0,2,1:T(8,128)S(1)}, f32[16,1,8,128]{3,0,2,1:T(8,128)S(1)}, u32[]{:S(2)}, u32[]{:S(2)}) collective-permute-start(f32[16,1,8,128]{3,0,2,1:T(8,128)S(1)} %get-tuple-element.1216), channel_id=1, source_target_pairs={{32,0},{64,32},{96,64},{128,96},{160,128},{192,160},{224,192},{256... | collective-permute-start | bytes 196616 | tf_op jit(solution)/shard_map/ppermute | solution.py:25
  68.3 21.7 collective-permute-start.7
  103.5 21.1 collective-permute-start.14
  105.4 27.7 %collective-permute-start.12 = (f32[16,1,8,128]{3,0,2,1:T(8,128)}, f32[16,1,8,128]{3,0,2,1:T(8,128)}, u32[]{:S(2)}, u32[]{:S(2)}) collective-permute-start(f32[16,1,8,128]{3,0,2,1:T(8,128)} %get-tuple-element.1208), channel_id=1, source_target_pairs={{32,0},{64,32},{96,64},{128,96},{160,128},{192,160},{224,192},{256... | collective-permute-start | bytes 196616 | tf_op jit(solution)/shard_map/ppermute | solution.py:25
  107.3 25.8 %collective-permute-start.13 = (f32[16,1,8,128]{3,0,2,1:T(8,128)}, f32[16,1,8,128]{3,0,2,1:T(8,128)}, u32[]{:S(2)}, u32[]{:S(2)}) collective-permute-start(f32[16,1,8,128]{3,0,2,1:T(8,128)} %get-tuple-element.1207), channel_id=1, source_target_pairs={{0,32},{32,64},{64,96},{96,128},{128,160},{160,192},{192,224},{224... | collective-permute-start | bytes 196616 | tf_op jit(solution)/shard_map/ppermute | solution.py:22
  144.4 23.7 %collective-permute-start.18 = (f32[4,1,8,128]{3,0,2,1:T(4,128)S(1)}, f32[4,1,8,128]{3,0,2,1:T(4,128)S(1)}, u32[]{:S(2)}, u32[]{:S(2)}) collective-permute-start(f32[4,1,8,128]{3,0,2,1:T(4,128)S(1)} %get-tuple-element.1264), channel_id=1, source_target_pairs={{32,0},{64,32},{96,64},{128,96},{160,128},{192,160},{224,192},{256... | collective-permute-start | bytes 49160 | tf_op jit(solution)/shard_map/ppermute | solution.py:25
  146.4 21.8 collective-permute-start.19
  175.0 23.7 %collective-permute-start.24 = (f32[4,1,8,128]{3,0,2,1:T(4,128)S(1)}, f32[4,1,8,128]{3,0,2,1:T(4,128)S(1)}, u32[]{:S(2)}, u32[]{:S(2)}) collective-permute-start(f32[4,1,8,128]{3,0,2,1:T(4,128)S(1)} %get-tuple-element.1256), channel_id=1, source_target_pairs={{32,0},{64,32},{96,64},{128,96},{160,128},{192,160},{224,192},{256... | collective-permute-start | bytes 49160 | tf_op jit(solution)/shard_map/ppermute | solution.py:25
  176.9 21.8 collective-permute-start.25
  205.5 23.7 %collective-permute-start.30 = (f32[4,1,8,128]{3,0,2,1:T(4,128)S(1)}, f32[4,1,8,128]{3,0,2,1:T(4,128)S(1)}, u32[]{:S(2)}, u32[]{:S(2)}) collective-permute-start(f32[4,1,8,128]{3,0,2,1:T(4,128)S(1)} %get-tuple-element.1248), channel_id=1, source_target_pairs={{32,0},{64,32},{96,64},{128,96},{160,128},{192,160},{224,192},{256... | collective-permute-start | bytes 49160 | tf_op jit(solution)/shard_map/ppermute | solution.py:25
  207.4 21.8 collective-permute-start.31
  1932.5 23.4 %collective-permute-start.85 = (f32[4,1,8,128]{3,0,2,1:T(4,128)S(1)}, f32[4,1,8,128]{3,0,2,1:T(4,128)S(1)}, u32[]{:S(2)}, u32[]{:S(2)}) collective-permute-start(f32[4,1,8,128]{3,0,2,1:T(4,128)S(1)} %reshape_squeeze.140), channel_id=1, source_target_pairs={{0,32},{32,64},{64,96},{96,128},{128,160},{160,192},{192,224},{224... | collective-permute-start | bytes 49160 | tf_op jit(solution)/shard_map/ppermute | solution.py:22
  1967.2 23.7 %collective-permute-start.90 = (f32[4,1,8,128]{3,0,2,1:T(4,128)S(1)}, f32[4,1,8,128]{3,0,2,1:T(4,128)S(1)}, u32[]{:S(2)}, u32[]{:S(2)}) collective-permute-start(f32[4,1,8,128]{3,0,2,1:T(4,128)S(1)} %get-tuple-element.1240), channel_id=1, source_target_pairs={{32,0},{64,32},{96,64},{128,96},{160,128},{192,160},{224,192},{256... | collective-permute-start | bytes 49160 | tf_op jit(solution)/shard_map/ppermute | solution.py:25
  1997.7 23.7 %collective-permute-start.96 = (f32[4,1,8,128]{3,0,2,1:T(4,128)S(1)}, f32[4,1,8,128]{3,0,2,1:T(4,128)S(1)}, u32[]{:S(2)}, u32[]{:S(2)}) collective-permute-start(f32[4,1,8,128]{3,0,2,1:T(4,128)S(1)} %get-tuple-element.1232), channel_id=1, source_target_pairs={{32,0},{64,32},{96,64},{128,96},{160,128},{192,160},{224,192},{256... | collective-permute-start | bytes 49160 | tf_op jit(solution)/shard_map/ppermute | solution.py:25
  1999.6 21.8 collective-permute-start.97
  2032.0 21.1 collective-permute-start.104
  2034.0 27.7 %collective-permute-start.102 = (f32[16,1,8,128]{3,0,2,1:T(8,128)}, f32[16,1,8,128]{3,0,2,1:T(8,128)S(1)}, u32[]{:S(2)}, u32[]{:S(2)}) collective-permute-start(f32[16,1,8,128]{3,0,2,1:T(8,128)} %get-tuple-element.1190), channel_id=1, source_target_pairs={{32,0},{64,32},{96,64},{128,96},{160,128},{192,160},{224,192},{256... | collective-permute-start | bytes 196616 | tf_op jit(solution)/shard_map/ppermute | solution.py:25
  2035.9 25.8 %collective-permute-start.103 = (f32[16,1,8,128]{3,0,2,1:T(8,128)}, f32[16,1,8,128]{3,0,2,1:T(8,128)S(1)}, u32[]{:S(2)}, u32[]{:S(2)}) collective-permute-start(f32[16,1,8,128]{3,0,2,1:T(8,128)} %get-tuple-element.1189), channel_id=1, source_target_pairs={{0,32},{32,64},{64,96},{96,128},{128,160},{160,192},{192,224},{224... | collective-permute-start | bytes 196616 | tf_op jit(solution)/shard_map/ppermute | solution.py:22
  2077.2 26.5 %collective-permute-start.108 = (f32[16,1,8,128]{3,0,2,1:T(8,128)}, f32[16,1,8,128]{3,0,2,1:T(8,128)}, u32[]{:S(2)}, u32[]{:S(2)}) collective-permute-start(f32[16,1,8,128]{3,0,2,1:T(8,128)} %get-tuple-element.1182), channel_id=1, source_target_pairs={{32,0},{64,32},{96,64},{128,96},{160,128},{192,160},{224,192},{256... | collective-permute-start | bytes 196616 | tf_op jit(solution)/shard_map/ppermute | solution.py:25
  2079.1 24.6 %collective-permute-start.109 = (f32[16,1,8,128]{3,0,2,1:T(8,128)}, f32[16,1,8,128]{3,0,2,1:T(8,128)}, u32[]{:S(2)}, u32[]{:S(2)}) collective-permute-start(f32[16,1,8,128]{3,0,2,1:T(8,128)} %get-tuple-element.1181), channel_id=1, source_target_pairs={{0,32},{32,64},{64,96},{96,128},{128,160},{160,192},{192,224},{224... | collective-permute-start | bytes 196616 | tf_op jit(solution)/shard_map/ppermute | solution.py:22
  (161 other events, 1543.2 us)
where the time goes:
time: 2210 us; the launch traced here: 2200 us
  blocking collectives  1450 us (66%)
  starting transfers between devices  355 us (16%)
  waiting for transfers between devices  167 us (8%)
  local copies, waits for them, and re-layouts  87.9 us (4%)
  matrix products  69.1 us (3%)
  other arithmetic  37.2 us (2%)
  between operations  26.8 us (1%)
    psum x15, blocking collectives, coarse_total(): return lax.psum(scalar, ('gx', 'yz', 'lvl'))  1450 us
    ppermute x63, starting transfers between devices, with_halo(): lax.ppermute(lax.slice_in_dim(block, block.shape[dim] - width, None, axis...  230 us
    ppermute x63, starting transfers between devices, with_halo(): lax.ppermute(lax.slice_in_dim(block, 0, width, axis=dim), axis, backward)  124 us
    ppermute x63, waiting for transfers between devices, with_halo(): lax.ppermute(lax.slice_in_dim(block, block.shape[dim] - width, None, axis...  90.6 us
    ppermute x63, waiting for transfers between devices, with_halo(): lax.ppermute(lax.slice_in_dim(block, 0, width, axis=dim), axis, backward)  76.1 us
    dot_general x312, matrix products, select(): jnp.einsum('ij,jxyz->ixyz', blocks[k], jump_vals, precision=HIGHEST)  62.1 us
  transfers between devices with their start and end apart: 126, of which 51 were waited for; matrix products, arithmetic and copies ran while one was open for 4% of the time, Pallas kernels for 0%

commit v1 on v0

v1 whole, which is shorter than its diff:
```python
import functools
import math

import jax
import jax.numpy as jnp
import numpy as np
from jax import lax
from jax.experimental import pallas as pl
from jax.experimental.pallas import tpu as pltpu
from jax.sharding import PartitionSpec as P

NX = 16
NY = 128
NZ = 256
KINDS = 4
F32 = jnp.float32
BF16 = jnp.bfloat16
HIGHEST = lax.Precision.HIGHEST
LOW_EIG = 0.3
HIGH_EIG = 3.0
MIDDLE = 0.5 * (HIGH_EIG + LOW_EIG)
SPREAD = 0.5 * (HIGH_EIG - LOW_EIG)
SCALED = MIDDLE / SPREAD
RHO0 = 1.0 / SCALED
RHO1 = 1.0 / (2.0 * SCALED - RHO0)
RHO2 = 1.0 / (2.0 * SCALED - RHO1)
STEPS = ((RHO1 * RHO0, 2.0 * RHO1 / SPREAD), (RHO2 * RHO1, 2.0 * RHO2 / SPREAD))
BASIS = 8
VMEM_LIMIT = 48 * 2**20


def lanes(shape):
    return lax.broadcasted_iota(jnp.int32, shape, len(shape) - 1)


def roll(x, shift, axis=None):
    axis = x.ndim - 1 if axis is None else axis
    shift = shift % x.shape[axis]
    return x if shift == 0 else pltpu.roll(x, shift, axis)


def call(body, name, out_shape, in_specs, scratch=(), flops=1000000):
    single = not isinstance(out_shape, (tuple, list))
    outs = [out_shape] if single else list(out_shape)
    vm = pl.BlockSpec(memory_space=pltpu.VMEM)
    return pl.pallas_call(
        body,
        out_shape=outs[0] if single else outs,
        in_specs=[pl.BlockSpec(memory_space=pltpu.SMEM) if s else vm for s in in_specs],
        out_specs=vm if single else [vm] * len(outs),
        scratch_shapes=list(scratch),
        compiler_params=pltpu.CompilerParams(vmem_limit_bytes=VMEM_LIMIT),
        cost_estimate=pl.CostEstimate(flops=flops, bytes_accessed=1000000, transcendentals=0),
        name=name,
    )


def f32s(*shape):
    return jax.ShapeDtypeStruct(shape, F32)


def split3(x):
    high = x.astype(BF16).astype(F32)
    low = x - high
    return high, low


def stack_hlh(x):
    high, low = split3(x)
    return jnp.concatenate([high, low, high], axis=0).astype(BF16)


def mm(a, b):
    return jnp.dot(a, b, preferred_element_type=F32)


def edges_body(pos, res, cf, out):
    first = pos[2] == 0
    lane = lanes((16, 128))
    acc = [jnp.zeros((16, 128), F32)]
    packed = jnp.zeros((16, 128), F32)
    packed_cf = jnp.zeros((8, 128), F32)
    lane8 = lanes((8, 128))
    for y in range(8):
        rows = res[pl.ds(y, 64, stride=8), :]
        rows = jnp.where(first, roll(rows, 4), rows)
        for j in range(4):
            at = 32 * j + 4 * y
            packed = jnp.where(
                (lane >= at) & (lane < at + 4), roll(rows[16 * j : 16 * j + 16], at), packed
            )
        rows = cf[pl.ds(y, 8, stride=8), :]
        rows = jnp.where(first, roll(rows, 12), rows)
        at = 12 * y
        packed_cf = jnp.where((lane8 >= at) & (lane8 < at + 12), roll(rows, at), packed_cf)
    out[0:16, :] = packed
    out[16:24, :] = packed_cf


def slots_body(pos, res, cf, halo, out, rows, rows_cf):
    first = pos[2] == 0
    lane = lanes((64, 128))
    lane8 = lanes((8, 128))
    for y in range(8):
        mine = res[pl.ds(y, 64, stride=8), :]
        got = jnp.concatenate([roll(halo[0:16, :], -(32 * j + 4 * y)) for j in range(4)], axis=0)
        rows[0, y] = jnp.where(lane >= 124, jnp.where(first, 0.0, roll(got, 124)), mine)
        rows[1, y] = mine
        rows[2, y] = jnp.where(lane < 4, jnp.where(first, got, 0.0), mine)
        mine = cf[pl.ds(y, 8, stride=8), :]
        got = roll(halo[16:24, :], -12 * y)
        rows_cf[0, y] = jnp.where(lane8 >= 116, jnp.where(first, 0.0, roll(got, 116)), mine)
        rows_cf[1, y] = mine
        rows_cf[2, y] = jnp.where(lane8 < 12, jnp.where(first, got, 0.0), mine)
    for g in range(NX):
        source = 0 if g == 0 else (2 if g == NX - 1 else 1)
        acc = jnp.zeros((64, 128), F32)
        for y in range(8):
            acc = jnp.where(lane // 16 == y, roll(rows[source, y], 16 * y - (8 * g - 4)), acc)
        out[g, 0:64, :] = acc
        source = 0 if g <= 1 else (2 if g >= NX - 2 else 1)
        for h in range(2):
            acc = jnp.zeros((8, 128), F32)
            for y in range(4):
                acc = jnp.where(
                    lane8 // 32 == y, roll(rows_cf[source, 4 * h + y], 32 * y - (8 * g - 12)), acc
                )
            out[g, 64 + 8 * h : 72 + 8 * h, :] = acc


def fine_update(x, u, r, sol, inv, step):
    if step is None:
        return
    keep, gain = STEPS[step]
    new = keep * u[x] + gain * (inv[x] * r[x])
    u[x] = new
    sol[x] = sol[x] + new


def fine_apply(u, r, w, coef, wide, spread, px, qx, step, sol, inv):
    def first(x, carry):
        prod = mm(wide[...], stack_hlh(u[x]))

        def pick(base, row):
            total = w[x, pl.ds(row, 1), :] * prod[base : base + 16]
            for k in range(1, KINDS):
                total = total + w[x, pl.ds(row + k, 1), :] * prod[base + 16 * k : base + 16 * k + 16]
            return total

        px[x + 1] = pick(64, 0)
        py = pick(128, 4)
        pz = pick(192, 8)
        qx[x] = pick(256, 12)
        qy = pick(320, 16)
        qz = pick(384, 20)
        flux = jnp.concatenate(
            [py - roll(qy, -16), roll(py, 16) - qy, pz - roll(qz, -1), roll(pz, 1) - qz], axis=0
        )
        high, low = split3(flux)
        faces = mm(spread[...], jnp.concatenate([high, low], axis=0).astype(BF16))
        r[x] = r[x] - (coef[x, pl.ds(0, 1), :] * prod[0:64] + faces)
        return carry

    lax.fori_loop(0, NX, first, 0)

    def second(x, carry):
        r[x, 48:64, :] = r[x, 48:64, :] - (px[x + 1] - qx[x + 1])
        r[x, 0:16, :] = r[x, 0:16, :] + (px[x] - qx[x])
        fine_update(x, u, r, sol, inv, step)
        return carry

    lax.fori_loop(0, NX, second, 0)


def fine_pre_body(
    pos,
    own,
    below,
    above,
    wide,
    spread,
    diag_w,
    diag_e,
    down,
    mid_diag_w,
    mid_diag_e,
    sol,
    r,
    w,
    coef,
    inv,
    cfm,
    send_up,
    send_down,
    u,
    px,
    qx,
    gather,
):
    low = lanes((64, 128)) < 64
    low8 = lanes((8, 128)) < 64
    lane8 = lanes((8, 128))
    place = lanes((1, 256))
    y_at = pos[0] * 8 - 4 + place // 16
    z_at = pos[1] * 8 - 4 + place % 16
    inside = (y_at >= 0) & (y_at < NY) & (z_at >= 0) & (z_at < NZ)
    has_y = inside & (y_at < NY - 1)
    has_z = inside & (z_at < NZ - 1)
    inside_f = jnp.where(inside, 1.0, 0.0)
    px[0] = jnp.zeros((16, 256), F32)
    qx[NX] = jnp.zeros((16, 256), F32)
    cfm[:, 0:128] = jnp.zeros((128, 128), F32)
    cfm[:, 896:1024] = jnp.zeros((128, 128), F32)
    for x in range(NX):
        turned = roll(own[x, 0:64, :], 64)
        r[x, :, 0:128] = jnp.where(low, roll(below[x, 0:64, :], 64), turned)
        r[x, :, 128:256] = jnp.where(low, turned, roll(above[x, 0:64, :], 64))
        blocks = [
            below[x, 64:72, :],
            below[x, 72:80, :],
            own[x, 64:72, :],
            own[x, 72:80, :],
            above[x, 64:72, :],
            above[x, 72:80, :],
        ]
        for m in range(6):
            gather[pl.ds(128 * m + x, 8, stride=16), :] = blocks[m]
        for half in range(2):
            acc = jnp.zeros((8, 128), F32)
            for row in range(8):
                n = 8 * half + row
                acc = jnp.where(
                    lane8 // 16 == row,
                    roll(blocks[1 + n // 4], 16 * row - (n % 4) * 32 - 8),
                    acc,
                )
            coef[x, :, 128 * half : 128 * half + 128] = acc
    for m in range(6):
        cfm[:, 128 * (m + 1) : 128 * (m + 2)] = gather[128 * m : 128 * m + 128, :]
    for x in range(NX):
        rows = coef[x]
        opens = [
            inside & (rows[4:5] == 0.0) if x < NX - 1 else jnp.zeros((1, 256), jnp.bool_),
            has_y & (rows[5:6] == 0.0),
            has_z & (rows[6:7] == 0.0),
        ]
        plus = [
            [jnp.where(opens[d] & (rows[1 + d : 2 + d] == float(k)), 1.0, 0.0) for k in range(KINDS)]
            for d in range(3)
        ]
        plus_all = jnp.concatenate(plus[0] + plus[1] + plus[2] , axis=0)
        w[x, 0:12, :] = plus_all
        if x == 0:
            w[0, 12:16, :] = jnp.zeros((4, 256), F32)
        if x < NX - 1:
            w[x + 1, 12:16, :] = plus_all[0:4]
        w[x, 16:20, :] = roll(plus_all[4:8], 16)
        w[x, 20:24, :] = roll(plus_all[8:12], 1)

    def prepare(x, carry):
        ws = w[x]
        ws = jnp.concatenate([ws, ws, ws, jnp.zeros((8, 256), F32)], axis=0).astype(BF16)
        diag = diag_e[...] * coef[x, pl.ds(0, 1), :] + mm(diag_w[...], ws)
        inverse = jnp.where(inside, 1.0 / diag, 0.0)
        inv[x] = inverse
        update = inverse * r[x] / MIDDLE
        u[x] = update
        sol[x] = update
        return carry

    lax.fori_loop(0, NX, prepare, 0)
    fine_apply(u, r, w, coef, wide, spread, px, qx, 0, sol, inv)
    fine_apply(u, r, w, coef, wide, spread, px, qx, 1, sol, inv)
    fine_apply(u, r, w, coef, wide, spread, px, qx, None, sol, inv)
    lane16 = lanes((16, 128)) % 16 // 4
    for x in range(NX):
        rx = r[x]
        ws = w[x]
        ws = jnp.concatenate([ws, ws, ws, jnp.zeros((8, 256), F32)], axis=0).astype(BF16)
        rhs = mm(down[...], stack_hlh(rx))
        diag = mid_diag_e[...] * coef[x, 0:1, :] + mm(mid_diag_w[...], ws)
        update = jnp.where(inside, 1.0 / diag, 0.0) * rhs / MIDDLE
        for half in range(2):
            piece = update[:, 128 * half : 128 * half + 128]
            send_up[pl.ds(128 * half + x, 8, stride=16), :] = piece
            send_down[pl.ds(128 * half + x, 8, stride=16), :] = piece
        mine = jnp.where(low, roll(rx[:, 0:128], 64), roll(rx[:, 128:256], 64))
        up = jnp.zeros((16, 128), F32)
        dn = jnp.zeros((16, 128), F32)
        for j in range(4):
            part = mine[16 * j : 16 * j + 16]
            up = jnp.where(lane16 == j, roll(part, 4 * j - 8), up)
            dn = jnp.where(lane16 == j, roll(part, 4 * j - 4), dn)
        send_up[256 + 16 * x : 272 + 16 * x, :] = up
        send_down[256 + 16 * x : 272 + 16 * x, :] = dn


def mid_z_body(own, dn, up, r, cfm, slab, fwd, bwd, frz):
    lane = lanes((128, 128))
    for m in range(4):
        acc = jnp.zeros((128, 128), F32)
        for n in range(4):
            y = 4 * (m - 1) + n
            if y < -1 or y > 8:
                continue
            to = 32 * n
            half, at = (y + 4) // 8, 16 * ((y + 4) % 8)
            rows = slice(128 * half, 128 * half + 128)
            acc = jnp.where((lane >= to + 12) & (lane < to + 20), roll(own[rows, :], to + 8 - at), acc)
            acc = jnp.where((lane >= to + 3) & (lane < to + 12), roll(dn[rows, :], to - at), acc)
            acc = jnp.where((lane >= to + 20) & (lane < to + 29), roll(up[rows, :], to + 16 - at), acc)
        if 1 <= m <= 2:
            slab[:, 128 * (m - 1) : 128 * m] = acc
        if m <= 2:
            fwd[128 * m : 128 * m + 128, :] = acc
        if m >= 1:
            bwd[128 * (m - 1) : 128 * m, :] = acc
    fwd[896:912, :] = cfm[32:48, 256:384]
    fwd[912:928, :] = cfm[80:96, 256:384]
    low = lanes((64, 128)) < 64
    l16 = lanes((16, 128)) % 16
    for x in range(NX):
        rx = r[x]
        mine = jnp.where(low, roll(rx[:, 0:128], 64), roll(rx[:, 128:256], 64))
        pack_dn = dn[256 + 16 * x : 272 + 16 * x, :]
        pack_up = up[256 + 16 * x : 272 + 16 * x, :]
        for j in range(4):
            rows = slice(16 * j, 16 * j + 16)
            part = jnp.where(l16 < 4, roll(pack_dn, -4 * j), mine[rows])
            part = jnp.where(l16 >= 12, roll(pack_up, 12 - 4 * j), part)
            frz[x, rows, :] = part
    for x in range(8):
        fwd[384 + 64 * x : 448 + 64 * x, :] = jnp.where(low, roll(frz[x], 64), frz[x + 8])
        bwd[384 + 64 * x : 448 + 64 * x, :] = jnp.where(low, frz[x], roll(frz[x + 8], 64))


MID_PAIRS = ((0, 0), (0, 1), (0, 2), (0, 3), (1, 1), (1, 2), (1, 3), (2, 2), (2, 3), (3, 3))
MID_SLOT = {}
for _n, (_i, _j) in enumerate(MID_PAIRS):
    MID_SLOT[(_i, _j)] = _n
    MID_SLOT[(_j, _i)] = _n
LOWS = ((0, 1, 2, 3), (0, 1, 4, 5), (0, 2, 4, 6))
HIGHS = ((4, 5, 6, 7), (2, 3, 6, 7), (1, 3, 5, 7))


def ahead(v, d):
    if d == 0:
        return roll(v, -1, 0)
    return roll(v, -32 if d == 1 else -1, 1)


def behind(v, d):
    if d == 0:
        return roll(v, 1, 0)
    return roll(v, 32 if d == 1 else 1, 1)


def mid_setup(pos, scal, cfm, sel, faces, inv, diag):
    place = lanes((16, 1024))
    x_at = lax.broadcasted_iota(jnp.int32, (16, 1024), 0)
    y_at = pos[0] * 8 - 12 + place // 32
    z_at = pos[1] * 8 - 12 + place % 32
    domain = (y_at >= 0) & (y_at < NY) & (z_at >= 0) & (z_at < NZ)
    known = domain & (place >= 128) & (place < 896)
    lasts = (x_at < NX - 1, y_at < NY - 1, z_at < NZ - 1)
    for d in range(3):
        is_open = domain & lasts[d] & (cfm[64 + 16 * d : 80 + 16 * d, :] == 0.0)
        sel[d] = jnp.where(is_open, cfm[16 + 16 * d : 32 + 16 * d, :], 4.0)
    coef = cfm[0:16, :]

    def table(n, carry):
        at = 64 + n
        for d in range(3):
            kind = sel[d]
            value = jnp.zeros((16, 1024), F32)
            for k in range(KINDS):
                value = jnp.where(kind == float(k), scal[at + 16 * k], value)
            faces[d, n] = value
        return carry

    lax.fori_loop(0, 16, table, 0)
    if inv is None:
        return known
    for i in range(8):
        total = coef * scal[9 * i]
        for d in range(3):
            if i in HIGHS[d]:
                total = total + faces[d, 5 * HIGHS[d].index(i)]
            else:
                total = total + behind(faces[d, 5 * LOWS[d].index(i)], d)
        if diag is not None:
            diag[i] = total
        inv[i] = jnp.where(known, 1.0 / total, 0.0)
    return known


def mid_apply(v, r, scal, cfm, faces, jump, flux):
    for d in range(3):
        for j in range(4):
            jump[j] = v[HIGHS[d][j]] - ahead(v[LOWS[d][j]], d)

        def face(c, carry):
            at = pl.ds(pl.multiple_of(c * 128, 128), 128)
            jumps = [jump[j, :, at] for j in range(4)]
            for i in range(4):
                total = faces[d, 4 * i, :, at] * jumps[0]
                for j in range(1, 4):
                    total = total + faces[d, 4 * i + j, :, at] * jumps[j]
                flux[4 * d + i, :, at] = total
            return carry

        lax.fori_loop(0, 8, face, 0)

    def block(c, carry):
        at = pl.ds(pl.multiple_of(c * 128, 128), 128)
        values = [v[j, :, at] for j in range(8)]
        coef = cfm[0:16, at]
        for i in range(8):
            total = scal[8 * i] * values[0]
            for j in range(1, 8):
                total = total + scal[8 * i + j] * values[j]
            r[i, :, at] = r[i, :, at] - coef * total
        return carry

    lax.fori_loop(0, 8, block, 0)
    for d in range(3):
        for j in range(4):
            value = flux[4 * d + j]
            r[HIGHS[d][j]] = r[HIGHS[d][j]] - value
            r[LOWS[d][j]] = r[LOWS[d][j]] + behind(value, d)


def mid_step(step, u, r, sol, inv):
    keep, gain = STEPS[step]
    for i in range(8):
        new = keep * u[i] + gain * (inv[i] * r[i])
        u[i] = new
        sol[i] = sol[i] + new


def mid_pre_body(
    pos, scal, slab, below, above, cfm_in, sol, r, coarse, send_up, send_down,
    cfm, sel, faces, inv, diag, u, jump, flux,
):
    cfm[...] = cfm_in[...]
    cfm[32:48, 0:128] = below[896:912, :]
    cfm[80:96, 0:128] = below[912:928, :]
    for i in range(8):
        rows = slice(16 * i, 16 * i + 16)
        for m in range(3):
            u[i, :, 128 * m : 128 * m + 128] = below[128 * m + 16 * i : 128 * m + 16 * i + 16, :]
            u[i, :, 128 * (m + 5) : 128 * (m + 6)] = above[128 * m + 16 * i : 128 * m + 16 * i + 16, :]
        u[i, :, 384:640] = slab[rows, :]
    mid_setup(pos, scal, cfm, sel, faces, inv, diag)
    for i in range(8):
        r[i] = (MIDDLE * diag[i]) * u[i]
        sol[i] = u[i]
    mid_apply(u, r, scal, cfm, faces, jump, flux)
    mid_step(0, u, r, sol, inv)
    mid_apply(u, r, scal, cfm, faces, jump, flux)
    mid_step(1, u, r, sol, inv)
    mid_apply(u, r, scal, cfm, faces, jump, flux)
    total = r[0]
    for i in range(1, 8):
        total = total + r[i]
    coarse[0] = total
    center = cfm[0:16, :] * scal[128]
    for d in range(3):
        kind = sel[d]
        value = jnp.zeros((16, 1024), F32)
        for k in range(KINDS):
            value = jnp.where(kind == float(k), scal[129 + k], value)
        coarse[2 + d] = value
        center = center + value + behind(value, d)
    coarse[1] = center
    l32 = lanes((16, 768)) % 32
    for out, first in ((send_up, 6), (send_down, 18)):
        acc = jnp.zeros((16, 768), F32)
        for f in range(4):
            acc = jnp.where(l32 // 8 == f, roll(coarse[f, :, 128:896], 8 * f - first), acc)
        out[0] = acc
        out[1] = roll(coarse[4, :, 128:896], -first)


def coarse_z_body(own, dn, up, slab, fwd, bwd):
    lane = lanes((16, 128))
    for f in range(5):
        part = 0 if f < 4 else 1
        shift = 8 * f if f < 4 else 0
        for m in range(10):
            acc = jnp.zeros((16, 128), F32)
            for n in range(2):
                y = 2 * m + n - 6
                tile, at = (y + 12) // 4, 32 * ((y + 12) % 4)
                to = 64 * n
                mine = own[f, :, 128 * tile : 128 * tile + 128]
                left = dn[part, :, 128 * (tile - 1) : 128 * tile]
                right = up[part, :, 128 * (tile - 1) : 128 * tile]
                acc = jnp.where(
                    (lane >= to + 22) & (lane < to + 42), roll(mine, to + 22 - (at + 6)), acc
                )
                acc = jnp.where(
                    (lane >= to + 14) & (lane < to + 22), roll(left, to + 14 - (at + shift)), acc
                )
                acc = jnp.where(
                    (lane >= to + 42) & (lane < to + 50), roll(right, to + 42 - (at + shift)), acc
                )
            slab[f, :, 128 * m : 128 * m + 128] = acc
            if m < 4:
                fwd[f, :, 128 * m : 128 * m + 128] = acc
            if m >= 6:
                bwd[f, :, 128 * (m - 6) : 128 * (m - 5)] = acc


def two_sum(a, b):
    s = a + b
    t = s - a
    return s, (a - (s - t)) + (b - t)


def halves(a):
    t = a * 4097.0
    high = t - (t - a)
    return high, a - high


def two_prod(a, b):
    ah, al = halves(a)
    bh, bl = halves(b)
    p = a * b
    return p, ((ah * bh - p) + ah * bl + al * bh) + al * bl


def pair_mul(a, b):
    p, e = two_prod(a[0], b[0])
    return two_sum(p, e + (a[0] * b[1] + a[1] * b[0]))


def pair_sub(a, b):
    s, e = two_sum(a[0], -b[0])
    return two_sum(s, e + (a[1] - b[1]))


def pair_div(a, b):
    first = a[0] / b[0]
    rest = pair_sub(a, pair_mul((first, jnp.zeros_like(first)), b))
    return two_sum(first, rest[0] / b[0])


START = (0, 9, 17, 24, 30, 35, 39, 42)
PAIRS = sum(9 - i for i in range(BASIS))


def krylov_body(scal, own, below, above, basis, gram, field, hold):
    for f in range(5):
        field[f, :, 0:512] = below[f]
        field[f, :, 512:1792] = own[f]
        field[f, :, 1792:2304] = above[f]
    center, half = scal[133], scal[134]
    lane8 = lanes((8, 128))

    def apply(v):
        total = field[1] * v
        for d in range(3):
            cond = field[2 + d]
            axis, step = ((0, 1), (1, 64), (1, 1))[d]
            total = total - cond * roll(v, -step, axis) - roll(cond * v, step, axis)
        return total

    def compact(v):
        acc = jnp.zeros((8, 128), F32)
        for t in range(2):
            for y in range(8):
                tile, at = (y + 14) // 2, 64 * ((y + 14) % 2) + 28
                to = 64 * t + 8 * y
                piece = v[8 * t : 8 * t + 8, 128 * tile : 128 * tile + 128]
                acc = jnp.where((lane8 >= to) & (lane8 < to + 8), roll(piece, to - at), acc)
        return acc

    before = None
    now = field[0]
    for j in range(BASIS):
        basis[j] = now[:, 384:1920]
        hold[j] = compact(now)
        image = apply(now)
        hold[BASIS + j] = compact(image)
        if j + 1 < BASIS:
            nxt = (image - center * now) * half
            if j > 0:
                nxt = 2.0 * nxt - before
            before, now = now, nxt
    high_rows, low_rows = [], []
    for i in range(BASIS):
        for j in range(i, BASIS + 1):
            other = hold[BASIS + j] if j < BASIS else hold[0]
            p, e = two_prod(hold[i], other)
            high_rows.append(p)
            low_rows.append(e)
    high = jnp.stack(high_rows)
    low = jnp.stack(low_rows)
    for axis, shifts in ((1, (4, 2, 1)), (2, (64, 32, 16, 8, 4, 2, 1))):
        for s in shifts:
            high, e = two_sum(high, roll(high, s, axis))
            low = low + roll(low, s, axis) + e
    row = jnp.zeros((8, 128), F32)
    for n in range(PAIRS):
        row = jnp.where(lane8 == n, high[n], row)
        row = jnp.where(lane8 == 64 + n, low[n], row)
    for m in range(64):
        gram[8 * m : 8 * m + 8, :] = row


def mid_post_body(
    pos, scal, gram, basis, cfm, pre, res, out,
    sel, faces, inv, u, r, sol, jump, flux,
):
    high = gram[...].reshape(64, 8, 128)
    low = jnp.zeros((64, 8, 128), F32)
    count = 64
    while count > 1:
        count //= 2
        high, e = two_sum(high[:count], high[count : 2 * count])
        low = low[:count] + low[count : 2 * count] + e
    high, low = high[0], low[0]
    for s in (4, 2, 1):
        high, e = two_sum(high, roll(high, s, 0))
        low = low + roll(low, s, 0) + e
    low = low + roll(high, 64)
    high, low = two_sum(high, low)
    lane = lanes((8, 128))
    sub = lax.broadcasted_iota(jnp.int32, (8, 128), 0)
    mat_h = jnp.zeros((8, 128), F32)
    mat_l = jnp.zeros((8, 128), F32)
    for i in range(BASIS):
        here = (sub == i) & (lane >= i) & (lane <= BASIS)
        mat_h = jnp.where(here, roll(high, i - START[i]), mat_h)
        mat_l = jnp.where(here, roll(low, i - START[i]), mat_l)
        for j in range(i + 1, BASIS):
            here = (sub == j) & (lane == i)
            shift = i - (START[i] + j - i)
            mat_h = jnp.where(here, roll(high, shift), mat_h)
            mat_l = jnp.where(here, roll(low, shift), mat_l)

    def spread_at(v, row, col):
        return jnp.broadcast_to(v[row : row + 1, col : col + 1], (8, 128))

    answers = []
    pivots = []
    for k in range(BASIS):
        start = spread_at(high, 0, START[k])
        piv = (spread_at(mat_h, k, k), spread_at(mat_l, k, k))
        good = jnp.abs(piv[0]) > 1e-12 * jnp.abs(start)
        safe = (jnp.where(good, piv[0], 1.0), jnp.where(good, piv[1], 0.0))
        pivots.append((safe, good))
        row = (
            jnp.broadcast_to(mat_h[k : k + 1, :], (8, 128)),
            jnp.broadcast_to(mat_l[k : k + 1, :], (8, 128)),
        )
        col = (
            jnp.broadcast_to(mat_h[:, k : k + 1], (8, 128)),
            jnp.broadcast_to(mat_l[:, k : k + 1], (8, 128)),
        )
        factor = pair_div(col, safe)
        use = good & (sub != k)
        factor = (jnp.where(use, factor[0], 0.0), jnp.where(use, factor[1], 0.0))
        mat_h, mat_l = pair_sub((mat_h, mat_l), pair_mul(factor, row))
    for k in range(BASIS):
        safe, good = pivots[k]
        value = pair_div((spread_at(mat_h, k, BASIS), spread_at(mat_l, k, BASIS)), safe)[0]
        answers.append(jnp.where(good, value, 0.0))
    weights = [jnp.concatenate([a, a], axis=0) for a in answers]
    lane16 = lanes((16, 128))
    tiles = []
    for m in range(12):
        total = weights[0] * basis[0, :, 128 * m : 128 * m + 128]
        for j in range(1, BASIS):
            total = total + weights[j] * basis[j, :, 128 * m : 128 * m + 128]
        tiles.append(total)
    for m in range(8):
        acc = jnp.zeros((16, 128), F32)
        if 1 <= m <= 6:
            for n in range(4):
                y = 4 * m + n - 12
                tile, at = (y + 14) // 2 - 3, 64 * ((y + 14) % 2)
                to = 32 * n
                acc = jnp.where(
                    (lane16 >= to + 5) & (lane16 < to + 27), roll(tiles[tile], to + 5 - (at + 21)), acc
                )
        for i in range(8):
            u[i, :, 128 * m : 128 * m + 128] = acc
    mid_setup(pos, scal, cfm, sel, faces, inv, None)
    for i in range(8):
        r[i] = res[i]
        sol[i] = pre[i] + u[i]
    mid_apply(u, r, scal, cfm, faces, jump, flux)
    for i in range(8):
        new = inv[i] * r[i] / MIDDLE
        u[i] = new
        sol[i] = sol[i] + new
    mid_apply(u, r, scal, cfm, faces, jump, flux)
    mid_step(0, u, r, sol, inv)
    mid_apply(u, r, scal, cfm, faces, jump, flux)
    mid_step(1, u, r, sol, inv)
    for i in range(8):
        for half in range(2):
            acc = jnp.zeros((16, 128), F32)
            for n in range(8):
                y = 8 * half + n - 4
                tile, at = (y + 12) // 4, 32 * ((y + 12) % 4) + 8
                acc = jnp.where(
                    lane16 // 16 == n,
                    roll(sol[i, :, 128 * tile : 128 * tile + 128], 16 * n - at),
                    acc,
                )
            out[128 * half + 16 * i : 128 * half + 16 * i + 16, :] = acc


def fine_post_body(
    mid, pre, frz, below, above, w, coef, inv, wide, spread, lift, out, u, r, sol, px, qx,
):
    low = lanes((64, 128)) < 64
    px[0] = jnp.zeros((16, 256), F32)
    qx[NX] = jnp.zeros((16, 256), F32)
    for x in range(NX):
        turned = roll(frz[x], 64)
        at = 384 + 64 * (x % 8)
        down = below[at : at + 64, :]
        over = above[at : at + 64, :]
        if x >= 8:
            down = roll(down, 64)
        else:
            over = roll(over, 64)
        r[x, :, 0:128] = jnp.where(low, down, turned)
        r[x, :, 128:256] = jnp.where(low, turned, over)
        halved = [mid[pl.ds(128 * half + x, 8, stride=16), :] for half in range(2)]
        high, rest = split3(jnp.concatenate(halved, axis=1))
        stacked = jnp.concatenate([high, rest, high, jnp.zeros((8, 256), F32)], axis=0)
        lifted = mm(lift[...], stacked.astype(BF16))
        u[x] = lifted
        sol[x] = pre[x] + lifted
    fine_apply(u, r, w, coef, wide, spread, px, qx, None, sol, inv)

    def begin(x, carry):
        new = inv[x] * r[x] / MIDDLE
        u[x] = new
        sol[x] = sol[x] + new
        return carry

    lax.fori_loop(0, NX, begin, 0)
    fine_apply(u, r, w, coef, wide, spread, px, qx, 0, sol, inv)
    fine_apply(u, r, w, coef, wide, spread, px, qx, 1, sol, inv)
    fine_apply(u, r, w, coef, wide, spread, px, qx, None, sol, inv)
    lane = lanes((64, 128))
    for x in range(NX):
        acc = jnp.zeros((64, 128), F32)
        for part, ref in enumerate((sol, r)):
            for y in range(8):
                half, at = (y + 4) // 8, 16 * ((y + 4) % 8) + 4
                acc = jnp.where(
                    lane // 8 == 8 * part + y,
                    roll(ref[x, :, 128 * half : 128 * half + 128], 64 * part + 8 * y - at),
                    acc,
                )
        out[x] = acc


def unpack_body(got, first, second):
    lane = lanes((64, 128)) // 8
    for part, out in enumerate((first, second)):
        for y in range(8):
            acc = jnp.zeros((64, 128), F32)
            for g in range(NX):
                acc = jnp.where(lane == g, roll(got[g], 8 * g - 8 * y - 64 * part), acc)
            out[pl.ds(y, 64, stride=8), :] = acc


def trace_tables():
    high = np.zeros((3, 16, 64), np.float32)
    low = np.zeros((3, 16, 64), np.float32)
    for p in range(4):
        for q in range(4):
            for d in range(3):
                for table, at in ((high, 3), (low, 0)):
                    index = [p, q]
                    index.insert(d, at)
                    table[d, 4 * p + q, 16 * index[0] + 4 * index[1] + index[2]] = 1.0
    return high, low


def mid_traces():
    high = np.zeros((3, 4, 8), np.float32)
    low = np.zeros((3, 4, 8), np.float32)
    for d in range(3):
        for n in range(4):
            high[d, n, HIGHS[d][n]] = 1.0
            low[d, n, LOWS[d][n]] = 1.0
    return high, low


def prolong_tables():
    node_points = jnp.array(
        [-1.0, -1.0 / math.sqrt(5.0), 1.0 / math.sqrt(5.0), 1.0], dtype=jnp.float32
    )
    basis_table = jnp.stack([(1.0 - node_points) * 0.5, (1.0 + node_points) * 0.5], axis=1)
    volume = (
        basis_table[:, None, None, :, None, None]
        * basis_table[None, :, None, None, :, None]
        * basis_table[None, None, :, None, None, :]
    ).reshape(64, 8)
    surface = (basis_table[:, None, :, None] * basis_table[None, :, None, :]).reshape(16, 4)
    return (volume, surface)


def cut(x):
    return lax.reduce_precision(x, 8, 7)


def two_parts(x):
    high = cut(x)
    return high, cut(x - high)


def three_parts(x):
    high = cut(x)
    rest = x - high
    mid = cut(rest)
    return high, mid, cut(rest - mid)


def tables(element, faces):
    volume, surface = prolong_tables()
    elem_mid = jnp.dot(volume.T, jnp.dot(element, volume, precision=HIGHEST), precision=HIGHEST)
    face_mid = jnp.einsum("kij,jb->kib", faces, surface, precision=HIGHEST)
    face_mid = jnp.einsum("ia,kib->kab", surface, face_mid, precision=HIGHEST)
    elem_coarse = jnp.sum(elem_mid)
    face_coarse = jnp.sum(face_mid, axis=(1, 2))
    high, low = trace_tables()
    both = np.concatenate([high, low], axis=0)
    rows = jnp.einsum("kij,djm->dkim", faces, both, precision=HIGHEST).reshape(384, 64)
    wide = jnp.concatenate([element, rows], axis=0)
    wh, wl = two_parts(wide)
    wide = jnp.concatenate([wh, wh, wl], axis=1).astype(BF16)
    spread = np.concatenate([high[1], -low[1], high[2], -low[2]], axis=0).T
    spread = np.concatenate([spread, spread], axis=1)
    face_diag = jnp.diagonal(faces, axis1=1, axis2=2)
    diag = jnp.einsum("dim,ki->mdk", both, face_diag, precision=HIGHEST).reshape(64, 24)
    diag_w = jnp.concatenate(three_parts(diag) + (jnp.zeros((64, 8), F32),), axis=1).astype(BF16)
    diag_e = jnp.diagonal(element)[:, None]
    mh, ml = mid_traces()
    both = np.concatenate([mh, ml], axis=0)
    diag = jnp.einsum(
        "dim,ki->mdk", both, jnp.diagonal(face_mid, axis1=1, axis2=2), precision=HIGHEST
    ).reshape(8, 24)
    mid_diag_w = jnp.concatenate(three_parts(diag) + (jnp.zeros((8, 8), F32),), axis=1).astype(BF16)
    mid_diag_e = jnp.diagonal(elem_mid)[:, None]
    vh, vl = two_parts(volume)
    down = jnp.concatenate([vh.T, vh.T, vl.T], axis=1).astype(BF16)
    lift = jnp.concatenate([vh, vh, vl, jnp.zeros((64, 8), F32)], axis=1).astype(BF16)
    least = 0.1 * elem_coarse
    most = 1.35 * elem_coarse + 9.0 * jnp.max(jnp.abs(face_coarse))
    half = 0.5 * (most - least)
    half = jnp.where(jnp.abs(half) > 0.0, half, 1.0)
    scal = jnp.concatenate(
        [
            elem_mid.reshape(-1),
            face_mid.reshape(-1),
            elem_coarse[None],
            face_coarse,
            (0.5 * (most + least))[None],
            (1.0 / half)[None],
            jnp.zeros((9,), F32),
        ]
    )
    return (
        wide,
        jnp.asarray(spread, BF16),
        diag_w,
        diag_e,
        down,
        mid_diag_w,
        mid_diag_e,
        lift,
        scal,
    )


def local(residual, coefficient, element, faces, kind, flag):
    shift_up = [(i, i + 1) for i in range(15)]
    shift_dn = [(i + 1, i) for i in range(15)]

    def z_index(zb):
        return (zb % 16) * 2 + zb // 16

    z_up = [(z_index(i), z_index(i + 1)) for i in range(31)]
    z_dn = [(z_index(i + 1), z_index(i)) for i in range(31)]
    z_axes = ("gx", "lvl")
    side = lax.axis_index("lvl")
    pos = jnp.stack(
        [
            lax.axis_index("yz"),
            side * 16 + lax.axis_index("gx"),
            side,
            jnp.zeros_like(side),
        ]
    ).astype(jnp.int32)
    wide, spread, diag_w, diag_e, down, mid_diag_w, mid_diag_e, lift, scal = tables(element, faces)
    res = residual.reshape(512, 128)
    cf = jnp.concatenate(
        [
            coefficient,
            kind[1].astype(F32),
            kind[3].astype(F32),
            kind[5].astype(F32),
            flag[1].astype(F32),
            flag[3].astype(F32),
            flag[5].astype(F32),
            jnp.zeros_like(coefficient),
        ],
        axis=0,
    ).reshape(64, 128)
    edges = call(edges_body, "edges", f32s(24, 128), (1, 0, 0))(pos, res, cf)
    halo = lax.ppermute(edges, "lvl", [(0, 1), (1, 0)])
    slots = call(
        slots_body,
        "slots",
        f32s(16, 80, 128),
        (1, 0, 0, 0),
        [pltpu.VMEM((3, 8, 64, 128), F32), pltpu.VMEM((3, 8, 8, 128), F32)],
    )(pos, res, cf, halo)
    own = lax.all_to_all(slots, "gx", 0, 0, tiled=True)
    below = lax.ppermute(own, "yz", shift_up)
    above = lax.ppermute(own, "yz", shift_dn)
    plane = (NX, 64, 256)
    pre, r, w, coef, inv, cfm, send_up, send_down = call(
        fine_pre_body,
        "fine_pre",
        [
            f32s(*plane),
            f32s(*plane),
            f32s(NX, 24, 256),
            f32s(NX, 8, 256),
            f32s(*plane),
            f32s(128, 1024),
            f32s(512, 128),
            f32s(512, 128),
        ],
        (1,) + (0,) * 10,
        [
            pltpu.VMEM(plane, F32),
            pltpu.VMEM((NX + 1, 16, 256), F32),
            pltpu.VMEM((NX + 1, 16, 256), F32),
            pltpu.VMEM((768, 128), F32),
        ],
    )(pos, own, below, above, wide, spread, diag_w, diag_e, down, mid_diag_w, mid_diag_e)
    dn = lax.ppermute(send_up, z_axes, z_up)
    up = lax.ppermute(send_down, z_axes, z_dn)
    slab, fwd, bwd, frz = call(
        mid_z_body,
        "mid_z",
        [f32s(128, 256), f32s(928, 128), f32s(896, 128), f32s(NX, 64, 128)],
        (0,) * 5,
    )(send_up, dn, up, r, cfm)
    below = lax.ppermute(fwd, "yz", shift_up)
    above = lax.ppermute(bwd, "yz", shift_dn)
    mid = (8, 16, 1024)
    mid_scratch = [
        pltpu.VMEM((3, 16, 1024), F32),
        pltpu.VMEM((3, 16, 16, 1024), F32),
        pltpu.VMEM(mid, F32),
    ]
    tail_scratch = [pltpu.VMEM((4, 16, 1024), F32), pltpu.VMEM((12, 16, 1024), F32)]
    mid_pre, mid_res, coarse, send_up, send_down = call(
        mid_pre_body,
        "mid_pre",
        [f32s(*mid), f32s(*mid), f32s(5, 16, 1024), f32s(2, 16, 768), f32s(2, 16, 768)],
        (1, 1, 0, 0, 0, 0),
        [pltpu.VMEM((128, 1024), F32)]
        + mid_scratch
        + [pltpu.VMEM(mid, F32), pltpu.VMEM(mid, F32)]
        + tail_scratch,
    )(pos, scal, slab, below, above, cfm)
    dn = lax.ppermute(send_up, z_axes, z_up)
    up = lax.ppermute(send_down, z_axes, z_dn)
    coarse_slab, fwd, bwd = call(
        coarse_z_body,
        "coarse_z",
        [f32s(5, 16, 1280), f32s(5, 16, 512), f32s(5, 16, 512)],
        (0, 0, 0),
    )(coarse, dn, up)
    coarse_below = lax.ppermute(fwd, "yz", shift_up)
    coarse_above = lax.ppermute(bwd, "yz", shift_dn)
    basis, gram = call(
        krylov_body,
        "krylov",
        [f32s(BASIS, 16, 1536), f32s(512, 128)],
        (1, 0, 0, 0),
        [pltpu.VMEM((5, 16, 2304), F32), pltpu.VMEM((2 * BASIS, 8, 128), F32)],
    )(scal, coarse_slab, coarse_below, coarse_above)
    grams = lax.all_to_all(gram, ("gx", "yz", "lvl"), 0, 0, tiled=True)
    mid_sol = call(
        mid_post_body,
        "mid_post",
        f32s(256, 128),
        (1, 1, 0, 0, 0, 0, 0),
        mid_scratch + [pltpu.VMEM(mid, F32)] * 3 + tail_scratch,
    )(pos, scal, grams, basis, cfm, mid_pre, mid_res)
    packed = call(
        fine_post_body,
        "fine_post",
        f32s(16, 64, 128),
        (0,) * 11,
        [
            pltpu.VMEM(plane, F32),
            pltpu.VMEM(plane, F32),
            pltpu.VMEM(plane, F32),
            pltpu.VMEM((NX + 1, 16, 256), F32),
            pltpu.VMEM((NX + 1, 16, 256), F32),
        ],
    )(mid_sol, pre, frz, below, above, w, coef, inv, wide, spread, lift)
    got = lax.all_to_all(packed, "gx", 0, 0, tiled=True)
    correction, rest = call(unpack_body, "unpack", [f32s(512, 128), f32s(512, 128)], (0,))(got)
    return (correction.reshape(64, 1, 8, 128), rest.reshape(64, 1, 8, 128))


def solution(mesh):
    in_specs = (
        P(None, "gx", "yz", "lvl"),
        P("gx", "yz", "lvl"),
        P(),
        P(),
        P(None, "gx", "yz", "lvl"),
        P(None, "gx", "yz", "lvl"),
    )
    out_specs = (P(None, "gx", "yz", "lvl"), P(None, "gx", "yz", "lvl"))
    return jax.shard_map(local, mesh=mesh, in_specs=in_specs, out_specs=out_specs, check_vma=False)
```

time: 2210 us -> 254 us (0.11)
  the two profiles are of different devices: /device:TPU:282 before, /device:TPU:2 now
where the time goes in v1:
time: 254 us; the launch traced here: 253 us
  Pallas kernels  88.8 us (35%)
  starting transfers between devices  70.8 us (28%)
  waiting for transfers between devices  50.5 us (20%)
  blocking collectives  20.7 us (8%)
  local copies, waits for them, and re-layouts  15.2 us (6%)
  between operations  3.11 us (1%)
    pallas_call x1, Pallas kernels, local(): call(fine_post_body, 'fine_post', f32s(16, 64, 128), (0,) * 11, [pltpu.VM...  31.9 us
    pallas_call x1, Pallas kernels, local(): call(fine_pre_body, 'fine_pre', [f32s(*plane), f32s(*plane), f32s(NX, 24,...  27.8 us
    all_to_all x1, starting transfers between devices, local(): grams = lax.all_to_all(gram, ('gx', 'yz', 'lvl'), 0, 0, tiled=True)  22.6 us
    all_to_all x1, blocking collectives, local(): got = lax.all_to_all(packed, 'gx', 0, 0, tiled=True)  20.7 us
    all_to_all x1, waiting for transfers between devices, local(): grams = lax.all_to_all(gram, ('gx', 'yz', 'lvl'), 0, 0, tiled=True)  16.3 us
    all_to_all x1, waiting for transfers between devices, local(): own = lax.all_to_all(slots, 'gx', 0, 0, tiled=True)  15 us
    unnamed x46, local copies, waits for them, and re-layouts  10.4 us
    all_to_all x1, starting transfers between devices, local(): own = lax.all_to_all(slots, 'gx', 0, 0, tiled=True)  8.57 us
  transfers between devices with their start and end apart: 13, of which 9 were waited for; matrix products, arithmetic and copies ran while one was open for 3% of the time, Pallas kernels for 0%

profile of v1, /device:TPU:2, one launch (start us, length us, event | category | flops | bytes accessed | tf_op | source)
XLA Modules:
  0.0 252.8 jit_solution(4275705252546300820)
XLA Ops:
  3.3 4.0 %collective-permute-start = (f32[24,128]{1,0:T(8,128)S(1)}, f32[24,128]{1,0:T(8,128)S(1)}, u32[]{:S(2)}, u32[]{:S(2)}) collective-permute-start(f32[24,128]{1,0:T(8,128)S(1)} %edges.1), channel_id=1, source_target_pairs={{0,1},{1,0},{2,3},{3,2},{4,5},{5,4},{6,7},{7,6},{8,9},{9,8},{10,11... | collective-permute-start | bytes 36872 | tf_op jit(solution)/shard_map/ppermute | solution.py:922
  13.0 3.2 %slots.1 = f32[16,80,128]{2,1,0:T(8,128)} custom-call(s32[4]{0:T(128)S(1)} %pad_add_fusion.pos, f32[512,128]{1,0:T(8,128)S(1)} %bitcast.82, f32[64,128]{1,0:T(8,128)S(1)} %bitcast.85, f32[24,128]{1,0:T(8,128)S(1)} %collective-permute-done.halo), custom_call_target="tpu_custom_call" | custom-call | flops 1000000 | bytes 1000000 | tf_op jit(solution)/shard_map/slots/pallas_call | solution.py:923
  16.2 8.6 %all-to-all-start = ((f32[16,80,128]{2,1,0:T(8,128)}), f32[16,80,128]{2,1,0:T(8,128)S(1)}, u32[]{:S(2)}, u32[]{:S(2)}) async-start(f32[16,80,128]{2,1,0:T(8,128)} %slots.1), calls=%async_computation | async-start | bytes 1310720 | tf_op jit(solution)/shard_map/all_to_all | solution.py:930
  27.9 15.0 %all-to-all-done.own = f32[16,80,128]{2,1,0:T(8,128)S(1)} async-done(((f32[16,80,128]{2,1,0:T(8,128)}), f32[16,80,128]{2,1,0:T(8,128)S(1)}, u32[]{:S(2)}, u32[]{:S(2)}) %all-to-all-start) | async-done | bytes 655392 | tf_op jit(solution)/shard_map/all_to_all | solution.py:930
  44.2 3.1 %collective-permute-start.1 = (f32[16,80,128]{2,1,0:T(8,128)S(1)}, f32[16,80,128]{2,1,0:T(8,128)S(1)}, u32[]{:S(2)}, u32[]{:S(2)}) collective-permute-start(f32[16,80,128]{2,1,0:T(8,128)S(1)} %all-to-all-done.own), channel_id=1, source_target_pairs={{0,2},{2,4},{4,6},{6,8},{8,10},{10,12},{12,14},{14,16},{16,18},{18... | collective-permute-start | bytes 1966088 | tf_op jit(solution)/shard_map/ppermute | solution.py:931
  48.9 27.8 %fine_pre.1 = (f32[16,64,256]{2,1,0:T(8,128)S(1)}, f32[16,64,256]{2,1,0:T(8,128)S(1)}, f32[16,24,256]{2,1,0:T(8,128)S(1)}, f32[16,8,256]{2,1,0:T(8,128)S(1)}, f3...) custom-call(s32[4]{0:T(128)S(1)} %pad_add_fusion.pos, ...), custom_call_target="tpu_custom_call" | custom-call | flops 1000000 | bytes 1000000 | tf_op jit(solution)/shard_map/fine_pre/pallas_call | solution.py:934
  76.7 3.4 %collective-permute-start.4 = (f32[512,128]{1,0:T(8,128)S(1)}, f32[512,128]{1,0:T(8,128)S(1)}, u32[]{:S(2)}, u32[]{:S(2)}) collective-permute-start(f32[512,128]{1,0:T(8,128)S(1)} %get-tuple-element.27), channel_id=1, source_target_pairs={{32,0},{64,32},{96,64},{128,96},{160,128},{192,160},{224,192},{256... | collective-permute-start | bytes 786440 | tf_op jit(solution)/shard_map/ppermute | solution.py:956
  80.2 3.3 %collective-permute-start.3 = (f32[512,128]{1,0:T(8,128)S(1)}, f32[512,128]{1,0:T(8,128)S(1)}, u32[]{:S(2)}, u32[]{:S(2)}) collective-permute-start(f32[512,128]{1,0:T(8,128)S(1)} %get-tuple-element.26.own), channel_id=1, source_target_pairs={{0,32},{32,64},{64,96},{96,128},{128,160},{160,192},{192,224},{224... | collective-permute-start | bytes 786440 | tf_op jit(solution)/shard_map/ppermute | solution.py:955
  83.5 2.4 collective-permute-done.4.up
  85.9 2.8 %collective-permute-done.3.dn = f32[512,128]{1,0:T(8,128)S(1)} collective-permute-done((f32[512,128]{1,0:T(8,128)S(1)}, f32[512,128]{1,0:T(8,128)S(1)}, u32[]{:S(2)}, u32[]{:S(2)}) %collective-permute-start.3) | collective-permute-done | bytes 262176 | tf_op jit(solution)/shard_map/ppermute | solution.py:955
  91.6 8.5 %collective-permute-start.5 = (f32[928,128]{1,0:T(8,128)}, f32[928,128]{1,0:T(8,128)S(1)}, u32[]{:S(2)}, u32[]{:S(2)}) collective-permute-start(f32[928,128]{1,0:T(8,128)} %get-tuple-element.31), channel_id=1, source_target_pairs={{0,2},{2,4},{4,6},{6,8},{8,10},{10,12},{12,14},{14,16},{16,18},{18... | collective-permute-start | bytes 1425416 | tf_op jit(solution)/shard_map/ppermute | solution.py:963
  105.1 6.7 %collective-permute-done.6.above = f32[896,128]{1,0:T(8,128)S(1)} collective-permute-done((f32[896,128]{1,0:T(8,128)}, f32[896,128]{1,0:T(8,128)S(1)}, u32[]{:S(2)}, u32[]{:S(2)}) %collective-permute-start.6) | collective-permute-done | bytes 458784 | tf_op jit(solution)/shard_map/ppermute | solution.py:964
  111.8 7.0 %mid_pre.1 = (f32[8,16,1024]{2,1,0:T(8,128)S(1)}, f32[8,16,1024]{2,1,0:T(8,128)S(1)}, f32[5,16,1024]{2,1,0:T(8,128)S(1)}, f32[2,16,768]{2,1,0:T(8,128)S(1)}, f32[2,16,768]{2,1,0:T(8,128)S(1)}) custom-call(s32[4]{0:T(128)S(1)} %pad_add_fusion.pos, f32[144]{0:T(256)S(1)} %concatenate.45.scal, f32[128,256]{1,0:T(8,128)S(1)} %get-tuple-element.30.slab, ...), custom_call_target="tpu_custom_call" | custom-call | flops 1000000 | bytes 1000000 | tf_op jit(solution)/shard_map/mid_pre/pallas_call | solution.py:972
  122.4 3.9 %collective-permute-start.8 = (f32[2,16,768]{2,1,0:T(8,128)S(1)}, f32[2,16,768]{2,1,0:T(8,128)S(1)}, u32[]{:S(2)}, u32[]{:S(2)}) collective-permute-start(f32[2,16,768]{2,1,0:T(8,128)S(1)} %get-tuple-element.35), channel_id=1, source_target_pairs={{32,0},{64,32},{96,64},{128,96},{160,128},{192,160},{224,192},{256... | collective-permute-start | bytes 294920 | tf_op jit(solution)/shard_map/ppermute | solution.py:983
  126.9 2.8 %collective-permute-done.8.up = f32[2,16,768]{2,1,0:T(8,128)S(1)} collective-permute-done((f32[2,16,768]{2,1,0:T(8,128)S(1)}, f32[2,16,768]{2,1,0:T(8,128)S(1)}, u32[]{:S(2)}, u32[]{:S(2)}) %collective-permute-start.8) | collective-permute-done | bytes 98336 | tf_op jit(solution)/shard_map/ppermute | solution.py:983
  130.5 7.3 %collective-permute-start.9 = (f32[5,16,512]{2,1,0:T(8,128)S(1)}, f32[5,16,512]{2,1,0:T(8,128)S(1)}, u32[]{:S(2)}, u32[]{:S(2)}) collective-permute-start(f32[5,16,512]{2,1,0:T(8,128)S(1)} %get-tuple-element.37), channel_id=1, source_target_pairs={{0,2},{2,4},{4,6},{6,8},{8,10},{10,12},{12,14},{14,16},{16,18},{18... | collective-permute-start | bytes 491528 | tf_op jit(solution)/shard_map/ppermute | solution.py:990
  139.3 2.4 collective-permute-done.10.above
  141.7 3.9 %krylov.1 = (f32[8,16,1536]{2,1,0:T(8,128)S(1)}, f32[512,128]{1,0:T(8,128)}) custom-call(f32[144]{0:T(256)S(1)} %concatenate.45.scal, f32[5,16,1280]{2,1,0:T(8,128)S(1)} %get-tuple-element.36.own, f32[5,16,512]{2,1,0:T(8,128)S(1)} %collective-permute-done.9.below, f32[5,16,512]{2,1,0:T(8,128)S(1)} %collective-permute-done.10.above), custom_call_target="tpu_custom_call" | custom-call | flops 1000000 | bytes 1000000 | tf_op jit(solution)/shard_map/krylov/pallas_call | solution.py:992
  146.5 22.6 %all-to-all-start.1 = ((f32[512,1,128]{2,1,0:T(1,128)}), f32[512,1,128]{2,1,0:T(1,128)S(1)}, u32[]{:S(2)}, u32[]{:S(2)}) async-start(f32[512,1,128]{2,1,0:T(1,128)} %bitcast.38), calls=%async_computation.1 | async-start | bytes 524288 | tf_op jit(solution)/shard_map/all_to_all | solution.py:999
  169.2 16.3 %all-to-all-done.1 = f32[512,1,128]{2,1,0:T(1,128)S(1)} async-done(((f32[512,1,128]{2,1,0:T(1,128)}), f32[512,1,128]{2,1,0:T(1,128)S(1)}, u32[]{:S(2)}, u32[]{:S(2)}) %all-to-all-start.1) | async-done | bytes 262176 | tf_op jit(solution)/shard_map/all_to_all | solution.py:999
  188.7 8.5 %mid_post.1.mid = f32[256,128]{1,0:T(8,128)S(1)} custom-call(s32[4]{0:T(128)S(1)} %pad_add_fusion.pos, f32[144]{0:T(256)S(1)} %concatenate.45.scal, f32[512,128]{1,0:T(8,128)S(1)} %bitcast.83, f32[8,16,1536]{2,1,0:T(8,128)S(1)} %copy-done.4, f32[128,1024]{1,0:T(8,128)S(1)} %get-tuple-element.29.cfm.cfm_in, f32[8,16,1024]{2,1,0:T(8,128)S(1)} %copy-done.8, ...), custom_call_target="tpu_custom_call" | custom-call | flops 1000000 | bytes 1000000 | tf_op jit(solution)/shard_map/mid_post/pallas_call | solution.py:1000
  197.3 31.9 %fine_post.1 = f32[16,64,128]{2,1,0:T(8,128)S(1)} custom-call(f32[256,128]{1,0:T(8,128)S(1)} %mid_post.1.mid, f32[16,64,256]{2,1,0:T(8,128)S(1)} %get-tuple-element.43.pre, f32[16,64,128]{2,1,0:T(8,128)S(1)} %copy-done.6, f32[928,128]{1,0:T(8,128)S(1)} %collective-permute-done.5.below, f32[896,128]{1,0:T(8,128)S(1)} %collective-permute-done.6.above, ...), custom_call_target="tpu_custom_call" | custom-call | flops 1000000 | bytes 1000000 | tf_op jit(solution)/shard_map/fine_post/pallas_call | solution.py:1007
  229.2 20.7 %all_to_all.21.got = f32[16,64,128]{2,1,0:T(8,128)S(1)} all-to-all(f32[16,64,128]{2,1,0:T(8,128)S(1)} %fine_post.1), channel_id=1, replica_groups=mesh['gx'=16,'yz'=16,'lvl'=2] {'gx'}, dimensions={0} | all-to-all | bytes 1048576 | tf_op jit(solution)/shard_map/all_to_all | solution.py:1020
  249.9 2.8 %unpack.1 = (f32[512,128]{1,0:T(8,128)}, f32[512,128]{1,0:T(8,128)}) custom-call(f32[16,64,128]{2,1,0:T(8,128)S(1)} %all_to_all.21.got), custom_call_target="tpu_custom_call" | custom-call | flops 1000000 | bytes 1000000 | tf_op jit(solution)/shard_map/unpack/pallas_call | solution.py:1021
  (116 shorter events, 30.4 us)
Async XLA Ops:
  1.5 1.0 copy-start.1
  3.3 9.7 %collective-permute-start = (f32[24,128]{1,0:T(8,128)S(1)}, f32[24,128]{1,0:T(8,128)S(1)}, u32[]{:S(2)}, u32[]{:S(2)}) collective-permute-start(f32[24,128]{1,0:T(8,128)S(1)} %edges.1), channel_id=1, source_target_pairs={{0,1},{1,0},{2,3},{3,2},{4,5},{5,4},{6,7},{7,6},{8,9},{9,8},{10,11... | collective-permute-start | bytes 36872 | tf_op jit(solution)/shard_map/ppermute | solution.py:922
  10.6 1.1 copy-start.16
  12.0 1.0 copy-start.2
  16.2 26.7 %all-to-all-start = ((f32[16,80,128]{2,1,0:T(8,128)}), f32[16,80,128]{2,1,0:T(8,128)S(1)}, u32[]{:S(2)}, u32[]{:S(2)}) async-start(f32[16,80,128]{2,1,0:T(8,128)} %slots.1), calls=%async_computation | async-start | bytes 1310720 | tf_op jit(solution)/shard_map/all_to_all | solution.py:930
  42.9 4.7 %collective-permute-start.2 = (f32[16,80,128]{2,1,0:T(8,128)S(1)}, f32[16,80,128]{2,1,0:T(8,128)S(1)}, u32[]{:S(2)}, u32[]{:S(2)}) collective-permute-start(f32[16,80,128]{2,1,0:T(8,128)S(1)} %all-to-all-done.own), channel_id=1, source_target_pairs={{2,0},{4,2},{6,4},{8,6},{10,8},{12,10},{14,12},{16,14},{18,16},{20... | collective-permute-start | bytes 1966088 | tf_op jit(solution)/shard_map/ppermute | solution.py:932
  44.2 4.7 %collective-permute-start.1 = (f32[16,80,128]{2,1,0:T(8,128)S(1)}, f32[16,80,128]{2,1,0:T(8,128)S(1)}, u32[]{:S(2)}, u32[]{:S(2)}) collective-permute-start(f32[16,80,128]{2,1,0:T(8,128)S(1)} %all-to-all-done.own), channel_id=1, source_target_pairs={{0,2},{2,4},{4,6},{6,8},{8,10},{10,12},{12,14},{14,16},{16,18},{18... | collective-permute-start | bytes 1966088 | tf_op jit(solution)/shard_map/ppermute | solution.py:931
  47.5 1.4 copy-start.13
  76.7 14.1 %copy-start.11 = (f32[16,24,256]{2,1,0:T(8,128)}, f32[16,24,256]{2,1,0:T(8,128)S(1)}, u32[]{:S(2)}) copy-start(f32[16,24,256]{2,1,0:T(8,128)S(1)} %get-tuple-element.45.w) | copy-start | bytes 1179652
  76.7 9.2 %collective-permute-start.4 = (f32[512,128]{1,0:T(8,128)S(1)}, f32[512,128]{1,0:T(8,128)S(1)}, u32[]{:S(2)}, u32[]{:S(2)}) collective-permute-start(f32[512,128]{1,0:T(8,128)S(1)} %get-tuple-element.27), channel_id=1, source_target_pairs={{32,0},{64,32},{96,64},{128,96},{160,128},{192,160},{224,192},{256... | collective-permute-start | bytes 786440 | tf_op jit(solution)/shard_map/ppermute | solution.py:956
  80.2 8.5 %collective-permute-start.3 = (f32[512,128]{1,0:T(8,128)S(1)}, f32[512,128]{1,0:T(8,128)S(1)}, u32[]{:S(2)}, u32[]{:S(2)}) collective-permute-start(f32[512,128]{1,0:T(8,128)S(1)} %get-tuple-element.26.own), channel_id=1, source_target_pairs={{0,32},{32,64},{64,96},{96,128},{128,160},{160,192},{192,224},{224... | collective-permute-start | bytes 786440 | tf_op jit(solution)/shard_map/ppermute | solution.py:955
  91.6 20.2 %collective-permute-start.5 = (f32[928,128]{1,0:T(8,128)}, f32[928,128]{1,0:T(8,128)S(1)}, u32[]{:S(2)}, u32[]{:S(2)}) collective-permute-start(f32[928,128]{1,0:T(8,128)} %get-tuple-element.31), channel_id=1, source_target_pairs={{0,2},{2,4},{4,6},{6,8},{8,10},{10,12},{12,14},{14,16},{16,18},{18... | collective-permute-start | bytes 1425416 | tf_op jit(solution)/shard_map/ppermute | solution.py:963
  100.1 11.7 %collective-permute-start.6 = (f32[896,128]{1,0:T(8,128)}, f32[896,128]{1,0:T(8,128)S(1)}, u32[]{:S(2)}, u32[]{:S(2)}) collective-permute-start(f32[896,128]{1,0:T(8,128)} %get-tuple-element.32), channel_id=1, source_target_pairs={{2,0},{4,2},{6,4},{8,6},{10,8},{12,10},{14,12},{16,14},{18,16},{20... | collective-permute-start | bytes 1376264 | tf_op jit(solution)/shard_map/ppermute | solution.py:964
  120.4 6.5 %collective-permute-start.7 = (f32[2,16,768]{2,1,0:T(8,128)S(1)}, f32[2,16,768]{2,1,0:T(8,128)S(1)}, u32[]{:S(2)}, u32[]{:S(2)}) collective-permute-start(f32[2,16,768]{2,1,0:T(8,128)S(1)} %get-tuple-element.34), channel_id=1, source_target_pairs={{0,32},{32,64},{64,96},{96,128},{128,160},{160,192},{192,224},{224... | collective-permute-start | bytes 294920 | tf_op jit(solution)/shard_map/ppermute | solution.py:982
  122.4 7.4 %collective-permute-start.8 = (f32[2,16,768]{2,1,0:T(8,128)S(1)}, f32[2,16,768]{2,1,0:T(8,128)S(1)}, u32[]{:S(2)}, u32[]{:S(2)}) collective-permute-start(f32[2,16,768]{2,1,0:T(8,128)S(1)} %get-tuple-element.35), channel_id=1, source_target_pairs={{32,0},{64,32},{96,64},{128,96},{160,128},{192,160},{224,192},{256... | collective-permute-start | bytes 294920 | tf_op jit(solution)/shard_map/ppermute | solution.py:983
  130.5 8.8 %collective-permute-start.9 = (f32[5,16,512]{2,1,0:T(8,128)S(1)}, f32[5,16,512]{2,1,0:T(8,128)S(1)}, u32[]{:S(2)}, u32[]{:S(2)}) collective-permute-start(f32[5,16,512]{2,1,0:T(8,128)S(1)} %get-tuple-element.37), channel_id=1, source_target_pairs={{0,2},{2,4},{4,6},{6,8},{8,10},{10,12},{12,14},{14,16},{16,18},{18... | collective-permute-start | bytes 491528 | tf_op jit(solution)/shard_map/ppermute | solution.py:990
  137.8 3.9 %collective-permute-start.10 = (f32[5,16,512]{2,1,0:T(8,128)S(1)}, f32[5,16,512]{2,1,0:T(8,128)S(1)}, u32[]{:S(2)}, u32[]{:S(2)}) collective-permute-start(f32[5,16,512]{2,1,0:T(8,128)S(1)} %get-tuple-element.38), channel_id=1, source_target_pairs={{2,0},{4,2},{6,4},{8,6},{10,8},{12,10},{14,12},{16,14},{18,16},{20... | collective-permute-start | bytes 491528 | tf_op jit(solution)/shard_map/ppermute | solution.py:991
  146.5 39.0 %all-to-all-start.1 = ((f32[512,1,128]{2,1,0:T(1,128)}), f32[512,1,128]{2,1,0:T(1,128)S(1)}, u32[]{:S(2)}, u32[]{:S(2)}) async-start(f32[512,1,128]{2,1,0:T(1,128)} %bitcast.38), calls=%async_computation.1 | async-start | bytes 524288 | tf_op jit(solution)/shard_map/all_to_all | solution.py:999
  185.5 1.1 copy-start.4
  186.7 1.0 copy-start.8
  187.7 1.0 copy-start.10
  188.7 8.6 %copy-start = (f32[16,64,256]{2,1,0:T(8,128)S(1)}, f32[16,64,256]{2,1,0:T(8,128)}, u32[]{:S(2)}) copy-start(f32[16,64,256]{2,1,0:T(8,128)} %get-tuple-element.47.inv) | copy-start | bytes 3145732
  188.7 8.6 %copy-start.6 = (f32[16,64,128]{2,1,0:T(8,128)S(1)}, f32[16,64,128]{2,1,0:T(8,128)}, u32[]{:S(2)}) copy-start(f32[16,64,128]{2,1,0:T(8,128)} %copy-done.5) | copy-start | bytes 1572868
  188.7 8.6 %copy-start.12 = (f32[16,24,256]{2,1,0:T(8,128)S(1)}, f32[16,24,256]{2,1,0:T(8,128)}, u32[]{:S(2)}) copy-start(f32[16,24,256]{2,1,0:T(8,128)} %copy-done.11) | copy-start | bytes 1179652
  (11 other events, 8.6 us)

commit v2 on v1

--- a/solution.py
+++ b/solution.py
@@ -26,7 +26,7 @@
 RHO2 = 1.0 / (2.0 * SCALED - RHO1)
 STEPS = ((RHO1 * RHO0, 2.0 * RHO1 / SPREAD), (RHO2 * RHO1, 2.0 * RHO2 / SPREAD))
 BASIS = 8
-VMEM_LIMIT = 48 * 2**20
+VMEM_LIMIT = 24 * 2**20
 
 
 def lanes(shape):
@@ -128,29 +128,26 @@
             out[g, 64 + 8 * h : 72 + 8 * h, :] = acc
 
 
-def fine_update(x, u, r, sol, inv, step):
-    if step is None:
-        return
-    keep, gain = STEPS[step]
-    new = keep * u[x] + gain * (inv[x] * r[x])
-    u[x] = new
-    sol[x] = sol[x] + new
+CHUNK = 4096
+CHUNKS = NX * 256 // CHUNK
 
 
 def fine_apply(u, r, w, coef, wide, spread, px, qx, step, sol, inv):
-    def first(x, carry):
-        prod = mm(wide[...], stack_hlh(u[x]))
+    for c in range(CHUNKS):
+        at = slice(CHUNK * c, CHUNK * (c + 1))
+        after = slice(CHUNK * c + 256, CHUNK * (c + 1) + 256)
+        prod = mm(wide[...], stack_hlh(u[:, at]))
 
         def pick(base, row):
-            total = w[x, pl.ds(row, 1), :] * prod[base : base + 16]
+            total = w[row : row + 1, at] * prod[base : base + 16]
             for k in range(1, KINDS):
-                total = total + w[x, pl.ds(row + k, 1), :] * prod[base + 16 * k : base + 16 * k + 16]
+                total = total + w[row + k : row + k + 1, at] * prod[base + 16 * k : base + 16 * k + 16]
             return total
 
-        px[x + 1] = pick(64, 0)
+        px[:, after] = pick(64, 0)
         py = pick(128, 4)
         pz = pick(192, 8)
-        qx[x] = pick(256, 12)
+        qx[:, at] = pick(256, 12)
         qy = pick(320, 16)
         qz = pick(384, 20)
         flux = jnp.concatenate(
@@ -158,18 +155,18 @@
         )
         high, low = split3(flux)
         faces = mm(spread[...], jnp.concatenate([high, low], axis=0).astype(BF16))
-        r[x] = r[x] - (coef[x, pl.ds(0, 1), :] * prod[0:64] + faces)
-        return carry
-
-    lax.fori_loop(0, NX, first, 0)
-
-    def second(x, carry):
-        r[x, 48:64, :] = r[x, 48:64, :] - (px[x + 1] - qx[x + 1])
-        r[x, 0:16, :] = r[x, 0:16, :] + (px[x] - qx[x])
-        fine_update(x, u, r, sol, inv, step)
-        return carry
-
-    lax.fori_loop(0, NX, second, 0)
+        r[:, at] = r[:, at] - (coef[0:1, at] * prod[0:64] + faces)
+
+    for c in range(CHUNKS):
+        at = slice(CHUNK * c, CHUNK * (c + 1))
+        after = slice(CHUNK * c + 256, CHUNK * (c + 1) + 256)
+        r[48:64, at] = r[48:64, at] - (px[:, after] - qx[:, after])
+        r[0:16, at] = r[0:16, at] + (px[:, at] - qx[:, at])
+        if step is not None:
+            keep, gain = STEPS[step]
+            new = keep * u[:, at] + gain * (inv[:, at] * r[:, at])
+            u[:, at] = new
+            sol[:, at] = sol[:, at] + new
 
 
 def fine_pre_body(
@@ -200,21 +197,22 @@
     low = lanes((64, 128)) < 64
     low8 = lanes((8, 128)) < 64
     lane8 = lanes((8, 128))
-    place = lanes((1, 256))
+    place = lanes((1, 256)) % 256
     y_at = pos[0] * 8 - 4 + place // 16
     z_at = pos[1] * 8 - 4 + place % 16
     inside = (y_at >= 0) & (y_at < NY) & (z_at >= 0) & (z_at < NZ)
     has_y = inside & (y_at < NY - 1)
     has_z = inside & (z_at < NZ - 1)
     inside_f = jnp.where(inside, 1.0, 0.0)
-    px[0] = jnp.zeros((16, 256), F32)
-    qx[NX] = jnp.zeros((16, 256), F32)
+    px[:, 0:256] = jnp.zeros((16, 256), F32)
+    qx[:, NX * 256 :] = jnp.zeros((16, 256), F32)
     cfm[:, 0:128] = jnp.zeros((128, 128), F32)
     cfm[:, 896:1024] = jnp.zeros((128, 128), F32)
     for x in range(NX):
+        first, second = slice(256 * x, 256 * x + 128), slice(256 * x + 128, 256 * x + 256)
         turned = roll(own[x, 0:64, :], 64)
-        r[x, :, 0:128] = jnp.where(low, roll(below[x, 0:64, :], 64), turned)
-        r[x, :, 128:256] = jnp.where(low, turned, roll(above[x, 0:64, :], 64))
+        r[:, first] = jnp.where(low, roll(below[x, 0:64, :], 64), turned)
+        r[:, second] = jnp.where(low, turned, roll(above[x, 0:64, :], 64))
         blocks = [
             below[x, 64:72, :],
             below[x, 72:80, :],
@@ -225,7 +223,7 @@
         ]
         for m in range(6):
             gather[pl.ds(128 * m + x, 8, stride=16), :] = blocks[m]
-        for half in range(2):
+        for half, at in enumerate((first, second)):
             acc = jnp.zeros((8, 128), F32)
             for row in range(8):
                 n = 8 * half + row
@@ -234,11 +232,13 @@
                     roll(blocks[1 + n // 4], 16 * row - (n % 4) * 32 - 8),
                     acc,
                 )
-            coef[x, :, 128 * half : 128 * half + 128] = acc
+            coef[:, at] = acc
     for m in range(6):
         cfm[:, 128 * (m + 1) : 128 * (m + 2)] = gather[128 * m : 128 * m + 128, :]
+    w[12:16, 0:256] = jnp.zeros((4, 256), F32)
     for x in range(NX):
-        rows = coef[x]
+        at = slice(256 * x, 256 * x + 256)
+        rows = coef[:, at]
         opens = [
             inside & (rows[4:5] == 0.0) if x < NX - 1 else jnp.zeros((1, 256), jnp.bool_),
             has_y & (rows[5:6] == 0.0),
@@ -248,43 +248,44 @@
             [jnp.where(opens[d] & (rows[1 + d : 2 + d] == float(k)), 1.0, 0.0) for k in range(KINDS)]
             for d in range(3)
         ]
-        plus_all = jnp.concatenate(plus[0] + plus[1] + plus[2] , axis=0)
-        w[x, 0:12, :] = plus_all
-        if x == 0:
-            w[0, 12:16, :] = jnp.zeros((4, 256), F32)
+        plus_all = jnp.concatenate(plus[0] + plus[1] + plus[2], axis=0)
+        w[0:12, at] = plus_all
         if x < NX - 1:
-            w[x + 1, 12:16, :] = plus_all[0:4]
-        w[x, 16:20, :] = roll(plus_all[4:8], 16)
-        w[x, 20:24, :] = roll(plus_all[8:12], 1)
-
-    def prepare(x, carry):
-        ws = w[x]
-        ws = jnp.concatenate([ws, ws, ws, jnp.zeros((8, 256), F32)], axis=0).astype(BF16)
-        diag = diag_e[...] * coef[x, pl.ds(0, 1), :] + mm(diag_w[...], ws)
-        inverse = jnp.where(inside, 1.0 / diag, 0.0)
-        inv[x] = inverse
-        update = inverse * r[x] / MIDDLE
-        u[x] = update
-        sol[x] = update
-        return carry
-
-    lax.fori_loop(0, NX, prepare, 0)
+            w[12:16, 256 * x + 256 : 256 * x + 512] = plus_all[0:4]
+        w[16:20, at] = roll(plus_all[4:8], 16)
+        w[20:24, at] = roll(plus_all[8:12], 1)
+    wide_inside = jnp.concatenate([inside] * (CHUNK // 256), axis=1)
+
+    def kinds_of(at):
+        ws = w[:, at]
+        return jnp.concatenate([ws, ws, ws, jnp.zeros((8, CHUNK), F32)], axis=0).astype(BF16)
+
+    for c in range(CHUNKS):
+        at = slice(CHUNK * c, CHUNK * (c + 1))
+        diag = diag_e[...] * coef[0:1, at] + mm(diag_w[...], kinds_of(at))
+        inverse = jnp.where(wide_inside, 1.0 / diag, 0.0)
+        inv[:, at] = inverse
+        update = inverse * r[:, at] / MIDDLE
+        u[:, at] = update
+        sol[:, at] = update
     fine_apply(u, r, w, coef, wide, spread, px, qx, 0, sol, inv)
     fine_apply(u, r, w, coef, wide, spread, px, qx, 1, sol, inv)
     fine_apply(u, r, w, coef, wide, spread, px, qx, None, sol, inv)
     lane16 = lanes((16, 128)) % 16 // 4
+    for c in range(CHUNKS):
+        at = slice(CHUNK * c, CHUNK * (c + 1))
+        rhs = mm(down[...], stack_hlh(r[:, at]))
+        diag = mid_diag_e[...] * coef[0:1, at] + mm(mid_diag_w[...], kinds_of(at))
+        update = jnp.where(wide_inside, 1.0 / diag, 0.0) * rhs / MIDDLE
+        for n in range(CHUNK // 256):
+            x = (CHUNK // 256) * c + n
+            for half in range(2):
+                piece = update[:, 256 * n + 128 * half : 256 * n + 128 * half + 128]
+                send_up[pl.ds(128 * half + x, 8, stride=16), :] = piece
+                send_down[pl.ds(128 * half + x, 8, stride=16), :] = piece
     for x in range(NX):
-        rx = r[x]
-        ws = w[x]
-        ws = jnp.concatenate([ws, ws, ws, jnp.zeros((8, 256), F32)], axis=0).astype(BF16)
-        rhs = mm(down[...], stack_hlh(rx))
-        diag = mid_diag_e[...] * coef[x, 0:1, :] + mm(mid_diag_w[...], ws)
-        update = jnp.where(inside, 1.0 / diag, 0.0) * rhs / MIDDLE
-        for half in range(2):
-            piece = update[:, 128 * half : 128 * half + 128]
-            send_up[pl.ds(128 * half + x, 8, stride=16), :] = piece
-            send_down[pl.ds(128 * half + x, 8, stride=16), :] = piece
-        mine = jnp.where(low, roll(rx[:, 0:128], 64), roll(rx[:, 128:256], 64))
+        first, second = slice(256 * x, 256 * x + 128), slice(256 * x + 128, 256 * x + 256)
+        mine = jnp.where(low, roll(r[:, first], 64), roll(r[:, second], 64))
         up = jnp.zeros((16, 128), F32)
         dn = jnp.zeros((16, 128), F32)
         for j in range(4):
@@ -320,8 +321,8 @@
     low = lanes((64, 128)) < 64
     l16 = lanes((16, 128)) % 16
     for x in range(NX):
-        rx = r[x]
-        mine = jnp.where(low, roll(rx[:, 0:128], 64), roll(rx[:, 128:256], 64))
+        at = 256 * x
+        mine = jnp.where(low, roll(r[:, at : at + 128], 64), roll(r[:, at + 128 : at + 256], 64))
         pack_dn = dn[256 + 16 * x : 272 + 16 * x, :]
         pack_up = up[256 + 16 * x : 272 + 16 * x, :]
         for j in range(4):
@@ -334,11 +335,6 @@
         bwd[384 + 64 * x : 448 + 64 * x, :] = jnp.where(low, frz[x], roll(frz[x + 8], 64))
 
 
-MID_PAIRS = ((0, 0), (0, 1), (0, 2), (0, 3), (1, 1), (1, 2), (1, 3), (2, 2), (2, 3), (3, 3))
-MID_SLOT = {}
-for _n, (_i, _j) in enumerate(MID_PAIRS):
-    MID_SLOT[(_i, _j)] = _n
-    MID_SLOT[(_j, _i)] = _n
 LOWS = ((0, 1, 2, 3), (0, 1, 4, 5), (0, 2, 4, 6))
 HIGHS = ((4, 5, 6, 7), (2, 3, 6, 7), (1, 3, 5, 7))
 
@@ -368,17 +364,17 @@
         sel[d] = jnp.where(is_open, cfm[16 + 16 * d : 32 + 16 * d, :], 4.0)
     coef = cfm[0:16, :]
 
-    def table(n, carry):
-        at = 64 + n
-        for d in range(3):
-            kind = sel[d]
-            value = jnp.zeros((16, 1024), F32)
-            for k in range(KINDS):
-                value = jnp.where(kind == float(k), scal[at + 16 * k], value)
-            faces[d, n] = value
-        return carry
-
-    lax.fori_loop(0, 16, table, 0)
+    for d in range(3):
+        for c in range(8):
+            at = slice(128 * c, 128 * c + 128)
+            kind = sel[d, :, at]
+            ones = [kind == float(k) for k in range(KINDS)]
+            for i in range(4):
+                for j in range(i, 4):
+                    value = jnp.zeros((16, 128), F32)
+                    for k in range(KINDS):
+                        value = jnp.where(ones[k], scal[64 + 16 * k + 4 * i + j], value)
+                    faces[d, 4 * i + j, :, at] = value
     if inv is None:
         return known
     for i in range(8):
@@ -399,20 +395,17 @@
         for j in range(4):
             jump[j] = v[HIGHS[d][j]] - ahead(v[LOWS[d][j]], d)
 
-        def face(c, carry):
-            at = pl.ds(pl.multiple_of(c * 128, 128), 128)
+        for c in range(8):
+            at = slice(128 * c, 128 * c + 128)
             jumps = [jump[j, :, at] for j in range(4)]
             for i in range(4):
-                total = faces[d, 4 * i, :, at] * jumps[0]
+                total = faces[d, i, :, at] * jumps[0]
                 for j in range(1, 4):
-                    total = total + faces[d, 4 * i + j, :, at] * jumps[j]
+                    total = total + faces[d, 4 * min(i, j) + max(i, j), :, at] * jumps[j]
                 flux[4 * d + i, :, at] = total
-            return carry
-
-        lax.fori_loop(0, 8, face, 0)
-
-    def block(c, carry):
-        at = pl.ds(pl.multiple_of(c * 128, 128), 128)
+
+    for c in range(1, 7):
+        at = slice(128 * c, 128 * c + 128)
         values = [v[j, :, at] for j in range(8)]
         coef = cfm[0:16, at]
         for i in range(8):
@@ -420,9 +413,6 @@
             for j in range(1, 8):
                 total = total + scal[8 * i + j] * values[j]
             r[i, :, at] = r[i, :, at] - coef * total
-        return carry
-
-    lax.fori_loop(0, 8, block, 0)
     for d in range(3):
         for j in range(4):
             value = flux[4 * d + j]
@@ -719,9 +709,10 @@
     mid, pre, frz, below, above, w, coef, inv, wide, spread, lift, out, u, r, sol, px, qx,
 ):
     low = lanes((64, 128)) < 64
-    px[0] = jnp.zeros((16, 256), F32)
-    qx[NX] = jnp.zeros((16, 256), F32)
+    px[:, 0:256] = jnp.zeros((16, 256), F32)
+    qx[:, NX * 256 :] = jnp.zeros((16, 256), F32)
     for x in range(NX):
+        first, second = slice(256 * x, 256 * x + 128), slice(256 * x + 128, 256 * x + 256)
         turned = roll(frz[x], 64)
         at = 384 + 64 * (x % 8)
         down = below[at : at + 64, :]
@@ -730,23 +721,27 @@
             down = roll(down, 64)
         else:
             over = roll(over, 64)
-        r[x, :, 0:128] = jnp.where(low, down, turned)
-        r[x, :, 128:256] = jnp.where(low, turned, over)
-        halved = [mid[pl.ds(128 * half + x, 8, stride=16), :] for half in range(2)]
-        high, rest = split3(jnp.concatenate(halved, axis=1))
-        stacked = jnp.concatenate([high, rest, high, jnp.zeros((8, 256), F32)], axis=0)
+        r[:, first] = jnp.where(low, down, turned)
+        r[:, second] = jnp.where(low, turned, over)
+    planes = CHUNK // 256
+    for c in range(CHUNKS):
+        at = slice(CHUNK * c, CHUNK * (c + 1))
+        pieces = [
+            mid[pl.ds(128 * half + planes * c + n, 8, stride=16), :]
+            for n in range(planes)
+            for half in range(2)
+        ]
+        high, rest = split3(jnp.concatenate(pieces, axis=1))
+        stacked = jnp.concatenate([high, rest, high, jnp.zeros((8, CHUNK), F32)], axis=0)
         lifted = mm(lift[...], stacked.astype(BF16))
-        u[x] = lifted
-        sol[x] = pre[x] + lifted
+        u[:, at] = lifted
+        sol[:, at] = pre[:, at] + lifted
     fine_apply(u, r, w, coef, wide, spread, px, qx, None, sol, inv)
-
-    def begin(x, carry):
-        new = inv[x] * r[x] / MIDDLE
-        u[x] = new
-        sol[x] = sol[x] + new
-        return carry
-
-    lax.fori_loop(0, NX, begin, 0)
+    for c in range(CHUNKS):
+        at = slice(CHUNK * c, CHUNK * (c + 1))
+        new = inv[:, at] * r[:, at] / MIDDLE
+        u[:, at] = new
+        sol[:, at] = sol[:, at] + new
     fine_apply(u, r, w, coef, wide, spread, px, qx, 0, sol, inv)
     fine_apply(u, r, w, coef, wide, spread, px, qx, 1, sol, inv)
     fine_apply(u, r, w, coef, wide, spread, px, qx, None, sol, inv)
@@ -756,9 +751,10 @@
         for part, ref in enumerate((sol, r)):
             for y in range(8):
                 half, at = (y + 4) // 8, 16 * ((y + 4) % 8) + 4
+                start = 256 * x + 128 * half
                 acc = jnp.where(
                     lane // 8 == 8 * part + y,
-                    roll(ref[x, :, 128 * half : 128 * half + 128], 64 * part + 8 * y - at),
+                    roll(ref[:, start : start + 128], 64 * part + 8 * y - at),
                     acc,
                 )
         out[x] = acc
@@ -903,7 +899,6 @@
             jnp.zeros_like(side),
         ]
     ).astype(jnp.int32)
-    wide, spread, diag_w, diag_e, down, mid_diag_w, mid_diag_e, lift, scal = tables(element, faces)
     res = residual.reshape(512, 128)
     cf = jnp.concatenate(
         [
@@ -927,18 +922,21 @@
         (1, 0, 0, 0),
         [pltpu.VMEM((3, 8, 64, 128), F32), pltpu.VMEM((3, 8, 8, 128), F32)],
     )(pos, res, cf, halo)
+    element, faces, slots = lax.optimization_barrier((element, faces, slots))
+    wide, spread, diag_w, diag_e, down, mid_diag_w, mid_diag_e, lift, scal = tables(element, faces)
     own = lax.all_to_all(slots, "gx", 0, 0, tiled=True)
     below = lax.ppermute(own, "yz", shift_up)
     above = lax.ppermute(own, "yz", shift_dn)
-    plane = (NX, 64, 256)
+    plane = (64, NX * 256)
+    strip = (16, NX * 256 + 256)
     pre, r, w, coef, inv, cfm, send_up, send_down = call(
         fine_pre_body,
         "fine_pre",
         [
             f32s(*plane),
             f32s(*plane),
-            f32s(NX, 24, 256),
-            f32s(NX, 8, 256),
+            f32s(24, NX * 256),
+            f32s(8, NX * 256),
             f32s(*plane),
             f32s(128, 1024),
             f32s(512, 128),
@@ -947,8 +945,8 @@
         (1,) + (0,) * 10,
         [
             pltpu.VMEM(plane, F32),
-            pltpu.VMEM((NX + 1, 16, 256), F32),
-            pltpu.VMEM((NX + 1, 16, 256), F32),
+            pltpu.VMEM(strip, F32),
+            pltpu.VMEM(strip, F32),
             pltpu.VMEM((768, 128), F32),
         ],
     )(pos, own, below, above, wide, spread, diag_w, diag_e, down, mid_diag_w, mid_diag_e)
@@ -1013,8 +1011,8 @@
             pltpu.VMEM(plane, F32),
             pltpu.VMEM(plane, F32),
             pltpu.VMEM(plane, F32),
-            pltpu.VMEM((NX + 1, 16, 256), F32),
-            pltpu.VMEM((NX + 1, 16, 256), F32),
+            pltpu.VMEM(strip, F32),
+            pltpu.VMEM(strip, F32),
         ],
     )(mid_sol, pre, frz, below, above, w, coef, inv, wide, spread, lift)
     got = lax.all_to_all(packed, "gx", 0, 0, tiled=True)

time: 254 us -> 203 us (0.80)
  Pallas kernels: 88.8 us -> 35.1 us
    pallas_call x1, Pallas kernels: 31.9 us -> 6.88 us  [local(): call(fine_post_body, 'fine_post', f32s(16, 64, 128), (0,) * 11, [pltpu.VM...]
    pallas_call x1, Pallas kernels: 27.8 us -> 6.23 us  [local(): call(fine_pre_body, 'fine_pre', [f32s(*plane), f32s(*plane), f32s(24, NX...]
    pallas_call x1, Pallas kernels: 8.54 us -> 4.59 us  [local(): call(mid_post_body, 'mid_post', f32s(256, 128), (1, 1, 0, 0, 0, 0, 0), mi...]
    pallas_call x1, Pallas kernels: 7.01 us -> 3.83 us  [local(): call(mid_pre_body, 'mid_pre', [f32s(*mid), f32s(*mid), f32s(5, 16, 1024),...]
    unnamed x46 -> x47, local copies, waits for them, and re-layouts: 10.4 us -> 10.5 us
  transfers between devices with their start and end apart: 13 -> 13, of which waited for: 9 -> 10; matrix products, arithmetic and copies ran while one was open for 3% -> 2% of each run, Pallas kernels for 0% -> 0%
where the time goes in v2:
time: 203 us; the launch traced here: 202 us
  starting transfers between devices  71.7 us (35%)
  waiting for transfers between devices  51.9 us (26%)
  Pallas kernels  35.1 us (17%)
  blocking collectives  20.6 us (10%)
  local copies, waits for them, and re-layouts  15.5 us (8%)
  between operations  3.1 us (2%)
  matrix products  2.2 us (1%)
    all_to_all x1, starting transfers between devices, local(): grams = lax.all_to_all(gram, ('gx', 'yz', 'lvl'), 0, 0, tiled=True)  22.7 us
    all_to_all x1, blocking collectives, local(): got = lax.all_to_all(packed, 'gx', 0, 0, tiled=True)  20.6 us
    all_to_all x1, waiting for transfers between devices, local(): grams = lax.all_to_all(gram, ('gx', 'yz', 'lvl'), 0, 0, tiled=True)  16.3 us
    all_to_all x1, waiting for transfers between devices, local(): own = lax.all_to_all(slots, 'gx', 0, 0, tiled=True)  13.6 us
    unnamed x47, local copies, waits for them, and re-layouts  10.5 us
    all_to_all x1, starting transfers between devices, local(): own = lax.all_to_all(slots, 'gx', 0, 0, tiled=True)  9.3 us
    ppermute x1, starting transfers between devices, local(): below = lax.ppermute(fwd, 'yz', shift_up)  8.73 us
    ppermute x2, starting transfers between devices, local(): up = lax.ppermute(send_down, z_axes, z_dn)  7.18 us
  transfers between devices with their start and end apart: 13, of which 10 were waited for; matrix products, arithmetic and copies ran while one was open for 2% of the time, Pallas kernels for 0%

profile of v2, /device:TPU:2, one launch (start us, length us, event | category | flops | bytes accessed | tf_op | source)
XLA Modules:
  0.0 201.5 jit_solution(6949548254714363871)
XLA Ops:
  3.3 4.2 %collective-permute-start = (f32[24,128]{1,0:T(8,128)S(1)}, f32[24,128]{1,0:T(8,128)S(1)}, u32[]{:S(2)}, u32[]{:S(2)}) collective-permute-start(f32[24,128]{1,0:T(8,128)S(1)} %edges.1), channel_id=1, source_target_pairs={{0,1},{1,0},{2,3},{3,2},{4,5},{5,4},{6,7},{7,6},{8,9},{9,8},{10,11... | collective-permute-start | bytes 36872 | tf_op jit(solution)/shard_map/ppermute | solution.py:917
  10.5 3.2 %slots.1 = f32[16,80,128]{2,1,0:T(8,128)} custom-call(s32[4]{0:T(128)S(1)} %pad_add_fusion.pos, f32[512,128]{1,0:T(8,128)S(1)} %bitcast.80, f32[64,128]{1,0:T(8,128)S(1)} %bitcast.83, f32[24,128]{1,0:T(8,128)S(1)} %collective-permute-done.halo), custom_call_target="tpu_custom_call" | custom-call | flops 1000000 | bytes 1000000 | tf_op jit(solution)/shard_map/slots/pallas_call | solution.py:918
  17.9 9.3 %all-to-all-start = ((f32[16,80,128]{2,1,0:T(8,128)}), f32[16,80,128]{2,1,0:T(8,128)S(1)}, u32[]{:S(2)}, u32[]{:S(2)}) async-start(f32[16,80,128]{2,1,0:T(8,128)} %slots.1), calls=%async_computation | async-start | bytes 1310720 | tf_op jit(solution)/shard_map/all_to_all | solution.py:927
  30.1 13.6 %all-to-all-done.own = f32[16,80,128]{2,1,0:T(8,128)S(1)} async-done(((f32[16,80,128]{2,1,0:T(8,128)}), f32[16,80,128]{2,1,0:T(8,128)S(1)}, u32[]{:S(2)}, u32[]{:S(2)}) %all-to-all-start) | async-done | bytes 655392 | tf_op jit(solution)/shard_map/all_to_all | solution.py:927
  45.0 3.1 %collective-permute-start.1 = (f32[16,80,128]{2,1,0:T(8,128)S(1)}, f32[16,80,128]{2,1,0:T(8,128)S(1)}, u32[]{:S(2)}, u32[]{:S(2)}) collective-permute-start(f32[16,80,128]{2,1,0:T(8,128)S(1)} %all-to-all-done.own), channel_id=1, source_target_pairs={{0,2},{2,4},{4,6},{6,8},{8,10},{10,12},{12,14},{14,16},{16,18},{18... | collective-permute-start | bytes 1966088 | tf_op jit(solution)/shard_map/ppermute | solution.py:928
  49.7 6.2 %fine_pre.1 = (f32[64,4096]{1,0:T(8,128)S(1)}, f32[64,4096]{1,0:T(8,128)S(1)}, f32[24,4096]{1,0:T(8,128)S(1)}, f32[8,4096]{1,0:T(8,128)S(1)}, f32[64,4096]{1,0:T...) custom-call(s32[4]{0:T(128)S(1)} %pad_add_fusion.pos, ...), custom_call_target="tpu_custom_call" | custom-call | flops 1000000 | bytes 1000000 | tf_op jit(solution)/shard_map/fine_pre/pallas_call | solution.py:932
  57.0 3.7 %collective-permute-start.4 = (f32[512,128]{1,0:T(8,128)S(1)}, f32[512,128]{1,0:T(8,128)S(1)}, u32[]{:S(2)}, u32[]{:S(2)}) collective-permute-start(f32[512,128]{1,0:T(8,128)S(1)} %get-tuple-element.33), channel_id=1, source_target_pairs={{32,0},{64,32},{96,64},{128,96},{160,128},{192,160},{224,192},{256... | collective-permute-start | bytes 786440 | tf_op jit(solution)/shard_map/ppermute | solution.py:954
  60.7 3.0 %collective-permute-start.3 = (f32[512,128]{1,0:T(8,128)S(1)}, f32[512,128]{1,0:T(8,128)S(1)}, u32[]{:S(2)}, u32[]{:S(2)}) collective-permute-start(f32[512,128]{1,0:T(8,128)S(1)} %get-tuple-element.32.own), channel_id=1, source_target_pairs={{0,32},{32,64},{64,96},{96,128},{128,160},{160,192},{192,224},{224... | collective-permute-start | bytes 786440 | tf_op jit(solution)/shard_map/ppermute | solution.py:953
  63.7 2.4 %collective-permute-done.4.up = f32[512,128]{1,0:T(8,128)S(1)} collective-permute-done((f32[512,128]{1,0:T(8,128)S(1)}, f32[512,128]{1,0:T(8,128)S(1)}, u32[]{:S(2)}, u32[]{:S(2)}) %collective-permute-start.4) | collective-permute-done | bytes 262176 | tf_op jit(solution)/shard_map/ppermute | solution.py:954
  66.1 2.8 %collective-permute-done.3.dn = f32[512,128]{1,0:T(8,128)S(1)} collective-permute-done((f32[512,128]{1,0:T(8,128)S(1)}, f32[512,128]{1,0:T(8,128)S(1)}, u32[]{:S(2)}, u32[]{:S(2)}) %collective-permute-start.3) | collective-permute-done | bytes 262176 | tf_op jit(solution)/shard_map/ppermute | solution.py:953
  71.8 8.7 %collective-permute-start.5 = (f32[928,128]{1,0:T(8,128)}, f32[928,128]{1,0:T(8,128)S(1)}, u32[]{:S(2)}, u32[]{:S(2)}) collective-permute-start(f32[928,128]{1,0:T(8,128)} %get-tuple-element.37), channel_id=1, source_target_pairs={{0,2},{2,4},{4,6},{6,8},{8,10},{10,12},{12,14},{14,16},{16,18},{18... | collective-permute-start | bytes 1425416 | tf_op jit(solution)/shard_map/ppermute | solution.py:961
  85.7 6.6 %collective-permute-done.6.above = f32[896,128]{1,0:T(8,128)S(1)} collective-permute-done((f32[896,128]{1,0:T(8,128)}, f32[896,128]{1,0:T(8,128)S(1)}, u32[]{:S(2)}, u32[]{:S(2)}) %collective-permute-start.6) | collective-permute-done | bytes 458784 | tf_op jit(solution)/shard_map/ppermute | solution.py:962
  92.2 3.8 %mid_pre.1 = (f32[8,16,1024]{2,1,0:T(8,128)S(1)}, f32[8,16,1024]{2,1,0:T(8,128)S(1)}, f32[5,16,1024]{2,1,0:T(8,128)S(1)}, f32[2,16,768]{2,1,0:T(8,128)S(1)}, f32[2,16,768]{2,1,0:T(8,128)S(1)}) custom-call(s32[4]{0:T(128)S(1)} %pad_add_fusion.pos, f32[144]{0:T(256)S(1)} %concatenate.46.scal, f32[128,256]{1,0:T(8,128)S(1)} %get-tuple-element.36.slab, ...), custom_call_target="tpu_custom_call" | custom-call | flops 1000000 | bytes 1000000 | tf_op jit(solution)/shard_map/mid_pre/pallas_call | solution.py:970
  100.0 3.5 %collective-permute-start.8 = (f32[2,16,768]{2,1,0:T(8,128)S(1)}, f32[2,16,768]{2,1,0:T(8,128)S(1)}, u32[]{:S(2)}, u32[]{:S(2)}) collective-permute-start(f32[2,16,768]{2,1,0:T(8,128)S(1)} %get-tuple-element.41), channel_id=1, source_target_pairs={{32,0},{64,32},{96,64},{128,96},{160,128},{192,160},{224,192},{256... | collective-permute-start | bytes 294920 | tf_op jit(solution)/shard_map/ppermute | solution.py:981
  104.1 3.3 %collective-permute-done.8.up = f32[2,16,768]{2,1,0:T(8,128)S(1)} collective-permute-done((f32[2,16,768]{2,1,0:T(8,128)S(1)}, f32[2,16,768]{2,1,0:T(8,128)S(1)}, u32[]{:S(2)}, u32[]{:S(2)}) %collective-permute-start.8) | collective-permute-done | bytes 98336 | tf_op jit(solution)/shard_map/ppermute | solution.py:981
  108.1 7.1 %collective-permute-start.9 = (f32[5,16,512]{2,1,0:T(8,128)S(1)}, f32[5,16,512]{2,1,0:T(8,128)S(1)}, u32[]{:S(2)}, u32[]{:S(2)}) collective-permute-start(f32[5,16,512]{2,1,0:T(8,128)S(1)} %get-tuple-element.43), channel_id=1, source_target_pairs={{0,2},{2,4},{4,6},{6,8},{8,10},{10,12},{12,14},{14,16},{16,18},{18... | collective-permute-start | bytes 491528 | tf_op jit(solution)/shard_map/ppermute | solution.py:988
  116.5 2.8 %collective-permute-done.10.above = f32[5,16,512]{2,1,0:T(8,128)S(1)} collective-permute-done((f32[5,16,512]{2,1,0:T(8,128)S(1)}, f32[5,16,512]{2,1,0:T(8,128)S(1)}, u32[]{:S(2)}, u32[]{:S(2)}) %collective-permute-start.10) | collective-permute-done | bytes 163872 | tf_op jit(solution)/shard_map/ppermute | solution.py:989
  119.3 3.9 %krylov.1 = (f32[8,16,1536]{2,1,0:T(8,128)S(1)}, f32[512,128]{1,0:T(8,128)}) custom-call(f32[144]{0:T(256)S(1)} %concatenate.46.scal, f32[5,16,1280]{2,1,0:T(8,128)S(1)} %get-tuple-element.42.own, f32[5,16,512]{2,1,0:T(8,128)S(1)} %collective-permute-done.9.below, f32[5,16,512]{2,1,0:T(8,128)S(1)} %collective-permute-done.10.above), custom_call_target="tpu_custom_call" | custom-call | flops 1000000 | bytes 1000000 | tf_op jit(solution)/shard_map/krylov/pallas_call | solution.py:990
  124.1 22.7 %all-to-all-start.1 = ((f32[512,1,128]{2,1,0:T(1,128)}), f32[512,1,128]{2,1,0:T(1,128)S(1)}, u32[]{:S(2)}, u32[]{:S(2)}) async-start(f32[512,1,128]{2,1,0:T(1,128)} %bitcast.37), calls=%async_computation.1 | async-start | bytes 524288 | tf_op jit(solution)/shard_map/all_to_all | solution.py:997
  147.0 16.3 %all-to-all-done.1 = f32[512,1,128]{2,1,0:T(1,128)S(1)} async-done(((f32[512,1,128]{2,1,0:T(1,128)}), f32[512,1,128]{2,1,0:T(1,128)S(1)}, u32[]{:S(2)}, u32[]{:S(2)}) %all-to-all-start.1) | async-done | bytes 262176 | tf_op jit(solution)/shard_map/all_to_all | solution.py:997
  166.5 4.6 %mid_post.1.mid = f32[256,128]{1,0:T(8,128)S(1)} custom-call(s32[4]{0:T(128)S(1)} %pad_add_fusion.pos, f32[144]{0:T(256)S(1)} %concatenate.46.scal, f32[512,128]{1,0:T(8,128)S(1)} %bitcast.81, f32[8,16,1536]{2,1,0:T(8,128)S(1)} %copy-done.5, f32[128,1024]{1,0:T(8,128)S(1)} %get-tuple-element.35.cfm.cfm_in, f32[8,16,1024]{2,1,0:T(8,128)S(1)} %copy-done.9, ...), custom_call_target="tpu_custom_call" | custom-call | flops 1000000 | bytes 1000000 | tf_op jit(solution)/shard_map/mid_post/pallas_call | solution.py:998
  171.1 6.9 %fine_post.1 = f32[16,64,128]{2,1,0:T(8,128)S(1)} custom-call(f32[256,128]{1,0:T(8,128)S(1)} %mid_post.1.mid, f32[64,4096]{1,0:T(8,128)S(1)} %get-tuple-element.49.pre, f32[16,64,128]{2,1,0:T(8,128)S(1)} %copy-done.7, f32[928,128]{1,0:T(8,128)S(1)} %collective-permute-done.5.below, f32[896,128]{1,0:T(8,128)S(1)} %collective-permute-done.6.above, ...), custom_call_target="tpu_custom_call" | custom-call | flops 1000000 | bytes 1000000 | tf_op jit(solution)/shard_map/fine_post/pallas_call | solution.py:1005
  178.0 20.6 %all_to_all.21.got = f32[16,64,128]{2,1,0:T(8,128)S(1)} all-to-all(f32[16,64,128]{2,1,0:T(8,128)S(1)} %fine_post.1), channel_id=1, replica_groups=mesh['gx'=16,'yz'=16,'lvl'=2] {'gx'}, dimensions={0} | all-to-all | bytes 1048576 | tf_op jit(solution)/shard_map/all_to_all | solution.py:1018
  198.7 2.8 %unpack.1 = (f32[512,128]{1,0:T(8,128)}, f32[512,128]{1,0:T(8,128)}) custom-call(f32[16,64,128]{2,1,0:T(8,128)S(1)} %all_to_all.21.got), custom_call_target="tpu_custom_call" | custom-call | flops 1000000 | bytes 1000000 | tf_op jit(solution)/shard_map/unpack/pallas_call | solution.py:1019
  (119 shorter events, 33.2 us)
Async XLA Ops:
  2.5 5.1 %copy-start.20 = (f32[4,2]{0,1:T(2,128)S(1)}, f32[4,2]{0,1:T(2,128)}, u32[]{:S(2)}) copy-start(f32[4,2]{0,1:T(2,128)} %constant.81) | copy-start | bytes 100
  3.3 7.2 %copy-start.3 = (f32[64,1,8,128]{3,2,1,0:T(8,128)S(1)}, f32[64,1,8,128]{3,2,1,0:T(8,128)}, u32[]{:S(2)}) copy-start(f32[64,1,8,128]{3,2,1,0:T(8,128)} %param.11) | copy-start | bytes 786436
  3.3 7.2 %collective-permute-start = (f32[24,128]{1,0:T(8,128)S(1)}, f32[24,128]{1,0:T(8,128)S(1)}, u32[]{:S(2)}, u32[]{:S(2)}) collective-permute-start(f32[24,128]{1,0:T(8,128)S(1)} %edges.1), channel_id=1, source_target_pairs={{0,1},{1,0},{2,3},{3,2},{4,5},{5,4},{6,7},{7,6},{8,9},{9,8},{10,11... | collective-permute-start | bytes 36872 | tf_op jit(solution)/shard_map/ppermute | solution.py:917
  8.4 5.3 %copy-start.16 = (f32[4,16,16]{2,1,0:T(8,128)S(1)}, f32[4,16,16]{2,1,0:T(8,128)}, u32[]{:S(2)}) copy-start(f32[4,16,16]{2,1,0:T(8,128)} %param.14) | copy-start | bytes 12292
  17.9 25.8 %all-to-all-start = ((f32[16,80,128]{2,1,0:T(8,128)}), f32[16,80,128]{2,1,0:T(8,128)S(1)}, u32[]{:S(2)}, u32[]{:S(2)}) async-start(f32[16,80,128]{2,1,0:T(8,128)} %slots.1), calls=%async_computation | async-start | bytes 1310720 | tf_op jit(solution)/shard_map/all_to_all | solution.py:927
  43.7 4.7 %collective-permute-start.2 = (f32[16,80,128]{2,1,0:T(8,128)S(1)}, f32[16,80,128]{2,1,0:T(8,128)S(1)}, u32[]{:S(2)}, u32[]{:S(2)}) collective-permute-start(f32[16,80,128]{2,1,0:T(8,128)S(1)} %all-to-all-done.own), channel_id=1, source_target_pairs={{2,0},{4,2},{6,4},{8,6},{10,8},{12,10},{14,12},{16,14},{18,16},{20... | collective-permute-start | bytes 1966088 | tf_op jit(solution)/shard_map/ppermute | solution.py:929
  45.0 4.7 %collective-permute-start.1 = (f32[16,80,128]{2,1,0:T(8,128)S(1)}, f32[16,80,128]{2,1,0:T(8,128)S(1)}, u32[]{:S(2)}, u32[]{:S(2)}) collective-permute-start(f32[16,80,128]{2,1,0:T(8,128)S(1)} %all-to-all-done.own), channel_id=1, source_target_pairs={{0,2},{2,4},{4,6},{6,8},{8,10},{10,12},{12,14},{14,16},{16,18},{18... | collective-permute-start | bytes 1966088 | tf_op jit(solution)/shard_map/ppermute | solution.py:928
  48.3 1.4 copy-start.14
  57.0 14.0 %copy-start.12 = (f32[24,4096]{1,0:T(8,128)}, f32[24,4096]{1,0:T(8,128)S(1)}, u32[]{:S(2)}) copy-start(f32[24,4096]{1,0:T(8,128)S(1)} %get-tuple-element.51.w) | copy-start | bytes 1179652
  57.0 9.2 %collective-permute-start.4 = (f32[512,128]{1,0:T(8,128)S(1)}, f32[512,128]{1,0:T(8,128)S(1)}, u32[]{:S(2)}, u32[]{:S(2)}) collective-permute-start(f32[512,128]{1,0:T(8,128)S(1)} %get-tuple-element.33), channel_id=1, source_target_pairs={{32,0},{64,32},{96,64},{128,96},{160,128},{192,160},{224,192},{256... | collective-permute-start | bytes 786440 | tf_op jit(solution)/shard_map/ppermute | solution.py:954
  60.7 8.3 %collective-permute-start.3 = (f32[512,128]{1,0:T(8,128)S(1)}, f32[512,128]{1,0:T(8,128)S(1)}, u32[]{:S(2)}, u32[]{:S(2)}) collective-permute-start(f32[512,128]{1,0:T(8,128)S(1)} %get-tuple-element.32.own), channel_id=1, source_target_pairs={{0,32},{32,64},{64,96},{96,128},{128,160},{160,192},{192,224},{224... | collective-permute-start | bytes 786440 | tf_op jit(solution)/shard_map/ppermute | solution.py:953
  71.8 20.4 %collective-permute-start.5 = (f32[928,128]{1,0:T(8,128)}, f32[928,128]{1,0:T(8,128)S(1)}, u32[]{:S(2)}, u32[]{:S(2)}) collective-permute-start(f32[928,128]{1,0:T(8,128)} %get-tuple-element.37), channel_id=1, source_target_pairs={{0,2},{2,4},{4,6},{6,8},{8,10},{10,12},{12,14},{14,16},{16,18},{18... | collective-permute-start | bytes 1425416 | tf_op jit(solution)/shard_map/ppermute | solution.py:961
  80.5 11.7 %collective-permute-start.6 = (f32[896,128]{1,0:T(8,128)}, f32[896,128]{1,0:T(8,128)S(1)}, u32[]{:S(2)}, u32[]{:S(2)}) collective-permute-start(f32[896,128]{1,0:T(8,128)} %get-tuple-element.38), channel_id=1, source_target_pairs={{2,0},{4,2},{6,4},{8,6},{10,8},{12,10},{14,12},{16,14},{18,16},{20... | collective-permute-start | bytes 1376264 | tf_op jit(solution)/shard_map/ppermute | solution.py:962
  97.7 6.5 %collective-permute-start.7 = (f32[2,16,768]{2,1,0:T(8,128)S(1)}, f32[2,16,768]{2,1,0:T(8,128)S(1)}, u32[]{:S(2)}, u32[]{:S(2)}) collective-permute-start(f32[2,16,768]{2,1,0:T(8,128)S(1)} %get-tuple-element.40), channel_id=1, source_target_pairs={{0,32},{32,64},{64,96},{96,128},{128,160},{160,192},{192,224},{224... | collective-permute-start | bytes 294920 | tf_op jit(solution)/shard_map/ppermute | solution.py:980
  100.0 7.4 %collective-permute-start.8 = (f32[2,16,768]{2,1,0:T(8,128)S(1)}, f32[2,16,768]{2,1,0:T(8,128)S(1)}, u32[]{:S(2)}, u32[]{:S(2)}) collective-permute-start(f32[2,16,768]{2,1,0:T(8,128)S(1)} %get-tuple-element.41), channel_id=1, source_target_pairs={{32,0},{64,32},{96,64},{128,96},{160,128},{192,160},{224,192},{256... | collective-permute-start | bytes 294920 | tf_op jit(solution)/shard_map/ppermute | solution.py:981
  108.1 8.4 %collective-permute-start.9 = (f32[5,16,512]{2,1,0:T(8,128)S(1)}, f32[5,16,512]{2,1,0:T(8,128)S(1)}, u32[]{:S(2)}, u32[]{:S(2)}) collective-permute-start(f32[5,16,512]{2,1,0:T(8,128)S(1)} %get-tuple-element.43), channel_id=1, source_target_pairs={{0,2},{2,4},{4,6},{6,8},{8,10},{10,12},{12,14},{14,16},{16,18},{18... | collective-permute-start | bytes 491528 | tf_op jit(solution)/shard_map/ppermute | solution.py:988
  115.2 4.2 %collective-permute-start.10 = (f32[5,16,512]{2,1,0:T(8,128)S(1)}, f32[5,16,512]{2,1,0:T(8,128)S(1)}, u32[]{:S(2)}, u32[]{:S(2)}) collective-permute-start(f32[5,16,512]{2,1,0:T(8,128)S(1)} %get-tuple-element.44), channel_id=1, source_target_pairs={{2,0},{4,2},{6,4},{8,6},{10,8},{12,10},{14,12},{16,14},{18,16},{20... | collective-permute-start | bytes 491528 | tf_op jit(solution)/shard_map/ppermute | solution.py:989
  124.1 39.2 %all-to-all-start.1 = ((f32[512,1,128]{2,1,0:T(1,128)}), f32[512,1,128]{2,1,0:T(1,128)S(1)}, u32[]{:S(2)}, u32[]{:S(2)}) async-start(f32[512,1,128]{2,1,0:T(1,128)} %bitcast.37), calls=%async_computation.1 | async-start | bytes 524288 | tf_op jit(solution)/shard_map/all_to_all | solution.py:997
  163.3 1.1 copy-start.5
  164.4 1.0 copy-start.9
  165.5 1.0 copy-start.11
  166.5 4.6 %copy-start.1 = (f32[64,4096]{1,0:T(8,128)S(1)}, f32[64,4096]{1,0:T(8,128)}, u32[]{:S(2)}) copy-start(f32[64,4096]{1,0:T(8,128)} %copy-done) | copy-start | bytes 3145732
  166.5 4.6 %copy-start.7 = (f32[16,64,128]{2,1,0:T(8,128)S(1)}, f32[16,64,128]{2,1,0:T(8,128)}, u32[]{:S(2)}) copy-start(f32[16,64,128]{2,1,0:T(8,128)} %copy-done.6) | copy-start | bytes 1572868
  166.5 4.6 %copy-start.13 = (f32[24,4096]{1,0:T(8,128)S(1)}, f32[24,4096]{1,0:T(8,128)}, u32[]{:S(2)}) copy-start(f32[24,4096]{1,0:T(8,128)} %copy-done.12) | copy-start | bytes 1179652
  (12 other events, 9.8 us)

commit v3 on v2

--- a/solution.py
+++ b/solution.py
@@ -39,18 +39,23 @@
     return x if shift == 0 else pltpu.roll(x, shift, axis)
 
 
-def call(body, name, out_shape, in_specs, scratch=(), flops=1000000):
-    single = not isinstance(out_shape, (tuple, list))
-    outs = [out_shape] if single else list(out_shape)
-    vm = pl.BlockSpec(memory_space=pltpu.VMEM)
+SPACES = {
+    0: pl.BlockSpec(memory_space=pltpu.VMEM),
+    1: pl.BlockSpec(memory_space=pltpu.SMEM),
+    2: pl.BlockSpec(memory_space=pltpu.HBM),
+}
+
+
+def call(body, name, out_shape, in_specs, scratch=(), out_specs=None):
+    out_specs = out_specs or (0,) * len(out_shape)
     return pl.pallas_call(
         body,
-        out_shape=outs[0] if single else outs,
-        in_specs=[pl.BlockSpec(memory_space=pltpu.SMEM) if s else vm for s in in_specs],
-        out_specs=vm if single else [vm] * len(outs),
+        out_shape=list(out_shape),
+        in_specs=[SPACES[i] for i in in_specs],
+        out_specs=[SPACES[i] for i in out_specs],
         scratch_shapes=list(scratch),
         compiler_params=pltpu.CompilerParams(vmem_limit_bytes=VMEM_LIMIT),
-        cost_estimate=pl.CostEstimate(flops=flops, bytes_accessed=1000000, transcendentals=0),
+        cost_estimate=pl.CostEstimate(flops=1000000, bytes_accessed=1000000, transcendentals=0),
         name=name,
     )
 
@@ -74,58 +79,84 @@
     return jnp.dot(a, b, preferred_element_type=F32)
 
 
-def edges_body(pos, res, cf, out):
-    first = pos[2] == 0
-    lane = lanes((16, 128))
-    acc = [jnp.zeros((16, 128), F32)]
-    packed = jnp.zeros((16, 128), F32)
-    packed_cf = jnp.zeros((8, 128), F32)
-    lane8 = lanes((8, 128))
-    for y in range(8):
-        rows = res[pl.ds(y, 64, stride=8), :]
-        rows = jnp.where(first, roll(rows, 4), rows)
-        for j in range(4):
-            at = 32 * j + 4 * y
-            packed = jnp.where(
-                (lane >= at) & (lane < at + 4), roll(rows[16 * j : 16 * j + 16], at), packed
-            )
-        rows = cf[pl.ds(y, 8, stride=8), :]
-        rows = jnp.where(first, roll(rows, 12), rows)
-        at = 12 * y
-        packed_cf = jnp.where((lane8 >= at) & (lane8 < at + 12), roll(rows, at), packed_cf)
-    out[0:16, :] = packed
-    out[16:24, :] = packed_cf
-
-
-def slots_body(pos, res, cf, halo, out, rows, rows_cf):
-    first = pos[2] == 0
-    lane = lanes((64, 128))
-    lane8 = lanes((8, 128))
-    for y in range(8):
-        mine = res[pl.ds(y, 64, stride=8), :]
-        got = jnp.concatenate([roll(halo[0:16, :], -(32 * j + 4 * y)) for j in range(4)], axis=0)
-        rows[0, y] = jnp.where(lane >= 124, jnp.where(first, 0.0, roll(got, 124)), mine)
-        rows[1, y] = mine
-        rows[2, y] = jnp.where(lane < 4, jnp.where(first, got, 0.0), mine)
-        mine = cf[pl.ds(y, 8, stride=8), :]
-        got = roll(halo[16:24, :], -12 * y)
-        rows_cf[0, y] = jnp.where(lane8 >= 116, jnp.where(first, 0.0, roll(got, 116)), mine)
-        rows_cf[1, y] = mine
-        rows_cf[2, y] = jnp.where(lane8 < 12, jnp.where(first, got, 0.0), mine)
-    for g in range(NX):
-        source = 0 if g == 0 else (2 if g == NX - 1 else 1)
-        acc = jnp.zeros((64, 128), F32)
+def exchange(arrays, lane_block):
+    arrays = list(arrays)
+    group = lanes(arrays[0].shape) // lane_block
+    for bit in (1, 2, 4):
+        upper = (group // bit) % 2 == 1
+        for n in range(8):
+            if n & bit:
+                continue
+            a, b = arrays[n], arrays[n | bit]
+            arrays[n] = jnp.where(upper, roll(b, lane_block * bit), a)
+            arrays[n | bit] = jnp.where(upper, b, roll(a, -lane_block * bit))
+    return arrays
+
+
+def slots_body(res, cf, out):
+    low = lanes((32, 128)) < 64
+    low8 = lanes((8, 128)) < 64
+    values = exchange([res[pl.ds(y, 64, stride=8), :] for y in range(8)], 8)
+    kinds = exchange([cf[pl.ds(y, 16, stride=8), :] for y in range(8)], 8)
+    for j in range(8):
+        a, b = values[j][0:32], values[j][32:64]
+        out[j, 0:32, :] = jnp.where(low, a, roll(b, 64))
+        out[j + 8, 0:32, :] = jnp.where(low, roll(a, 64), b)
+        a, b = kinds[j][0:8], kinds[j][8:16]
+        out[j, 32:40, :] = jnp.where(low8, a, roll(b, 64))
+        out[j + 8, 32:40, :] = jnp.where(low8, roll(a, 64), b)
+
+
+def place_tables():
+    values = np.zeros((256, 256), np.float32)
+    kinds = np.zeros((384, 512), np.float32)
+    for half in range(2):
         for y in range(8):
-            acc = jnp.where(lane // 16 == y, roll(rows[source, y], 16 * y - (8 * g - 4)), acc)
-        out[g, 0:64, :] = acc
-        source = 0 if g <= 1 else (2 if g >= NX - 2 else 1)
-        for h in range(2):
-            acc = jnp.zeros((8, 128), F32)
-            for y in range(4):
-                acc = jnp.where(
-                    lane8 // 32 == y, roll(rows_cf[source, 4 * h + y], 32 * y - (8 * g - 12)), acc
-                )
-            out[g, 64 + 8 * h : 72 + 8 * h, :] = acc
+            for z in range(8):
+                lane = 64 * half + 8 * y + z
+                values[lane, 128 * half + 16 * y + z + 4] = 1.0
+                beside = z + 12 if z < 4 else z - 4
+                values[128 + lane, 128 * half + 16 * y + beside] = 1.0
+                for n, first in enumerate((12, 4, 20)):
+                    kinds[128 * n + lane, 256 * half + 32 * y + first + z] = 1.0
+    return values, kinds
+
+
+def three_rows(x):
+    high = x.astype(BF16).astype(F32)
+    rest = x - high
+    mid = rest.astype(BF16).astype(F32)
+    return jnp.concatenate([high, mid, rest - mid], axis=0).astype(BF16)
+
+
+def moved(x, table):
+    count = x.shape[0]
+    out = mm(three_rows(x), table)
+    return out[0:count] + out[count : 2 * count] + out[2 * count :]
+
+
+def join_body(own, dn, up, place_values, place_kinds, rows, fwd, bwd):
+    near = lanes((512, 128)) % 8 < 4
+    mine = own[:, 0:32, :].reshape(512, 128)
+    beside = jnp.where(near, up[:, 0:32, :].reshape(512, 128), dn[:, 0:32, :].reshape(512, 128))
+    out = moved(jnp.concatenate([mine, beside], axis=1), place_values[...])
+    for x in range(NX):
+        rows[x, 0:32, :] = out[32 * x : 32 * x + 32, 0:128]
+        rows[x, 32:64, :] = out[32 * x : 32 * x + 32, 128:256]
+    low = lanes((64, 128)) < 64
+    for x in range(8):
+        fwd[64 * x : 64 * x + 64, :] = jnp.where(low, roll(rows[x], 64), rows[x + 8])
+        bwd[64 * x : 64 * x + 64, :] = jnp.where(low, rows[x], roll(rows[x + 8], 64))
+    kinds = jnp.concatenate([v[:, 32:40, :].reshape(128, 128) for v in (own, dn, up)], axis=1)
+    out = moved(kinds, place_kinds[...])
+    array = lax.broadcasted_iota(jnp.int32, (128, 128), 0) % 8
+    edge = (lanes((128, 128)) % 32 == 3) & ((array == 3) | (array == 6))
+    for h in range(2):
+        minus = out[:, 256 + 128 * h : 384 + 128 * h]
+        plus = jnp.where(edge, roll(minus, -1), out[:, 128 * h : 128 * h + 128])
+        fwd[512 + 128 * h : 640 + 128 * h, :] = plus
+        bwd[512 + 128 * h : 640 + 128 * h, :] = plus
+    fwd[768:896, :] = out[:, 256:384]
 
 
 CHUNK = 4096
@@ -171,6 +202,7 @@
 
 def fine_pre_body(
     pos,
+    rows_in,
     own,
     below,
     above,
@@ -181,23 +213,27 @@
     down,
     mid_diag_w,
     mid_diag_e,
+    sol_out,
+    r,
+    w_out,
+    coef_out,
+    inv_out,
+    cfm,
+    send_up,
+    send_down,
     sol,
-    r,
     w,
     coef,
     inv,
-    cfm,
-    send_up,
-    send_down,
     u,
     px,
     qx,
     gather,
+    sems,
 ):
     low = lanes((64, 128)) < 64
-    low8 = lanes((8, 128)) < 64
     lane8 = lanes((8, 128))
-    place = lanes((1, 256)) % 256
+    place = lanes((1, 256))
     y_at = pos[0] * 8 - 4 + place // 16
     z_at = pos[1] * 8 - 4 + place % 16
     inside = (y_at >= 0) & (y_at < NY) & (z_at >= 0) & (z_at < NZ)
@@ -206,23 +242,30 @@
     inside_f = jnp.where(inside, 1.0, 0.0)
     px[:, 0:256] = jnp.zeros((16, 256), F32)
     qx[:, NX * 256 :] = jnp.zeros((16, 256), F32)
-    cfm[:, 0:128] = jnp.zeros((128, 128), F32)
     cfm[:, 896:1024] = jnp.zeros((128, 128), F32)
+    array = lax.broadcasted_iota(jnp.int32, (8, 128), 0)
+    edge = (lane8 >= 96) & ((array == 2) | (array == 5))
     for x in range(NX):
         first, second = slice(256 * x, 256 * x + 128), slice(256 * x + 128, 256 * x + 256)
-        turned = roll(own[x, 0:64, :], 64)
-        r[:, first] = jnp.where(low, roll(below[x, 0:64, :], 64), turned)
-        r[:, second] = jnp.where(low, turned, roll(above[x, 0:64, :], 64))
+        turned = roll(rows_in[x], 64)
+        at = 64 * (x % 8)
+        under = below[at : at + 64, :]
+        over = above[at : at + 64, :]
+        if x >= 8:
+            under = roll(under, 64)
+        else:
+            over = roll(over, 64)
+        r[:, first] = jnp.where(low, under, turned)
+        r[:, second] = jnp.where(low, turned, over)
         blocks = [
-            below[x, 64:72, :],
-            below[x, 72:80, :],
-            own[x, 64:72, :],
-            own[x, 72:80, :],
-            above[x, 64:72, :],
-            above[x, 72:80, :],
+            ref[512 + 128 * h + 8 * x : 520 + 128 * h + 8 * x, :]
+            for ref in (below, own, above)
+            for h in range(2)
         ]
+        minus = below[768 + 8 * x : 776 + 8 * x, :]
+        gather[pl.ds(x, 8, stride=16), :] = jnp.where(edge, roll(minus, 96), 0.0)
         for m in range(6):
-            gather[pl.ds(128 * m + x, 8, stride=16), :] = blocks[m]
+            gather[pl.ds(128 * (m + 1) + x, 8, stride=16), :] = blocks[m]
         for half, at in enumerate((first, second)):
             acc = jnp.zeros((8, 128), F32)
             for row in range(8):
@@ -233,8 +276,8 @@
                     acc,
                 )
             coef[:, at] = acc
-    for m in range(6):
-        cfm[:, 128 * (m + 1) : 128 * (m + 2)] = gather[128 * m : 128 * m + 128, :]
+    for m in range(7):
+        cfm[:, 128 * m : 128 * m + 128] = gather[128 * m : 128 * m + 128, :]
     w[12:16, 0:256] = jnp.zeros((4, 256), F32)
     for x in range(NX):
         at = slice(256 * x, 256 * x + 256)
@@ -268,8 +311,17 @@
         update = inverse * r[:, at] / MIDDLE
         u[:, at] = update
         sol[:, at] = update
+    copies = [
+        pltpu.make_async_copy(held, out, sems.at[n])
+        for n, (held, out) in enumerate(
+            ((w, w_out), (coef, coef_out), (inv, inv_out), (sol, sol_out))
+        )
+    ]
+    for copy in copies[:3]:
+        copy.start()
     fine_apply(u, r, w, coef, wide, spread, px, qx, 0, sol, inv)
     fine_apply(u, r, w, coef, wide, spread, px, qx, 1, sol, inv)
+    copies[3].start()
     fine_apply(u, r, w, coef, wide, spread, px, qx, None, sol, inv)
     lane16 = lanes((16, 128)) % 16 // 4
     for c in range(CHUNKS):
@@ -294,9 +346,28 @@
             dn = jnp.where(lane16 == j, roll(part, 4 * j - 4), dn)
         send_up[256 + 16 * x : 272 + 16 * x, :] = up
         send_down[256 + 16 * x : 272 + 16 * x, :] = dn
-
-
-def mid_z_body(own, dn, up, r, cfm, slab, fwd, bwd, frz):
+    for copy in copies:
+        copy.wait()
+
+
+def mid_z_body(own, dn, up, r, slab, fwd, bwd, frz_out, frz, sem):
+    low = lanes((64, 128)) < 64
+    l16 = lanes((16, 128)) % 16
+    for x in range(NX):
+        at = 256 * x
+        mine = jnp.where(low, roll(r[:, at : at + 128], 64), roll(r[:, at + 128 : at + 256], 64))
+        pack_dn = dn[256 + 16 * x : 272 + 16 * x, :]
+        pack_up = up[256 + 16 * x : 272 + 16 * x, :]
+        for j in range(4):
+            rows = slice(16 * j, 16 * j + 16)
+            part = jnp.where(l16 < 4, roll(pack_dn, -4 * j), mine[rows])
+            part = jnp.where(l16 >= 12, roll(pack_up, 12 - 4 * j), part)
+            frz[x, rows, :] = part
+    copy = pltpu.make_async_copy(frz, frz_out, sem)
+    copy.start()
+    for x in range(8):
+        fwd[384 + 64 * x : 448 + 64 * x, :] = jnp.where(low, roll(frz[x], 64), frz[x + 8])
+        bwd[384 + 64 * x : 448 + 64 * x, :] = jnp.where(low, frz[x], roll(frz[x + 8], 64))
     lane = lanes((128, 128))
     for m in range(4):
         acc = jnp.zeros((128, 128), F32)
@@ -316,23 +387,7 @@
             fwd[128 * m : 128 * m + 128, :] = acc
         if m >= 1:
             bwd[128 * (m - 1) : 128 * m, :] = acc
-    fwd[896:912, :] = cfm[32:48, 256:384]
-    fwd[912:928, :] = cfm[80:96, 256:384]
-    low = lanes((64, 128)) < 64
-    l16 = lanes((16, 128)) % 16
-    for x in range(NX):
-        at = 256 * x
-        mine = jnp.where(low, roll(r[:, at : at + 128], 64), roll(r[:, at + 128 : at + 256], 64))
-        pack_dn = dn[256 + 16 * x : 272 + 16 * x, :]
-        pack_up = up[256 + 16 * x : 272 + 16 * x, :]
-        for j in range(4):
-            rows = slice(16 * j, 16 * j + 16)
-            part = jnp.where(l16 < 4, roll(pack_dn, -4 * j), mine[rows])
-            part = jnp.where(l16 >= 12, roll(pack_up, 12 - 4 * j), part)
-            frz[x, rows, :] = part
-    for x in range(8):
-        fwd[384 + 64 * x : 448 + 64 * x, :] = jnp.where(low, roll(frz[x], 64), frz[x + 8])
-        bwd[384 + 64 * x : 448 + 64 * x, :] = jnp.where(low, frz[x], roll(frz[x + 8], 64))
+    copy.wait()
 
 
 LOWS = ((0, 1, 2, 3), (0, 1, 4, 5), (0, 2, 4, 6))
@@ -357,7 +412,7 @@
     y_at = pos[0] * 8 - 12 + place // 32
     z_at = pos[1] * 8 - 12 + place % 32
     domain = (y_at >= 0) & (y_at < NY) & (z_at >= 0) & (z_at < NZ)
-    known = domain & (place >= 128) & (place < 896)
+    known = domain & (place >= 128) & (place < 896) & (place % 32 >= 4) & (place % 32 < 28)
     lasts = (x_at < NX - 1, y_at < NY - 1, z_at < NZ - 1)
     for d in range(3):
         is_open = domain & lasts[d] & (cfm[64 + 16 * d : 80 + 16 * d, :] == 0.0)
@@ -429,12 +484,9 @@
 
 
 def mid_pre_body(
-    pos, scal, slab, below, above, cfm_in, sol, r, coarse, send_up, send_down,
-    cfm, sel, faces, inv, diag, u, jump, flux,
+    pos, scal, slab, below, above, cfm, sol_out, r_out, coarse, send_up, send_down,
+    sel, faces, inv, diag, u, sol, r, jump, flux, sems,
 ):
-    cfm[...] = cfm_in[...]
-    cfm[32:48, 0:128] = below[896:912, :]
-    cfm[80:96, 0:128] = below[912:928, :]
     for i in range(8):
         rows = slice(16 * i, 16 * i + 16)
         for m in range(3):
@@ -449,7 +501,13 @@
     mid_step(0, u, r, sol, inv)
     mid_apply(u, r, scal, cfm, faces, jump, flux)
     mid_step(1, u, r, sol, inv)
+    copies = [
+        pltpu.make_async_copy(sol, sol_out, sems.at[0]),
+        pltpu.make_async_copy(r, r_out, sems.at[1]),
+    ]
+    copies[0].start()
     mid_apply(u, r, scal, cfm, faces, jump, flux)
+    copies[1].start()
     total = r[0]
     for i in range(1, 8):
         total = total + r[i]
@@ -470,6 +528,8 @@
             acc = jnp.where(l32 // 8 == f, roll(coarse[f, :, 128:896], 8 * f - first), acc)
         out[0] = acc
         out[1] = roll(coarse[4, :, 128:896], -first)
+    for copy in copies:
+        copy.wait()
 
 
 def coarse_z_body(own, dn, up, slab, fwd, bwd):
@@ -541,7 +601,7 @@
 PAIRS = sum(9 - i for i in range(BASIS))
 
 
-def krylov_body(scal, own, below, above, basis, gram, field, hold):
+def krylov_body(scal, own, below, above, basis_out, gram, basis, field, hold, sem):
     for f in range(5):
         field[f, :, 0:512] = below[f]
         field[f, :, 512:1792] = own[f]
@@ -579,6 +639,8 @@
             if j > 0:
                 nxt = 2.0 * nxt - before
             before, now = now, nxt
+    copy = pltpu.make_async_copy(basis, basis_out, sem)
+    copy.start()
     high_rows, low_rows = [], []
     for i in range(BASIS):
         for j in range(i, BASIS + 1):
@@ -598,11 +660,11 @@
         row = jnp.where(lane8 == 64 + n, low[n], row)
     for m in range(64):
         gram[8 * m : 8 * m + 8, :] = row
-
-
-def mid_post_body(
-    pos, scal, gram, basis, cfm, pre, res, out,
-    sel, faces, inv, u, r, sol, jump, flux,
+    copy.wait()
+
+
+def mid_post(
+    pos, scal, gram, basis, cfm, out, sel, faces, inv, u, r, sol, jump, flux, wait_basis, wait_level
 ):
     high = gram[...].reshape(64, 8, 128)
     low = jnp.zeros((64, 8, 128), F32)
@@ -658,6 +720,7 @@
         safe, good = pivots[k]
         value = pair_div((spread_at(mat_h, k, BASIS), spread_at(mat_l, k, BASIS)), safe)[0]
         answers.append(jnp.where(good, value, 0.0))
+    wait_basis()
     weights = [jnp.concatenate([a, a], axis=0) for a in answers]
     lane16 = lanes((16, 128))
     tiles = []
@@ -679,9 +742,9 @@
         for i in range(8):
             u[i, :, 128 * m : 128 * m + 128] = acc
     mid_setup(pos, scal, cfm, sel, faces, inv, None)
+    wait_level()
     for i in range(8):
-        r[i] = res[i]
-        sol[i] = pre[i] + u[i]
+        sol[i] = sol[i] + u[i]
     mid_apply(u, r, scal, cfm, faces, jump, flux)
     for i in range(8):
         new = inv[i] * r[i] / MIDDLE
@@ -705,9 +768,40 @@
             out[128 * half + 16 * i : 128 * half + 16 * i + 16, :] = acc
 
 
-def fine_post_body(
-    mid, pre, frz, below, above, w, coef, inv, wide, spread, lift, out, u, r, sol, px, qx,
+def post_body(
+    pos, scal, gram, basis_in, cfm, mid_pre, mid_res, pre, frz_in, below, above, w_in, coef_in,
+    inv_in, wide, spread, lift, out,
+    basis, sel, faces, mid_inv, mid_u, mid_r, mid_sol, jump, flux, mid,
+    frz, w, coef, inv, u, r, sol, px, qx, sems,
 ):
+    copies = [
+        pltpu.make_async_copy(source, to, sems.at[n])
+        for n, (source, to) in enumerate(
+            (
+                (basis_in, basis),
+                (mid_pre, mid_sol),
+                (mid_res, mid_r),
+                (frz_in, frz),
+                (pre, sol),
+                (w_in, w),
+                (coef_in, coef),
+                (inv_in, inv),
+            )
+        )
+    ]
+    for copy in copies:
+        copy.start()
+
+    def wait_level():
+        copies[1].wait()
+        copies[2].wait()
+
+    mid_post(
+        pos, scal, gram, basis, cfm, mid, sel, faces, mid_inv, mid_u, mid_r, mid_sol, jump, flux,
+        copies[0].wait, wait_level,
+    )
+    for copy in copies[3:]:
+        copy.wait()
     low = lanes((64, 128)) < 64
     px[:, 0:256] = jnp.zeros((16, 256), F32)
     qx[:, NX * 256 :] = jnp.zeros((16, 256), F32)
@@ -735,7 +829,7 @@
         stacked = jnp.concatenate([high, rest, high, jnp.zeros((8, CHUNK), F32)], axis=0)
         lifted = mm(lift[...], stacked.astype(BF16))
         u[:, at] = lifted
-        sol[:, at] = pre[:, at] + lifted
+        sol[:, at] = sol[:, at] + lifted
     fine_apply(u, r, w, coef, wide, spread, px, qx, None, sol, inv)
     for c in range(CHUNKS):
         at = slice(CHUNK * c, CHUNK * (c + 1))
@@ -761,13 +855,17 @@
 
 
 def unpack_body(got, first, second):
-    lane = lanes((64, 128)) // 8
+    low = lanes((64, 128)) < 64
     for part, out in enumerate((first, second)):
-        for y in range(8):
-            acc = jnp.zeros((64, 128), F32)
-            for g in range(NX):
-                acc = jnp.where(lane == g, roll(got[g], 8 * g - 8 * y - 64 * part), acc)
-            out[pl.ds(y, 64, stride=8), :] = acc
+        held = []
+        for g in range(8):
+            a, b = got[g], got[g + 8]
+            if part == 0:
+                held.append(jnp.where(low, a, roll(b, 64)))
+            else:
+                held.append(jnp.where(low, roll(a, 64), b))
+        for y, rows in enumerate(exchange(held, 8)):
+            out[pl.ds(y, 64, stride=8), :] = rows
 
 
 def trace_tables():
@@ -895,38 +993,35 @@
         [
             lax.axis_index("yz"),
             side * 16 + lax.axis_index("gx"),
-            side,
-            jnp.zeros_like(side),
         ]
     ).astype(jnp.int32)
     res = residual.reshape(512, 128)
+    none = jnp.zeros_like(coefficient)
     cf = jnp.concatenate(
-        [
-            coefficient,
-            kind[1].astype(F32),
-            kind[3].astype(F32),
-            kind[5].astype(F32),
-            flag[1].astype(F32),
-            flag[3].astype(F32),
-            flag[5].astype(F32),
-            jnp.zeros_like(coefficient),
-        ],
+        [coefficient]
+        + [v[n].astype(F32) for v in (kind, flag) for n in (1, 3, 5)]
+        + [none, none, none]
+        + [kind[n].astype(F32) for n in (2, 4)]
+        + [none]
+        + [flag[n].astype(F32) for n in (2, 4)]
+        + [none],
         axis=0,
-    ).reshape(64, 128)
-    edges = call(edges_body, "edges", f32s(24, 128), (1, 0, 0))(pos, res, cf)
-    halo = lax.ppermute(edges, "lvl", [(0, 1), (1, 0)])
-    slots = call(
-        slots_body,
-        "slots",
-        f32s(16, 80, 128),
-        (1, 0, 0, 0),
-        [pltpu.VMEM((3, 8, 64, 128), F32), pltpu.VMEM((3, 8, 8, 128), F32)],
-    )(pos, res, cf, halo)
+    ).reshape(128, 128)
+    slots = call(slots_body, "slots", [f32s(16, 40, 128)], (0, 0))(res, cf)[0]
     element, faces, slots = lax.optimization_barrier((element, faces, slots))
     wide, spread, diag_w, diag_e, down, mid_diag_w, mid_diag_e, lift, scal = tables(element, faces)
     own = lax.all_to_all(slots, "gx", 0, 0, tiled=True)
+    dn = lax.ppermute(own, z_axes, z_up)
+    up = lax.ppermute(own, z_axes, z_dn)
+    place_values, place_kinds = place_tables()
+    rows, own, bwd = call(
+        join_body,
+        "join",
+        [f32s(NX, 64, 128), f32s(896, 128), f32s(768, 128)],
+        (0,) * 5,
+    )(own, dn, up, jnp.asarray(place_values, BF16), jnp.asarray(place_kinds, BF16))
     below = lax.ppermute(own, "yz", shift_up)
-    above = lax.ppermute(own, "yz", shift_dn)
+    above = lax.ppermute(bwd, "yz", shift_dn)
     plane = (64, NX * 256)
     strip = (16, NX * 256 + 256)
     pre, r, w, coef, inv, cfm, send_up, send_down = call(
@@ -942,22 +1037,30 @@
             f32s(512, 128),
             f32s(512, 128),
         ],
-        (1,) + (0,) * 10,
+        (1,) + (0,) * 11,
         [
+            pltpu.VMEM(plane, F32),
+            pltpu.VMEM((24, NX * 256), F32),
+            pltpu.VMEM((8, NX * 256), F32),
+            pltpu.VMEM(plane, F32),
             pltpu.VMEM(plane, F32),
             pltpu.VMEM(strip, F32),
             pltpu.VMEM(strip, F32),
-            pltpu.VMEM((768, 128), F32),
+            pltpu.VMEM((896, 128), F32),
+            pltpu.SemaphoreType.DMA((4,)),
         ],
-    )(pos, own, below, above, wide, spread, diag_w, diag_e, down, mid_diag_w, mid_diag_e)
+        (2, 0, 2, 2, 2, 0, 0, 0),
+    )(pos, rows, own, below, above, wide, spread, diag_w, diag_e, down, mid_diag_w, mid_diag_e)
     dn = lax.ppermute(send_up, z_axes, z_up)
     up = lax.ppermute(send_down, z_axes, z_dn)
     slab, fwd, bwd, frz = call(
         mid_z_body,
         "mid_z",
-        [f32s(128, 256), f32s(928, 128), f32s(896, 128), f32s(NX, 64, 128)],
-        (0,) * 5,
-    )(send_up, dn, up, r, cfm)
+        [f32s(128, 256), f32s(896, 128), f32s(896, 128), f32s(NX, 64, 128)],
+        (0,) * 4,
+        [pltpu.VMEM((NX, 64, 128), F32), pltpu.SemaphoreType.DMA],
+        (0, 0, 0, 2),
+    )(send_up, dn, up, r)
     below = lax.ppermute(fwd, "yz", shift_up)
     above = lax.ppermute(bwd, "yz", shift_dn)
     mid = (8, 16, 1024)
@@ -972,10 +1075,11 @@
         "mid_pre",
         [f32s(*mid), f32s(*mid), f32s(5, 16, 1024), f32s(2, 16, 768), f32s(2, 16, 768)],
         (1, 1, 0, 0, 0, 0),
-        [pltpu.VMEM((128, 1024), F32)]
-        + mid_scratch
-        + [pltpu.VMEM(mid, F32), pltpu.VMEM(mid, F32)]
-        + tail_scratch,
+        mid_scratch
+        + [pltpu.VMEM(mid, F32)] * 4
+        + tail_scratch
+        + [pltpu.SemaphoreType.DMA((2,))],
+        (2, 2, 0, 0, 0),
     )(pos, scal, slab, below, above, cfm)
     dn = lax.ppermute(send_up, z_axes, z_up)
     up = lax.ppermute(send_down, z_axes, z_dn)
@@ -992,29 +1096,41 @@
         "krylov",
         [f32s(BASIS, 16, 1536), f32s(512, 128)],
         (1, 0, 0, 0),
-        [pltpu.VMEM((5, 16, 2304), F32), pltpu.VMEM((2 * BASIS, 8, 128), F32)],
+        [
+            pltpu.VMEM((BASIS, 16, 1536), F32),
+            pltpu.VMEM((5, 16, 2304), F32),
+            pltpu.VMEM((2 * BASIS, 8, 128), F32),
+            pltpu.SemaphoreType.DMA,
+        ],
+        (2, 0),
     )(scal, coarse_slab, coarse_below, coarse_above)
     grams = lax.all_to_all(gram, ("gx", "yz", "lvl"), 0, 0, tiled=True)
-    mid_sol = call(
-        mid_post_body,
-        "mid_post",
-        f32s(256, 128),
-        (1, 1, 0, 0, 0, 0, 0),
-        mid_scratch + [pltpu.VMEM(mid, F32)] * 3 + tail_scratch,
-    )(pos, scal, grams, basis, cfm, mid_pre, mid_res)
     packed = call(
-        fine_post_body,
-        "fine_post",
-        f32s(16, 64, 128),
-        (0,) * 11,
-        [
+        post_body,
+        "post",
+        [f32s(16, 64, 128)],
+        (1, 1, 0, 2, 0, 2, 2, 2, 2, 0, 0, 2, 2, 2, 0, 0, 0),
+        [pltpu.VMEM((BASIS, 16, 1536), F32)]
+        + mid_scratch
+        + [pltpu.VMEM(mid, F32)] * 3
+        + tail_scratch
+        + [
+            pltpu.VMEM((256, 128), F32),
+            pltpu.VMEM((NX, 64, 128), F32),
+            pltpu.VMEM((24, NX * 256), F32),
+            pltpu.VMEM((8, NX * 256), F32),
+            pltpu.VMEM(plane, F32),
             pltpu.VMEM(plane, F32),
             pltpu.VMEM(plane, F32),
             pltpu.VMEM(plane, F32),
             pltpu.VMEM(strip, F32),
             pltpu.VMEM(strip, F32),
+            pltpu.SemaphoreType.DMA((8,)),
         ],
-    )(mid_sol, pre, frz, below, above, w, coef, inv, wide, spread, lift)
+    )(
+        pos, scal, grams, basis, cfm, mid_pre, mid_res, pre, frz, below, above, w, coef, inv,
+        wide, spread, lift,
+    )[0]
     got = lax.all_to_all(packed, "gx", 0, 0, tiled=True)
     correction, rest = call(unpack_body, "unpack", [f32s(512, 128), f32s(512, 128)], (0,))(got)
     return (correction.reshape(64, 1, 8, 128), rest.reshape(64, 1, 8, 128))

time: 203 us -> 213 us (1.049)
  local copies, waits for them, and re-layouts: 15.5 us -> 22.5 us
  other arithmetic: 1.44 us -> 5.67 us
    all_to_all x1, waiting for transfers between devices: 13.6 us -> 4.7 us  [local(): own = lax.all_to_all(slots, 'gx', 0, 0, tiled=True)]
    unnamed x47 -> x69, local copies, waits for them, and re-layouts: 10.5 us -> 17.7 us
    ppermute x2, waiting for transfers between devices: 2.12 us -> 8.95 us  [the longest x1 6.5 us: local(): dn = lax.ppermute(own, z_axes, z_up)]
    ppermute x1, starting transfers between devices: 8.73 us -> 4.12 us  [local(): below = lax.ppermute(fwd, 'yz', shift_up)]
    all_to_all x1, starting transfers between devices: 22.7 us -> 26.4 us  [local(): grams = lax.all_to_all(gram, ('gx', 'yz', 'lvl'), 0, 0, tiled=True)]
    unnamed x6 -> x10, other arithmetic: 0.02 us -> 3.46 us
    ppermute x2, waiting for transfers between devices: 3.46 us -> 6.6 us  [local(): dn = lax.ppermute(send_up, z_axes, z_up)]
    ppermute x1 -> x2, waiting for transfers between devices: 6.57 us -> 8.16 us  [local(): above = lax.ppermute(bwd, 'yz', shift_dn)]
  transfers between devices with their start and end apart: 13 -> 14, of which waited for: 10 -> 11; matrix products, arithmetic and copies ran while one was open for 2% -> 4% of each run, Pallas kernels for 0% -> 0%
where the time goes in v3:
time: 213 us; the launch traced here: 212 us
  starting transfers between devices  71.9 us (34%)
  waiting for transfers between devices  51.9 us (24%)
  Pallas kernels  34.2 us (16%)
  local copies, waits for them, and re-layouts  22.5 us (11%)
  blocking collectives  20.6 us (10%)
  other arithmetic  5.67 us (3%)
  between operations  2.97 us (1%)
  matrix products  2.19 us (1%)
    all_to_all x1, starting transfers between devices, local(): grams = lax.all_to_all(gram, ('gx', 'yz', 'lvl'), 0, 0, tiled=True)  26.4 us
    all_to_all x1, blocking collectives, local(): got = lax.all_to_all(packed, 'gx', 0, 0, tiled=True)  20.6 us
    unnamed x69, local copies, waits for them, and re-layouts  17.7 us
    all_to_all x1, waiting for transfers between devices, local(): grams = lax.all_to_all(gram, ('gx', 'yz', 'lvl'), 0, 0, tiled=True)  15.5 us
    pallas_call x1, Pallas kernels, local(): call(post_body, 'post', [f32s(16, 64, 128)], (1, 1, 0, 2, 0, 2, 2, 2, 2,...  13 us
    all_to_all x1, starting transfers between devices, local(): own = lax.all_to_all(slots, 'gx', 0, 0, tiled=True)  9.24 us
    ppermute x2, waiting for transfers between devices, local(): above = lax.ppermute(bwd, 'yz', shift_dn)  8.16 us
    pallas_call x1, Pallas kernels, local(): call(fine_pre_body, 'fine_pre', [f32s(*plane), f32s(*plane), f32s(24, NX...  7.4 us
  transfers between devices with their start and end apart: 14, of which 11 were waited for; matrix products, arithmetic and copies ran while one was open for 4% of the time, Pallas kernels for 0%

profile of v3, /device:TPU:2, one launch (start us, length us, event | category | flops | bytes accessed | tf_op | source)
XLA Modules:
  0.0 211.9 jit_solution(7125655324946829555)
XLA Ops:
  7.1 9.2 %all-to-all-start = ((f32[16,40,128]{2,1,0:T(8,128)}), f32[16,40,128]{2,1,0:T(8,128)S(1)}, u32[]{:S(2)}, u32[]{:S(2)}) async-start(f32[16,40,128]{2,1,0:T(8,128)} %slots.1), calls=%async_computation | async-start | bytes 655360 | tf_op jit(solution)/shard_map/all_to_all | solution.py:1013
  23.0 4.7 %all-to-all-done.own = f32[16,40,128]{2,1,0:T(8,128)S(1)} async-done(((f32[16,40,128]{2,1,0:T(8,128)}), f32[16,40,128]{2,1,0:T(8,128)S(1)}, u32[]{:S(2)}, u32[]{:S(2)}) %all-to-all-start) | async-done | bytes 327712 | tf_op jit(solution)/shard_map/all_to_all | solution.py:1013
  27.7 3.4 %collective-permute-start.1 = (f32[16,40,128]{2,1,0:T(8,128)S(1)}, f32[16,40,128]{2,1,0:T(8,128)S(1)}, u32[]{:S(2)}, u32[]{:S(2)}) collective-permute-start(f32[16,40,128]{2,1,0:T(8,128)S(1)} %all-to-all-done.own), channel_id=1, source_target_pairs={{32,0},{64,32},{96,64},{128,96},{160,128},{192,160},{224,192},{256... | collective-permute-start | bytes 983048 | tf_op jit(solution)/shard_map/ppermute | solution.py:1015
  31.1 3.3 %collective-permute-start = (f32[16,40,128]{2,1,0:T(8,128)S(1)}, f32[16,40,128]{2,1,0:T(8,128)S(1)}, u32[]{:S(2)}, u32[]{:S(2)}) collective-permute-start(f32[16,40,128]{2,1,0:T(8,128)S(1)} %all-to-all-done.own), channel_id=1, source_target_pairs={{0,32},{32,64},{64,96},{96,128},{128,160},{160,192},{192,224},{224... | collective-permute-start | bytes 983048 | tf_op jit(solution)/shard_map/ppermute | solution.py:1014
  35.1 2.5 %collective-permute-done.1.up = f32[16,40,128]{2,1,0:T(8,128)S(1)} collective-permute-done((f32[16,40,128]{2,1,0:T(8,128)S(1)}, f32[16,40,128]{2,1,0:T(8,128)S(1)}, u32[]{:S(2)}, u32[]{:S(2)}) %collective-permute-start.1) | collective-permute-done | bytes 327712 | tf_op jit(solution)/shard_map/ppermute | solution.py:1015
  37.6 6.5 %collective-permute-done.dn = f32[16,40,128]{2,1,0:T(8,128)S(1)} collective-permute-done((f32[16,40,128]{2,1,0:T(8,128)S(1)}, f32[16,40,128]{2,1,0:T(8,128)S(1)}, u32[]{:S(2)}, u32[]{:S(2)}) %collective-permute-start) | collective-permute-done | bytes 327712 | tf_op jit(solution)/shard_map/ppermute | solution.py:1014
  49.6 3.7 %collective-permute-done.3.above = f32[768,128]{1,0:T(8,128)S(1)} collective-permute-done((f32[768,128]{1,0:T(8,128)S(1)}, f32[768,128]{1,0:T(8,128)S(1)}, u32[]{:S(2)}, u32[]{:S(2)}) %collective-permute-start.3) | collective-permute-done | bytes 393248 | tf_op jit(solution)/shard_map/ppermute | solution.py:1024
  56.9 7.4 %fine_pre.1 = (f32[64,4096]{1,0:T(8,128)S(1)}, f32[64,4096]{1,0:T(8,128)S(1)}, f32[24,4096]{1,0:T(8,128)S(1)}, f32[8,4096]{1,0:T(8,128)S(1)}, f32[64,4096]{1,0:T...) custom-call(s32[2]{0:T(128)S(1)} %pad_add_fusion.pos, ...), custom_call_target="tpu_custom_call" | custom-call | flops 1000000 | bytes 1000000 | tf_op jit(solution)/shard_map/fine_pre/pallas_call | solution.py:1027
  66.9 4.8 %collective-permute-start.4 = (f32[512,128]{1,0:T(8,128)S(1)}, f32[512,128]{1,0:T(8,128)S(1)}, u32[]{:S(2)}, u32[]{:S(2)}) collective-permute-start(f32[512,128]{1,0:T(8,128)S(1)} %get-tuple-element.38.own), channel_id=1, source_target_pairs={{0,32},{32,64},{64,96},{96,128},{128,160},{160,192},{192,224},{224... | collective-permute-start | bytes 786440 | tf_op jit(solution)/shard_map/ppermute | solution.py:1054
  71.7 2.5 %collective-permute-done.5.up = f32[512,128]{1,0:T(8,128)S(1)} collective-permute-done((f32[512,128]{1,0:T(8,128)S(1)}, f32[512,128]{1,0:T(8,128)S(1)}, u32[]{:S(2)}, u32[]{:S(2)}) %collective-permute-start.5) | collective-permute-done | bytes 262176 | tf_op jit(solution)/shard_map/ppermute | solution.py:1055
  74.2 6.0 %collective-permute-done.4.dn = f32[512,128]{1,0:T(8,128)S(1)} collective-permute-done((f32[512,128]{1,0:T(8,128)S(1)}, f32[512,128]{1,0:T(8,128)S(1)}, u32[]{:S(2)}, u32[]{:S(2)}) %collective-permute-start.4) | collective-permute-done | bytes 262176 | tf_op jit(solution)/shard_map/ppermute | solution.py:1054
  80.1 2.2 %mid_z.1 = (f32[128,256]{1,0:T(8,128)S(1)}, f32[896,128]{1,0:T(8,128)}, f32[896,128]{1,0:T(8,128)}, f32[16,64,128]{2,1,0:T(8,128)S(1)}) custom-call(f32[512,128]{1,0:T(8,128)S(1)} %get-tuple-element.38.own, f32[512,128]{1,0:T(8,128)S(1)} %collective-permute-done.4.dn, f32[512,128]{1,0:T(8,128)S(1)} %collective-permute-done.5.up, ...), custom_call_target="tpu_custom_call" | custom-call | flops 1000000 | bytes 1000000 | tf_op jit(solution)/shard_map/mid_z/pallas_call | solution.py:1056
  82.4 4.1 %collective-permute-start.6 = (f32[896,128]{1,0:T(8,128)}, f32[896,128]{1,0:T(8,128)S(1)}, u32[]{:S(2)}, u32[]{:S(2)}) collective-permute-start(f32[896,128]{1,0:T(8,128)} %get-tuple-element.42), channel_id=1, source_target_pairs={{0,2},{2,4},{4,6},{6,8},{8,10},{10,12},{12,14},{14,16},{16,18},{18... | collective-permute-start | bytes 1376264 | tf_op jit(solution)/shard_map/ppermute | solution.py:1064
  91.3 4.5 %collective-permute-done.7.above = f32[896,128]{1,0:T(8,128)S(1)} collective-permute-done((f32[896,128]{1,0:T(8,128)}, f32[896,128]{1,0:T(8,128)S(1)}, u32[]{:S(2)}, u32[]{:S(2)}) %collective-permute-start.7) | collective-permute-done | bytes 458784 | tf_op jit(solution)/shard_map/ppermute | solution.py:1065
  95.8 4.0 %mid_pre.1 = (f32[8,16,1024]{2,1,0:T(8,128)S(1)}, f32[8,16,1024]{2,1,0:T(8,128)S(1)}, f32[5,16,1024]{2,1,0:T(8,128)S(1)}, f32[2,16,768]{2,1,0:T(8,128)S(1)}, f32[2,16,768]{2,1,0:T(8,128)S(1)}) custom-call(s32[2]{0:T(128)S(1)} %pad_add_fusion.pos, f32[144]{0:T(256)S(1)} %concatenate.50.scal, f32[128,256]{1,0:T(8,128)S(1)} %get-tuple-element.41.slab, ...), custom_call_target="tpu_custom_call" | custom-call | flops 1000000 | bytes 1000000 | tf_op jit(solution)/shard_map/mid_pre/pallas_call | solution.py:1073
  103.4 3.9 %collective-permute-start.9 = (f32[2,16,768]{2,1,0:T(8,128)S(1)}, f32[2,16,768]{2,1,0:T(8,128)S(1)}, u32[]{:S(2)}, u32[]{:S(2)}) collective-permute-start(f32[2,16,768]{2,1,0:T(8,128)S(1)} %get-tuple-element.47), channel_id=1, source_target_pairs={{32,0},{64,32},{96,64},{128,96},{160,128},{192,160},{224,192},{256... | collective-permute-start | bytes 294920 | tf_op jit(solution)/shard_map/ppermute | solution.py:1085
  108.0 2.8 %collective-permute-done.9.up = f32[2,16,768]{2,1,0:T(8,128)S(1)} collective-permute-done((f32[2,16,768]{2,1,0:T(8,128)S(1)}, f32[2,16,768]{2,1,0:T(8,128)S(1)}, u32[]{:S(2)}, u32[]{:S(2)}) %collective-permute-start.9) | collective-permute-done | bytes 98336 | tf_op jit(solution)/shard_map/ppermute | solution.py:1085
  111.5 7.3 %collective-permute-start.10 = (f32[5,16,512]{2,1,0:T(8,128)S(1)}, f32[5,16,512]{2,1,0:T(8,128)S(1)}, u32[]{:S(2)}, u32[]{:S(2)}) collective-permute-start(f32[5,16,512]{2,1,0:T(8,128)S(1)} %get-tuple-element.49), channel_id=1, source_target_pairs={{0,2},{2,4},{4,6},{6,8},{8,10},{10,12},{12,14},{14,16},{16,18},{18... | collective-permute-start | bytes 491528 | tf_op jit(solution)/shard_map/ppermute | solution.py:1092
  120.1 2.6 %collective-permute-done.11.above = f32[5,16,512]{2,1,0:T(8,128)S(1)} collective-permute-done((f32[5,16,512]{2,1,0:T(8,128)S(1)}, f32[5,16,512]{2,1,0:T(8,128)S(1)}, u32[]{:S(2)}, u32[]{:S(2)}) %collective-permute-start.11) | collective-permute-done | bytes 163872 | tf_op jit(solution)/shard_map/ppermute | solution.py:1093
  122.7 3.4 %krylov.1 = (f32[8,16,1536]{2,1,0:T(8,128)S(1)}, f32[512,128]{1,0:T(8,128)S(1)}) custom-call(f32[144]{0:T(256)S(1)} %concatenate.50.scal, f32[5,16,1280]{2,1,0:T(8,128)S(1)} %get-tuple-element.48.own, f32[5,16,512]{2,1,0:T(8,128)S(1)} %collective-permute-done.10.below, f32[5,16,512]{2,1,0:T(8,128)S(1)} %collective-permute-done.11.above), custom_call_target="tpu_custom_call" | custom-call | flops 1000000 | bytes 1000000 | tf_op jit(solution)/shard_map/krylov/pallas_call | solution.py:1094
  127.7 26.4 %all-to-all-start.1 = ((f32[512,1,128]{2,1,0:T(1,128)}), f32[512,1,128]{2,1,0:T(1,128)S(1)}, u32[]{:S(2)}, u32[]{:S(2)}) async-start(f32[512,1,128]{2,1,0:T(1,128)} %bitcast.88), calls=%async_computation.1 | async-start | bytes 524288 | tf_op jit(solution)/shard_map/all_to_all | solution.py:1107
  155.0 15.5 %all-to-all-done.1 = f32[512,1,128]{2,1,0:T(1,128)S(1)} async-done(((f32[512,1,128]{2,1,0:T(1,128)}), f32[512,1,128]{2,1,0:T(1,128)S(1)}, u32[]{:S(2)}, u32[]{:S(2)}) %all-to-all-start.1) | async-done | bytes 262176 | tf_op jit(solution)/shard_map/all_to_all | solution.py:1107
  176.8 13.0 %post.1 = f32[16,64,128]{2,1,0:T(8,128)S(1)} custom-call(s32[2]{0:T(128)S(1)} %pad_add_fusion.pos, f32[144]{0:T(256)S(1)} %concatenate.50.scal, f32[512,128]{1,0:T(8,128)S(1)} %bitcast.86, f32[8,16,1536]{2,1,0:T(8,128)S(1)} %copy-done.3, f32[128,1024]{1,0:T(8,128)S(1)} %get-tuple-element.44.cfm, f32[8,16,1024]{2,1,0:T(8,128)S(1)} %copy-done.5, ...), custom_call_target="tpu_custom_call" | custom-call | flops 1000000 | bytes 1000000 | tf_op jit(solution)/shard_map/post/pallas_call | solution.py:1108
  189.8 20.6 %all_to_all.21.got = f32[16,64,128]{2,1,0:T(8,128)S(1)} all-to-all(f32[16,64,128]{2,1,0:T(8,128)S(1)} %post.1), channel_id=1, replica_groups=mesh['gx'=16,'yz'=16,'lvl'=2] {'gx'}, dimensions={0} | all-to-all | bytes 1048576 | tf_op jit(solution)/shard_map/all_to_all | solution.py:1134
  (146 shorter events, 44.5 us)
Async XLA Ops:
  0.6 2.8 %copy-start.30 = (s32[6,1,8,128]{3,2,1,0:T(8,128)S(1)}, s32[6,1,8,128]{3,2,1,0:T(8,128)}, u32[]{:S(2)}) copy-start(s32[6,1,8,128]{3,2,1,0:T(8,128)} %param.18) | copy-start | bytes 73732
  7.1 20.6 %all-to-all-start = ((f32[16,40,128]{2,1,0:T(8,128)}), f32[16,40,128]{2,1,0:T(8,128)S(1)}, u32[]{:S(2)}, u32[]{:S(2)}) async-start(f32[16,40,128]{2,1,0:T(8,128)} %slots.1), calls=%async_computation | async-start | bytes 655360 | tf_op jit(solution)/shard_map/all_to_all | solution.py:1013
  22.6 21.5 %copy-start.14 = (bf16[384,512]{1,0:T(8,128)(2,1)S(1)}, bf16[384,512]{1,0:T(8,128)(2,1)}, u32[]{:S(2)}) copy-start(bf16[384,512]{1,0:T(8,128)(2,1)} %constant.74.clone.place_kinds) | copy-start | bytes 1179652
  22.8 21.3 %copy-start.21 = (bf16[256,256]{1,0:T(8,128)(2,1)S(1)}, bf16[256,256]{1,0:T(8,128)(2,1)}, u32[]{:S(2)}) copy-start(bf16[256,256]{1,0:T(8,128)(2,1)} %constant.73.clone.place_values) | copy-start | bytes 393220
  27.7 9.9 %collective-permute-start.1 = (f32[16,40,128]{2,1,0:T(8,128)S(1)}, f32[16,40,128]{2,1,0:T(8,128)S(1)}, u32[]{:S(2)}, u32[]{:S(2)}) collective-permute-start(f32[16,40,128]{2,1,0:T(8,128)S(1)} %all-to-all-done.own), channel_id=1, source_target_pairs={{32,0},{64,32},{96,64},{128,96},{160,128},{192,160},{224,192},{256... | collective-permute-start | bytes 983048 | tf_op jit(solution)/shard_map/ppermute | solution.py:1015
  31.1 13.0 %collective-permute-start = (f32[16,40,128]{2,1,0:T(8,128)S(1)}, f32[16,40,128]{2,1,0:T(8,128)S(1)}, u32[]{:S(2)}, u32[]{:S(2)}) collective-permute-start(f32[16,40,128]{2,1,0:T(8,128)S(1)} %all-to-all-done.own), channel_id=1, source_target_pairs={{0,32},{32,64},{64,96},{96,128},{128,160},{160,192},{192,224},{224... | collective-permute-start | bytes 983048 | tf_op jit(solution)/shard_map/ppermute | solution.py:1014
  44.8 4.3 %copy-start.8 = (f32[896,128]{1,0:T(8,128)}, f32[896,128]{1,0:T(8,128)S(1)}, u32[]{:S(2)}) copy-start(f32[896,128]{1,0:T(8,128)S(1)} %get-tuple-element.36.own) | copy-start | bytes 1376260
  44.8 9.2 %collective-permute-start.2 = (f32[896,128]{1,0:T(8,128)S(1)}, f32[896,128]{1,0:T(8,128)S(1)}, u32[]{:S(2)}, u32[]{:S(2)}) collective-permute-start(f32[896,128]{1,0:T(8,128)S(1)} %get-tuple-element.36.own), channel_id=1, source_target_pairs={{0,2},{2,4},{4,6},{6,8},{8,10},{10,12},{12,14},{14,16},{16,18},{18... | collective-permute-start | bytes 1376264 | tf_op jit(solution)/shard_map/ppermute | solution.py:1023
  46.3 7.0 %collective-permute-start.3 = (f32[768,128]{1,0:T(8,128)S(1)}, f32[768,128]{1,0:T(8,128)S(1)}, u32[]{:S(2)}, u32[]{:S(2)}) collective-permute-start(f32[768,128]{1,0:T(8,128)S(1)} %get-tuple-element.37), channel_id=1, source_target_pairs={{2,0},{4,2},{6,4},{8,6},{10,8},{12,10},{14,12},{16,14},{18,16},{20... | collective-permute-start | bytes 1179656 | tf_op jit(solution)/shard_map/ppermute | solution.py:1024
  49.3 5.5 %copy-start.9 = (f32[896,128]{1,0:T(8,128)S(1)}, f32[896,128]{1,0:T(8,128)}, u32[]{:S(2)}) copy-start(f32[896,128]{1,0:T(8,128)} %copy-done.8) | copy-start | bytes 1376260
  49.5 5.3 %copy-start.22 = (bf16[64,128]{1,0:T(8,128)(2,1)S(1)}, bf16[64,128]{1,0:T(8,128)(2,1)}, u32[]{:S(2)}) copy-start(bf16[64,128]{1,0:T(8,128)(2,1)} %constant.72.clone.spread) | copy-start | bytes 49156
  64.9 17.4 %copy-start = (f32[64,4096]{1,0:T(8,128)}, f32[64,4096]{1,0:T(8,128)S(1)}, u32[]{:S(2)}) copy-start(f32[64,4096]{1,0:T(8,128)S(1)} %get-tuple-element.59.inv_in) | copy-start | bytes 3145732
  64.9 17.4 %copy-start.12 = (f32[24,4096]{1,0:T(8,128)}, f32[24,4096]{1,0:T(8,128)S(1)}, u32[]{:S(2)}) copy-start(f32[24,4096]{1,0:T(8,128)S(1)} %get-tuple-element.57.w_in) | copy-start | bytes 1179652
  64.9 9.3 %collective-permute-start.5 = (f32[512,128]{1,0:T(8,128)S(1)}, f32[512,128]{1,0:T(8,128)S(1)}, u32[]{:S(2)}, u32[]{:S(2)}) collective-permute-start(f32[512,128]{1,0:T(8,128)S(1)} %get-tuple-element.39), channel_id=1, source_target_pairs={{32,0},{64,32},{96,64},{128,96},{160,128},{192,160},{224,192},{256... | collective-permute-start | bytes 786440 | tf_op jit(solution)/shard_map/ppermute | solution.py:1055
  66.9 13.3 %collective-permute-start.4 = (f32[512,128]{1,0:T(8,128)S(1)}, f32[512,128]{1,0:T(8,128)S(1)}, u32[]{:S(2)}, u32[]{:S(2)}) collective-permute-start(f32[512,128]{1,0:T(8,128)S(1)} %get-tuple-element.38.own), channel_id=1, source_target_pairs={{0,32},{32,64},{64,96},{96,128},{128,160},{160,192},{192,224},{224... | collective-permute-start | bytes 786440 | tf_op jit(solution)/shard_map/ppermute | solution.py:1054
  82.4 8.9 %collective-permute-start.6 = (f32[896,128]{1,0:T(8,128)}, f32[896,128]{1,0:T(8,128)S(1)}, u32[]{:S(2)}, u32[]{:S(2)}) collective-permute-start(f32[896,128]{1,0:T(8,128)} %get-tuple-element.42), channel_id=1, source_target_pairs={{0,2},{2,4},{4,6},{6,8},{8,10},{10,12},{12,14},{14,16},{16,18},{18... | collective-permute-start | bytes 1376264 | tf_op jit(solution)/shard_map/ppermute | solution.py:1064
  86.5 9.3 %collective-permute-start.7 = (f32[896,128]{1,0:T(8,128)}, f32[896,128]{1,0:T(8,128)S(1)}, u32[]{:S(2)}, u32[]{:S(2)}) collective-permute-start(f32[896,128]{1,0:T(8,128)} %get-tuple-element.43), channel_id=1, source_target_pairs={{2,0},{4,2},{6,4},{8,6},{10,8},{12,10},{14,12},{16,14},{18,16},{20... | collective-permute-start | bytes 1376264 | tf_op jit(solution)/shard_map/ppermute | solution.py:1065
  101.5 6.5 %collective-permute-start.8 = (f32[2,16,768]{2,1,0:T(8,128)S(1)}, f32[2,16,768]{2,1,0:T(8,128)S(1)}, u32[]{:S(2)}, u32[]{:S(2)}) collective-permute-start(f32[2,16,768]{2,1,0:T(8,128)S(1)} %get-tuple-element.46), channel_id=1, source_target_pairs={{0,32},{32,64},{64,96},{96,128},{128,160},{160,192},{192,224},{224... | collective-permute-start | bytes 294920 | tf_op jit(solution)/shard_map/ppermute | solution.py:1084
  103.4 7.4 %collective-permute-start.9 = (f32[2,16,768]{2,1,0:T(8,128)S(1)}, f32[2,16,768]{2,1,0:T(8,128)S(1)}, u32[]{:S(2)}, u32[]{:S(2)}) collective-permute-start(f32[2,16,768]{2,1,0:T(8,128)S(1)} %get-tuple-element.47), channel_id=1, source_target_pairs={{32,0},{64,32},{96,64},{128,96},{160,128},{192,160},{224,192},{256... | collective-permute-start | bytes 294920 | tf_op jit(solution)/shard_map/ppermute | solution.py:1085
  111.5 8.7 %collective-permute-start.10 = (f32[5,16,512]{2,1,0:T(8,128)S(1)}, f32[5,16,512]{2,1,0:T(8,128)S(1)}, u32[]{:S(2)}, u32[]{:S(2)}) collective-permute-start(f32[5,16,512]{2,1,0:T(8,128)S(1)} %get-tuple-element.49), channel_id=1, source_target_pairs={{0,2},{2,4},{4,6},{6,8},{8,10},{10,12},{12,14},{14,16},{16,18},{18... | collective-permute-start | bytes 491528 | tf_op jit(solution)/shard_map/ppermute | solution.py:1092
  118.8 3.9 %collective-permute-start.11 = (f32[5,16,512]{2,1,0:T(8,128)S(1)}, f32[5,16,512]{2,1,0:T(8,128)S(1)}, u32[]{:S(2)}, u32[]{:S(2)}) collective-permute-start(f32[5,16,512]{2,1,0:T(8,128)S(1)} %get-tuple-element.50), channel_id=1, source_target_pairs={{2,0},{4,2},{6,4},{8,6},{10,8},{12,10},{14,12},{16,14},{18,16},{20... | collective-permute-start | bytes 491528 | tf_op jit(solution)/shard_map/ppermute | solution.py:1093
  127.7 42.8 %all-to-all-start.1 = ((f32[512,1,128]{2,1,0:T(1,128)}), f32[512,1,128]{2,1,0:T(1,128)S(1)}, u32[]{:S(2)}, u32[]{:S(2)}) async-start(f32[512,1,128]{2,1,0:T(1,128)} %bitcast.88), calls=%async_computation.1 | async-start | bytes 524288 | tf_op jit(solution)/shard_map/all_to_all | solution.py:1107
  170.5 1.2 copy-start.1
  171.7 1.1 copy-start.3
  (23 other events, 19.1 us)

commit v4 on v3

--- a/solution.py
+++ b/solution.py
@@ -93,7 +93,18 @@
     return arrays
 
 
-def slots_body(res, cf, out):
+def slots_body(res, coef, kind, flag, out, cf):
+    for n in range(16):
+        cf[8 * n : 8 * n + 8, :] = jnp.zeros((8, 128), F32)
+    cf[0:8, :] = coef[...]
+    for first, ref in ((8, kind), (32, flag)):
+        for n in range(3):
+            at = 8 * (2 * n + 1)
+            cf[first + 8 * n : first + 8 * n + 8, :] = ref[at : at + 8, :].astype(F32)
+    for first, ref in ((80, kind), (104, flag)):
+        for n in range(2):
+            at = 8 * (2 * n + 2)
+            cf[first + 8 * n : first + 8 * n + 8, :] = ref[at : at + 8, :].astype(F32)
     low = lanes((32, 128)) < 64
     low8 = lanes((8, 128)) < 64
     values = exchange([res[pl.ds(y, 64, stride=8), :] for y in range(8)], 8)
@@ -200,6 +211,54 @@
             sol[:, at] = sol[:, at] + new
 
 
+def fine_places(pos):
+    place = lanes((1, 256))
+    y_at = pos[0] * 8 - 4 + place // 16
+    z_at = pos[1] * 8 - 4 + place % 16
+    inside = (y_at >= 0) & (y_at < NY) & (z_at >= 0) & (z_at < NZ)
+    return inside, inside & (y_at < NY - 1), inside & (z_at < NZ - 1)
+
+
+def fine_weights(pos, coef, w):
+    inside, has_y, has_z = fine_places(pos)
+    w[12:16, 0:256] = jnp.zeros((4, 256), F32)
+    for x in range(NX):
+        at = slice(256 * x, 256 * x + 256)
+        rows = coef[:, at]
+        opens = [
+            inside & (rows[4:5] == 0.0) if x < NX - 1 else jnp.zeros((1, 256), jnp.bool_),
+            has_y & (rows[5:6] == 0.0),
+            has_z & (rows[6:7] == 0.0),
+        ]
+        plus = [
+            [jnp.where(opens[d] & (rows[1 + d : 2 + d] == float(k)), 1.0, 0.0) for k in range(KINDS)]
+            for d in range(3)
+        ]
+        plus_all = jnp.concatenate(plus[0] + plus[1] + plus[2], axis=0)
+        w[0:12, at] = plus_all
+        if x < NX - 1:
+            w[12:16, 256 * x + 256 : 256 * x + 512] = plus_all[0:4]
+        w[16:20, at] = roll(plus_all[4:8], 16)
+        w[20:24, at] = roll(plus_all[8:12], 1)
+
+
+def kinds_of(w, at):
+    ws = w[:, at]
+    return jnp.concatenate([ws, ws, ws, jnp.zeros((8, CHUNK), F32)], axis=0).astype(BF16)
+
+
+def fine_inverse(coef, w, diag_w, diag_e, inside, at):
+    diag = diag_e[...] * coef[0:1, at] + mm(diag_w[...], kinds_of(w, at))
+    return jnp.where(inside, 1.0 / diag, 0.0)
+
+
+def compacted(first, second, lane):
+    v = roll(jnp.where(lane < 64, roll(first, 64), roll(second, 64)), -4)
+    for size in (8, 16, 32):
+        v = jnp.where(lane % (4 * size) < size, v, roll(v, -size))
+    return v
+
+
 def fine_pre_body(
     pos,
     rows_in,
@@ -213,33 +272,23 @@
     down,
     mid_diag_w,
     mid_diag_e,
-    sol_out,
+    keep,
     r,
-    w_out,
-    coef_out,
-    inv_out,
+    coef,
     cfm,
     send_up,
     send_down,
     sol,
     w,
-    coef,
     inv,
     u,
     px,
     qx,
     gather,
-    sems,
 ):
     low = lanes((64, 128)) < 64
     lane8 = lanes((8, 128))
-    place = lanes((1, 256))
-    y_at = pos[0] * 8 - 4 + place // 16
-    z_at = pos[1] * 8 - 4 + place % 16
-    inside = (y_at >= 0) & (y_at < NY) & (z_at >= 0) & (z_at < NZ)
-    has_y = inside & (y_at < NY - 1)
-    has_z = inside & (z_at < NZ - 1)
-    inside_f = jnp.where(inside, 1.0, 0.0)
+    inside = fine_places(pos)[0]
     px[:, 0:256] = jnp.zeros((16, 256), F32)
     qx[:, NX * 256 :] = jnp.zeros((16, 256), F32)
     cfm[:, 896:1024] = jnp.zeros((128, 128), F32)
@@ -278,56 +327,23 @@
             coef[:, at] = acc
     for m in range(7):
         cfm[:, 128 * m : 128 * m + 128] = gather[128 * m : 128 * m + 128, :]
-    w[12:16, 0:256] = jnp.zeros((4, 256), F32)
-    for x in range(NX):
-        at = slice(256 * x, 256 * x + 256)
-        rows = coef[:, at]
-        opens = [
-            inside & (rows[4:5] == 0.0) if x < NX - 1 else jnp.zeros((1, 256), jnp.bool_),
-            has_y & (rows[5:6] == 0.0),
-            has_z & (rows[6:7] == 0.0),
-        ]
-        plus = [
-            [jnp.where(opens[d] & (rows[1 + d : 2 + d] == float(k)), 1.0, 0.0) for k in range(KINDS)]
-            for d in range(3)
-        ]
-        plus_all = jnp.concatenate(plus[0] + plus[1] + plus[2], axis=0)
-        w[0:12, at] = plus_all
-        if x < NX - 1:
-            w[12:16, 256 * x + 256 : 256 * x + 512] = plus_all[0:4]
-        w[16:20, at] = roll(plus_all[4:8], 16)
-        w[20:24, at] = roll(plus_all[8:12], 1)
+    fine_weights(pos, coef, w)
     wide_inside = jnp.concatenate([inside] * (CHUNK // 256), axis=1)
-
-    def kinds_of(at):
-        ws = w[:, at]
-        return jnp.concatenate([ws, ws, ws, jnp.zeros((8, CHUNK), F32)], axis=0).astype(BF16)
-
     for c in range(CHUNKS):
         at = slice(CHUNK * c, CHUNK * (c + 1))
-        diag = diag_e[...] * coef[0:1, at] + mm(diag_w[...], kinds_of(at))
-        inverse = jnp.where(wide_inside, 1.0 / diag, 0.0)
+        inverse = fine_inverse(coef, w, diag_w, diag_e, wide_inside, at)
         inv[:, at] = inverse
         update = inverse * r[:, at] / MIDDLE
         u[:, at] = update
         sol[:, at] = update
-    copies = [
-        pltpu.make_async_copy(held, out, sems.at[n])
-        for n, (held, out) in enumerate(
-            ((w, w_out), (coef, coef_out), (inv, inv_out), (sol, sol_out))
-        )
-    ]
-    for copy in copies[:3]:
-        copy.start()
     fine_apply(u, r, w, coef, wide, spread, px, qx, 0, sol, inv)
     fine_apply(u, r, w, coef, wide, spread, px, qx, 1, sol, inv)
-    copies[3].start()
     fine_apply(u, r, w, coef, wide, spread, px, qx, None, sol, inv)
     lane16 = lanes((16, 128)) % 16 // 4
     for c in range(CHUNKS):
         at = slice(CHUNK * c, CHUNK * (c + 1))
         rhs = mm(down[...], stack_hlh(r[:, at]))
-        diag = mid_diag_e[...] * coef[0:1, at] + mm(mid_diag_w[...], kinds_of(at))
+        diag = mid_diag_e[...] * coef[0:1, at] + mm(mid_diag_w[...], kinds_of(w, at))
         update = jnp.where(wide_inside, 1.0 / diag, 0.0) * rhs / MIDDLE
         for n in range(CHUNK // 256):
             x = (CHUNK // 256) * c + n
@@ -346,11 +362,16 @@
             dn = jnp.where(lane16 == j, roll(part, 4 * j - 4), dn)
         send_up[256 + 16 * x : 272 + 16 * x, :] = up
         send_down[256 + 16 * x : 272 + 16 * x, :] = dn
-    for copy in copies:
-        copy.wait()
-
-
-def mid_z_body(own, dn, up, r, slab, fwd, bwd, frz_out, frz, sem):
+    lane = lanes((64, 128))
+    for x in range(8):
+        a, b = [
+            compacted(sol[:, 256 * n : 256 * n + 128], sol[:, 256 * n + 128 : 256 * n + 256], lane)
+            for n in (x, x + 8)
+        ]
+        keep[x] = jnp.where(low, a, roll(b, 64))
+
+
+def mid_z_body(own, dn, up, r, slab, fwd, bwd, frz):
     low = lanes((64, 128)) < 64
     l16 = lanes((16, 128)) % 16
     for x in range(NX):
@@ -363,8 +384,6 @@
             part = jnp.where(l16 < 4, roll(pack_dn, -4 * j), mine[rows])
             part = jnp.where(l16 >= 12, roll(pack_up, 12 - 4 * j), part)
             frz[x, rows, :] = part
-    copy = pltpu.make_async_copy(frz, frz_out, sem)
-    copy.start()
     for x in range(8):
         fwd[384 + 64 * x : 448 + 64 * x, :] = jnp.where(low, roll(frz[x], 64), frz[x + 8])
         bwd[384 + 64 * x : 448 + 64 * x, :] = jnp.where(low, frz[x], roll(frz[x + 8], 64))
@@ -387,7 +406,6 @@
             fwd[128 * m : 128 * m + 128, :] = acc
         if m >= 1:
             bwd[128 * (m - 1) : 128 * m, :] = acc
-    copy.wait()
 
 
 LOWS = ((0, 1, 2, 3), (0, 1, 4, 5), (0, 2, 4, 6))
@@ -485,7 +503,7 @@
 
 def mid_pre_body(
     pos, scal, slab, below, above, cfm, sol_out, r_out, coarse, send_up, send_down,
-    sel, faces, inv, diag, u, sol, r, jump, flux, sems,
+    sel, faces, inv, diag, u, sol, r, jump, flux,
 ):
     for i in range(8):
         rows = slice(16 * i, 16 * i + 16)
@@ -501,13 +519,9 @@
     mid_step(0, u, r, sol, inv)
     mid_apply(u, r, scal, cfm, faces, jump, flux)
     mid_step(1, u, r, sol, inv)
-    copies = [
-        pltpu.make_async_copy(sol, sol_out, sems.at[0]),
-        pltpu.make_async_copy(r, r_out, sems.at[1]),
-    ]
-    copies[0].start()
     mid_apply(u, r, scal, cfm, faces, jump, flux)
-    copies[1].start()
+    sol_out[...] = sol[:, :, 128:896]
+    r_out[...] = r[:, :, 128:896]
     total = r[0]
     for i in range(1, 8):
         total = total + r[i]
@@ -528,8 +542,6 @@
             acc = jnp.where(l32 // 8 == f, roll(coarse[f, :, 128:896], 8 * f - first), acc)
         out[0] = acc
         out[1] = roll(coarse[4, :, 128:896], -first)
-    for copy in copies:
-        copy.wait()
 
 
 def coarse_z_body(own, dn, up, slab, fwd, bwd):
@@ -562,6 +574,19 @@
                 bwd[f, :, 128 * (m - 6) : 128 * (m - 5)] = acc
 
 
+def settle(v, basis, j):
+    lane = lanes((16, 128))
+    for m in range(6):
+        acc = jnp.zeros((16, 128), F32)
+        for n in range(4):
+            y = 4 * m + n - 8
+            tile, at = (y + 14) // 2, 64 * ((y + 14) % 2)
+            to = 32 * n
+            piece = roll(v[:, 128 * tile : 128 * tile + 128], to + 5 - (at + 21))
+            acc = jnp.where((lane >= to + 5) & (lane < to + 27), piece, acc)
+        basis[j, :, 128 * m : 128 * m + 128] = acc
+
+
 def two_sum(a, b):
     s = a + b
     t = s - a
@@ -601,7 +626,7 @@
 PAIRS = sum(9 - i for i in range(BASIS))
 
 
-def krylov_body(scal, own, below, above, basis_out, gram, basis, field, hold, sem):
+def krylov_body(scal, own, below, above, basis, gram, field, hold):
     for f in range(5):
         field[f, :, 0:512] = below[f]
         field[f, :, 512:1792] = own[f]
@@ -630,7 +655,7 @@
     before = None
     now = field[0]
     for j in range(BASIS):
-        basis[j] = now[:, 384:1920]
+        settle(now, basis, j)
         hold[j] = compact(now)
         image = apply(now)
         hold[BASIS + j] = compact(image)
@@ -639,8 +664,6 @@
             if j > 0:
                 nxt = 2.0 * nxt - before
             before, now = now, nxt
-    copy = pltpu.make_async_copy(basis, basis_out, sem)
-    copy.start()
     high_rows, low_rows = [], []
     for i in range(BASIS):
         for j in range(i, BASIS + 1):
@@ -658,17 +681,14 @@
     for n in range(PAIRS):
         row = jnp.where(lane8 == n, high[n], row)
         row = jnp.where(lane8 == 64 + n, low[n], row)
-    for m in range(64):
+    for m in range(2):
         gram[8 * m : 8 * m + 8, :] = row
-    copy.wait()
-
-
-def mid_post(
-    pos, scal, gram, basis, cfm, out, sel, faces, inv, u, r, sol, jump, flux, wait_basis, wait_level
-):
-    high = gram[...].reshape(64, 8, 128)
-    low = jnp.zeros((64, 8, 128), F32)
-    count = 64
+
+
+def summed(gram):
+    count = gram.shape[0] // 8
+    high = gram[...].reshape(count, 8, 128)
+    low = jnp.zeros((count, 8, 128), F32)
     while count > 1:
         count //= 2
         high, e = two_sum(high[:count], high[count : 2 * count])
@@ -677,8 +697,18 @@
     for s in (4, 2, 1):
         high, e = two_sum(high, roll(high, s, 0))
         low = low + roll(low, s, 0) + e
-    low = low + roll(high, 64)
-    high, low = two_sum(high, low)
+    return two_sum(high, low + roll(high, 64))
+
+
+def gram_body(gram, out):
+    high, low = summed(gram)
+    row = jnp.where(lanes((8, 128)) < 64, high, roll(low, 64))
+    for m in range(4):
+        out[8 * m : 8 * m + 8, :] = row
+
+
+def mid_post(pos, scal, gram, basis, cfm, pre, res, out, sel, faces, inv, u, r, sol, jump, flux):
+    high, low = summed(gram)
     lane = lanes((8, 128))
     sub = lax.broadcasted_iota(jnp.int32, (8, 128), 0)
     mat_h = jnp.zeros((8, 128), F32)
@@ -720,31 +750,24 @@
         safe, good = pivots[k]
         value = pair_div((spread_at(mat_h, k, BASIS), spread_at(mat_l, k, BASIS)), safe)[0]
         answers.append(jnp.where(good, value, 0.0))
-    wait_basis()
     weights = [jnp.concatenate([a, a], axis=0) for a in answers]
     lane16 = lanes((16, 128))
-    tiles = []
-    for m in range(12):
-        total = weights[0] * basis[0, :, 128 * m : 128 * m + 128]
-        for j in range(1, BASIS):
-            total = total + weights[j] * basis[j, :, 128 * m : 128 * m + 128]
-        tiles.append(total)
     for m in range(8):
-        acc = jnp.zeros((16, 128), F32)
+        total = jnp.zeros((16, 128), F32)
         if 1 <= m <= 6:
-            for n in range(4):
-                y = 4 * m + n - 12
-                tile, at = (y + 14) // 2 - 3, 64 * ((y + 14) % 2)
-                to = 32 * n
-                acc = jnp.where(
-                    (lane16 >= to + 5) & (lane16 < to + 27), roll(tiles[tile], to + 5 - (at + 21)), acc
-                )
+            at = slice(128 * (m - 1), 128 * m)
+            for j in range(BASIS):
+                total = total + weights[j] * basis[j, :, at]
         for i in range(8):
-            u[i, :, 128 * m : 128 * m + 128] = acc
+            u[i, :, 128 * m : 128 * m + 128] = total
     mid_setup(pos, scal, cfm, sel, faces, inv, None)
-    wait_level()
+    ends = jnp.zeros((16, 128), F32)
     for i in range(8):
-        sol[i] = sol[i] + u[i]
+        for ref in (r, sol):
+            ref[i, :, 0:128] = ends
+            ref[i, :, 896:1024] = ends
+        r[i, :, 128:896] = res[i]
+        sol[i, :, 128:896] = pre[i] + u[i, :, 128:896]
     mid_apply(u, r, scal, cfm, faces, jump, flux)
     for i in range(8):
         new = inv[i] * r[i] / MIDDLE
@@ -769,39 +792,19 @@
 
 
 def post_body(
-    pos, scal, gram, basis_in, cfm, mid_pre, mid_res, pre, frz_in, below, above, w_in, coef_in,
-    inv_in, wide, spread, lift, out,
-    basis, sel, faces, mid_inv, mid_u, mid_r, mid_sol, jump, flux, mid,
-    frz, w, coef, inv, u, r, sol, px, qx, sems,
+    pos, scal, gram, basis, cfm, mid_pre, mid_res, keep, frz, below, above, coef, wide, spread,
+    lift, diag_w, diag_e, out,
+    sel, faces, mid_inv, mid_u, mid_r, mid_sol, jump, flux, mid, w, inv, u, r, sol, px, qx,
 ):
-    copies = [
-        pltpu.make_async_copy(source, to, sems.at[n])
-        for n, (source, to) in enumerate(
-            (
-                (basis_in, basis),
-                (mid_pre, mid_sol),
-                (mid_res, mid_r),
-                (frz_in, frz),
-                (pre, sol),
-                (w_in, w),
-                (coef_in, coef),
-                (inv_in, inv),
-            )
-        )
-    ]
-    for copy in copies:
-        copy.start()
-
-    def wait_level():
-        copies[1].wait()
-        copies[2].wait()
-
+    fine_weights(pos, coef, w)
+    wide_inside = jnp.concatenate([fine_places(pos)[0]] * (CHUNK // 256), axis=1)
+    for c in range(CHUNKS):
+        at = slice(CHUNK * c, CHUNK * (c + 1))
+        inv[:, at] = fine_inverse(coef, w, diag_w, diag_e, wide_inside, at)
     mid_post(
-        pos, scal, gram, basis, cfm, mid, sel, faces, mid_inv, mid_u, mid_r, mid_sol, jump, flux,
-        copies[0].wait, wait_level,
+        pos, scal, gram, basis, cfm, mid_pre, mid_res, mid, sel, faces, mid_inv, mid_u, mid_r,
+        mid_sol, jump, flux,
     )
-    for copy in copies[3:]:
-        copy.wait()
     low = lanes((64, 128)) < 64
     px[:, 0:256] = jnp.zeros((16, 256), F32)
     qx[:, NX * 256 :] = jnp.zeros((16, 256), F32)
@@ -829,7 +832,7 @@
         stacked = jnp.concatenate([high, rest, high, jnp.zeros((8, CHUNK), F32)], axis=0)
         lifted = mm(lift[...], stacked.astype(BF16))
         u[:, at] = lifted
-        sol[:, at] = sol[:, at] + lifted
+        sol[:, at] = lifted
     fine_apply(u, r, w, coef, wide, spread, px, qx, None, sol, inv)
     for c in range(CHUNKS):
         at = slice(CHUNK * c, CHUNK * (c + 1))
@@ -851,7 +854,8 @@
                     roll(ref[:, start : start + 128], 64 * part + 8 * y - at),
                     acc,
                 )
-        out[x] = acc
+        kept = keep[x % 8] if x < 8 else roll(keep[x % 8], 64)
+        out[x] = acc + jnp.where(low, kept, 0.0)
 
 
 def unpack_body(got, first, second):
@@ -996,18 +1000,9 @@
         ]
     ).astype(jnp.int32)
     res = residual.reshape(512, 128)
-    none = jnp.zeros_like(coefficient)
-    cf = jnp.concatenate(
-        [coefficient]
-        + [v[n].astype(F32) for v in (kind, flag) for n in (1, 3, 5)]
-        + [none, none, none]
-        + [kind[n].astype(F32) for n in (2, 4)]
-        + [none]
-        + [flag[n].astype(F32) for n in (2, 4)]
-        + [none],
-        axis=0,
-    ).reshape(128, 128)
-    slots = call(slots_body, "slots", [f32s(16, 40, 128)], (0, 0))(res, cf)[0]
+    slots = call(
+        slots_body, "slots", [f32s(16, 40, 128)], (0,) * 4, [pltpu.VMEM((128, 128), F32)]
+    )(res, coefficient.reshape(8, 128), kind.reshape(48, 128), flag.reshape(48, 128))[0]
     element, faces, slots = lax.optimization_barrier((element, faces, slots))
     wide, spread, diag_w, diag_e, down, mid_diag_w, mid_diag_e, lift, scal = tables(element, faces)
     own = lax.all_to_all(slots, "gx", 0, 0, tiled=True)
@@ -1024,15 +1019,13 @@
     above = lax.ppermute(bwd, "yz", shift_dn)
     plane = (64, NX * 256)
     strip = (16, NX * 256 + 256)
-    pre, r, w, coef, inv, cfm, send_up, send_down = call(
+    keep, r, coef, cfm, send_up, send_down = call(
         fine_pre_body,
         "fine_pre",
         [
+            f32s(8, 64, 128),
             f32s(*plane),
-            f32s(*plane),
-            f32s(24, NX * 256),
             f32s(8, NX * 256),
-            f32s(*plane),
             f32s(128, 1024),
             f32s(512, 128),
             f32s(512, 128),
@@ -1041,15 +1034,12 @@
         [
             pltpu.VMEM(plane, F32),
             pltpu.VMEM((24, NX * 256), F32),
-            pltpu.VMEM((8, NX * 256), F32),
             pltpu.VMEM(plane, F32),
             pltpu.VMEM(plane, F32),
             pltpu.VMEM(strip, F32),
             pltpu.VMEM(strip, F32),
             pltpu.VMEM((896, 128), F32),
-            pltpu.SemaphoreType.DMA((4,)),
         ],
-        (2, 0, 2, 2, 2, 0, 0, 0),
     )(pos, rows, own, below, above, wide, spread, diag_w, diag_e, down, mid_diag_w, mid_diag_e)
     dn = lax.ppermute(send_up, z_axes, z_up)
     up = lax.ppermute(send_down, z_axes, z_dn)
@@ -1058,8 +1048,6 @@
         "mid_z",
         [f32s(128, 256), f32s(896, 128), f32s(896, 128), f32s(NX, 64, 128)],
         (0,) * 4,
-        [pltpu.VMEM((NX, 64, 128), F32), pltpu.SemaphoreType.DMA],
-        (0, 0, 0, 2),
     )(send_up, dn, up, r)
     below = lax.ppermute(fwd, "yz", shift_up)
     above = lax.ppermute(bwd, "yz", shift_dn)
@@ -1073,13 +1061,11 @@
     mid_pre, mid_res, coarse, send_up, send_down = call(
         mid_pre_body,
         "mid_pre",
-        [f32s(*mid), f32s(*mid), f32s(5, 16, 1024), f32s(2, 16, 768), f32s(2, 16, 768)],
+        [f32s(8, 16, 768), f32s(8, 16, 768), f32s(5, 16, 1024), f32s(2, 16, 768), f32s(2, 16, 768)],
         (1, 1, 0, 0, 0, 0),
         mid_scratch
         + [pltpu.VMEM(mid, F32)] * 4
-        + tail_scratch
-        + [pltpu.SemaphoreType.DMA((2,))],
-        (2, 2, 0, 0, 0),
+        + tail_scratch,
     )(pos, scal, slab, below, above, cfm)
     dn = lax.ppermute(send_up, z_axes, z_up)
     up = lax.ppermute(send_down, z_axes, z_dn)
@@ -1094,42 +1080,37 @@
     basis, gram = call(
         krylov_body,
         "krylov",
-        [f32s(BASIS, 16, 1536), f32s(512, 128)],
+        [f32s(BASIS, 16, 768), f32s(16, 128)],
         (1, 0, 0, 0),
         [
-            pltpu.VMEM((BASIS, 16, 1536), F32),
             pltpu.VMEM((5, 16, 2304), F32),
             pltpu.VMEM((2 * BASIS, 8, 128), F32),
-            pltpu.SemaphoreType.DMA,
         ],
-        (2, 0),
     )(scal, coarse_slab, coarse_below, coarse_above)
-    grams = lax.all_to_all(gram, ("gx", "yz", "lvl"), 0, 0, tiled=True)
+    gram = lax.all_to_all(gram, "yz", 0, 0, tiled=True)
+    gram = call(gram_body, "gram", [f32s(32, 128)], (0,))(gram)[0]
+    gram = lax.all_to_all(gram, z_axes, 0, 0, tiled=True)
     packed = call(
         post_body,
         "post",
         [f32s(16, 64, 128)],
-        (1, 1, 0, 2, 0, 2, 2, 2, 2, 0, 0, 2, 2, 2, 0, 0, 0),
-        [pltpu.VMEM((BASIS, 16, 1536), F32)]
-        + mid_scratch
+        (1, 1) + (0,) * 15,
+        mid_scratch
         + [pltpu.VMEM(mid, F32)] * 3
         + tail_scratch
         + [
             pltpu.VMEM((256, 128), F32),
-            pltpu.VMEM((NX, 64, 128), F32),
             pltpu.VMEM((24, NX * 256), F32),
-            pltpu.VMEM((8, NX * 256), F32),
             pltpu.VMEM(plane, F32),
             pltpu.VMEM(plane, F32),
             pltpu.VMEM(plane, F32),
             pltpu.VMEM(plane, F32),
             pltpu.VMEM(strip, F32),
             pltpu.VMEM(strip, F32),
-            pltpu.SemaphoreType.DMA((8,)),
         ],
     )(
-        pos, scal, grams, basis, cfm, mid_pre, mid_res, pre, frz, below, above, w, coef, inv,
-        wide, spread, lift,
+        pos, scal, gram, basis, cfm, mid_pre, mid_res, keep, frz, below, above, coef, wide, spread,
+        lift, diag_w, diag_e,
     )[0]
     got = lax.all_to_all(packed, "gx", 0, 0, tiled=True)
     correction, rest = call(unpack_body, "unpack", [f32s(512, 128), f32s(512, 128)], (0,))(got)

time: 213 us -> 197 us (0.925)
  blocking collectives: 20.6 us -> 42.2 us
  starting transfers between devices: 71.9 us -> 55.8 us
  waiting for transfers between devices: 51.9 us -> 43 us
  local copies, waits for them, and re-layouts: 22.5 us -> 14.1 us
  other arithmetic: 5.67 us -> 2.81 us
    all_to_all x0 -> x1, blocking collectives: none -> 22.9 us  [local(): gram = lax.all_to_all(gram, 'yz', 0, 0, tiled=True)]
    all_to_all x1, starting transfers between devices: 26.4 us -> 10.3 us  [local(): gram = lax.all_to_all(gram, z_axes, 0, 0, tiled=True)]
    all_to_all x1, waiting for transfers between devices: 15.5 us -> 6.88 us  [local(): gram = lax.all_to_all(gram, z_axes, 0, 0, tiled=True)]
    unnamed x69 -> x52, local copies, waits for them, and re-layouts: 17.7 us -> 9.11 us
    unnamed x10 -> x0, other arithmetic: 3.46 us -> none
    pallas_call x5 -> x6, Pallas kernels: 29.1 us -> 26.7 us  [the longest x1 12 us: local(): call(post_body, 'post', [f32s(16, 64, 128)], (1, 1) + (0,) * 15, mid_scra...]
  transfers between devices with their start and end apart: 14 -> 14, of which waited for: 11 -> 11; matrix products, arithmetic and copies ran while one was open for 4% -> 5% of each run, Pallas kernels for 0% -> 0%
where the time goes in v4:
time: 197 us; the launch traced here: 196 us
  starting transfers between devices  55.8 us (28%)
  waiting for transfers between devices  43 us (22%)
  blocking collectives  42.2 us (21%)
  Pallas kernels  32.3 us (16%)
  local copies, waits for them, and re-layouts  14.1 us (7%)
  between operations  3.14 us (2%)
  other arithmetic  2.81 us (1%)
  matrix products  2.29 us (1%)
    all_to_all x1, blocking collectives, local(): gram = lax.all_to_all(gram, 'yz', 0, 0, tiled=True)  22.9 us
    all_to_all x1, blocking collectives, local(): got = lax.all_to_all(packed, 'gx', 0, 0, tiled=True)  19.2 us
    pallas_call x1, Pallas kernels, local(): call(post_body, 'post', [f32s(16, 64, 128)], (1, 1) + (0,) * 15, mid_scra...  12 us
    all_to_all x1, starting transfers between devices, local(): gram = lax.all_to_all(gram, z_axes, 0, 0, tiled=True)  10.3 us
    all_to_all x1, starting transfers between devices, local(): own = lax.all_to_all(slots, 'gx', 0, 0, tiled=True)  9.24 us
    unnamed x52, local copies, waits for them, and re-layouts  9.11 us
    ppermute x2, waiting for transfers between devices, local(): above = lax.ppermute(bwd, 'yz', shift_dn)  8.08 us
    ppermute x1, starting transfers between devices, local(): coarse_below = lax.ppermute(fwd, 'yz', shift_up)  7.35 us
  transfers between devices with their start and end apart: 14, of which 11 were waited for; matrix products, arithmetic and copies ran while one was open for 5% of the time, Pallas kernels for 0%

profile of v4, /device:TPU:2, one launch (start us, length us, event | category | flops | bytes accessed | tf_op | source)
XLA Modules:
  0.0 195.6 jit_solution(8875639168650607258)
XLA Ops:
  5.1 9.2 %all-to-all-start = ((f32[16,40,128]{2,1,0:T(8,128)}), f32[16,40,128]{2,1,0:T(8,128)S(1)}, u32[]{:S(2)}, u32[]{:S(2)}) async-start(f32[16,40,128]{2,1,0:T(8,128)} %slots.1), calls=%async_computation | async-start | bytes 655360 | tf_op jit(solution)/shard_map/all_to_all | solution.py:1008
  20.9 4.7 %all-to-all-done.own = f32[16,40,128]{2,1,0:T(8,128)S(1)} async-done(((f32[16,40,128]{2,1,0:T(8,128)}), f32[16,40,128]{2,1,0:T(8,128)S(1)}, u32[]{:S(2)}, u32[]{:S(2)}) %all-to-all-start) | async-done | bytes 327712 | tf_op jit(solution)/shard_map/all_to_all | solution.py:1008
  25.6 3.4 %collective-permute-start.1 = (f32[16,40,128]{2,1,0:T(8,128)S(1)}, f32[16,40,128]{2,1,0:T(8,128)S(1)}, u32[]{:S(2)}, u32[]{:S(2)}) collective-permute-start(f32[16,40,128]{2,1,0:T(8,128)S(1)} %all-to-all-done.own), channel_id=1, source_target_pairs={{32,0},{64,32},{96,64},{128,96},{160,128},{192,160},{224,192},{256... | collective-permute-start | bytes 983048 | tf_op jit(solution)/shard_map/ppermute | solution.py:1010
  29.1 3.3 %collective-permute-start = (f32[16,40,128]{2,1,0:T(8,128)S(1)}, f32[16,40,128]{2,1,0:T(8,128)S(1)}, u32[]{:S(2)}, u32[]{:S(2)}) collective-permute-start(f32[16,40,128]{2,1,0:T(8,128)S(1)} %all-to-all-done.own), channel_id=1, source_target_pairs={{0,32},{32,64},{64,96},{96,128},{128,160},{160,192},{192,224},{224... | collective-permute-start | bytes 983048 | tf_op jit(solution)/shard_map/ppermute | solution.py:1009
  33.2 2.4 %collective-permute-done.1.up = f32[16,40,128]{2,1,0:T(8,128)S(1)} collective-permute-done((f32[16,40,128]{2,1,0:T(8,128)S(1)}, f32[16,40,128]{2,1,0:T(8,128)S(1)}, u32[]{:S(2)}, u32[]{:S(2)}) %collective-permute-start.1) | collective-permute-done | bytes 327712 | tf_op jit(solution)/shard_map/ppermute | solution.py:1010
  35.6 6.5 %collective-permute-done.dn = f32[16,40,128]{2,1,0:T(8,128)S(1)} collective-permute-done((f32[16,40,128]{2,1,0:T(8,128)S(1)}, f32[16,40,128]{2,1,0:T(8,128)S(1)}, u32[]{:S(2)}, u32[]{:S(2)}) %collective-permute-start) | collective-permute-done | bytes 327712 | tf_op jit(solution)/shard_map/ppermute | solution.py:1009
  48.3 3.9 %collective-permute-done.3.above = f32[768,128]{1,0:T(8,128)S(1)} collective-permute-done((f32[768,128]{1,0:T(8,128)}, f32[768,128]{1,0:T(8,128)S(1)}, u32[]{:S(2)}, u32[]{:S(2)}) %collective-permute-start.3) | collective-permute-done | bytes 393248 | tf_op jit(solution)/shard_map/ppermute | solution.py:1019
  52.2 6.2 %fine_pre.1 = (f32[8,64,128]{2,1,0:T(8,128)S(1)}, f32[64,4096]{1,0:T(8,128)S(1)}, f32[8,4096]{1,0:T(8,128)S(1)}, f32[128,1024]{1,0:T(8,128)S(1)}, f32[512,128]{1,0:T(8,128)S(1)}, /*index=5*/f32[512,128]{1,0:T(8,128)S(1)}) custom-call(s32[2]{0:T(128)S(1)} %pad_add_fusion.pos, f32[16,64,128]{2,1,0:T(8,128)S(1)} %get-tuple-element.33.rows_in, ...), custom_call_target="tpu_custom_call" | custom-call | flops 1000000 | bytes 1000000 | tf_op jit(solution)/shard_map/fine_pre/pallas_call | solution.py:1022
  60.4 4.8 %collective-permute-start.4 = (f32[512,128]{1,0:T(8,128)S(1)}, f32[512,128]{1,0:T(8,128)S(1)}, u32[]{:S(2)}, u32[]{:S(2)}) collective-permute-start(f32[512,128]{1,0:T(8,128)S(1)} %get-tuple-element.36.own), channel_id=1, source_target_pairs={{0,32},{32,64},{64,96},{96,128},{128,160},{160,192},{192,224},{224... | collective-permute-start | bytes 786440 | tf_op jit(solution)/shard_map/ppermute | solution.py:1044
  65.2 2.5 %collective-permute-done.5.up = f32[512,128]{1,0:T(8,128)S(1)} collective-permute-done((f32[512,128]{1,0:T(8,128)S(1)}, f32[512,128]{1,0:T(8,128)S(1)}, u32[]{:S(2)}, u32[]{:S(2)}) %collective-permute-start.5) | collective-permute-done | bytes 262176 | tf_op jit(solution)/shard_map/ppermute | solution.py:1045
  67.7 6.0 %collective-permute-done.4.dn = f32[512,128]{1,0:T(8,128)S(1)} collective-permute-done((f32[512,128]{1,0:T(8,128)S(1)}, f32[512,128]{1,0:T(8,128)S(1)}, u32[]{:S(2)}, u32[]{:S(2)}) %collective-permute-start.4) | collective-permute-done | bytes 262176 | tf_op jit(solution)/shard_map/ppermute | solution.py:1044
  75.7 4.1 %collective-permute-start.6 = (f32[896,128]{1,0:T(8,128)}, f32[896,128]{1,0:T(8,128)S(1)}, u32[]{:S(2)}, u32[]{:S(2)}) collective-permute-start(f32[896,128]{1,0:T(8,128)} %get-tuple-element.40), channel_id=1, source_target_pairs={{0,2},{2,4},{4,6},{6,8},{8,10},{10,12},{12,14},{14,16},{16,18},{18... | collective-permute-start | bytes 1376264 | tf_op jit(solution)/shard_map/ppermute | solution.py:1052
  85.0 4.2 %collective-permute-done.7.above = f32[896,128]{1,0:T(8,128)S(1)} collective-permute-done((f32[896,128]{1,0:T(8,128)}, f32[896,128]{1,0:T(8,128)S(1)}, u32[]{:S(2)}, u32[]{:S(2)}) %collective-permute-start.7) | collective-permute-done | bytes 458784 | tf_op jit(solution)/shard_map/ppermute | solution.py:1053
  89.2 3.5 %mid_pre.1 = (f32[8,16,768]{2,1,0:T(8,128)S(1)}, f32[8,16,768]{2,1,0:T(8,128)S(1)}, f32[5,16,1024]{2,1,0:T(8,128)S(1)}, f32[2,16,768]{2,1,0:T(8,128)S(1)}, f32[2,16,768]{2,1,0:T(8,128)S(1)}) custom-call(s32[2]{0:T(128)S(1)} %pad_add_fusion.pos, f32[144]{0:T(256)S(1)} %concatenate.42.scal, f32[128,256]{1,0:T(8,128)S(1)} %get-tuple-element.39.slab, ...), custom_call_target="tpu_custom_call" | custom-call | flops 1000000 | bytes 1000000 | tf_op jit(solution)/shard_map/mid_pre/pallas_call | solution.py:1061
  94.7 3.9 %collective-permute-start.9 = (f32[2,16,768]{2,1,0:T(8,128)S(1)}, f32[2,16,768]{2,1,0:T(8,128)S(1)}, u32[]{:S(2)}, u32[]{:S(2)}) collective-permute-start(f32[2,16,768]{2,1,0:T(8,128)S(1)} %get-tuple-element.45), channel_id=1, source_target_pairs={{32,0},{64,32},{96,64},{128,96},{160,128},{192,160},{224,192},{256... | collective-permute-start | bytes 294920 | tf_op jit(solution)/shard_map/ppermute | solution.py:1071
  99.3 2.8 %collective-permute-done.9.up = f32[2,16,768]{2,1,0:T(8,128)S(1)} collective-permute-done((f32[2,16,768]{2,1,0:T(8,128)S(1)}, f32[2,16,768]{2,1,0:T(8,128)S(1)}, u32[]{:S(2)}, u32[]{:S(2)}) %collective-permute-start.9) | collective-permute-done | bytes 98336 | tf_op jit(solution)/shard_map/ppermute | solution.py:1071
  102.8 7.3 %collective-permute-start.10 = (f32[5,16,512]{2,1,0:T(8,128)S(1)}, f32[5,16,512]{2,1,0:T(8,128)S(1)}, u32[]{:S(2)}, u32[]{:S(2)}) collective-permute-start(f32[5,16,512]{2,1,0:T(8,128)S(1)} %get-tuple-element.47), channel_id=1, source_target_pairs={{0,2},{2,4},{4,6},{6,8},{8,10},{10,12},{12,14},{14,16},{16,18},{18... | collective-permute-start | bytes 491528 | tf_op jit(solution)/shard_map/ppermute | solution.py:1078
  111.5 2.6 %collective-permute-done.11.above = f32[5,16,512]{2,1,0:T(8,128)S(1)} collective-permute-done((f32[5,16,512]{2,1,0:T(8,128)S(1)}, f32[5,16,512]{2,1,0:T(8,128)S(1)}, u32[]{:S(2)}, u32[]{:S(2)}) %collective-permute-start.11) | collective-permute-done | bytes 163872 | tf_op jit(solution)/shard_map/ppermute | solution.py:1079
  114.1 3.5 %krylov.1 = (f32[8,16,768]{2,1,0:T(8,128)S(1)}, f32[16,128]{1,0:T(8,128)S(1)}) custom-call(f32[144]{0:T(256)S(1)} %copy-done.12, f32[5,16,1280]{2,1,0:T(8,128)S(1)} %get-tuple-element.46.own, f32[5,16,512]{2,1,0:T(8,128)S(1)} %collective-permute-done.10.below, f32[5,16,512]{2,1,0:T(8,128)S(1)} %collective-permute-done.11.above), custom_call_target="tpu_custom_call" | custom-call | flops 1000000 | bytes 1000000 | tf_op jit(solution)/shard_map/krylov/pallas_call | solution.py:1080
  117.5 22.9 %all_to_all.32 = f32[16,1,128]{2,1,0:T(1,128)S(1)} all-to-all(f32[16,1,128]{2,1,0:T(1,128)S(1)} %bitcast.77), channel_id=1, replica_groups=mesh['gx'=16,'yz'=16,'lvl'=2] {'yz'}, dimensions={0} | all-to-all | bytes 16384 | tf_op jit(solution)/shard_map/all_to_all | solution.py:1090
  141.2 10.3 %all-to-all-start.2 = ((f32[32,1,128]{2,1,0:T(1,128)}), f32[32,1,128]{2,1,0:T(1,128)}, u32[]{:S(2)}, u32[]{:S(2)}) async-start(f32[32,1,128]{2,1,0:T(1,128)} %bitcast.73), calls=%async_computation.2 | async-start | bytes 32768 | tf_op jit(solution)/shard_map/all_to_all | solution.py:1092
  153.0 6.9 %all-to-all-done.2 = f32[32,1,128]{2,1,0:T(1,128)} async-done(((f32[32,1,128]{2,1,0:T(1,128)}), f32[32,1,128]{2,1,0:T(1,128)}, u32[]{:S(2)}, u32[]{:S(2)}) %all-to-all-start.2) | async-done | bytes 16416 | tf_op jit(solution)/shard_map/all_to_all | solution.py:1092
  162.9 12.0 %post.1 = f32[16,64,128]{2,1,0:T(8,128)S(1)} custom-call(s32[2]{0:T(128)S(1)} %copy-done.15, f32[144]{0:T(256)S(1)} %copy-done.13, f32[32,128]{1,0:T(8,128)} %bitcast.36.gram, f32[8,16,768]{2,1,0:T(8,128)S(1)} %get-tuple-element.50.basis, f32[128,1024]{1,0:T(8,128)S(1)} %get-tuple-element.42.cfm, f32[8,16,768]{2,1,0:T(8,128)S(1)} %get-tuple-element.51.mid_pre, ...), custom_call_target="tpu_custom_call" | custom-call | flops 1000000 | bytes 1000000 | tf_op jit(solution)/shard_map/post/pallas_call | solution.py:1093
  174.9 19.2 %all_to_all.33.got = f32[16,64,128]{2,1,0:T(8,128)S(1)} all-to-all(f32[16,64,128]{2,1,0:T(8,128)S(1)} %post.1), channel_id=1, replica_groups=mesh['gx'=16,'yz'=16,'lvl'=2] {'gx'}, dimensions={0} | all-to-all | bytes 1048576 | tf_op jit(solution)/shard_map/all_to_all | solution.py:1115
  (120 shorter events, 36.3 us)
Async XLA Ops:
  1.3 0.9 copy-start.3
  5.1 20.6 %all-to-all-start = ((f32[16,40,128]{2,1,0:T(8,128)}), f32[16,40,128]{2,1,0:T(8,128)S(1)}, u32[]{:S(2)}, u32[]{:S(2)}) async-start(f32[16,40,128]{2,1,0:T(8,128)} %slots.1), calls=%async_computation | async-start | bytes 655360 | tf_op jit(solution)/shard_map/all_to_all | solution.py:1008
  17.9 0.8 copy-start.23
  20.6 21.4 %copy-start = (bf16[384,512]{1,0:T(8,128)(2,1)S(1)}, bf16[384,512]{1,0:T(8,128)(2,1)}, u32[]{:S(2)}) copy-start(bf16[384,512]{1,0:T(8,128)(2,1)} %constant.72.clone.place_kinds) | copy-start | bytes 1179652
  20.7 21.3 %copy-start.4 = (bf16[256,256]{1,0:T(8,128)(2,1)S(1)}, bf16[256,256]{1,0:T(8,128)(2,1)}, u32[]{:S(2)}) copy-start(bf16[256,256]{1,0:T(8,128)(2,1)} %constant.71.clone.place_values) | copy-start | bytes 393220
  25.6 9.9 %collective-permute-start.1 = (f32[16,40,128]{2,1,0:T(8,128)S(1)}, f32[16,40,128]{2,1,0:T(8,128)S(1)}, u32[]{:S(2)}, u32[]{:S(2)}) collective-permute-start(f32[16,40,128]{2,1,0:T(8,128)S(1)} %all-to-all-done.own), channel_id=1, source_target_pairs={{32,0},{64,32},{96,64},{128,96},{160,128},{192,160},{224,192},{256... | collective-permute-start | bytes 983048 | tf_op jit(solution)/shard_map/ppermute | solution.py:1010
  29.1 13.0 %collective-permute-start = (f32[16,40,128]{2,1,0:T(8,128)S(1)}, f32[16,40,128]{2,1,0:T(8,128)S(1)}, u32[]{:S(2)}, u32[]{:S(2)}) collective-permute-start(f32[16,40,128]{2,1,0:T(8,128)S(1)} %all-to-all-done.own), channel_id=1, source_target_pairs={{0,32},{32,64},{64,96},{96,128},{128,160},{160,192},{192,224},{224... | collective-permute-start | bytes 983048 | tf_op jit(solution)/shard_map/ppermute | solution.py:1009
  43.5 8.7 %collective-permute-start.2 = (f32[896,128]{1,0:T(8,128)S(1)}, f32[896,128]{1,0:T(8,128)S(1)}, u32[]{:S(2)}, u32[]{:S(2)}) collective-permute-start(f32[896,128]{1,0:T(8,128)S(1)} %get-tuple-element.34.own), channel_id=1, source_target_pairs={{0,2},{2,4},{4,6},{6,8},{8,10},{10,12},{12,14},{14,16},{16,18},{18... | collective-permute-start | bytes 1376264 | tf_op jit(solution)/shard_map/ppermute | solution.py:1018
  45.0 7.2 %collective-permute-start.3 = (f32[768,128]{1,0:T(8,128)}, f32[768,128]{1,0:T(8,128)S(1)}, u32[]{:S(2)}, u32[]{:S(2)}) collective-permute-start(f32[768,128]{1,0:T(8,128)} %get-tuple-element.35), channel_id=1, source_target_pairs={{2,0},{4,2},{6,4},{8,6},{10,8},{12,10},{14,12},{16,14},{18,16},{20... | collective-permute-start | bytes 1179656 | tf_op jit(solution)/shard_map/ppermute | solution.py:1019
  46.4 42.9 %copy-start.14 = (s32[2]{0:T(128)}, s32[2]{0:T(128)S(1)}, u32[]{:S(2)}) copy-start(s32[2]{0:T(128)S(1)} %pad_add_fusion.pos) | copy-start | bytes 28
  48.2 4.0 %copy-start.5 = (bf16[64,128]{1,0:T(8,128)(2,1)S(1)}, bf16[64,128]{1,0:T(8,128)(2,1)}, u32[]{:S(2)}) copy-start(bf16[64,128]{1,0:T(8,128)(2,1)} %constant.70.clone.spread) | copy-start | bytes 49156
  58.4 17.3 %copy-start.1 = (f32[8,64,128]{2,1,0:T(8,128)}, f32[8,64,128]{2,1,0:T(8,128)S(1)}, u32[]{:S(2)}) copy-start(f32[8,64,128]{2,1,0:T(8,128)S(1)} %get-tuple-element.53.keep) | copy-start | bytes 786436
  58.4 9.3 %collective-permute-start.5 = (f32[512,128]{1,0:T(8,128)S(1)}, f32[512,128]{1,0:T(8,128)S(1)}, u32[]{:S(2)}, u32[]{:S(2)}) collective-permute-start(f32[512,128]{1,0:T(8,128)S(1)} %get-tuple-element.37), channel_id=1, source_target_pairs={{32,0},{64,32},{96,64},{128,96},{160,128},{192,160},{224,192},{256... | collective-permute-start | bytes 786440 | tf_op jit(solution)/shard_map/ppermute | solution.py:1045
  60.4 13.3 %collective-permute-start.4 = (f32[512,128]{1,0:T(8,128)S(1)}, f32[512,128]{1,0:T(8,128)S(1)}, u32[]{:S(2)}, u32[]{:S(2)}) collective-permute-start(f32[512,128]{1,0:T(8,128)S(1)} %get-tuple-element.36.own), channel_id=1, source_target_pairs={{0,32},{32,64},{64,96},{96,128},{128,160},{160,192},{192,224},{224... | collective-permute-start | bytes 786440 | tf_op jit(solution)/shard_map/ppermute | solution.py:1044
  75.7 9.3 %collective-permute-start.6 = (f32[896,128]{1,0:T(8,128)}, f32[896,128]{1,0:T(8,128)S(1)}, u32[]{:S(2)}, u32[]{:S(2)}) collective-permute-start(f32[896,128]{1,0:T(8,128)} %get-tuple-element.40), channel_id=1, source_target_pairs={{0,2},{2,4},{4,6},{6,8},{8,10},{10,12},{12,14},{14,16},{16,18},{18... | collective-permute-start | bytes 1376264 | tf_op jit(solution)/shard_map/ppermute | solution.py:1052
  79.8 9.4 %collective-permute-start.7 = (f32[896,128]{1,0:T(8,128)}, f32[896,128]{1,0:T(8,128)S(1)}, u32[]{:S(2)}, u32[]{:S(2)}) collective-permute-start(f32[896,128]{1,0:T(8,128)} %get-tuple-element.41), channel_id=1, source_target_pairs={{2,0},{4,2},{6,4},{8,6},{10,8},{12,10},{14,12},{16,14},{18,16},{20... | collective-permute-start | bytes 1376264 | tf_op jit(solution)/shard_map/ppermute | solution.py:1053
  85.0 4.2 %copy-start.11 = (f32[144]{0:T(256)}, f32[144]{0:T(256)S(1)}, u32[]{:S(2)}) copy-start(f32[144]{0:T(256)S(1)} %concatenate.42.scal) | copy-start | bytes 1732
  92.8 6.5 %collective-permute-start.8 = (f32[2,16,768]{2,1,0:T(8,128)S(1)}, f32[2,16,768]{2,1,0:T(8,128)S(1)}, u32[]{:S(2)}, u32[]{:S(2)}) collective-permute-start(f32[2,16,768]{2,1,0:T(8,128)S(1)} %get-tuple-element.44), channel_id=1, source_target_pairs={{0,32},{32,64},{64,96},{96,128},{128,160},{160,192},{192,224},{224... | collective-permute-start | bytes 294920 | tf_op jit(solution)/shard_map/ppermute | solution.py:1070
  94.7 7.4 %collective-permute-start.9 = (f32[2,16,768]{2,1,0:T(8,128)S(1)}, f32[2,16,768]{2,1,0:T(8,128)S(1)}, u32[]{:S(2)}, u32[]{:S(2)}) collective-permute-start(f32[2,16,768]{2,1,0:T(8,128)S(1)} %get-tuple-element.45), channel_id=1, source_target_pairs={{32,0},{64,32},{96,64},{128,96},{160,128},{192,160},{224,192},{256... | collective-permute-start | bytes 294920 | tf_op jit(solution)/shard_map/ppermute | solution.py:1071
  102.8 8.7 %collective-permute-start.10 = (f32[5,16,512]{2,1,0:T(8,128)S(1)}, f32[5,16,512]{2,1,0:T(8,128)S(1)}, u32[]{:S(2)}, u32[]{:S(2)}) collective-permute-start(f32[5,16,512]{2,1,0:T(8,128)S(1)} %get-tuple-element.47), channel_id=1, source_target_pairs={{0,2},{2,4},{4,6},{6,8},{8,10},{10,12},{12,14},{14,16},{16,18},{18... | collective-permute-start | bytes 491528 | tf_op jit(solution)/shard_map/ppermute | solution.py:1078
  110.2 3.9 %copy-start.12 = (f32[144]{0:T(256)S(1)}, f32[144]{0:T(256)}, u32[]{:S(2)}) copy-start(f32[144]{0:T(256)} %copy-done.11) | copy-start | bytes 1732
  110.2 3.9 %collective-permute-start.11 = (f32[5,16,512]{2,1,0:T(8,128)S(1)}, f32[5,16,512]{2,1,0:T(8,128)S(1)}, u32[]{:S(2)}, u32[]{:S(2)}) collective-permute-start(f32[5,16,512]{2,1,0:T(8,128)S(1)} %get-tuple-element.48), channel_id=1, source_target_pairs={{2,0},{4,2},{6,4},{8,6},{10,8},{12,10},{14,12},{16,14},{18,16},{20... | collective-permute-start | bytes 491528 | tf_op jit(solution)/shard_map/ppermute | solution.py:1079
  141.2 18.6 %all-to-all-start.2 = ((f32[32,1,128]{2,1,0:T(1,128)}), f32[32,1,128]{2,1,0:T(1,128)}, u32[]{:S(2)}, u32[]{:S(2)}) async-start(f32[32,1,128]{2,1,0:T(1,128)} %bitcast.73), calls=%async_computation.2 | async-start | bytes 32768 | tf_op jit(solution)/shard_map/all_to_all | solution.py:1092
  160.5 1.0 copy-start.2
  (16 other events, 11.5 us)

commit v5 on v4

--- a/solution.py
+++ b/solution.py
@@ -26,7 +26,9 @@
 RHO2 = 1.0 / (2.0 * SCALED - RHO1)
 STEPS = ((RHO1 * RHO0, 2.0 * RHO1 / SPREAD), (RHO2 * RHO1, 2.0 * RHO2 / SPREAD))
 BASIS = 8
+ORDER = tuple(2 * n if n < 8 else 2 * (15 - n) + 1 for n in range(16))
 VMEM_LIMIT = 24 * 2**20
+LARGE_LIMIT = 60 * 2**20
 
 
 def lanes(shape):
@@ -42,11 +44,10 @@
 SPACES = {
     0: pl.BlockSpec(memory_space=pltpu.VMEM),
     1: pl.BlockSpec(memory_space=pltpu.SMEM),
-    2: pl.BlockSpec(memory_space=pltpu.HBM),
 }
 
 
-def call(body, name, out_shape, in_specs, scratch=(), out_specs=None):
+def call(body, name, out_shape, in_specs, scratch=(), out_specs=None, limit=VMEM_LIMIT):
     out_specs = out_specs or (0,) * len(out_shape)
     return pl.pallas_call(
         body,
@@ -54,7 +55,7 @@
         in_specs=[SPACES[i] for i in in_specs],
         out_specs=[SPACES[i] for i in out_specs],
         scratch_shapes=list(scratch),
-        compiler_params=pltpu.CompilerParams(vmem_limit_bytes=VMEM_LIMIT),
+        compiler_params=pltpu.CompilerParams(vmem_limit_bytes=limit),
         cost_estimate=pl.CostEstimate(flops=1000000, bytes_accessed=1000000, transcendentals=0),
         name=name,
     )
@@ -105,32 +106,42 @@
         for n in range(2):
             at = 8 * (2 * n + 2)
             cf[first + 8 * n : first + 8 * n + 8, :] = ref[at : at + 8, :].astype(F32)
-    low = lanes((32, 128)) < 64
+    low = lanes((16, 128)) < 64
     low8 = lanes((8, 128)) < 64
+    near = lanes((32, 128)) % 8 < 4
     values = exchange([res[pl.ds(y, 64, stride=8), :] for y in range(8)], 8)
     kinds = exchange([cf[pl.ds(y, 16, stride=8), :] for y in range(8)], 8)
     for j in range(8):
+        first, second = ORDER[j], ORDER[j + 8]
         a, b = values[j][0:32], values[j][32:64]
-        out[j, 0:32, :] = jnp.where(low, a, roll(b, 64))
-        out[j + 8, 0:32, :] = jnp.where(low, roll(a, 64), b)
+        for at, v in (
+            (0, jnp.where(near, a, roll(b, 4))),
+            (24, jnp.where(near, roll(a, -4), b)),
+        ):
+            out[first, at : at + 16, :] = jnp.where(low, v[0:16], roll(v[16:32], 64))
+            out[second, at : at + 16, :] = jnp.where(low, roll(v[0:16], 64), v[16:32])
         a, b = kinds[j][0:8], kinds[j][8:16]
-        out[j, 32:40, :] = jnp.where(low8, a, roll(b, 64))
-        out[j + 8, 32:40, :] = jnp.where(low8, roll(a, 64), b)
+        out[first, 16:24, :] = jnp.where(low8, a, roll(b, 64))
+        out[second, 16:24, :] = jnp.where(low8, roll(a, 64), b)
 
 
 def place_tables():
-    values = np.zeros((256, 256), np.float32)
+    values = np.zeros((512, 512), np.float32)
     kinds = np.zeros((384, 512), np.float32)
+    pack = np.zeros((256, 128), np.float32)
     for half in range(2):
         for y in range(8):
             for z in range(8):
                 lane = 64 * half + 8 * y + z
-                values[lane, 128 * half + 16 * y + z + 4] = 1.0
-                beside = z + 12 if z < 4 else z - 4
-                values[128 + lane, 128 * half + 16 * y + beside] = 1.0
+                to = 128 * (2 * (z // 4) + half) + 16 * y + z % 4
+                for n, first in enumerate((4, 8, 12, 0)):
+                    values[128 * n + lane, to + first] = 1.0
                 for n, first in enumerate((12, 4, 20)):
                     kinds[128 * n + lane, 256 * half + 32 * y + first + z] = 1.0
-    return values, kinds
+    for y in range(-1, 9):
+        for z in range(-1, 9):
+            pack[16 * (y + 4) + z + 4, 12 * (y + 1) + z + 1] = 1.0
+    return [jnp.asarray(v, BF16) for v in (values, kinds, pack)]
 
 
 def three_rows(x):
@@ -147,18 +158,18 @@
 
 
 def join_body(own, dn, up, place_values, place_kinds, rows, fwd, bwd):
-    near = lanes((512, 128)) % 8 < 4
-    mine = own[:, 0:32, :].reshape(512, 128)
-    beside = jnp.where(near, up[:, 0:32, :].reshape(512, 128), dn[:, 0:32, :].reshape(512, 128))
-    out = moved(jnp.concatenate([mine, beside], axis=1), place_values[...])
+    parts = (own[:, 0:16, :], own[:, 24:40, :], up[:, 0:16, :], dn[:, 8:24, :])
+    values = jnp.concatenate([v.reshape(256, 128) for v in parts], axis=1)
+    out = moved(values, place_values[...])
     for x in range(NX):
-        rows[x, 0:32, :] = out[32 * x : 32 * x + 32, 0:128]
-        rows[x, 32:64, :] = out[32 * x : 32 * x + 32, 128:256]
+        for n in range(4):
+            rows[x, 16 * n : 16 * n + 16, :] = out[16 * x : 16 * x + 16, 128 * n : 128 * n + 128]
     low = lanes((64, 128)) < 64
     for x in range(8):
         fwd[64 * x : 64 * x + 64, :] = jnp.where(low, roll(rows[x], 64), rows[x + 8])
         bwd[64 * x : 64 * x + 64, :] = jnp.where(low, rows[x], roll(rows[x + 8], 64))
-    kinds = jnp.concatenate([v[:, 32:40, :].reshape(128, 128) for v in (own, dn, up)], axis=1)
+    parts = (own[:, 16:24, :], dn[:, 0:8, :], up[:, 16:24, :])
+    kinds = jnp.concatenate([v.reshape(128, 128) for v in parts], axis=1)
     out = moved(kinds, place_kinds[...])
     array = lax.broadcasted_iota(jnp.int32, (128, 128), 0) % 8
     edge = (lanes((128, 128)) % 32 == 3) & ((array == 3) | (array == 6))
@@ -272,6 +283,7 @@
     down,
     mid_diag_w,
     mid_diag_e,
+    pack,
     keep,
     r,
     coef,
@@ -285,6 +297,7 @@
     px,
     qx,
     gather,
+    held,
 ):
     low = lanes((64, 128)) < 64
     lane8 = lanes((8, 128))
@@ -349,8 +362,10 @@
             x = (CHUNK // 256) * c + n
             for half in range(2):
                 piece = update[:, 256 * n + 128 * half : 256 * n + 128 * half + 128]
-                send_up[pl.ds(128 * half + x, 8, stride=16), :] = piece
-                send_down[pl.ds(128 * half + x, 8, stride=16), :] = piece
+                held[pl.ds(128 * half + x, 8, stride=16), :] = piece
+    packed = moved(jnp.concatenate([held[0:128, :], held[128:256, :]], axis=1), pack[...])
+    send_up[0:128, :] = packed
+    send_down[0:128, :] = packed
     for x in range(NX):
         first, second = slice(256 * x, 256 * x + 128), slice(256 * x + 128, 256 * x + 256)
         mine = jnp.where(low, roll(r[:, first], 64), roll(r[:, second], 64))
@@ -360,8 +375,8 @@
             part = mine[16 * j : 16 * j + 16]
             up = jnp.where(lane16 == j, roll(part, 4 * j - 8), up)
             dn = jnp.where(lane16 == j, roll(part, 4 * j - 4), dn)
-        send_up[256 + 16 * x : 272 + 16 * x, :] = up
-        send_down[256 + 16 * x : 272 + 16 * x, :] = dn
+        send_up[128 + 16 * x : 144 + 16 * x, :] = up
+        send_down[128 + 16 * x : 144 + 16 * x, :] = dn
     lane = lanes((64, 128))
     for x in range(8):
         a, b = [
@@ -377,8 +392,8 @@
     for x in range(NX):
         at = 256 * x
         mine = jnp.where(low, roll(r[:, at : at + 128], 64), roll(r[:, at + 128 : at + 256], 64))
-        pack_dn = dn[256 + 16 * x : 272 + 16 * x, :]
-        pack_up = up[256 + 16 * x : 272 + 16 * x, :]
+        pack_dn = dn[128 + 16 * x : 144 + 16 * x, :]
+        pack_up = up[128 + 16 * x : 144 + 16 * x, :]
         for j in range(4):
             rows = slice(16 * j, 16 * j + 16)
             part = jnp.where(l16 < 4, roll(pack_dn, -4 * j), mine[rows])
@@ -395,11 +410,11 @@
             if y < -1 or y > 8:
                 continue
             to = 32 * n
-            half, at = (y + 4) // 8, 16 * ((y + 4) % 8)
-            rows = slice(128 * half, 128 * half + 128)
-            acc = jnp.where((lane >= to + 12) & (lane < to + 20), roll(own[rows, :], to + 8 - at), acc)
-            acc = jnp.where((lane >= to + 3) & (lane < to + 12), roll(dn[rows, :], to - at), acc)
-            acc = jnp.where((lane >= to + 20) & (lane < to + 29), roll(up[rows, :], to + 16 - at), acc)
+            at = 12 * (y + 1)
+            rows = slice(0, 128)
+            acc = jnp.where((lane >= to + 12) & (lane < to + 20), roll(own[rows, :], to + 11 - at), acc)
+            acc = jnp.where((lane >= to + 3) & (lane < to + 12), roll(dn[rows, :], to + 3 - at), acc)
+            acc = jnp.where((lane >= to + 20) & (lane < to + 29), roll(up[rows, :], to + 19 - at), acc)
         if 1 <= m <= 2:
             slab[:, 128 * (m - 1) : 128 * m] = acc
         if m <= 2:
@@ -863,7 +878,7 @@
     for part, out in enumerate((first, second)):
         held = []
         for g in range(8):
-            a, b = got[g], got[g + 8]
+            a, b = got[ORDER[g]], got[ORDER[g + 8]]
             if part == 0:
                 held.append(jnp.where(low, a, roll(b, 64)))
             else:
@@ -987,34 +1002,40 @@
     shift_dn = [(i + 1, i) for i in range(15)]
 
     def z_index(zb):
-        return (zb % 16) * 2 + zb // 16
+        return ORDER[zb % 16] * 2 + zb // 16
 
     z_up = [(z_index(i), z_index(i + 1)) for i in range(31)]
     z_dn = [(z_index(i + 1), z_index(i)) for i in range(31)]
     z_axes = ("gx", "lvl")
     side = lax.axis_index("lvl")
+    chip = lax.axis_index("gx")
     pos = jnp.stack(
         [
             lax.axis_index("yz"),
-            side * 16 + lax.axis_index("gx"),
+            side * 16 + jnp.where(chip % 2 == 0, chip // 2, 15 - chip // 2),
         ]
     ).astype(jnp.int32)
     res = residual.reshape(512, 128)
     slots = call(
-        slots_body, "slots", [f32s(16, 40, 128)], (0,) * 4, [pltpu.VMEM((128, 128), F32)]
+        slots_body,
+        "slots",
+        [f32s(16, 40, 128)],
+        (0,) * 4,
+        [pltpu.VMEM((128, 128), F32)],
+        limit=LARGE_LIMIT,
     )(res, coefficient.reshape(8, 128), kind.reshape(48, 128), flag.reshape(48, 128))[0]
     element, faces, slots = lax.optimization_barrier((element, faces, slots))
     wide, spread, diag_w, diag_e, down, mid_diag_w, mid_diag_e, lift, scal = tables(element, faces)
     own = lax.all_to_all(slots, "gx", 0, 0, tiled=True)
-    dn = lax.ppermute(own, z_axes, z_up)
-    up = lax.ppermute(own, z_axes, z_dn)
-    place_values, place_kinds = place_tables()
+    dn = lax.ppermute(own[:, 16:40], z_axes, z_up)
+    up = lax.ppermute(own[:, 0:24], z_axes, z_dn)
+    place_values, place_kinds, pack = place_tables()
     rows, own, bwd = call(
         join_body,
         "join",
         [f32s(NX, 64, 128), f32s(896, 128), f32s(768, 128)],
         (0,) * 5,
-    )(own, dn, up, jnp.asarray(place_values, BF16), jnp.asarray(place_kinds, BF16))
+    )(own, dn, up, place_values, place_kinds)
     below = lax.ppermute(own, "yz", shift_up)
     above = lax.ppermute(bwd, "yz", shift_dn)
     plane = (64, NX * 256)
@@ -1027,10 +1048,10 @@
             f32s(*plane),
             f32s(8, NX * 256),
             f32s(128, 1024),
-            f32s(512, 128),
-            f32s(512, 128),
+            f32s(384, 128),
+            f32s(384, 128),
         ],
-        (1,) + (0,) * 11,
+        (1,) + (0,) * 12,
         [
             pltpu.VMEM(plane, F32),
             pltpu.VMEM((24, NX * 256), F32),
@@ -1039,8 +1060,11 @@
             pltpu.VMEM(strip, F32),
             pltpu.VMEM(strip, F32),
             pltpu.VMEM((896, 128), F32),
+            pltpu.VMEM((256, 128), F32),
         ],
-    )(pos, rows, own, below, above, wide, spread, diag_w, diag_e, down, mid_diag_w, mid_diag_e)
+    )(
+        pos, rows, own, below, above, wide, spread, diag_w, diag_e, down, mid_diag_w, mid_diag_e, pack
+    )
     dn = lax.ppermute(send_up, z_axes, z_up)
     up = lax.ppermute(send_down, z_axes, z_dn)
     slab, fwd, bwd, frz = call(
@@ -1108,6 +1132,7 @@
             pltpu.VMEM(strip, F32),
             pltpu.VMEM(strip, F32),
         ],
+        limit=LARGE_LIMIT,
     )(
         pos, scal, gram, basis, cfm, mid_pre, mid_res, keep, frz, below, above, coef, wide, spread,
         lift, diag_w, diag_e,

time: 197 us -> 187 us (0.949)
  waiting for transfers between devices: 43 us -> 29.4 us
  Pallas kernels: 32.3 us -> 35.6 us
  local copies, waits for them, and re-layouts: 14.1 us -> 11.9 us
    ppermute x2, waiting for transfers between devices: 8.08 us -> 2.79 us  [local(): above = lax.ppermute(bwd, 'yz', shift_dn)]
    ppermute x2, waiting for transfers between devices: 8.86 us -> 4.04 us  [the longest x1 2.35 us: local(): dn = lax.ppermute(own[:, 16:40], z_axes, z_up)]
    ppermute x2, waiting for transfers between devices: 6.6 us -> 3.64 us  [local(): dn = lax.ppermute(send_up, z_axes, z_up)]
    ppermute x1, starting transfers between devices: 4.11 us -> 6.47 us  [local(): below = lax.ppermute(fwd, 'yz', shift_up)]
    unnamed x52 -> x50, local copies, waits for them, and re-layouts: 9.11 us -> 6.91 us
    pallas_call x1, Pallas kernels: 12 us -> 14.1 us  [local(): call(post_body, 'post', [f32s(16, 64, 128)], (1, 1) + (0,) * 15, mid_scra...]
  transfers between devices with their start and end apart: 14 -> 14, of which waited for: 11 -> 10; matrix products, arithmetic and copies ran while one was open for 5% -> 5% of each run, Pallas kernels for 0% -> 0%
where the time goes in v5:
time: 187 us; the launch traced here: 185 us
  starting transfers between devices  57.3 us (31%)
  blocking collectives  43.9 us (23%)
  Pallas kernels  35.6 us (19%)
  waiting for transfers between devices  29.4 us (16%)
  local copies, waits for them, and re-layouts  11.9 us (6%)
  between operations  3.09 us (2%)
  matrix products  2.26 us (1%)
  other arithmetic  2.06 us (1%)
    all_to_all x1, blocking collectives, local(): gram = lax.all_to_all(gram, 'yz', 0, 0, tiled=True)  23.8 us
    all_to_all x1, blocking collectives, local(): got = lax.all_to_all(packed, 'gx', 0, 0, tiled=True)  20.1 us
    pallas_call x1, Pallas kernels, local(): call(post_body, 'post', [f32s(16, 64, 128)], (1, 1) + (0,) * 15, mid_scra...  14.1 us
    all_to_all x1, starting transfers between devices, local(): gram = lax.all_to_all(gram, z_axes, 0, 0, tiled=True)  11.6 us
    all_to_all x1, starting transfers between devices, local(): own = lax.all_to_all(slots, 'gx', 0, 0, tiled=True)  9.24 us
    all_to_all x1, waiting for transfers between devices, local(): gram = lax.all_to_all(gram, z_axes, 0, 0, tiled=True)  7.87 us
    ppermute x1, starting transfers between devices, local(): coarse_below = lax.ppermute(fwd, 'yz', shift_up)  7.04 us
    unnamed x50, local copies, waits for them, and re-layouts  6.91 us
  transfers between devices with their start and end apart: 14, of which 10 were waited for; matrix products, arithmetic and copies ran while one was open for 5% of the time, Pallas kernels for 0%

profile of v5, /device:TPU:2, one launch (start us, length us, event | category | flops | bytes accessed | tf_op | source)
XLA Modules:
  0.0 185.4 jit_solution(5663534919213523834)
XLA Ops:
  0.6 2.6 %slots.1 = f32[16,40,128]{2,1,0:T(8,128)} custom-call(f32[512,128]{1,0:T(8,128)} %bitcast.75, f32[8,128]{1,0:T(8,128)} %bitcast.86, s32[48,128]{1,0:T(8,128)} %bitcast.84, s32[48,128]{1,0:T(8,128)} %bitcast.85), custom_call_target="tpu_custom_call" | custom-call | flops 1000000 | bytes 1000000 | tf_op jit(solution)/shard_map/slots/pallas_call | solution.py:1019
  3.2 9.2 %all-to-all-start = ((f32[16,40,128]{2,1,0:T(8,128)}), f32[16,40,128]{2,1,0:T(8,128)S(1)}, u32[]{:S(2)}, u32[]{:S(2)}) async-start(f32[16,40,128]{2,1,0:T(8,128)} %slots.1), calls=%async_computation | async-start | bytes 655360 | tf_op jit(solution)/shard_map/all_to_all | solution.py:1029
  20.1 3.7 %all-to-all-done.own = f32[16,40,128]{2,1,0:T(8,128)S(1)} async-done(((f32[16,40,128]{2,1,0:T(8,128)}), f32[16,40,128]{2,1,0:T(8,128)S(1)}, u32[]{:S(2)}, u32[]{:S(2)}) %all-to-all-start) | async-done | bytes 327712 | tf_op jit(solution)/shard_map/all_to_all | solution.py:1029
  23.8 2.4 %collective-permute-start.1 = (f32[16,24,128]{2,1,0:T(8,128)S(1)}, f32[16,24,128]{2,1,0:T(8,128)S(1)}, u32[]{:S(2)}, u32[]{:S(2)}) collective-permute-start(f32[16,24,128]{2,1,0:T(8,128)S(1)} %get-tuple-element.66), channel_id=1, source_target_pairs={{64,0},{128,64},{192,128},{256,192},{320,256},{384,320},{448,384},... | collective-permute-start | bytes 589832 | tf_op jit(solution)/shard_map/ppermute | solution.py:1031
  26.2 3.5 %collective-permute-start = (f32[16,24,128]{2,1,0:T(8,128)S(1)}, f32[16,24,128]{2,1,0:T(8,128)S(1)}, u32[]{:S(2)}, u32[]{:S(2)}) collective-permute-start(f32[16,24,128]{2,1,0:T(8,128)S(1)} %get-tuple-element.67), channel_id=1, source_target_pairs={{0,64},{64,128},{128,192},{192,256},{256,320},{320,384},{384,448},... | collective-permute-start | bytes 589832 | tf_op jit(solution)/shard_map/ppermute | solution.py:1030
  31.4 2.4 %collective-permute-done.dn = f32[16,24,128]{2,1,0:T(8,128)S(1)} collective-permute-done((f32[16,24,128]{2,1,0:T(8,128)S(1)}, f32[16,24,128]{2,1,0:T(8,128)S(1)}, u32[]{:S(2)}, u32[]{:S(2)}) %collective-permute-start) | collective-permute-done | bytes 196640 | tf_op jit(solution)/shard_map/ppermute | solution.py:1030
  39.3 2.8 %collective-permute-done.3.above = f32[768,128]{1,0:T(8,128)S(1)} collective-permute-done((f32[768,128]{1,0:T(8,128)S(1)}, f32[768,128]{1,0:T(8,128)S(1)}, u32[]{:S(2)}, u32[]{:S(2)}) %collective-permute-start.3) | collective-permute-done | bytes 393248 | tf_op jit(solution)/shard_map/ppermute | solution.py:1040
  42.1 6.8 %fine_pre.1 = (f32[8,64,128]{2,1,0:T(8,128)S(1)}, f32[64,4096]{1,0:T(8,128)S(1)}, f32[8,4096]{1,0:T(8,128)S(1)}, f32[128,1024]{1,0:T(8,128)S(1)}, f32[384,128]{1,0:T(8,128)S(1)}, /*index=5*/f32[384,128]{1,0:T(8,128)S(1)}) custom-call(s32[2]{0:T(128)S(1)} %pad_add_fusion.pos, f32[16,64,128]{2,1,0:T(8,128)S(1)} %get-tuple-element.33.rows_in, ...), custom_call_target="tpu_custom_call" | custom-call | flops 1000000 | bytes 1000000 | tf_op jit(solution)/shard_map/fine_pre/pallas_call | solution.py:1043
  49.6 3.0 %collective-permute-start.5 = (f32[384,128]{1,0:T(8,128)S(1)}, f32[384,128]{1,0:T(8,128)S(1)}, u32[]{:S(2)}, u32[]{:S(2)}) collective-permute-start(f32[384,128]{1,0:T(8,128)S(1)} %get-tuple-element.37), channel_id=1, source_target_pairs={{64,0},{128,64},{192,128},{256,192},{320,256},{384,320},{448,384},... | collective-permute-start | bytes 589832 | tf_op jit(solution)/shard_map/ppermute | solution.py:1069
  52.6 2.9 %collective-permute-start.4 = (f32[384,128]{1,0:T(8,128)S(1)}, f32[384,128]{1,0:T(8,128)S(1)}, u32[]{:S(2)}, u32[]{:S(2)}) collective-permute-start(f32[384,128]{1,0:T(8,128)S(1)} %get-tuple-element.36.own), channel_id=1, source_target_pairs={{0,64},{64,128},{128,192},{192,256},{256,320},{320,384},{384,448},... | collective-permute-start | bytes 589832 | tf_op jit(solution)/shard_map/ppermute | solution.py:1068
  57.2 3.0 %collective-permute-done.4.dn = f32[384,128]{1,0:T(8,128)S(1)} collective-permute-done((f32[384,128]{1,0:T(8,128)S(1)}, f32[384,128]{1,0:T(8,128)S(1)}, u32[]{:S(2)}, u32[]{:S(2)}) %collective-permute-start.4) | collective-permute-done | bytes 196640 | tf_op jit(solution)/shard_map/ppermute | solution.py:1068
  62.2 6.5 %collective-permute-start.6 = (f32[896,128]{1,0:T(8,128)S(1)}, f32[896,128]{1,0:T(8,128)S(1)}, u32[]{:S(2)}, u32[]{:S(2)}) collective-permute-start(f32[896,128]{1,0:T(8,128)S(1)} %get-tuple-element.40), channel_id=1, source_target_pairs={{0,2},{2,4},{4,6},{6,8},{8,10},{10,12},{12,14},{14,16},{16,18},{18... | collective-permute-start | bytes 1376264 | tf_op jit(solution)/shard_map/ppermute | solution.py:1076
  73.8 3.7 %mid_pre.1 = (f32[8,16,768]{2,1,0:T(8,128)S(1)}, f32[8,16,768]{2,1,0:T(8,128)S(1)}, f32[5,16,1024]{2,1,0:T(8,128)S(1)}, f32[2,16,768]{2,1,0:T(8,128)S(1)}, f32[2,16,768]{2,1,0:T(8,128)S(1)}) custom-call(s32[2]{0:T(128)S(1)} %pad_add_fusion.pos, f32[144]{0:T(256)S(1)} %concatenate.42.scal, f32[128,256]{1,0:T(8,128)S(1)} %get-tuple-element.39.slab, ...), custom_call_target="tpu_custom_call" | custom-call | flops 1000000 | bytes 1000000 | tf_op jit(solution)/shard_map/mid_pre/pallas_call | solution.py:1085
  79.0 2.9 %collective-permute-start.8 = (f32[2,16,768]{2,1,0:T(8,128)S(1)}, f32[2,16,768]{2,1,0:T(8,128)S(1)}, u32[]{:S(2)}, u32[]{:S(2)}) collective-permute-start(f32[2,16,768]{2,1,0:T(8,128)S(1)} %get-tuple-element.44), channel_id=1, source_target_pairs={{0,64},{64,128},{128,192},{192,256},{256,320},{320,384},{384,448},... | collective-permute-start | bytes 294920 | tf_op jit(solution)/shard_map/ppermute | solution.py:1094
  81.9 3.0 %collective-permute-start.9 = (f32[2,16,768]{2,1,0:T(8,128)S(1)}, f32[2,16,768]{2,1,0:T(8,128)S(1)}, u32[]{:S(2)}, u32[]{:S(2)}) collective-permute-start(f32[2,16,768]{2,1,0:T(8,128)S(1)} %get-tuple-element.45), channel_id=1, source_target_pairs={{64,0},{128,64},{192,128},{256,192},{320,256},{384,320},{448,384},... | collective-permute-start | bytes 294920 | tf_op jit(solution)/shard_map/ppermute | solution.py:1095
  85.5 2.9 %collective-permute-done.9.up = f32[2,16,768]{2,1,0:T(8,128)S(1)} collective-permute-done((f32[2,16,768]{2,1,0:T(8,128)S(1)}, f32[2,16,768]{2,1,0:T(8,128)S(1)}, u32[]{:S(2)}, u32[]{:S(2)}) %collective-permute-start.9) | collective-permute-done | bytes 98336 | tf_op jit(solution)/shard_map/ppermute | solution.py:1095
  89.1 7.0 %collective-permute-start.10 = (f32[5,16,512]{2,1,0:T(8,128)S(1)}, f32[5,16,512]{2,1,0:T(8,128)S(1)}, u32[]{:S(2)}, u32[]{:S(2)}) collective-permute-start(f32[5,16,512]{2,1,0:T(8,128)S(1)} %get-tuple-element.47), channel_id=1, source_target_pairs={{0,2},{2,4},{4,6},{6,8},{8,10},{10,12},{12,14},{14,16},{16,18},{18... | collective-permute-start | bytes 491528 | tf_op jit(solution)/shard_map/ppermute | solution.py:1102
  97.5 2.7 %collective-permute-done.11.above = f32[5,16,512]{2,1,0:T(8,128)S(1)} collective-permute-done((f32[5,16,512]{2,1,0:T(8,128)S(1)}, f32[5,16,512]{2,1,0:T(8,128)S(1)}, u32[]{:S(2)}, u32[]{:S(2)}) %collective-permute-start.11) | collective-permute-done | bytes 163872 | tf_op jit(solution)/shard_map/ppermute | solution.py:1103
  100.2 3.5 %krylov.1 = (f32[8,16,768]{2,1,0:T(8,128)S(1)}, f32[16,128]{1,0:T(8,128)S(1)}) custom-call(f32[144]{0:T(256)S(1)} %concatenate.42.scal, f32[5,16,1280]{2,1,0:T(8,128)S(1)} %get-tuple-element.46.own, f32[5,16,512]{2,1,0:T(8,128)S(1)} %collective-permute-done.10.below, f32[5,16,512]{2,1,0:T(8,128)S(1)} %collective-permute-done.11.above), custom_call_target="tpu_custom_call" | custom-call | flops 1000000 | bytes 1000000 | tf_op jit(solution)/shard_map/krylov/pallas_call | solution.py:1104
  104.4 23.8 %all_to_all.32 = f32[16,1,128]{2,1,0:T(1,128)S(1)} all-to-all(f32[16,1,128]{2,1,0:T(1,128)S(1)} %bitcast.73), channel_id=1, replica_groups=mesh['gx'=16,'yz'=16,'lvl'=2] {'yz'}, dimensions={0} | all-to-all | bytes 16384 | tf_op jit(solution)/shard_map/all_to_all | solution.py:1114
  129.0 11.6 %all-to-all-start.2 = ((f32[32,1,128]{2,1,0:T(1,128)}), f32[32,1,128]{2,1,0:T(1,128)S(1)}, u32[]{:S(2)}, u32[]{:S(2)}) async-start(f32[32,1,128]{2,1,0:T(1,128)} %bitcast.35), calls=%async_computation.2 | async-start | bytes 32768 | tf_op jit(solution)/shard_map/all_to_all | solution.py:1116
  141.3 7.9 %all-to-all-done.2 = f32[32,1,128]{2,1,0:T(1,128)S(1)} async-done(((f32[32,1,128]{2,1,0:T(1,128)}), f32[32,1,128]{2,1,0:T(1,128)S(1)}, u32[]{:S(2)}, u32[]{:S(2)}) %all-to-all-start.2) | async-done | bytes 16416 | tf_op jit(solution)/shard_map/all_to_all | solution.py:1116
  149.7 14.1 %post.1 = f32[16,64,128]{2,1,0:T(8,128)} custom-call(s32[2]{0:T(128)} %copy-done.17, f32[144]{0:T(256)} %copy-done.16, f32[32,128]{1,0:T(8,128)} %bitcast.82, f32[8,16,768]{2,1,0:T(8,128)} %copy-done.8, f32[128,1024]{1,0:T(8,128)} %copy-done, f32[8,16,768]{2,1,0:T(8,128)} %copy-done.6, f32[8,16,768]{2,1,0:T(8,128)} %copy-done.7, f32[8,64,128]{2,1,0:T(8,128)} %copy-done.11, ...), custom_call_target="tpu_custom_call" | custom-call | flops 1000000 | bytes 1000000 | tf_op jit(solution)/shard_map/post/pallas_call | solution.py:1117
  163.8 20.1 %all_to_all.33.got = f32[16,64,128]{2,1,0:T(8,128)S(1)} all-to-all(f32[16,64,128]{2,1,0:T(8,128)} %post.1), channel_id=1, replica_groups=mesh['gx'=16,'yz'=16,'lvl'=2] {'gx'}, dimensions={0} | all-to-all | bytes 1048576 | tf_op jit(solution)/shard_map/all_to_all | solution.py:1140
  (119 shorter events, 30.6 us)
Async XLA Ops:
  3.2 20.6 %all-to-all-start = ((f32[16,40,128]{2,1,0:T(8,128)}), f32[16,40,128]{2,1,0:T(8,128)S(1)}, u32[]{:S(2)}, u32[]{:S(2)}) async-start(f32[16,40,128]{2,1,0:T(8,128)} %slots.1), calls=%async_computation | async-start | bytes 655360 | tf_op jit(solution)/shard_map/all_to_all | solution.py:1029
  18.3 23.8 %copy-start.12 = (bf16[64,80]{1,0:T(8,128)(2,1)}, bf16[64,80]{1,0:T(8,128)(2,1)S(1)}, u32[]{:S(2)}) copy-start(bf16[64,80]{1,0:T(8,128)(2,1)S(1)} %pad_maximum_fusion.2.diag_w) | copy-start | bytes 30724
  19.1 14.6 %copy-start.9 = (bf16[384,512]{1,0:T(8,128)(2,1)S(1)}, bf16[384,512]{1,0:T(8,128)(2,1)}, u32[]{:S(2)}) copy-start(bf16[384,512]{1,0:T(8,128)(2,1)} %constant.103.clone.place_kinds) | copy-start | bytes 1179652
  19.2 14.6 %copy-start.5 = (bf16[512,512]{1,0:T(8,128)(2,1)S(1)}, bf16[512,512]{1,0:T(8,128)(2,1)}, u32[]{:S(2)}) copy-start(bf16[512,512]{1,0:T(8,128)(2,1)} %constant.102.clone.place_values) | copy-start | bytes 1572868
  23.8 7.6 %collective-permute-start.1 = (f32[16,24,128]{2,1,0:T(8,128)S(1)}, f32[16,24,128]{2,1,0:T(8,128)S(1)}, u32[]{:S(2)}, u32[]{:S(2)}) collective-permute-start(f32[16,24,128]{2,1,0:T(8,128)S(1)} %get-tuple-element.66), channel_id=1, source_target_pairs={{64,0},{128,64},{192,128},{256,192},{320,256},{384,320},{448,384},... | collective-permute-start | bytes 589832 | tf_op jit(solution)/shard_map/ppermute | solution.py:1031
  26.2 7.6 %collective-permute-start = (f32[16,24,128]{2,1,0:T(8,128)S(1)}, f32[16,24,128]{2,1,0:T(8,128)S(1)}, u32[]{:S(2)}, u32[]{:S(2)}) collective-permute-start(f32[16,24,128]{2,1,0:T(8,128)S(1)} %get-tuple-element.67), channel_id=1, source_target_pairs={{0,64},{64,128},{128,192},{192,256},{256,320},{320,384},{384,448},... | collective-permute-start | bytes 589832 | tf_op jit(solution)/shard_map/ppermute | solution.py:1030
  34.6 7.5 %collective-permute-start.2 = (f32[896,128]{1,0:T(8,128)S(1)}, f32[896,128]{1,0:T(8,128)S(1)}, u32[]{:S(2)}, u32[]{:S(2)}) collective-permute-start(f32[896,128]{1,0:T(8,128)S(1)} %get-tuple-element.34.own), channel_id=1, source_target_pairs={{0,2},{2,4},{4,6},{6,8},{8,10},{10,12},{12,14},{14,16},{16,18},{18... | collective-permute-start | bytes 1376264 | tf_op jit(solution)/shard_map/ppermute | solution.py:1039
  36.0 6.1 %collective-permute-start.3 = (f32[768,128]{1,0:T(8,128)S(1)}, f32[768,128]{1,0:T(8,128)S(1)}, u32[]{:S(2)}, u32[]{:S(2)}) collective-permute-start(f32[768,128]{1,0:T(8,128)S(1)} %get-tuple-element.35), channel_id=1, source_target_pairs={{2,0},{4,2},{6,4},{8,6},{10,8},{12,10},{14,12},{16,14},{18,16},{20... | collective-permute-start | bytes 1179656 | tf_op jit(solution)/shard_map/ppermute | solution.py:1040
  37.4 36.4 %copy-start.17 = (s32[2]{0:T(128)}, s32[2]{0:T(128)S(1)}, u32[]{:S(2)}) copy-start(s32[2]{0:T(128)S(1)} %pad_add_fusion.pos) | copy-start | bytes 28
  39.2 9.7 %copy-start.1 = (bf16[448,192]{1,0:T(8,128)(2,1)}, bf16[448,192]{1,0:T(8,128)(2,1)S(1)}, u32[]{:S(2)}) copy-start(bf16[448,192]{1,0:T(8,128)(2,1)S(1)} %pad_maximum_fusion.1.wide) | copy-start | bytes 516100
  49.6 11.7 %copy-start.11 = (f32[8,64,128]{2,1,0:T(8,128)}, f32[8,64,128]{2,1,0:T(8,128)S(1)}, u32[]{:S(2)}) copy-start(f32[8,64,128]{2,1,0:T(8,128)S(1)} %get-tuple-element.53.keep) | copy-start | bytes 786436
  49.6 24.2 %copy-start = (f32[128,1024]{1,0:T(8,128)}, f32[128,1024]{1,0:T(8,128)S(1)}, u32[]{:S(2)}) copy-start(f32[128,1024]{1,0:T(8,128)S(1)} %get-tuple-element.42.cfm) | copy-start | bytes 1572868
  49.6 7.6 %collective-permute-start.5 = (f32[384,128]{1,0:T(8,128)S(1)}, f32[384,128]{1,0:T(8,128)S(1)}, u32[]{:S(2)}, u32[]{:S(2)}) collective-permute-start(f32[384,128]{1,0:T(8,128)S(1)} %get-tuple-element.37), channel_id=1, source_target_pairs={{64,0},{128,64},{192,128},{256,192},{320,256},{384,320},{448,384},... | collective-permute-start | bytes 589832 | tf_op jit(solution)/shard_map/ppermute | solution.py:1069
  52.6 7.6 %collective-permute-start.4 = (f32[384,128]{1,0:T(8,128)S(1)}, f32[384,128]{1,0:T(8,128)S(1)}, u32[]{:S(2)}, u32[]{:S(2)}) collective-permute-start(f32[384,128]{1,0:T(8,128)S(1)} %get-tuple-element.36.own), channel_id=1, source_target_pairs={{0,64},{64,128},{128,192},{192,256},{256,320},{320,384},{384,448},... | collective-permute-start | bytes 589832 | tf_op jit(solution)/shard_map/ppermute | solution.py:1068
  62.2 11.6 %collective-permute-start.6 = (f32[896,128]{1,0:T(8,128)S(1)}, f32[896,128]{1,0:T(8,128)S(1)}, u32[]{:S(2)}, u32[]{:S(2)}) collective-permute-start(f32[896,128]{1,0:T(8,128)S(1)} %get-tuple-element.40), channel_id=1, source_target_pairs={{0,2},{2,4},{4,6},{6,8},{8,10},{10,12},{12,14},{14,16},{16,18},{18... | collective-permute-start | bytes 1376264 | tf_op jit(solution)/shard_map/ppermute | solution.py:1076
  68.7 5.1 %collective-permute-start.7 = (f32[896,128]{1,0:T(8,128)S(1)}, f32[896,128]{1,0:T(8,128)S(1)}, u32[]{:S(2)}, u32[]{:S(2)}) collective-permute-start(f32[896,128]{1,0:T(8,128)S(1)} %get-tuple-element.41), channel_id=1, source_target_pairs={{2,0},{4,2},{6,4},{8,6},{10,8},{12,10},{14,12},{16,14},{18,16},{20... | collective-permute-start | bytes 1376264 | tf_op jit(solution)/shard_map/ppermute | solution.py:1077
  73.8 26.5 %copy-start.16 = (f32[144]{0:T(256)}, f32[144]{0:T(256)S(1)}, u32[]{:S(2)}) copy-start(f32[144]{0:T(256)S(1)} %concatenate.42.scal) | copy-start | bytes 1732
  73.8 3.8 %copy-start.2 = (f32[896,128]{1,0:T(8,128)}, f32[896,128]{1,0:T(8,128)S(1)}, u32[]{:S(2)}) copy-start(f32[896,128]{1,0:T(8,128)S(1)} %collective-permute-done.6.below) | copy-start | bytes 1376260
  73.8 3.7 %copy-start.3 = (f32[896,128]{1,0:T(8,128)}, f32[896,128]{1,0:T(8,128)S(1)}, u32[]{:S(2)}) copy-start(f32[896,128]{1,0:T(8,128)S(1)} %collective-permute-done.7.above) | copy-start | bytes 1376260
  79.0 6.5 %collective-permute-start.8 = (f32[2,16,768]{2,1,0:T(8,128)S(1)}, f32[2,16,768]{2,1,0:T(8,128)S(1)}, u32[]{:S(2)}, u32[]{:S(2)}) collective-permute-start(f32[2,16,768]{2,1,0:T(8,128)S(1)} %get-tuple-element.44), channel_id=1, source_target_pairs={{0,64},{64,128},{128,192},{192,256},{256,320},{320,384},{384,448},... | collective-permute-start | bytes 294920 | tf_op jit(solution)/shard_map/ppermute | solution.py:1094
  81.9 6.5 %collective-permute-start.9 = (f32[2,16,768]{2,1,0:T(8,128)S(1)}, f32[2,16,768]{2,1,0:T(8,128)S(1)}, u32[]{:S(2)}, u32[]{:S(2)}) collective-permute-start(f32[2,16,768]{2,1,0:T(8,128)S(1)} %get-tuple-element.45), channel_id=1, source_target_pairs={{64,0},{128,64},{192,128},{256,192},{320,256},{384,320},{448,384},... | collective-permute-start | bytes 294920 | tf_op jit(solution)/shard_map/ppermute | solution.py:1095
  89.1 8.4 %collective-permute-start.10 = (f32[5,16,512]{2,1,0:T(8,128)S(1)}, f32[5,16,512]{2,1,0:T(8,128)S(1)}, u32[]{:S(2)}, u32[]{:S(2)}) collective-permute-start(f32[5,16,512]{2,1,0:T(8,128)S(1)} %get-tuple-element.47), channel_id=1, source_target_pairs={{0,2},{2,4},{4,6},{6,8},{8,10},{10,12},{12,14},{14,16},{16,18},{18... | collective-permute-start | bytes 491528 | tf_op jit(solution)/shard_map/ppermute | solution.py:1102
  96.2 4.1 %collective-permute-start.11 = (f32[5,16,512]{2,1,0:T(8,128)S(1)}, f32[5,16,512]{2,1,0:T(8,128)S(1)}, u32[]{:S(2)}, u32[]{:S(2)}) collective-permute-start(f32[5,16,512]{2,1,0:T(8,128)S(1)} %get-tuple-element.48), channel_id=1, source_target_pairs={{2,0},{4,2},{6,4},{8,6},{10,8},{12,10},{14,12},{16,14},{18,16},{20... | collective-permute-start | bytes 491528 | tf_op jit(solution)/shard_map/ppermute | solution.py:1103
  129.0 20.2 %all-to-all-start.2 = ((f32[32,1,128]{2,1,0:T(1,128)}), f32[32,1,128]{2,1,0:T(1,128)S(1)}, u32[]{:S(2)}, u32[]{:S(2)}) async-start(f32[32,1,128]{2,1,0:T(1,128)} %bitcast.35), calls=%async_computation.2 | async-start | bytes 32768 | tf_op jit(solution)/shard_map/all_to_all | solution.py:1116
  (15 other events, 17.9 us)

commit v6 on v5

--- a/solution.py
+++ b/solution.py
@@ -59,6 +59,27 @@
         cost_estimate=pl.CostEstimate(flops=1000000, bytes_accessed=1000000, transcendentals=0),
         name=name,
     )
+
+
+def even(pos):
+    return pos[0] % 2 == 0
+
+
+def put(pos, first, second, at, fwd, bwd):
+    if fwd is None:
+        fwd = bwd
+    if bwd is None:
+        bwd = fwd
+    first[at] = jnp.where(even(pos), fwd, bwd)
+    second[at] = jnp.where(even(pos), bwd, fwd)
+
+
+def from_below(pos, first, second, at):
+    return jnp.where(even(pos), second[at], first[at])
+
+
+def from_above(pos, first, second, at):
+    return jnp.where(even(pos), first[at], second[at])
 
 
 def f32s(*shape):
@@ -157,7 +178,7 @@
     return out[0:count] + out[count : 2 * count] + out[2 * count :]
 
 
-def join_body(own, dn, up, place_values, place_kinds, rows, fwd, bwd):
+def join_body(pos, own, dn, up, place_values, place_kinds, rows, first, second):
     parts = (own[:, 0:16, :], own[:, 24:40, :], up[:, 0:16, :], dn[:, 8:24, :])
     values = jnp.concatenate([v.reshape(256, 128) for v in parts], axis=1)
     out = moved(values, place_values[...])
@@ -166,19 +187,25 @@
             rows[x, 16 * n : 16 * n + 16, :] = out[16 * x : 16 * x + 16, 128 * n : 128 * n + 128]
     low = lanes((64, 128)) < 64
     for x in range(8):
-        fwd[64 * x : 64 * x + 64, :] = jnp.where(low, roll(rows[x], 64), rows[x + 8])
-        bwd[64 * x : 64 * x + 64, :] = jnp.where(low, rows[x], roll(rows[x + 8], 64))
+        fwd = jnp.where(low, roll(rows[x], 64), rows[x + 8])
+        bwd = jnp.where(low, rows[x], roll(rows[x + 8], 64))
+        put(pos, first, second, slice(64 * x, 64 * x + 64), fwd, bwd)
     parts = (own[:, 16:24, :], dn[:, 0:8, :], up[:, 16:24, :])
     kinds = jnp.concatenate([v.reshape(128, 128) for v in parts], axis=1)
     out = moved(kinds, place_kinds[...])
     array = lax.broadcasted_iota(jnp.int32, (128, 128), 0) % 8
     edge = (lanes((128, 128)) % 32 == 3) & ((array == 3) | (array == 6))
+    lane = lanes((128, 128))
     for h in range(2):
         minus = out[:, 256 + 128 * h : 384 + 128 * h]
         plus = jnp.where(edge, roll(minus, -1), out[:, 128 * h : 128 * h + 128])
-        fwd[512 + 128 * h : 640 + 128 * h, :] = plus
-        bwd[512 + 128 * h : 640 + 128 * h, :] = plus
-    fwd[768:896, :] = out[:, 256:384]
+        if h == 0:
+            plus = jnp.where((array == 7) & (lane < 32), roll(minus, 5, 0), plus)
+            plus = jnp.where(
+                (array == 7) & (lane >= 32) & (lane < 64), roll(roll(minus, 2, 0), 32), plus
+            )
+        first[512 + 128 * h : 640 + 128 * h, :] = plus
+        second[512 + 128 * h : 640 + 128 * h, :] = plus
 
 
 CHUNK = 4096
@@ -274,8 +301,8 @@
     pos,
     rows_in,
     own,
-    below,
-    above,
+    got_first,
+    got_second,
     wide,
     spread,
     diag_w,
@@ -311,21 +338,22 @@
         first, second = slice(256 * x, 256 * x + 128), slice(256 * x + 128, 256 * x + 256)
         turned = roll(rows_in[x], 64)
         at = 64 * (x % 8)
-        under = below[at : at + 64, :]
-        over = above[at : at + 64, :]
+        under = from_below(pos, got_first, got_second, slice(at, at + 64))
+        over = from_above(pos, got_first, got_second, slice(at, at + 64))
         if x >= 8:
             under = roll(under, 64)
         else:
             over = roll(over, 64)
         r[:, first] = jnp.where(low, under, turned)
         r[:, second] = jnp.where(low, turned, over)
-        blocks = [
-            ref[512 + 128 * h + 8 * x : 520 + 128 * h + 8 * x, :]
-            for ref in (below, own, above)
-            for h in range(2)
-        ]
-        minus = below[768 + 8 * x : 776 + 8 * x, :]
-        gather[pl.ds(x, 8, stride=16), :] = jnp.where(edge, roll(minus, 96), 0.0)
+        places = [slice(512 + 128 * h + 8 * x, 520 + 128 * h + 8 * x) for h in range(2)]
+        blocks = (
+            [from_below(pos, got_first, got_second, p) for p in places]
+            + [own[p] for p in places]
+            + [from_above(pos, got_first, got_second, p) for p in places]
+        )
+        minus = jnp.where(array == 2, roll(roll(blocks[0], 3, 0), 96), roll(roll(blocks[0], 6, 0), 64))
+        gather[pl.ds(x, 8, stride=16), :] = jnp.where(edge, minus, 0.0)
         for m in range(6):
             gather[pl.ds(128 * (m + 1) + x, 8, stride=16), :] = blocks[m]
         for half, at in enumerate((first, second)):
@@ -386,7 +414,7 @@
         keep[x] = jnp.where(low, a, roll(b, 64))
 
 
-def mid_z_body(own, dn, up, r, slab, fwd, bwd, frz):
+def mid_z_body(pos, own, dn, up, r, slab, first, second, frz):
     low = lanes((64, 128)) < 64
     l16 = lanes((16, 128)) % 16
     for x in range(NX):
@@ -400,9 +428,11 @@
             part = jnp.where(l16 >= 12, roll(pack_up, 12 - 4 * j), part)
             frz[x, rows, :] = part
     for x in range(8):
-        fwd[384 + 64 * x : 448 + 64 * x, :] = jnp.where(low, roll(frz[x], 64), frz[x + 8])
-        bwd[384 + 64 * x : 448 + 64 * x, :] = jnp.where(low, frz[x], roll(frz[x + 8], 64))
+        fwd = jnp.where(low, roll(frz[x], 64), frz[x + 8])
+        bwd = jnp.where(low, frz[x], roll(frz[x + 8], 64))
+        put(pos, first, second, slice(384 + 64 * x, 448 + 64 * x), fwd, bwd)
     lane = lanes((128, 128))
+    tiles = []
     for m in range(4):
         acc = jnp.zeros((128, 128), F32)
         for n in range(4):
@@ -417,10 +447,9 @@
             acc = jnp.where((lane >= to + 20) & (lane < to + 29), roll(up[rows, :], to + 19 - at), acc)
         if 1 <= m <= 2:
             slab[:, 128 * (m - 1) : 128 * m] = acc
-        if m <= 2:
-            fwd[128 * m : 128 * m + 128, :] = acc
-        if m >= 1:
-            bwd[128 * (m - 1) : 128 * m, :] = acc
+        tiles.append(acc)
+    for m in range(3):
+        put(pos, first, second, slice(128 * m, 128 * m + 128), tiles[m], tiles[m + 1])
 
 
 LOWS = ((0, 1, 2, 3), (0, 1, 4, 5), (0, 2, 4, 6))
@@ -517,14 +546,15 @@
 
 
 def mid_pre_body(
-    pos, scal, slab, below, above, cfm, sol_out, r_out, coarse, send_up, send_down,
+    pos, scal, slab, got_first, got_second, cfm, level, coarse, send_up, send_down,
     sel, faces, inv, diag, u, sol, r, jump, flux,
 ):
     for i in range(8):
         rows = slice(16 * i, 16 * i + 16)
         for m in range(3):
-            u[i, :, 128 * m : 128 * m + 128] = below[128 * m + 16 * i : 128 * m + 16 * i + 16, :]
-            u[i, :, 128 * (m + 5) : 128 * (m + 6)] = above[128 * m + 16 * i : 128 * m + 16 * i + 16, :]
+            at = slice(128 * m + 16 * i, 128 * m + 16 * i + 16)
+            u[i, :, 128 * m : 128 * m + 128] = from_below(pos, got_first, got_second, at)
+            u[i, :, 128 * (m + 5) : 128 * (m + 6)] = from_above(pos, got_first, got_second, at)
         u[i, :, 384:640] = slab[rows, :]
     mid_setup(pos, scal, cfm, sel, faces, inv, diag)
     for i in range(8):
@@ -535,8 +565,8 @@
     mid_apply(u, r, scal, cfm, faces, jump, flux)
     mid_step(1, u, r, sol, inv)
     mid_apply(u, r, scal, cfm, faces, jump, flux)
-    sol_out[...] = sol[:, :, 128:896]
-    r_out[...] = r[:, :, 128:896]
+    level[0] = sol[:, :, 128:896]
+    level[1] = r[:, :, 128:896]
     total = r[0]
     for i in range(1, 8):
         total = total + r[i]
@@ -559,7 +589,7 @@
         out[1] = roll(coarse[4, :, 128:896], -first)
 
 
-def coarse_z_body(own, dn, up, slab, fwd, bwd):
+def coarse_z_body(pos, own, dn, up, slab, first, second):
     lane = lanes((16, 128))
     for f in range(5):
         part = 0 if f < 4 else 1
@@ -583,10 +613,10 @@
                     (lane >= to + 42) & (lane < to + 50), roll(right, to + 42 - (at + shift)), acc
                 )
             slab[f, :, 128 * m : 128 * m + 128] = acc
-            if m < 4:
-                fwd[f, :, 128 * m : 128 * m + 128] = acc
-            if m >= 6:
-                bwd[f, :, 128 * (m - 6) : 128 * (m - 5)] = acc
+        for m in range(4):
+            at = (f, slice(None), slice(128 * m, 128 * m + 128))
+            after = (f, slice(None), slice(128 * (m + 6), 128 * (m + 7)))
+            put(pos, first, second, at, slab[at], slab[after])
 
 
 def settle(v, basis, j):
@@ -641,11 +671,11 @@
 PAIRS = sum(9 - i for i in range(BASIS))
 
 
-def krylov_body(scal, own, below, above, basis, gram, field, hold):
+def krylov_body(pos, scal, own, got_first, got_second, basis, gram, field, hold):
     for f in range(5):
-        field[f, :, 0:512] = below[f]
+        field[f, :, 0:512] = from_below(pos, got_first, got_second, f)
         field[f, :, 512:1792] = own[f]
-        field[f, :, 1792:2304] = above[f]
+        field[f, :, 1792:2304] = from_above(pos, got_first, got_second, f)
     center, half = scal[133], scal[134]
     lane8 = lanes((8, 128))
 
@@ -722,7 +752,7 @@
         out[8 * m : 8 * m + 8, :] = row
 
 
-def mid_post(pos, scal, gram, basis, cfm, pre, res, out, sel, faces, inv, u, r, sol, jump, flux):
+def mid_post(pos, scal, gram, basis, cfm, level, out, sel, faces, inv, u, r, sol, jump, flux):
     high, low = summed(gram)
     lane = lanes((8, 128))
     sub = lax.broadcasted_iota(jnp.int32, (8, 128), 0)
@@ -781,8 +811,8 @@
         for ref in (r, sol):
             ref[i, :, 0:128] = ends
             ref[i, :, 896:1024] = ends
-        r[i, :, 128:896] = res[i]
-        sol[i, :, 128:896] = pre[i] + u[i, :, 128:896]
+        r[i, :, 128:896] = level[1, i]
+        sol[i, :, 128:896] = level[0, i] + u[i, :, 128:896]
     mid_apply(u, r, scal, cfm, faces, jump, flux)
     for i in range(8):
         new = inv[i] * r[i] / MIDDLE
@@ -807,7 +837,7 @@
 
 
 def post_body(
-    pos, scal, gram, basis, cfm, mid_pre, mid_res, keep, frz, below, above, coef, wide, spread,
+    pos, scal, gram, basis, cfm, level, keep, frz, got_first, got_second, coef, wide, spread,
     lift, diag_w, diag_e, out,
     sel, faces, mid_inv, mid_u, mid_r, mid_sol, jump, flux, mid, w, inv, u, r, sol, px, qx,
 ):
@@ -817,7 +847,7 @@
         at = slice(CHUNK * c, CHUNK * (c + 1))
         inv[:, at] = fine_inverse(coef, w, diag_w, diag_e, wide_inside, at)
     mid_post(
-        pos, scal, gram, basis, cfm, mid_pre, mid_res, mid, sel, faces, mid_inv, mid_u, mid_r,
+        pos, scal, gram, basis, cfm, level, mid, sel, faces, mid_inv, mid_u, mid_r,
         mid_sol, jump, flux,
     )
     low = lanes((64, 128)) < 64
@@ -827,8 +857,8 @@
         first, second = slice(256 * x, 256 * x + 128), slice(256 * x + 128, 256 * x + 256)
         turned = roll(frz[x], 64)
         at = 384 + 64 * (x % 8)
-        down = below[at : at + 64, :]
-        over = above[at : at + 64, :]
+        down = from_below(pos, got_first, got_second, slice(at, at + 64))
+        over = from_above(pos, got_first, got_second, slice(at, at + 64))
         if x >= 8:
             down = roll(down, 64)
         else:
@@ -998,8 +1028,8 @@
 
 
 def local(residual, coefficient, element, faces, kind, flag):
-    shift_up = [(i, i + 1) for i in range(15)]
-    shift_dn = [(i + 1, i) for i in range(15)]
+    y_first = [(i, i ^ 1) for i in range(16)]
+    y_second = [p for i in range(1, 15, 2) for p in ((i, i + 1), (i + 1, i))]
 
     def z_index(zb):
         return ORDER[zb % 16] * 2 + zb // 16
@@ -1030,14 +1060,14 @@
     dn = lax.ppermute(own[:, 16:40], z_axes, z_up)
     up = lax.ppermute(own[:, 0:24], z_axes, z_dn)
     place_values, place_kinds, pack = place_tables()
-    rows, own, bwd = call(
+    rows, own, other = call(
         join_body,
         "join",
-        [f32s(NX, 64, 128), f32s(896, 128), f32s(768, 128)],
-        (0,) * 5,
-    )(own, dn, up, place_values, place_kinds)
-    below = lax.ppermute(own, "yz", shift_up)
-    above = lax.ppermute(bwd, "yz", shift_dn)
+        [f32s(NX, 64, 128), f32s(768, 128), f32s(768, 128)],
+        (1,) + (0,) * 5,
+    )(pos, own, dn, up, place_values, place_kinds)
+    got_first = lax.ppermute(own, "yz", y_first)
+    got_second = lax.ppermute(other, "yz", y_second)
     plane = (64, NX * 256)
     strip = (16, NX * 256 + 256)
     keep, r, coef, cfm, send_up, send_down = call(
@@ -1063,18 +1093,18 @@
             pltpu.VMEM((256, 128), F32),
         ],
     )(
-        pos, rows, own, below, above, wide, spread, diag_w, diag_e, down, mid_diag_w, mid_diag_e, pack
+        pos, rows, own, got_first, got_second, wide, spread, diag_w, diag_e, down, mid_diag_w, mid_diag_e, pack
     )
     dn = lax.ppermute(send_up, z_axes, z_up)
     up = lax.ppermute(send_down, z_axes, z_dn)
-    slab, fwd, bwd, frz = call(
+    slab, first, second, frz = call(
         mid_z_body,
         "mid_z",
         [f32s(128, 256), f32s(896, 128), f32s(896, 128), f32s(NX, 64, 128)],
-        (0,) * 4,
-    )(send_up, dn, up, r)
-    below = lax.ppermute(fwd, "yz", shift_up)
-    above = lax.ppermute(bwd, "yz", shift_dn)
+        (1,) + (0,) * 4,
+    )(pos, send_up, dn, up, r)
+    got_first = lax.ppermute(first, "yz", y_first)
+    got_second = lax.ppermute(second, "yz", y_second)
     mid = (8, 16, 1024)
     mid_scratch = [
         pltpu.VMEM((3, 16, 1024), F32),
@@ -1082,35 +1112,35 @@
         pltpu.VMEM(mid, F32),
     ]
     tail_scratch = [pltpu.VMEM((4, 16, 1024), F32), pltpu.VMEM((12, 16, 1024), F32)]
-    mid_pre, mid_res, coarse, send_up, send_down = call(
+    level, coarse, send_up, send_down = call(
         mid_pre_body,
         "mid_pre",
-        [f32s(8, 16, 768), f32s(8, 16, 768), f32s(5, 16, 1024), f32s(2, 16, 768), f32s(2, 16, 768)],
+        [f32s(2, 8, 16, 768), f32s(5, 16, 1024), f32s(2, 16, 768), f32s(2, 16, 768)],
         (1, 1, 0, 0, 0, 0),
         mid_scratch
         + [pltpu.VMEM(mid, F32)] * 4
         + tail_scratch,
-    )(pos, scal, slab, below, above, cfm)
+    )(pos, scal, slab, got_first, got_second, cfm)
     dn = lax.ppermute(send_up, z_axes, z_up)
     up = lax.ppermute(send_down, z_axes, z_dn)
-    coarse_slab, fwd, bwd = call(
+    coarse_slab, first, second = call(
         coarse_z_body,
         "coarse_z",
         [f32s(5, 16, 1280), f32s(5, 16, 512), f32s(5, 16, 512)],
-        (0, 0, 0),
-    )(coarse, dn, up)
-    coarse_below = lax.ppermute(fwd, "yz", shift_up)
-    coarse_above = lax.ppermute(bwd, "yz", shift_dn)
+        (1, 0, 0, 0),
+    )(pos, coarse, dn, up)
+    coarse_first = lax.ppermute(first, "yz", y_first)
+    coarse_second = lax.ppermute(second, "yz", y_second)
     basis, gram = call(
         krylov_body,
         "krylov",
         [f32s(BASIS, 16, 768), f32s(16, 128)],
-        (1, 0, 0, 0),
+        (1, 1, 0, 0, 0),
         [
             pltpu.VMEM((5, 16, 2304), F32),
             pltpu.VMEM((2 * BASIS, 8, 128), F32),
         ],
-    )(scal, coarse_slab, coarse_below, coarse_above)
+    )(pos, scal, coarse_slab, coarse_first, coarse_second)
     gram = lax.all_to_all(gram, "yz", 0, 0, tiled=True)
     gram = call(gram_body, "gram", [f32s(32, 128)], (0,))(gram)[0]
     gram = lax.all_to_all(gram, z_axes, 0, 0, tiled=True)
@@ -1118,7 +1148,7 @@
         post_body,
         "post",
         [f32s(16, 64, 128)],
-        (1, 1) + (0,) * 15,
+        (1, 1) + (0,) * 14,
         mid_scratch
         + [pltpu.VMEM(mid, F32)] * 3
         + tail_scratch
@@ -1134,7 +1164,7 @@
         ],
         limit=LARGE_LIMIT,
     )(
-        pos, scal, gram, basis, cfm, mid_pre, mid_res, keep, frz, below, above, coef, wide, spread,
+        pos, scal, gram, basis, cfm, level, keep, frz, got_first, got_second, coef, wide, spread,
         lift, diag_w, diag_e,
     )[0]
     got = lax.all_to_all(packed, "gx", 0, 0, tiled=True)

time: 187 us -> 184 us (0.984)
  waiting for transfers between devices: 29.4 us -> 25.8 us
  starting transfers between devices: 57.3 us -> 54.5 us
  blocking collectives: 43.9 us -> 46 us
  Pallas kernels: 35.6 us -> 37.5 us
    ppermute x6, waiting for transfers between devices: 5.54 us -> 0.34 us  [the longest x1 0.33 us: local(): coarse_first = lax.ppermute(first, 'yz', y_first)]
    ppermute x6, starting transfers between devices: 18.9 us -> 16.3 us  [the longest x1 6.63 us: local(): coarse_first = lax.ppermute(first, 'yz', y_first)]
    all_to_all x1, blocking collectives: 23.8 us -> 25.9 us  [local(): gram = lax.all_to_all(gram, 'yz', 0, 0, tiled=True)]
    ppermute x2, waiting for transfers between devices: 4.58 us -> 6.66 us  [local(): up = lax.ppermute(send_down, z_axes, z_dn)]
    unnamed x50 -> x48, local copies, waits for them, and re-layouts: 6.91 us -> 6.9 us
  transfers between devices with their start and end apart: 14 -> 14, of which waited for: 10 -> 9; matrix products, arithmetic and copies ran while one was open for 5% -> 5% of each run, Pallas kernels for 0% -> 0%
where the time goes in v6:
time: 184 us; the launch traced here: 183 us
  starting transfers between devices  54.5 us (30%)
  blocking collectives  46 us (25%)
  Pallas kernels  37.5 us (20%)
  waiting for transfers between devices  25.8 us (14%)
  local copies, waits for them, and re-layouts  11.9 us (6%)
  between operations  3.17 us (2%)
  matrix products  2.31 us (1%)
  other arithmetic  2.02 us (1%)
    all_to_all x1, blocking collectives, local(): gram = lax.all_to_all(gram, 'yz', 0, 0, tiled=True)  25.9 us
    all_to_all x1, blocking collectives, local(): got = lax.all_to_all(packed, 'gx', 0, 0, tiled=True)  20.1 us
    pallas_call x1, Pallas kernels, local(): call(post_body, 'post', [f32s(16, 64, 128)], (1, 1) + (0,) * 14, mid_scra...  14.1 us
    all_to_all x1, starting transfers between devices, local(): gram = lax.all_to_all(gram, z_axes, 0, 0, tiled=True)  11.4 us
    all_to_all x1, starting transfers between devices, local(): own = lax.all_to_all(slots, 'gx', 0, 0, tiled=True)  9.24 us
    all_to_all x1, waiting for transfers between devices, local(): gram = lax.all_to_all(gram, z_axes, 0, 0, tiled=True)  7.86 us
    pallas_call x1, Pallas kernels, local(): call(fine_pre_body, 'fine_pre', [f32s(8, 64, 128), f32s(*plane), f32s(8,...  7.13 us
    unnamed x48, local copies, waits for them, and re-layouts  6.9 us
  transfers between devices with their start and end apart: 14, of which 9 were waited for; matrix products, arithmetic and copies ran while one was open for 5% of the time, Pallas kernels for 0%

profile of v6, /device:TPU:2, one launch (start us, length us, event | category | flops | bytes accessed | tf_op | source)
XLA Modules:
  0.0 183.2 jit_solution(11240387347406402300)
XLA Ops:
  0.6 2.6 %slots.1 = f32[16,40,128]{2,1,0:T(8,128)} custom-call(f32[512,128]{1,0:T(8,128)} %bitcast.75, f32[8,128]{1,0:T(8,128)} %bitcast.86, s32[48,128]{1,0:T(8,128)} %bitcast.84, s32[48,128]{1,0:T(8,128)} %bitcast.85), custom_call_target="tpu_custom_call" | custom-call | flops 1000000 | bytes 1000000 | tf_op jit(solution)/shard_map/slots/pallas_call | solution.py:1049
  3.2 9.2 %all-to-all-start = ((f32[16,40,128]{2,1,0:T(8,128)}), f32[16,40,128]{2,1,0:T(8,128)S(1)}, u32[]{:S(2)}, u32[]{:S(2)}) async-start(f32[16,40,128]{2,1,0:T(8,128)} %slots.1), calls=%async_computation | async-start | bytes 655360 | tf_op jit(solution)/shard_map/all_to_all | solution.py:1059
  20.3 3.5 %all-to-all-done.own = f32[16,40,128]{2,1,0:T(8,128)S(1)} async-done(((f32[16,40,128]{2,1,0:T(8,128)}), f32[16,40,128]{2,1,0:T(8,128)S(1)}, u32[]{:S(2)}, u32[]{:S(2)}) %all-to-all-start) | async-done | bytes 327712 | tf_op jit(solution)/shard_map/all_to_all | solution.py:1059
  23.8 2.4 %collective-permute-start.1 = (f32[16,24,128]{2,1,0:T(8,128)S(1)}, f32[16,24,128]{2,1,0:T(8,128)S(1)}, u32[]{:S(2)}, u32[]{:S(2)}) collective-permute-start(f32[16,24,128]{2,1,0:T(8,128)S(1)} %get-tuple-element.64), channel_id=1, source_target_pairs={{64,0},{128,64},{192,128},{256,192},{320,256},{384,320},{448,384},... | collective-permute-start | bytes 589832 | tf_op jit(solution)/shard_map/ppermute | solution.py:1061
  26.2 3.5 %collective-permute-start = (f32[16,24,128]{2,1,0:T(8,128)S(1)}, f32[16,24,128]{2,1,0:T(8,128)S(1)}, u32[]{:S(2)}, u32[]{:S(2)}) collective-permute-start(f32[16,24,128]{2,1,0:T(8,128)S(1)} %get-tuple-element.65), channel_id=1, source_target_pairs={{0,64},{64,128},{128,192},{192,256},{256,320},{320,384},{384,448},... | collective-permute-start | bytes 589832 | tf_op jit(solution)/shard_map/ppermute | solution.py:1060
  31.4 2.4 %collective-permute-done.dn = f32[16,24,128]{2,1,0:T(8,128)S(1)} collective-permute-done((f32[16,24,128]{2,1,0:T(8,128)S(1)}, f32[16,24,128]{2,1,0:T(8,128)S(1)}, u32[]{:S(2)}, u32[]{:S(2)}) %collective-permute-start) | collective-permute-done | bytes 196640 | tf_op jit(solution)/shard_map/ppermute | solution.py:1060
  35.9 5.5 %collective-permute-start.2 = (f32[768,128]{1,0:T(8,128)S(1)}, f32[768,128]{1,0:T(8,128)S(1)}, u32[]{:S(2)}, u32[]{:S(2)}) collective-permute-start(f32[768,128]{1,0:T(8,128)S(1)} %get-tuple-element.33.own), channel_id=1, source_target_pairs={{0,2},{2,0},{4,6},{6,4},{8,10},{10,8},{12,14},{14,12},{16,18},{18,... | collective-permute-start | bytes 1179656 | tf_op jit(solution)/shard_map/ppermute | solution.py:1069
  44.1 7.1 %fine_pre.1 = (f32[8,64,128]{2,1,0:T(8,128)S(1)}, f32[64,4096]{1,0:T(8,128)S(1)}, f32[8,4096]{1,0:T(8,128)S(1)}, f32[128,1024]{1,0:T(8,128)S(1)}, f32[384,128]{1,0:T(8,128)S(1)}, /*index=5*/f32[384,128]{1,0:T(8,128)S(1)}) custom-call(s32[2]{0:T(128)S(1)} %pad_add_fusion.pos, f32[16,64,128]{2,1,0:T(8,128)S(1)} %get-tuple-element.32.rows_in, ...), custom_call_target="tpu_custom_call" | custom-call | flops 1000000 | bytes 1000000 | tf_op jit(solution)/shard_map/fine_pre/pallas_call | solution.py:1073
  51.8 3.0 %collective-permute-start.5 = (f32[384,128]{1,0:T(8,128)S(1)}, f32[384,128]{1,0:T(8,128)S(1)}, u32[]{:S(2)}, u32[]{:S(2)}) collective-permute-start(f32[384,128]{1,0:T(8,128)S(1)} %get-tuple-element.36), channel_id=1, source_target_pairs={{64,0},{128,64},{192,128},{256,192},{320,256},{384,320},{448,384},... | collective-permute-start | bytes 589832 | tf_op jit(solution)/shard_map/ppermute | solution.py:1099
  54.8 2.9 %collective-permute-start.4 = (f32[384,128]{1,0:T(8,128)S(1)}, f32[384,128]{1,0:T(8,128)S(1)}, u32[]{:S(2)}, u32[]{:S(2)}) collective-permute-start(f32[384,128]{1,0:T(8,128)S(1)} %get-tuple-element.35.own), channel_id=1, source_target_pairs={{0,64},{64,128},{128,192},{192,256},{256,320},{320,384},{384,448},... | collective-permute-start | bytes 589832 | tf_op jit(solution)/shard_map/ppermute | solution.py:1098
  57.7 3.8 %collective-permute-done.5.up = f32[384,128]{1,0:T(8,128)S(1)} collective-permute-done((f32[384,128]{1,0:T(8,128)S(1)}, f32[384,128]{1,0:T(8,128)S(1)}, u32[]{:S(2)}, u32[]{:S(2)}) %collective-permute-start.5) | collective-permute-done | bytes 196640 | tf_op jit(solution)/shard_map/ppermute | solution.py:1099
  61.5 2.7 %collective-permute-done.4.dn = f32[384,128]{1,0:T(8,128)S(1)} collective-permute-done((f32[384,128]{1,0:T(8,128)S(1)}, f32[384,128]{1,0:T(8,128)S(1)}, u32[]{:S(2)}, u32[]{:S(2)}) %collective-permute-start.4) | collective-permute-done | bytes 196640 | tf_op jit(solution)/shard_map/ppermute | solution.py:1098
  66.7 1.9 %collective-permute-start.6 = (f32[896,128]{1,0:T(8,128)S(1)}, f32[896,128]{1,0:T(8,128)S(1)}, u32[]{:S(2)}, u32[]{:S(2)}) collective-permute-start(f32[896,128]{1,0:T(8,128)S(1)} %get-tuple-element.39), channel_id=1, source_target_pairs={{0,2},{2,0},{4,6},{6,4},{8,10},{10,8},{12,14},{14,12},{16,18},{18,... | collective-permute-start | bytes 1376264 | tf_op jit(solution)/shard_map/ppermute | solution.py:1106
  73.3 3.6 %mid_pre.1 = (f32[2,8,16,768]{3,2,1,0:T(8,128)S(1)}, f32[5,16,1024]{2,1,0:T(8,128)S(1)}, f32[2,16,768]{2,1,0:T(8,128)S(1)}, f32[2,16,768]{2,1,0:T(8,128)S(1)}) custom-call(s32[2]{0:T(128)S(1)} %pad_add_fusion.pos, f32[144]{0:T(256)S(1)} %concatenate.42.scal, f32[128,256]{1,0:T(8,128)S(1)} %get-tuple-element.38.slab, ...), custom_call_target="tpu_custom_call" | custom-call | flops 1000000 | bytes 1000000 | tf_op jit(solution)/shard_map/mid_pre/pallas_call | solution.py:1115
  77.8 2.9 %collective-permute-start.8 = (f32[2,16,768]{2,1,0:T(8,128)S(1)}, f32[2,16,768]{2,1,0:T(8,128)S(1)}, u32[]{:S(2)}, u32[]{:S(2)}) collective-permute-start(f32[2,16,768]{2,1,0:T(8,128)S(1)} %get-tuple-element.43), channel_id=1, source_target_pairs={{0,64},{64,128},{128,192},{192,256},{256,320},{320,384},{384,448},... | collective-permute-start | bytes 294920 | tf_op jit(solution)/shard_map/ppermute | solution.py:1124
  80.7 3.0 %collective-permute-start.9 = (f32[2,16,768]{2,1,0:T(8,128)S(1)}, f32[2,16,768]{2,1,0:T(8,128)S(1)}, u32[]{:S(2)}, u32[]{:S(2)}) collective-permute-start(f32[2,16,768]{2,1,0:T(8,128)S(1)} %get-tuple-element.44), channel_id=1, source_target_pairs={{64,0},{128,64},{192,128},{256,192},{320,256},{384,320},{448,384},... | collective-permute-start | bytes 294920 | tf_op jit(solution)/shard_map/ppermute | solution.py:1125
  84.3 2.9 %collective-permute-done.9.up = f32[2,16,768]{2,1,0:T(8,128)S(1)} collective-permute-done((f32[2,16,768]{2,1,0:T(8,128)S(1)}, f32[2,16,768]{2,1,0:T(8,128)S(1)}, u32[]{:S(2)}, u32[]{:S(2)}) %collective-permute-start.9) | collective-permute-done | bytes 98336 | tf_op jit(solution)/shard_map/ppermute | solution.py:1125
  88.4 6.6 %collective-permute-start.10 = (f32[5,16,512]{2,1,0:T(8,128)S(1)}, f32[5,16,512]{2,1,0:T(8,128)S(1)}, u32[]{:S(2)}, u32[]{:S(2)}) collective-permute-start(f32[5,16,512]{2,1,0:T(8,128)S(1)} %get-tuple-element.46), channel_id=1, source_target_pairs={{0,2},{2,0},{4,6},{6,4},{8,10},{10,8},{12,14},{14,12},{16,18},{18,... | collective-permute-start | bytes 491528 | tf_op jit(solution)/shard_map/ppermute | solution.py:1132
  96.1 3.5 %krylov.1 = (f32[8,16,768]{2,1,0:T(8,128)S(1)}, f32[16,128]{1,0:T(8,128)S(1)}) custom-call(s32[2]{0:T(128)S(1)} %pad_add_fusion.pos, f32[144]{0:T(256)S(1)} %concatenate.42.scal, f32[5,16,1280]{2,1,0:T(8,128)S(1)} %get-tuple-element.45.own, f32[5,16,512]{2,1,0:T(8,128)S(1)} %collective-permute-done.10.got_first, ...), custom_call_target="tpu_custom_call" | custom-call | flops 1000000 | bytes 1000000 | tf_op jit(solution)/shard_map/krylov/pallas_call | solution.py:1134
  100.3 25.9 %all_to_all.32 = f32[16,1,128]{2,1,0:T(1,128)S(1)} all-to-all(f32[16,1,128]{2,1,0:T(1,128)S(1)} %bitcast.73), channel_id=1, replica_groups=mesh['gx'=16,'yz'=16,'lvl'=2] {'yz'}, dimensions={0} | all-to-all | bytes 16384 | tf_op jit(solution)/shard_map/all_to_all | solution.py:1144
  126.9 11.4 %all-to-all-start.2 = ((f32[32,1,128]{2,1,0:T(1,128)}), f32[32,1,128]{2,1,0:T(1,128)S(1)}, u32[]{:S(2)}, u32[]{:S(2)}) async-start(f32[32,1,128]{2,1,0:T(1,128)} %bitcast.35), calls=%async_computation.2 | async-start | bytes 32768 | tf_op jit(solution)/shard_map/all_to_all | solution.py:1146
  139.0 7.9 %all-to-all-done.2 = f32[32,1,128]{2,1,0:T(1,128)S(1)} async-done(((f32[32,1,128]{2,1,0:T(1,128)}), f32[32,1,128]{2,1,0:T(1,128)S(1)}, u32[]{:S(2)}, u32[]{:S(2)}) %all-to-all-start.2) | async-done | bytes 16416 | tf_op jit(solution)/shard_map/all_to_all | solution.py:1146
  147.5 14.1 %post.1 = f32[16,64,128]{2,1,0:T(8,128)} custom-call(s32[2]{0:T(128)} %copy-done.15, f32[144]{0:T(256)} %copy-done.16, f32[32,128]{1,0:T(8,128)} %bitcast.82, f32[8,16,768]{2,1,0:T(8,128)} %copy-done.7, f32[128,1024]{1,0:T(8,128)} %copy-done, f32[2,8,16,768]{3,2,1,0:T(8,128)} %copy-done.4, f32[8,64,128]{2,1,0:T(8,128)} %copy-done.10, ...), custom_call_target="tpu_custom_call" | custom-call | flops 1000000 | bytes 1000000 | tf_op jit(solution)/shard_map/post/pallas_call | solution.py:1147
  161.6 20.1 %all_to_all.33.got = f32[16,64,128]{2,1,0:T(8,128)S(1)} all-to-all(f32[16,64,128]{2,1,0:T(8,128)} %post.1), channel_id=1, replica_groups=mesh['gx'=16,'yz'=16,'lvl'=2] {'gx'}, dimensions={0} | all-to-all | bytes 1048576 | tf_op jit(solution)/shard_map/all_to_all | solution.py:1170
  (117 shorter events, 27.7 us)
Async XLA Ops:
  3.2 20.6 %all-to-all-start = ((f32[16,40,128]{2,1,0:T(8,128)}), f32[16,40,128]{2,1,0:T(8,128)S(1)}, u32[]{:S(2)}, u32[]{:S(2)}) async-start(f32[16,40,128]{2,1,0:T(8,128)} %slots.1), calls=%async_computation | async-start | bytes 655360 | tf_op jit(solution)/shard_map/all_to_all | solution.py:1059
  18.3 25.1 %copy-start.11 = (bf16[64,80]{1,0:T(8,128)(2,1)}, bf16[64,80]{1,0:T(8,128)(2,1)S(1)}, u32[]{:S(2)}) copy-start(bf16[64,80]{1,0:T(8,128)(2,1)S(1)} %pad_maximum_fusion.2.diag_w) | copy-start | bytes 30724
  18.4 77.7 %copy-start.15 = (s32[2]{0:T(128)}, s32[2]{0:T(128)S(1)}, u32[]{:S(2)}) copy-start(s32[2]{0:T(128)S(1)} %pad_add_fusion.pos) | copy-start | bytes 28
  19.2 14.5 %copy-start.8 = (bf16[384,512]{1,0:T(8,128)(2,1)S(1)}, bf16[384,512]{1,0:T(8,128)(2,1)}, u32[]{:S(2)}) copy-start(bf16[384,512]{1,0:T(8,128)(2,1)} %constant.103.clone.place_kinds) | copy-start | bytes 1179652
  19.3 14.5 %copy-start.6 = (bf16[512,512]{1,0:T(8,128)(2,1)S(1)}, bf16[512,512]{1,0:T(8,128)(2,1)}, u32[]{:S(2)}) copy-start(bf16[512,512]{1,0:T(8,128)(2,1)} %constant.102.clone.place_values) | copy-start | bytes 1572868
  23.8 7.6 %collective-permute-start.1 = (f32[16,24,128]{2,1,0:T(8,128)S(1)}, f32[16,24,128]{2,1,0:T(8,128)S(1)}, u32[]{:S(2)}, u32[]{:S(2)}) collective-permute-start(f32[16,24,128]{2,1,0:T(8,128)S(1)} %get-tuple-element.64), channel_id=1, source_target_pairs={{64,0},{128,64},{192,128},{256,192},{320,256},{384,320},{448,384},... | collective-permute-start | bytes 589832 | tf_op jit(solution)/shard_map/ppermute | solution.py:1061
  26.2 7.6 %collective-permute-start = (f32[16,24,128]{2,1,0:T(8,128)S(1)}, f32[16,24,128]{2,1,0:T(8,128)S(1)}, u32[]{:S(2)}, u32[]{:S(2)}) collective-permute-start(f32[16,24,128]{2,1,0:T(8,128)S(1)} %get-tuple-element.65), channel_id=1, source_target_pairs={{0,64},{64,128},{128,192},{192,256},{256,320},{320,384},{384,448},... | collective-permute-start | bytes 589832 | tf_op jit(solution)/shard_map/ppermute | solution.py:1060
  35.2 8.2 %collective-permute-start.3 = (f32[768,128]{1,0:T(8,128)S(1)}, f32[768,128]{1,0:T(8,128)S(1)}, u32[]{:S(2)}, u32[]{:S(2)}) collective-permute-start(f32[768,128]{1,0:T(8,128)S(1)} %get-tuple-element.34), channel_id=1, source_target_pairs={{2,4},{4,2},{6,8},{8,6},{10,12},{12,10},{14,16},{16,14},{18,20},{2... | collective-permute-start | bytes 1179656 | tf_op jit(solution)/shard_map/ppermute | solution.py:1070
  35.9 7.5 %collective-permute-start.2 = (f32[768,128]{1,0:T(8,128)S(1)}, f32[768,128]{1,0:T(8,128)S(1)}, u32[]{:S(2)}, u32[]{:S(2)}) collective-permute-start(f32[768,128]{1,0:T(8,128)S(1)} %get-tuple-element.33.own), channel_id=1, source_target_pairs={{0,2},{2,0},{4,6},{6,4},{8,10},{10,8},{12,14},{14,12},{16,18},{18,... | collective-permute-start | bytes 1179656 | tf_op jit(solution)/shard_map/ppermute | solution.py:1069
  43.3 7.9 %copy-start.1 = (bf16[448,192]{1,0:T(8,128)(2,1)}, bf16[448,192]{1,0:T(8,128)(2,1)S(1)}, u32[]{:S(2)}) copy-start(bf16[448,192]{1,0:T(8,128)(2,1)S(1)} %pad_maximum_fusion.1.wide) | copy-start | bytes 516100
  51.8 14.1 %copy-start.10 = (f32[8,64,128]{2,1,0:T(8,128)}, f32[8,64,128]{2,1,0:T(8,128)S(1)}, u32[]{:S(2)}) copy-start(f32[8,64,128]{2,1,0:T(8,128)S(1)} %get-tuple-element.51.keep) | copy-start | bytes 786436
  51.8 21.4 %copy-start = (f32[128,1024]{1,0:T(8,128)}, f32[128,1024]{1,0:T(8,128)S(1)}, u32[]{:S(2)}) copy-start(f32[128,1024]{1,0:T(8,128)S(1)} %get-tuple-element.41.cfm) | copy-start | bytes 1572868
  51.8 9.6 %collective-permute-start.5 = (f32[384,128]{1,0:T(8,128)S(1)}, f32[384,128]{1,0:T(8,128)S(1)}, u32[]{:S(2)}, u32[]{:S(2)}) collective-permute-start(f32[384,128]{1,0:T(8,128)S(1)} %get-tuple-element.36), channel_id=1, source_target_pairs={{64,0},{128,64},{192,128},{256,192},{320,256},{384,320},{448,384},... | collective-permute-start | bytes 589832 | tf_op jit(solution)/shard_map/ppermute | solution.py:1099
  54.8 9.4 %collective-permute-start.4 = (f32[384,128]{1,0:T(8,128)S(1)}, f32[384,128]{1,0:T(8,128)S(1)}, u32[]{:S(2)}, u32[]{:S(2)}) collective-permute-start(f32[384,128]{1,0:T(8,128)S(1)} %get-tuple-element.35.own), channel_id=1, source_target_pairs={{0,64},{64,128},{128,192},{192,256},{256,320},{320,384},{384,448},... | collective-permute-start | bytes 589832 | tf_op jit(solution)/shard_map/ppermute | solution.py:1098
  66.7 6.5 %collective-permute-start.6 = (f32[896,128]{1,0:T(8,128)S(1)}, f32[896,128]{1,0:T(8,128)S(1)}, u32[]{:S(2)}, u32[]{:S(2)}) collective-permute-start(f32[896,128]{1,0:T(8,128)S(1)} %get-tuple-element.39), channel_id=1, source_target_pairs={{0,2},{2,0},{4,6},{6,4},{8,10},{10,8},{12,14},{14,12},{16,18},{18,... | collective-permute-start | bytes 1376264 | tf_op jit(solution)/shard_map/ppermute | solution.py:1106
  68.7 4.6 %collective-permute-start.7 = (f32[896,128]{1,0:T(8,128)S(1)}, f32[896,128]{1,0:T(8,128)S(1)}, u32[]{:S(2)}, u32[]{:S(2)}) collective-permute-start(f32[896,128]{1,0:T(8,128)S(1)} %get-tuple-element.40), channel_id=1, source_target_pairs={{2,4},{4,2},{6,8},{8,6},{10,12},{12,10},{14,16},{16,14},{18,20},{2... | collective-permute-start | bytes 1376264 | tf_op jit(solution)/shard_map/ppermute | solution.py:1107
  73.2 22.8 %copy-start.16 = (f32[144]{0:T(256)}, f32[144]{0:T(256)S(1)}, u32[]{:S(2)}) copy-start(f32[144]{0:T(256)S(1)} %concatenate.42.scal) | copy-start | bytes 1732
  73.2 3.6 %copy-start.2 = (f32[896,128]{1,0:T(8,128)}, f32[896,128]{1,0:T(8,128)S(1)}, u32[]{:S(2)}) copy-start(f32[896,128]{1,0:T(8,128)S(1)} %collective-permute-done.6.got_first) | copy-start | bytes 1376260
  73.3 3.6 %copy-start.3 = (f32[896,128]{1,0:T(8,128)}, f32[896,128]{1,0:T(8,128)S(1)}, u32[]{:S(2)}) copy-start(f32[896,128]{1,0:T(8,128)S(1)} %collective-permute-done.7.got_second) | copy-start | bytes 1376260
  77.8 6.5 %collective-permute-start.8 = (f32[2,16,768]{2,1,0:T(8,128)S(1)}, f32[2,16,768]{2,1,0:T(8,128)S(1)}, u32[]{:S(2)}, u32[]{:S(2)}) collective-permute-start(f32[2,16,768]{2,1,0:T(8,128)S(1)} %get-tuple-element.43), channel_id=1, source_target_pairs={{0,64},{64,128},{128,192},{192,256},{256,320},{320,384},{384,448},... | collective-permute-start | bytes 294920 | tf_op jit(solution)/shard_map/ppermute | solution.py:1124
  80.7 6.5 %collective-permute-start.9 = (f32[2,16,768]{2,1,0:T(8,128)S(1)}, f32[2,16,768]{2,1,0:T(8,128)S(1)}, u32[]{:S(2)}, u32[]{:S(2)}) collective-permute-start(f32[2,16,768]{2,1,0:T(8,128)S(1)} %get-tuple-element.44), channel_id=1, source_target_pairs={{64,0},{128,64},{192,128},{256,192},{320,256},{384,320},{448,384},... | collective-permute-start | bytes 294920 | tf_op jit(solution)/shard_map/ppermute | solution.py:1125
  88.4 7.6 %collective-permute-start.10 = (f32[5,16,512]{2,1,0:T(8,128)S(1)}, f32[5,16,512]{2,1,0:T(8,128)S(1)}, u32[]{:S(2)}, u32[]{:S(2)}) collective-permute-start(f32[5,16,512]{2,1,0:T(8,128)S(1)} %get-tuple-element.46), channel_id=1, source_target_pairs={{0,2},{2,0},{4,6},{6,4},{8,10},{10,8},{12,14},{14,12},{16,18},{18,... | collective-permute-start | bytes 491528 | tf_op jit(solution)/shard_map/ppermute | solution.py:1132
  95.0 1.0 collective-permute-start.11
  126.9 20.0 %all-to-all-start.2 = ((f32[32,1,128]{2,1,0:T(1,128)}), f32[32,1,128]{2,1,0:T(1,128)S(1)}, u32[]{:S(2)}, u32[]{:S(2)}) async-start(f32[32,1,128]{2,1,0:T(1,128)} %bitcast.35), calls=%async_computation.2 | async-start | bytes 32768 | tf_op jit(solution)/shard_map/all_to_all | solution.py:1146
  (14 other events, 10.4 us)

commit v7 on v6

--- a/solution.py
+++ b/solution.py
@@ -65,13 +65,10 @@
     return pos[0] % 2 == 0
 
 
-def put(pos, first, second, at, fwd, bwd):
-    if fwd is None:
-        fwd = bwd
-    if bwd is None:
-        bwd = fwd
-    first[at] = jnp.where(even(pos), fwd, bwd)
-    second[at] = jnp.where(even(pos), bwd, fwd)
+def put(parity, first, second, at, fwd, bwd):
+    is_even = jnp.broadcast_to(parity[0:1, :], fwd.shape) == 0.0
+    first[at] = jnp.where(is_even, fwd, bwd)
+    second[at] = jnp.where(is_even, bwd, fwd)
 
 
 def from_below(pos, first, second, at):
@@ -178,7 +175,7 @@
     return out[0:count] + out[count : 2 * count] + out[2 * count :]
 
 
-def join_body(pos, own, dn, up, place_values, place_kinds, rows, first, second):
+def join_body(parity, own, dn, up, place_values, place_kinds, rows, first, second):
     parts = (own[:, 0:16, :], own[:, 24:40, :], up[:, 0:16, :], dn[:, 8:24, :])
     values = jnp.concatenate([v.reshape(256, 128) for v in parts], axis=1)
     out = moved(values, place_values[...])
@@ -189,7 +186,7 @@
     for x in range(8):
         fwd = jnp.where(low, roll(rows[x], 64), rows[x + 8])
         bwd = jnp.where(low, rows[x], roll(rows[x + 8], 64))
-        put(pos, first, second, slice(64 * x, 64 * x + 64), fwd, bwd)
+        put(parity, first, second, slice(64 * x, 64 * x + 64), fwd, bwd)
     parts = (own[:, 16:24, :], dn[:, 0:8, :], up[:, 16:24, :])
     kinds = jnp.concatenate([v.reshape(128, 128) for v in parts], axis=1)
     out = moved(kinds, place_kinds[...])
@@ -414,7 +411,7 @@
         keep[x] = jnp.where(low, a, roll(b, 64))
 
 
-def mid_z_body(pos, own, dn, up, r, slab, first, second, frz):
+def mid_z_body(parity, own, dn, up, r, slab, first, second, frz):
     low = lanes((64, 128)) < 64
     l16 = lanes((16, 128)) % 16
     for x in range(NX):
@@ -430,7 +427,7 @@
     for x in range(8):
         fwd = jnp.where(low, roll(frz[x], 64), frz[x + 8])
         bwd = jnp.where(low, frz[x], roll(frz[x + 8], 64))
-        put(pos, first, second, slice(384 + 64 * x, 448 + 64 * x), fwd, bwd)
+        put(parity, first, second, slice(384 + 64 * x, 448 + 64 * x), fwd, bwd)
     lane = lanes((128, 128))
     tiles = []
     for m in range(4):
@@ -449,7 +446,7 @@
             slab[:, 128 * (m - 1) : 128 * m] = acc
         tiles.append(acc)
     for m in range(3):
-        put(pos, first, second, slice(128 * m, 128 * m + 128), tiles[m], tiles[m + 1])
+        put(parity, first, second, slice(128 * m, 128 * m + 128), tiles[m], tiles[m + 1])
 
 
 LOWS = ((0, 1, 2, 3), (0, 1, 4, 5), (0, 2, 4, 6))
@@ -589,7 +586,7 @@
         out[1] = roll(coarse[4, :, 128:896], -first)
 
 
-def coarse_z_body(pos, own, dn, up, slab, first, second):
+def coarse_z_body(parity, own, dn, up, slab, first, second):
     lane = lanes((16, 128))
     for f in range(5):
         part = 0 if f < 4 else 1
@@ -616,7 +613,7 @@
         for m in range(4):
             at = (f, slice(None), slice(128 * m, 128 * m + 128))
             after = (f, slice(None), slice(128 * (m + 6), 128 * (m + 7)))
-            put(pos, first, second, at, slab[at], slab[after])
+            put(parity, first, second, at, slab[at], slab[after])
 
 
 def settle(v, basis, j):
@@ -941,17 +938,17 @@
 
 
 def prolong_tables():
-    node_points = jnp.array(
-        [-1.0, -1.0 / math.sqrt(5.0), 1.0 / math.sqrt(5.0), 1.0], dtype=jnp.float32
-    )
-    basis_table = jnp.stack([(1.0 - node_points) * 0.5, (1.0 + node_points) * 0.5], axis=1)
+    half = np.float32(0.5)
+    one = np.float32(1.0)
+    node = np.array([-1.0, -1.0 / math.sqrt(5.0), 1.0 / math.sqrt(5.0), 1.0], np.float32)
+    table = np.stack([(one - node) * half, (one + node) * half], axis=1)
     volume = (
-        basis_table[:, None, None, :, None, None]
-        * basis_table[None, :, None, None, :, None]
-        * basis_table[None, None, :, None, None, :]
+        table[:, None, None, :, None, None]
+        * table[None, :, None, None, :, None]
+        * table[None, None, :, None, None, :]
     ).reshape(64, 8)
-    surface = (basis_table[:, None, :, None] * basis_table[None, :, None, :]).reshape(16, 4)
-    return (volume, surface)
+    surface = (table[:, None, :, None] * table[None, :, None, :]).reshape(16, 4)
+    return volume, surface
 
 
 def cut(x):
@@ -973,6 +970,7 @@
 def tables(element, faces):
     volume, surface = prolong_tables()
     elem_mid = jnp.dot(volume.T, jnp.dot(element, volume, precision=HIGHEST), precision=HIGHEST)
+    eye = np.eye(16, dtype=np.float32)
     face_mid = jnp.einsum("kij,jb->kib", faces, surface, precision=HIGHEST)
     face_mid = jnp.einsum("ia,kib->kab", surface, face_mid, precision=HIGHEST)
     elem_coarse = jnp.sum(elem_mid)
@@ -985,20 +983,20 @@
     wide = jnp.concatenate([wh, wh, wl], axis=1).astype(BF16)
     spread = np.concatenate([high[1], -low[1], high[2], -low[2]], axis=0).T
     spread = np.concatenate([spread, spread], axis=1)
-    face_diag = jnp.diagonal(faces, axis1=1, axis2=2)
+    face_diag = jnp.sum(faces * eye, axis=2)
     diag = jnp.einsum("dim,ki->mdk", both, face_diag, precision=HIGHEST).reshape(64, 24)
     diag_w = jnp.concatenate(three_parts(diag) + (jnp.zeros((64, 8), F32),), axis=1).astype(BF16)
-    diag_e = jnp.diagonal(element)[:, None]
+    diag_e = jnp.sum(element * np.eye(64, dtype=np.float32), axis=1, keepdims=True)
     mh, ml = mid_traces()
     both = np.concatenate([mh, ml], axis=0)
-    diag = jnp.einsum(
-        "dim,ki->mdk", both, jnp.diagonal(face_mid, axis1=1, axis2=2), precision=HIGHEST
-    ).reshape(8, 24)
+    face_diag = jnp.sum(face_mid * eye[:4, :4], axis=2)
+    diag = jnp.einsum("dim,ki->mdk", both, face_diag, precision=HIGHEST).reshape(8, 24)
     mid_diag_w = jnp.concatenate(three_parts(diag) + (jnp.zeros((8, 8), F32),), axis=1).astype(BF16)
-    mid_diag_e = jnp.diagonal(elem_mid)[:, None]
-    vh, vl = two_parts(volume)
-    down = jnp.concatenate([vh.T, vh.T, vl.T], axis=1).astype(BF16)
-    lift = jnp.concatenate([vh, vh, vl, jnp.zeros((64, 8), F32)], axis=1).astype(BF16)
+    mid_diag_e = jnp.sum(elem_mid * eye[:8, :8], axis=1, keepdims=True)
+    vh = volume.astype(BF16).astype(np.float32)
+    vl = (volume - vh).astype(BF16).astype(np.float32)
+    down = jnp.asarray(np.concatenate([vh.T, vh.T, vl.T], axis=1), BF16)
+    lift = jnp.asarray(np.concatenate([vh, vh, vl, np.zeros((64, 8), np.float32)], axis=1), BF16)
     least = 0.1 * elem_coarse
     most = 1.35 * elem_coarse + 9.0 * jnp.max(jnp.abs(face_coarse))
     half = 0.5 * (most - least)
@@ -1056,7 +1054,11 @@
     )(res, coefficient.reshape(8, 128), kind.reshape(48, 128), flag.reshape(48, 128))[0]
     element, faces, slots = lax.optimization_barrier((element, faces, slots))
     wide, spread, diag_w, diag_e, down, mid_diag_w, mid_diag_e, lift, scal = tables(element, faces)
+    parity = jnp.broadcast_to((lax.axis_index("yz") % 2).astype(F32), (8, 128))
     own = lax.all_to_all(slots, "gx", 0, 0, tiled=True)
+    own, wide, diag_w, diag_e, mid_diag_w, mid_diag_e, scal, parity, pos = lax.optimization_barrier(
+        (own, wide, diag_w, diag_e, mid_diag_w, mid_diag_e, scal, parity, pos)
+    )
     dn = lax.ppermute(own[:, 16:40], z_axes, z_up)
     up = lax.ppermute(own[:, 0:24], z_axes, z_dn)
     place_values, place_kinds, pack = place_tables()
@@ -1064,8 +1066,8 @@
         join_body,
         "join",
         [f32s(NX, 64, 128), f32s(768, 128), f32s(768, 128)],
-        (1,) + (0,) * 5,
-    )(pos, own, dn, up, place_values, place_kinds)
+        (0,) * 6,
+    )(parity, own, dn, up, place_values, place_kinds)
     got_first = lax.ppermute(own, "yz", y_first)
     got_second = lax.ppermute(other, "yz", y_second)
     plane = (64, NX * 256)
@@ -1101,8 +1103,8 @@
         mid_z_body,
         "mid_z",
         [f32s(128, 256), f32s(896, 128), f32s(896, 128), f32s(NX, 64, 128)],
-        (1,) + (0,) * 4,
-    )(pos, send_up, dn, up, r)
+        (0,) * 5,
+    )(parity, send_up, dn, up, r)
     got_first = lax.ppermute(first, "yz", y_first)
     got_second = lax.ppermute(second, "yz", y_second)
     mid = (8, 16, 1024)
@@ -1127,8 +1129,8 @@
         coarse_z_body,
         "coarse_z",
         [f32s(5, 16, 1280), f32s(5, 16, 512), f32s(5, 16, 512)],
-        (1, 0, 0, 0),
-    )(pos, coarse, dn, up)
+        (0,) * 4,
+    )(parity, coarse, dn, up)
     coarse_first = lax.ppermute(first, "yz", y_first)
     coarse_second = lax.ppermute(second, "yz", y_second)
     basis, gram = call(

time: 184 us -> 182 us (0.989)
  blocking collectives: 46 us -> 66 us
  waiting for transfers between devices: 25.8 us -> 15.6 us
  starting transfers between devices: 54.5 us -> 50.2 us
  local copies, waits for them, and re-layouts: 11.9 us -> 8 us
  Pallas kernels: 37.5 us -> 34.9 us
    all_to_all x0 -> x1, blocking collectives: none -> 20.8 us  [local(): gram = lax.all_to_all(gram, z_axes, 0, 0, tiled=True)]
    all_to_all x1 -> x0, starting transfers between devices: 11.4 us -> none  [local(): gram = lax.all_to_all(gram, z_axes, 0, 0, tiled=True)]
    all_to_all x1 -> x0, waiting for transfers between devices: 7.86 us -> none  [local(): gram = lax.all_to_all(gram, z_axes, 0, 0, tiled=True)]
    ppermute x1, starting transfers between devices: 6.63 us -> 11.9 us  [local(): coarse_first = lax.ppermute(first, 'yz', y_first)]
    all_to_all x1, waiting for transfers between devices: 3.54 us -> 0.14 us  [local(): own = lax.all_to_all(slots, 'gx', 0, 0, tiled=True)]
    gather x4 -> x0, local copies, waits for them, and re-layouts: 2.63 us -> none  [the longest x1 0.81 us: tables(): diag_e = jnp.diagonal(element)[:, None]]
    ppermute x2, waiting for transfers between devices: 6.66 us -> 4.07 us  [local(): up = lax.ppermute(send_down, z_axes, z_dn)]
    ppermute x2, starting transfers between devices: 5.95 us -> 8.05 us  [local(): up = lax.ppermute(send_down, z_axes, z_dn)]
  transfers between devices with their start and end apart: 14 -> 13, of which waited for: 9 -> 10; matrix products, arithmetic and copies ran while one was open for 5% -> 3% of each run, Pallas kernels for 0% -> 0%
where the time goes in v7:
time: 182 us; the launch traced here: 181 us
  blocking collectives  66 us (36%)
  starting transfers between devices  50.2 us (28%)
  Pallas kernels  34.9 us (19%)
  waiting for transfers between devices  15.6 us (9%)
  local copies, waits for them, and re-layouts  8 us (4%)
  between operations  3.1 us (2%)
  other arithmetic  2.03 us (1%)
    all_to_all x1, blocking collectives, local(): gram = lax.all_to_all(gram, 'yz', 0, 0, tiled=True)  25 us
    all_to_all x1, blocking collectives, local(): gram = lax.all_to_all(gram, z_axes, 0, 0, tiled=True)  20.8 us
    all_to_all x1, blocking collectives, local(): got = lax.all_to_all(packed, 'gx', 0, 0, tiled=True)  20.2 us
    pallas_call x1, Pallas kernels, local(): call(post_body, 'post', [f32s(16, 64, 128)], (1, 1) + (0,) * 14, mid_scra...  14.1 us
    ppermute x1, starting transfers between devices, local(): coarse_first = lax.ppermute(first, 'yz', y_first)  11.9 us
    all_to_all x1, starting transfers between devices, local(): own = lax.all_to_all(slots, 'gx', 0, 0, tiled=True)  9.37 us
    ppermute x2, starting transfers between devices, local(): up = lax.ppermute(send_down, z_axes, z_dn)  8.05 us
    pallas_call x1, Pallas kernels, local(): call(fine_pre_body, 'fine_pre', [f32s(8, 64, 128), f32s(*plane), f32s(8,...  6.85 us
  transfers between devices with their start and end apart: 13, of which 10 were waited for; matrix products, arithmetic and copies ran while one was open for 3% of the time, Pallas kernels for 0%

profile of v7, /device:TPU:2, one launch (start us, length us, event | category | flops | bytes accessed | tf_op | source)
XLA Modules:
  0.0 181.3 jit_solution(1161047571863927579)
XLA Ops:
  0.6 2.6 %slots.1 = f32[16,40,128]{2,1,0:T(8,128)} custom-call(f32[512,128]{1,0:T(8,128)} %bitcast.66, f32[8,128]{1,0:T(8,128)} %bitcast.75, s32[48,128]{1,0:T(8,128)} %bitcast.73, s32[48,128]{1,0:T(8,128)} %bitcast.74), custom_call_target="tpu_custom_call" | custom-call | flops 1000000 | bytes 1000000 | tf_op jit(solution)/shard_map/slots/pallas_call | solution.py:1047
  3.2 9.4 %all-to-all-start = ((f32[16,40,128]{2,1,0:T(8,128)}), f32[16,40,128]{2,1,0:T(8,128)S(1)}, u32[]{:S(2)}, u32[]{:S(2)}) async-start(f32[16,40,128]{2,1,0:T(8,128)} %slots.1), calls=%async_computation | async-start | bytes 655360 | tf_op jit(solution)/shard_map/all_to_all | solution.py:1058
  24.0 3.4 %collective-permute-start.1 = (f32[16,24,128]{2,1,0:T(8,128)S(1)}, f32[16,24,128]{2,1,0:T(8,128)S(1)}, u32[]{:S(2)}, u32[]{:S(2)}) collective-permute-start(f32[16,24,128]{2,1,0:T(8,128)S(1)} %get-tuple-element.82), channel_id=1, source_target_pairs={{64,0},{128,64},{192,128},{256,192},{320,256},{384,320},{448,384},... | collective-permute-start | bytes 589832 | tf_op jit(solution)/shard_map/ppermute | solution.py:1063
  27.4 2.6 %collective-permute-start = (f32[16,24,128]{2,1,0:T(8,128)S(1)}, f32[16,24,128]{2,1,0:T(8,128)S(1)}, u32[]{:S(2)}, u32[]{:S(2)}) collective-permute-start(f32[16,24,128]{2,1,0:T(8,128)S(1)} %get-tuple-element.83), channel_id=1, source_target_pairs={{0,64},{64,128},{128,192},{192,256},{256,320},{320,384},{384,448},... | collective-permute-start | bytes 589832 | tf_op jit(solution)/shard_map/ppermute | solution.py:1062
  30.0 1.7 collective-permute-done.1.up
  31.7 3.3 %collective-permute-done.dn = f32[16,24,128]{2,1,0:T(8,128)S(1)} collective-permute-done((f32[16,24,128]{2,1,0:T(8,128)S(1)}, f32[16,24,128]{2,1,0:T(8,128)S(1)}, u32[]{:S(2)}, u32[]{:S(2)}) %collective-permute-start) | collective-permute-done | bytes 196640 | tf_op jit(solution)/shard_map/ppermute | solution.py:1062
  36.5 5.1 %collective-permute-start.2 = (f32[768,128]{1,0:T(8,128)S(1)}, f32[768,128]{1,0:T(8,128)S(1)}, u32[]{:S(2)}, u32[]{:S(2)}) collective-permute-start(f32[768,128]{1,0:T(8,128)S(1)} %get-tuple-element.46.own), channel_id=1, source_target_pairs={{0,2},{2,0},{4,6},{6,4},{8,10},{10,8},{12,14},{14,12},{16,18},{18,... | collective-permute-start | bytes 1179656 | tf_op jit(solution)/shard_map/ppermute | solution.py:1071
  43.0 6.8 %fine_pre.1 = (f32[8,64,128]{2,1,0:T(8,128)S(1)}, f32[64,4096]{1,0:T(8,128)S(1)}, f32[8,4096]{1,0:T(8,128)S(1)}, f32[128,1024]{1,0:T(8,128)S(1)}, f32[384,128]{1,0:T(8,128)S(1)}, /*index=5*/f32[384,128]{1,0:T(8,128)S(1)}) custom-call(s32[2]{0:T(128)S(1)} %pad_add_fusion.pos, f32[16,64,128]{2,1,0:T(8,128)S(1)} %get-tuple-element.45.rows_in, ...), custom_call_target="tpu_custom_call" | custom-call | flops 1000000 | bytes 1000000 | tf_op jit(solution)/shard_map/fine_pre/pallas_call | solution.py:1075
  50.5 3.4 %collective-permute-start.5 = (f32[384,128]{1,0:T(8,128)S(1)}, f32[384,128]{1,0:T(8,128)S(1)}, u32[]{:S(2)}, u32[]{:S(2)}) collective-permute-start(f32[384,128]{1,0:T(8,128)S(1)} %get-tuple-element.54), channel_id=1, source_target_pairs={{64,0},{128,64},{192,128},{256,192},{320,256},{384,320},{448,384},... | collective-permute-start | bytes 589832 | tf_op jit(solution)/shard_map/ppermute | solution.py:1101
  53.9 2.5 %collective-permute-start.4 = (f32[384,128]{1,0:T(8,128)S(1)}, f32[384,128]{1,0:T(8,128)S(1)}, u32[]{:S(2)}, u32[]{:S(2)}) collective-permute-start(f32[384,128]{1,0:T(8,128)S(1)} %get-tuple-element.53.own), channel_id=1, source_target_pairs={{0,64},{64,128},{128,192},{192,256},{256,320},{320,384},{384,448},... | collective-permute-start | bytes 589832 | tf_op jit(solution)/shard_map/ppermute | solution.py:1100
  56.3 2.5 %collective-permute-done.5.up = f32[384,128]{1,0:T(8,128)S(1)} collective-permute-done((f32[384,128]{1,0:T(8,128)S(1)}, f32[384,128]{1,0:T(8,128)S(1)}, u32[]{:S(2)}, u32[]{:S(2)}) %collective-permute-start.5) | collective-permute-done | bytes 196640 | tf_op jit(solution)/shard_map/ppermute | solution.py:1101
  58.9 3.8 %collective-permute-done.4.dn = f32[384,128]{1,0:T(8,128)S(1)} collective-permute-done((f32[384,128]{1,0:T(8,128)S(1)}, f32[384,128]{1,0:T(8,128)S(1)}, u32[]{:S(2)}, u32[]{:S(2)}) %collective-permute-start.4) | collective-permute-done | bytes 196640 | tf_op jit(solution)/shard_map/ppermute | solution.py:1100
  63.9 3.0 %collective-permute-start.6 = (f32[896,128]{1,0:T(8,128)S(1)}, f32[896,128]{1,0:T(8,128)S(1)}, u32[]{:S(2)}, u32[]{:S(2)}) collective-permute-start(f32[896,128]{1,0:T(8,128)S(1)} %get-tuple-element.57), channel_id=1, source_target_pairs={{0,2},{2,0},{4,6},{6,4},{8,10},{10,8},{12,14},{14,12},{16,18},{18,... | collective-permute-start | bytes 1376264 | tf_op jit(solution)/shard_map/ppermute | solution.py:1108
  68.3 3.6 %mid_pre.1 = (f32[2,8,16,768]{3,2,1,0:T(8,128)S(1)}, f32[5,16,1024]{2,1,0:T(8,128)S(1)}, f32[2,16,768]{2,1,0:T(8,128)S(1)}, f32[2,16,768]{2,1,0:T(8,128)S(1)}) custom-call(s32[2]{0:T(128)S(1)} %pad_add_fusion.pos, f32[144]{0:T(256)S(1)} %concatenate.22.scal, f32[128,256]{1,0:T(8,128)S(1)} %get-tuple-element.56.slab, ...), custom_call_target="tpu_custom_call" | custom-call | flops 1000000 | bytes 1000000 | tf_op jit(solution)/shard_map/mid_pre/pallas_call | solution.py:1117
  72.8 2.1 %collective-permute-start.8 = (f32[2,16,768]{2,1,0:T(8,128)S(1)}, f32[2,16,768]{2,1,0:T(8,128)S(1)}, u32[]{:S(2)}, u32[]{:S(2)}) collective-permute-start(f32[2,16,768]{2,1,0:T(8,128)S(1)} %get-tuple-element.61), channel_id=1, source_target_pairs={{0,64},{64,128},{128,192},{192,256},{256,320},{320,384},{384,448},... | collective-permute-start | bytes 294920 | tf_op jit(solution)/shard_map/ppermute | solution.py:1126
  74.9 4.7 %collective-permute-start.9 = (f32[2,16,768]{2,1,0:T(8,128)S(1)}, f32[2,16,768]{2,1,0:T(8,128)S(1)}, u32[]{:S(2)}, u32[]{:S(2)}) collective-permute-start(f32[2,16,768]{2,1,0:T(8,128)S(1)} %get-tuple-element.62), channel_id=1, source_target_pairs={{64,0},{128,64},{192,128},{256,192},{320,256},{384,320},{448,384},... | collective-permute-start | bytes 294920 | tf_op jit(solution)/shard_map/ppermute | solution.py:1127
  80.2 1.5 collective-permute-done.9.up
  82.5 11.9 %collective-permute-start.10 = (f32[5,16,512]{2,1,0:T(8,128)S(1)}, f32[5,16,512]{2,1,0:T(8,128)S(1)}, u32[]{:S(2)}, u32[]{:S(2)}) collective-permute-start(f32[5,16,512]{2,1,0:T(8,128)S(1)} %get-tuple-element.64), channel_id=1, source_target_pairs={{0,2},{2,0},{4,6},{6,4},{8,10},{10,8},{12,14},{14,12},{16,18},{18,... | collective-permute-start | bytes 491528 | tf_op jit(solution)/shard_map/ppermute | solution.py:1134
  95.4 3.5 %krylov.1 = (f32[8,16,768]{2,1,0:T(8,128)S(1)}, f32[16,128]{1,0:T(8,128)S(1)}) custom-call(s32[2]{0:T(128)S(1)} %pad_add_fusion.pos, f32[144]{0:T(256)S(1)} %concatenate.22.scal, f32[5,16,1280]{2,1,0:T(8,128)S(1)} %get-tuple-element.63.own, f32[5,16,512]{2,1,0:T(8,128)S(1)} %collective-permute-done.10.got_first, ...), custom_call_target="tpu_custom_call" | custom-call | flops 1000000 | bytes 1000000 | tf_op jit(solution)/shard_map/krylov/pallas_call | solution.py:1136
  99.6 25.0 %all_to_all.32 = f32[16,1,128]{2,1,0:T(1,128)S(1)} all-to-all(f32[16,1,128]{2,1,0:T(1,128)S(1)} %bitcast.64), channel_id=1, replica_groups=mesh['gx'=16,'yz'=16,'lvl'=2] {'yz'}, dimensions={0} | all-to-all | bytes 16384 | tf_op jit(solution)/shard_map/all_to_all | solution.py:1146
  124.8 20.8 %all_to_all.33 = f32[32,1,128]{2,1,0:T(1,128)} all-to-all(f32[32,1,128]{2,1,0:T(1,128)S(1)} %bitcast.62), channel_id=1, replica_groups=mesh['gx'=16,'yz'=16,'lvl'=2] {'gx','lvl'}, dimensions={0} | all-to-all | bytes 32768 | tf_op jit(solution)/shard_map/all_to_all | solution.py:1148
  145.6 14.1 %post.1 = f32[16,64,128]{2,1,0:T(8,128)} custom-call(s32[2]{0:T(128)} %copy-done.16, f32[144]{0:T(256)} %copy-done.15, f32[32,128]{1,0:T(8,128)} %bitcast.70, f32[8,16,768]{2,1,0:T(8,128)} %copy-done.7, f32[128,1024]{1,0:T(8,128)} %copy-done, f32[2,8,16,768]{3,2,1,0:T(8,128)} %copy-done.4, f32[8,64,128]{2,1,0:T(8,128)} %copy-done.10, ...), custom_call_target="tpu_custom_call" | custom-call | flops 1000000 | bytes 1000000 | tf_op jit(solution)/shard_map/post/pallas_call | solution.py:1149
  159.7 20.2 %all_to_all.34.got = f32[16,64,128]{2,1,0:T(8,128)S(1)} all-to-all(f32[16,64,128]{2,1,0:T(8,128)} %post.1), channel_id=1, replica_groups=mesh['gx'=16,'yz'=16,'lvl'=2] {'gx'}, dimensions={0} | all-to-all | bytes 1048576 | tf_op jit(solution)/shard_map/all_to_all | solution.py:1172
  179.9 1.4 unpack.1
  (111 shorter events, 19.4 us)
Async XLA Ops:
  3.2 9.4 %copy-start.23 = (f32[64,64]{1,0:T(8,128)S(1)}, f32[64,64]{1,0:T(8,128)}, u32[]{:S(2)}) copy-start(f32[64,64]{1,0:T(8,128)} %constant.101.clone) | copy-start | bytes 49156
  3.2 20.7 %all-to-all-start = ((f32[16,40,128]{2,1,0:T(8,128)}), f32[16,40,128]{2,1,0:T(8,128)S(1)}, u32[]{:S(2)}, u32[]{:S(2)}) async-start(f32[16,40,128]{2,1,0:T(8,128)} %slots.1), calls=%async_computation | async-start | bytes 655360 | tf_op jit(solution)/shard_map/all_to_all | solution.py:1058
  19.6 75.8 %copy-start.16 = (s32[2]{0:T(128)}, s32[2]{0:T(128)S(1)}, u32[]{:S(2)}) copy-start(s32[2]{0:T(128)S(1)} %pad_add_fusion.pos) | copy-start | bytes 28
  23.5 71.9 %copy-start.15 = (f32[144]{0:T(256)}, f32[144]{0:T(256)S(1)}, u32[]{:S(2)}) copy-start(f32[144]{0:T(256)S(1)} %concatenate.22.scal) | copy-start | bytes 1732
  23.7 19.3 %copy-start.1 = (bf16[448,192]{1,0:T(8,128)(2,1)}, bf16[448,192]{1,0:T(8,128)(2,1)S(1)}, u32[]{:S(2)}) copy-start(bf16[448,192]{1,0:T(8,128)(2,1)S(1)} %pad_maximum_fusion.1.wide) | copy-start | bytes 516100
  23.7 11.3 %copy-start.5 = (bf16[512,512]{1,0:T(8,128)(2,1)S(1)}, bf16[512,512]{1,0:T(8,128)(2,1)}, u32[]{:S(2)}) copy-start(bf16[512,512]{1,0:T(8,128)(2,1)} %constant.108.clone.place_values) | copy-start | bytes 1572868
  23.8 19.2 %copy-start.11 = (bf16[64,80]{1,0:T(8,128)(2,1)}, bf16[64,80]{1,0:T(8,128)(2,1)S(1)}, u32[]{:S(2)}) copy-start(bf16[64,80]{1,0:T(8,128)(2,1)S(1)} %maximum_maximum_fusion.diag_w) | copy-start | bytes 30724
  24.0 11.0 %copy-start.8 = (bf16[384,512]{1,0:T(8,128)(2,1)S(1)}, bf16[384,512]{1,0:T(8,128)(2,1)}, u32[]{:S(2)}) copy-start(bf16[384,512]{1,0:T(8,128)(2,1)} %constant.109.clone.place_kinds) | copy-start | bytes 1179652
  24.0 7.7 %collective-permute-start.1 = (f32[16,24,128]{2,1,0:T(8,128)S(1)}, f32[16,24,128]{2,1,0:T(8,128)S(1)}, u32[]{:S(2)}, u32[]{:S(2)}) collective-permute-start(f32[16,24,128]{2,1,0:T(8,128)S(1)} %get-tuple-element.82), channel_id=1, source_target_pairs={{64,0},{128,64},{192,128},{256,192},{320,256},{384,320},{448,384},... | collective-permute-start | bytes 589832 | tf_op jit(solution)/shard_map/ppermute | solution.py:1063
  27.4 7.6 %collective-permute-start = (f32[16,24,128]{2,1,0:T(8,128)S(1)}, f32[16,24,128]{2,1,0:T(8,128)S(1)}, u32[]{:S(2)}, u32[]{:S(2)}) collective-permute-start(f32[16,24,128]{2,1,0:T(8,128)S(1)} %get-tuple-element.83), channel_id=1, source_target_pairs={{0,64},{64,128},{128,192},{192,256},{256,320},{320,384},{384,448},... | collective-permute-start | bytes 589832 | tf_op jit(solution)/shard_map/ppermute | solution.py:1062
  35.8 6.0 %collective-permute-start.3 = (f32[768,128]{1,0:T(8,128)S(1)}, f32[768,128]{1,0:T(8,128)S(1)}, u32[]{:S(2)}, u32[]{:S(2)}) collective-permute-start(f32[768,128]{1,0:T(8,128)S(1)} %get-tuple-element.47), channel_id=1, source_target_pairs={{2,4},{4,2},{6,8},{8,6},{10,12},{12,10},{14,16},{16,14},{18,20},{2... | collective-permute-start | bytes 1179656 | tf_op jit(solution)/shard_map/ppermute | solution.py:1072
  36.5 6.4 %collective-permute-start.2 = (f32[768,128]{1,0:T(8,128)S(1)}, f32[768,128]{1,0:T(8,128)S(1)}, u32[]{:S(2)}, u32[]{:S(2)}) collective-permute-start(f32[768,128]{1,0:T(8,128)S(1)} %get-tuple-element.46.own), channel_id=1, source_target_pairs={{0,2},{2,0},{4,6},{6,4},{8,10},{10,8},{12,14},{14,12},{16,18},{18,... | collective-permute-start | bytes 1179656 | tf_op jit(solution)/shard_map/ppermute | solution.py:1071
  41.8 8.0 %copy-start.9 = (f32[64,1]{1,0:T(8,128)}, f32[64,1]{1,0:T(8,128)S(1)}, u32[]{:S(2)}) copy-start(f32[64,1]{1,0:T(8,128)S(1)} %copy.69.diag_e) | copy-start | bytes 772
  50.5 13.4 %copy-start.10 = (f32[8,64,128]{2,1,0:T(8,128)}, f32[8,64,128]{2,1,0:T(8,128)S(1)}, u32[]{:S(2)}) copy-start(f32[8,64,128]{2,1,0:T(8,128)S(1)} %get-tuple-element.69.keep) | copy-start | bytes 786436
  50.5 17.8 %copy-start = (f32[128,1024]{1,0:T(8,128)}, f32[128,1024]{1,0:T(8,128)S(1)}, u32[]{:S(2)}) copy-start(f32[128,1024]{1,0:T(8,128)S(1)} %get-tuple-element.59.cfm) | copy-start | bytes 1572868
  50.5 8.4 %collective-permute-start.5 = (f32[384,128]{1,0:T(8,128)S(1)}, f32[384,128]{1,0:T(8,128)S(1)}, u32[]{:S(2)}, u32[]{:S(2)}) collective-permute-start(f32[384,128]{1,0:T(8,128)S(1)} %get-tuple-element.54), channel_id=1, source_target_pairs={{64,0},{128,64},{192,128},{256,192},{320,256},{384,320},{448,384},... | collective-permute-start | bytes 589832 | tf_op jit(solution)/shard_map/ppermute | solution.py:1101
  53.9 8.8 %collective-permute-start.4 = (f32[384,128]{1,0:T(8,128)S(1)}, f32[384,128]{1,0:T(8,128)S(1)}, u32[]{:S(2)}, u32[]{:S(2)}) collective-permute-start(f32[384,128]{1,0:T(8,128)S(1)} %get-tuple-element.53.own), channel_id=1, source_target_pairs={{0,64},{64,128},{128,192},{192,256},{256,320},{320,384},{384,448},... | collective-permute-start | bytes 589832 | tf_op jit(solution)/shard_map/ppermute | solution.py:1100
  63.9 8.0 %copy-start.6 = (f32[16,64,128]{2,1,0:T(8,128)}, f32[16,64,128]{2,1,0:T(8,128)S(1)}, u32[]{:S(2)}) copy-start(f32[16,64,128]{2,1,0:T(8,128)S(1)} %get-tuple-element.70.frz) | copy-start | bytes 1572868
  63.9 4.4 %collective-permute-start.6 = (f32[896,128]{1,0:T(8,128)S(1)}, f32[896,128]{1,0:T(8,128)S(1)}, u32[]{:S(2)}, u32[]{:S(2)}) collective-permute-start(f32[896,128]{1,0:T(8,128)S(1)} %get-tuple-element.57), channel_id=1, source_target_pairs={{0,2},{2,0},{4,6},{6,4},{8,10},{10,8},{12,14},{14,12},{16,18},{18,... | collective-permute-start | bytes 1376264 | tf_op jit(solution)/shard_map/ppermute | solution.py:1108
  66.9 1.4 collective-permute-start.7
  72.8 7.4 %collective-permute-start.8 = (f32[2,16,768]{2,1,0:T(8,128)S(1)}, f32[2,16,768]{2,1,0:T(8,128)S(1)}, u32[]{:S(2)}, u32[]{:S(2)}) collective-permute-start(f32[2,16,768]{2,1,0:T(8,128)S(1)} %get-tuple-element.61), channel_id=1, source_target_pairs={{0,64},{64,128},{128,192},{192,256},{256,320},{320,384},{384,448},... | collective-permute-start | bytes 294920 | tf_op jit(solution)/shard_map/ppermute | solution.py:1126
  74.9 6.9 %collective-permute-start.9 = (f32[2,16,768]{2,1,0:T(8,128)S(1)}, f32[2,16,768]{2,1,0:T(8,128)S(1)}, u32[]{:S(2)}, u32[]{:S(2)}) collective-permute-start(f32[2,16,768]{2,1,0:T(8,128)S(1)} %get-tuple-element.62), channel_id=1, source_target_pairs={{64,0},{128,64},{192,128},{256,192},{320,256},{384,320},{448,384},... | collective-permute-start | bytes 294920 | tf_op jit(solution)/shard_map/ppermute | solution.py:1127
  82.5 12.9 %collective-permute-start.10 = (f32[5,16,512]{2,1,0:T(8,128)S(1)}, f32[5,16,512]{2,1,0:T(8,128)S(1)}, u32[]{:S(2)}, u32[]{:S(2)}) collective-permute-start(f32[5,16,512]{2,1,0:T(8,128)S(1)} %get-tuple-element.64), channel_id=1, source_target_pairs={{0,2},{2,0},{4,6},{6,4},{8,10},{10,8},{12,14},{14,12},{16,18},{18,... | collective-permute-start | bytes 491528 | tf_op jit(solution)/shard_map/ppermute | solution.py:1134
  94.4 1.0 collective-permute-start.11
  (19 other events, 29.4 us)

commit v8 on v7

--- a/solution.py
+++ b/solution.py
@@ -61,8 +61,15 @@
     )
 
 
+def position():
+    chip = lax.axis_index("gx")
+    up = lax.rem(chip, 2) == 0
+    block = jnp.where(up, lax.div(chip, 2), 15 - lax.div(chip, 2))
+    return lax.axis_index("yz"), lax.axis_index("lvl") * 16 + block
+
+
 def even(pos):
-    return pos[0] % 2 == 0
+    return lax.rem(pos[0], 2) == 0
 
 
 def put(parity, first, second, at, fwd, bwd):
@@ -295,7 +302,6 @@
 
 
 def fine_pre_body(
-    pos,
     rows_in,
     own,
     got_first,
@@ -323,6 +329,7 @@
     gather,
     held,
 ):
+    pos = position()
     low = lanes((64, 128)) < 64
     lane8 = lanes((8, 128))
     inside = fine_places(pos)[0]
@@ -543,9 +550,10 @@
 
 
 def mid_pre_body(
-    pos, scal, slab, got_first, got_second, cfm, level, coarse, send_up, send_down,
+    scal, slab, got_first, got_second, cfm, level, coarse, send_up, send_down,
     sel, faces, inv, diag, u, sol, r, jump, flux,
 ):
+    pos = position()
     for i in range(8):
         rows = slice(16 * i, 16 * i + 16)
         for m in range(3):
@@ -668,7 +676,8 @@
 PAIRS = sum(9 - i for i in range(BASIS))
 
 
-def krylov_body(pos, scal, own, got_first, got_second, basis, gram, field, hold):
+def krylov_body(scal, own, got_first, got_second, basis, gram, field, hold):
+    pos = position()
     for f in range(5):
         field[f, :, 0:512] = from_below(pos, got_first, got_second, f)
         field[f, :, 512:1792] = own[f]
@@ -834,10 +843,11 @@
 
 
 def post_body(
-    pos, scal, gram, basis, cfm, level, keep, frz, got_first, got_second, coef, wide, spread,
+    scal, gram, basis, cfm, level, keep, frz, got_first, got_second, coef, wide, spread,
     lift, diag_w, diag_e, out,
     sel, faces, mid_inv, mid_u, mid_r, mid_sol, jump, flux, mid, w, inv, u, r, sol, px, qx,
 ):
+    pos = position()
     fine_weights(pos, coef, w)
     wide_inside = jnp.concatenate([fine_places(pos)[0]] * (CHUNK // 256), axis=1)
     for c in range(CHUNKS):
@@ -1035,14 +1045,6 @@
     z_up = [(z_index(i), z_index(i + 1)) for i in range(31)]
     z_dn = [(z_index(i + 1), z_index(i)) for i in range(31)]
     z_axes = ("gx", "lvl")
-    side = lax.axis_index("lvl")
-    chip = lax.axis_index("gx")
-    pos = jnp.stack(
-        [
-            lax.axis_index("yz"),
-            side * 16 + jnp.where(chip % 2 == 0, chip // 2, 15 - chip // 2),
-        ]
-    ).astype(jnp.int32)
     res = residual.reshape(512, 128)
     slots = call(
         slots_body,
@@ -1056,8 +1058,8 @@
     wide, spread, diag_w, diag_e, down, mid_diag_w, mid_diag_e, lift, scal = tables(element, faces)
     parity = jnp.broadcast_to((lax.axis_index("yz") % 2).astype(F32), (8, 128))
     own = lax.all_to_all(slots, "gx", 0, 0, tiled=True)
-    own, wide, diag_w, diag_e, mid_diag_w, mid_diag_e, scal, parity, pos = lax.optimization_barrier(
-        (own, wide, diag_w, diag_e, mid_diag_w, mid_diag_e, scal, parity, pos)
+    own, wide, diag_w, diag_e, mid_diag_w, mid_diag_e, scal, parity = lax.optimization_barrier(
+        (own, wide, diag_w, diag_e, mid_diag_w, mid_diag_e, scal, parity)
     )
     dn = lax.ppermute(own[:, 16:40], z_axes, z_up)
     up = lax.ppermute(own[:, 0:24], z_axes, z_dn)
@@ -1083,7 +1085,7 @@
             f32s(384, 128),
             f32s(384, 128),
         ],
-        (1,) + (0,) * 12,
+        (0,) * 12,
         [
             pltpu.VMEM(plane, F32),
             pltpu.VMEM((24, NX * 256), F32),
@@ -1095,7 +1097,7 @@
             pltpu.VMEM((256, 128), F32),
         ],
     )(
-        pos, rows, own, got_first, got_second, wide, spread, diag_w, diag_e, down, mid_diag_w, mid_diag_e, pack
+        rows, own, got_first, got_second, wide, spread, diag_w, diag_e, down, mid_diag_w, mid_diag_e, pack
     )
     dn = lax.ppermute(send_up, z_axes, z_up)
     up = lax.ppermute(send_down, z_axes, z_dn)
@@ -1118,11 +1120,11 @@
         mid_pre_body,
         "mid_pre",
         [f32s(2, 8, 16, 768), f32s(5, 16, 1024), f32s(2, 16, 768), f32s(2, 16, 768)],
-        (1, 1, 0, 0, 0, 0),
+        (1, 0, 0, 0, 0),
         mid_scratch
         + [pltpu.VMEM(mid, F32)] * 4
         + tail_scratch,
-    )(pos, scal, slab, got_first, got_second, cfm)
+    )(scal, slab, got_first, got_second, cfm)
     dn = lax.ppermute(send_up, z_axes, z_up)
     up = lax.ppermute(send_down, z_axes, z_dn)
     coarse_slab, first, second = call(
@@ -1137,12 +1139,12 @@
         krylov_body,
         "krylov",
         [f32s(BASIS, 16, 768), f32s(16, 128)],
-        (1, 1, 0, 0, 0),
+        (1, 0, 0, 0),
         [
             pltpu.VMEM((5, 16, 2304), F32),
             pltpu.VMEM((2 * BASIS, 8, 128), F32),
         ],
-    )(pos, scal, coarse_slab, coarse_first, coarse_second)
+    )(scal, coarse_slab, coarse_first, coarse_second)
     gram = lax.all_to_all(gram, "yz", 0, 0, tiled=True)
     gram = call(gram_body, "gram", [f32s(32, 128)], (0,))(gram)[0]
     gram = lax.all_to_all(gram, z_axes, 0, 0, tiled=True)
@@ -1150,7 +1152,7 @@
         post_body,
         "post",
         [f32s(16, 64, 128)],
-        (1, 1) + (0,) * 14,
+        (1,) + (0,) * 14,
         mid_scratch
         + [pltpu.VMEM(mid, F32)] * 3
         + tail_scratch
@@ -1166,7 +1168,7 @@
         ],
         limit=LARGE_LIMIT,
     )(
-        pos, scal, gram, basis, cfm, level, keep, frz, got_first, got_second, coef, wide, spread,
+        scal, gram, basis, cfm, level, keep, frz, got_first, got_second, coef, wide, spread,
         lift, diag_w, diag_e,
     )[0]
     got = lax.all_to_all(packed, "gx", 0, 0, tiled=True)

time: 182 us -> 182 us (level)
    unnamed x60 -> x58, local copies, waits for them, and re-layouts: 6.39 us -> 6.75 us
where the time goes in v8:
time: 182 us; the launch traced here: 181 us
  blocking collectives  66 us (36%)
  starting transfers between devices  50.4 us (28%)
  Pallas kernels  34.6 us (19%)
  waiting for transfers between devices  15.4 us (8%)
  local copies, waits for them, and re-layouts  8.37 us (5%)
  between operations  3.04 us (2%)
  other arithmetic  1.89 us (1%)
    all_to_all x1, blocking collectives, local(): gram = lax.all_to_all(gram, 'yz', 0, 0, tiled=True)  25 us
    all_to_all x1, blocking collectives, local(): gram = lax.all_to_all(gram, z_axes, 0, 0, tiled=True)  20.8 us
    all_to_all x1, blocking collectives, local(): got = lax.all_to_all(packed, 'gx', 0, 0, tiled=True)  20.1 us
    pallas_call x1, Pallas kernels, local(): call(post_body, 'post', [f32s(16, 64, 128)], (1,) + (0,) * 14, mid_scratc...  14.1 us
    ppermute x1, starting transfers between devices, local(): coarse_first = lax.ppermute(first, 'yz', y_first)  11.9 us
    all_to_all x1, starting transfers between devices, local(): own = lax.all_to_all(slots, 'gx', 0, 0, tiled=True)  9.37 us
    ppermute x2, starting transfers between devices, local(): up = lax.ppermute(send_down, z_axes, z_dn)  7.67 us
    unnamed x58, local copies, waits for them, and re-layouts  6.75 us
  transfers between devices with their start and end apart: 13, of which 10 were waited for; matrix products, arithmetic and copies ran while one was open for 3% of the time, Pallas kernels for 0%

profile of v8, /device:TPU:2, one launch (start us, length us, event | category | flops | bytes accessed | tf_op | source)
XLA Modules:
  0.0 181.1 jit_solution(3314795590463193067)
XLA Ops:
  0.6 2.6 %slots.1 = f32[16,40,128]{2,1,0:T(8,128)} custom-call(f32[512,128]{1,0:T(8,128)} %bitcast.64, f32[8,128]{1,0:T(8,128)} %bitcast.73, s32[48,128]{1,0:T(8,128)} %bitcast.71, s32[48,128]{1,0:T(8,128)} %bitcast.72), custom_call_target="tpu_custom_call" | custom-call | flops 1000000 | bytes 1000000 | tf_op jit(solution)/shard_map/slots/pallas_call | solution.py:1049
  3.2 9.4 %all-to-all-start = ((f32[16,40,128]{2,1,0:T(8,128)}), f32[16,40,128]{2,1,0:T(8,128)S(1)}, u32[]{:S(2)}, u32[]{:S(2)}) async-start(f32[16,40,128]{2,1,0:T(8,128)} %slots.1), calls=%async_computation | async-start | bytes 655360 | tf_op jit(solution)/shard_map/all_to_all | solution.py:1060
  24.0 2.7 %collective-permute-start.1 = (f32[16,24,128]{2,1,0:T(8,128)S(1)}, f32[16,24,128]{2,1,0:T(8,128)S(1)}, u32[]{:S(2)}, u32[]{:S(2)}) collective-permute-start(f32[16,24,128]{2,1,0:T(8,128)S(1)} %get-tuple-element.80), channel_id=1, source_target_pairs={{64,0},{128,64},{192,128},{256,192},{320,256},{384,320},{448,384},... | collective-permute-start | bytes 589832 | tf_op jit(solution)/shard_map/ppermute | solution.py:1065
  26.7 3.2 %collective-permute-start = (f32[16,24,128]{2,1,0:T(8,128)S(1)}, f32[16,24,128]{2,1,0:T(8,128)S(1)}, u32[]{:S(2)}, u32[]{:S(2)}) collective-permute-start(f32[16,24,128]{2,1,0:T(8,128)S(1)} %get-tuple-element.81), channel_id=1, source_target_pairs={{0,64},{64,128},{128,192},{192,256},{256,320},{320,384},{384,448},... | collective-permute-start | bytes 589832 | tf_op jit(solution)/shard_map/ppermute | solution.py:1064
  30.0 1.7 collective-permute-done.1.up
  31.7 2.6 %collective-permute-done.dn = f32[16,24,128]{2,1,0:T(8,128)S(1)} collective-permute-done((f32[16,24,128]{2,1,0:T(8,128)S(1)}, f32[16,24,128]{2,1,0:T(8,128)S(1)}, u32[]{:S(2)}, u32[]{:S(2)}) %collective-permute-start) | collective-permute-done | bytes 196640 | tf_op jit(solution)/shard_map/ppermute | solution.py:1064
  35.9 5.3 %collective-permute-start.2 = (f32[768,128]{1,0:T(8,128)S(1)}, f32[768,128]{1,0:T(8,128)S(1)}, u32[]{:S(2)}, u32[]{:S(2)}) collective-permute-start(f32[768,128]{1,0:T(8,128)S(1)} %get-tuple-element.44.own), channel_id=1, source_target_pairs={{0,2},{2,0},{4,6},{6,4},{8,10},{10,8},{12,14},{14,12},{16,18},{18,... | collective-permute-start | bytes 1179656 | tf_op jit(solution)/shard_map/ppermute | solution.py:1073
  42.5 6.5 %fine_pre.1 = (f32[8,64,128]{2,1,0:T(8,128)S(1)}, f32[64,4096]{1,0:T(8,128)S(1)}, f32[8,4096]{1,0:T(8,128)S(1)}, f32[128,1024]{1,0:T(8,128)S(1)}, f32[384,128]{1,0:T(8,128)S(1)}, /*index=5*/f32[384,128]{1,0:T(8,128)S(1)}) custom-call(f32[16,64,128]{2,1,0:T(8,128)S(1)} %get-tuple-element.43.rows_in, f32[768,128]{1,0:T(8,128)S(1)} %get-tuple-element.44.own, ...), custom_call_target="tpu_custom_call" | custom-call | flops 1000000 | bytes 1000000 | tf_op jit(solution)/shard_map/fine_pre/pallas_call | solution.py:1077
  49.7 3.2 %collective-permute-start.5 = (f32[384,128]{1,0:T(8,128)S(1)}, f32[384,128]{1,0:T(8,128)S(1)}, u32[]{:S(2)}, u32[]{:S(2)}) collective-permute-start(f32[384,128]{1,0:T(8,128)S(1)} %get-tuple-element.52), channel_id=1, source_target_pairs={{64,0},{128,64},{192,128},{256,192},{320,256},{384,320},{448,384},... | collective-permute-start | bytes 589832 | tf_op jit(solution)/shard_map/ppermute | solution.py:1103
  52.8 2.7 %collective-permute-start.4 = (f32[384,128]{1,0:T(8,128)S(1)}, f32[384,128]{1,0:T(8,128)S(1)}, u32[]{:S(2)}, u32[]{:S(2)}) collective-permute-start(f32[384,128]{1,0:T(8,128)S(1)} %get-tuple-element.51.own), channel_id=1, source_target_pairs={{0,64},{64,128},{128,192},{192,256},{256,320},{320,384},{384,448},... | collective-permute-start | bytes 589832 | tf_op jit(solution)/shard_map/ppermute | solution.py:1102
  55.5 2.5 %collective-permute-done.5.up = f32[384,128]{1,0:T(8,128)S(1)} collective-permute-done((f32[384,128]{1,0:T(8,128)S(1)}, f32[384,128]{1,0:T(8,128)S(1)}, u32[]{:S(2)}, u32[]{:S(2)}) %collective-permute-start.5) | collective-permute-done | bytes 196640 | tf_op jit(solution)/shard_map/ppermute | solution.py:1103
  58.0 3.6 %collective-permute-done.4.dn = f32[384,128]{1,0:T(8,128)S(1)} collective-permute-done((f32[384,128]{1,0:T(8,128)S(1)}, f32[384,128]{1,0:T(8,128)S(1)}, u32[]{:S(2)}, u32[]{:S(2)}) %collective-permute-start.4) | collective-permute-done | bytes 196640 | tf_op jit(solution)/shard_map/ppermute | solution.py:1102
  63.7 3.0 %collective-permute-start.6 = (f32[896,128]{1,0:T(8,128)S(1)}, f32[896,128]{1,0:T(8,128)S(1)}, u32[]{:S(2)}, u32[]{:S(2)}) collective-permute-start(f32[896,128]{1,0:T(8,128)S(1)} %get-tuple-element.55), channel_id=1, source_target_pairs={{0,2},{2,0},{4,6},{6,4},{8,10},{10,8},{12,14},{14,12},{16,18},{18,... | collective-permute-start | bytes 1376264 | tf_op jit(solution)/shard_map/ppermute | solution.py:1110
  68.1 3.6 %mid_pre.1 = (f32[2,8,16,768]{3,2,1,0:T(8,128)S(1)}, f32[5,16,1024]{2,1,0:T(8,128)S(1)}, f32[2,16,768]{2,1,0:T(8,128)S(1)}, f32[2,16,768]{2,1,0:T(8,128)S(1)}) custom-call(f32[144]{0:T(256)S(1)} %concatenate.22.scal, f32[128,256]{1,0:T(8,128)S(1)} %get-tuple-element.54.slab, f32[896,128]{1,0:T(8,128)S(1)} %collective-permute-done.6.got_first, ...), custom_call_target="tpu_custom_call" | custom-call | flops 1000000 | bytes 1000000 | tf_op jit(solution)/shard_map/mid_pre/pallas_call | solution.py:1119
  72.6 2.3 %collective-permute-start.8 = (f32[2,16,768]{2,1,0:T(8,128)S(1)}, f32[2,16,768]{2,1,0:T(8,128)S(1)}, u32[]{:S(2)}, u32[]{:S(2)}) collective-permute-start(f32[2,16,768]{2,1,0:T(8,128)S(1)} %get-tuple-element.59), channel_id=1, source_target_pairs={{0,64},{64,128},{128,192},{192,256},{256,320},{320,384},{384,448},... | collective-permute-start | bytes 294920 | tf_op jit(solution)/shard_map/ppermute | solution.py:1128
  74.9 4.5 %collective-permute-start.9 = (f32[2,16,768]{2,1,0:T(8,128)S(1)}, f32[2,16,768]{2,1,0:T(8,128)S(1)}, u32[]{:S(2)}, u32[]{:S(2)}) collective-permute-start(f32[2,16,768]{2,1,0:T(8,128)S(1)} %get-tuple-element.60), channel_id=1, source_target_pairs={{64,0},{128,64},{192,128},{256,192},{320,256},{384,320},{448,384},... | collective-permute-start | bytes 294920 | tf_op jit(solution)/shard_map/ppermute | solution.py:1129
  80.0 1.5 collective-permute-done.9.up
  82.3 11.9 %collective-permute-start.10 = (f32[5,16,512]{2,1,0:T(8,128)S(1)}, f32[5,16,512]{2,1,0:T(8,128)S(1)}, u32[]{:S(2)}, u32[]{:S(2)}) collective-permute-start(f32[5,16,512]{2,1,0:T(8,128)S(1)} %get-tuple-element.62), channel_id=1, source_target_pairs={{0,2},{2,0},{4,6},{6,4},{8,10},{10,8},{12,14},{14,12},{16,18},{18,... | collective-permute-start | bytes 491528 | tf_op jit(solution)/shard_map/ppermute | solution.py:1136
  95.2 3.5 %krylov.1 = (f32[8,16,768]{2,1,0:T(8,128)S(1)}, f32[16,128]{1,0:T(8,128)S(1)}) custom-call(f32[144]{0:T(256)S(1)} %concatenate.22.scal, f32[5,16,1280]{2,1,0:T(8,128)S(1)} %get-tuple-element.61.own, f32[5,16,512]{2,1,0:T(8,128)S(1)} %collective-permute-done.10.got_first, f32[5,16,512]{2,1,0:T(8,128)S(1)} %collective-permute-done.11.got_second), custom_call_target="tpu_custom_call" | custom-call | flops 1000000 | bytes 1000000 | tf_op jit(solution)/shard_map/krylov/pallas_call | solution.py:1138
  99.4 25.0 %all_to_all.32 = f32[16,1,128]{2,1,0:T(1,128)S(1)} all-to-all(f32[16,1,128]{2,1,0:T(1,128)S(1)} %bitcast.62), channel_id=1, replica_groups=mesh['gx'=16,'yz'=16,'lvl'=2] {'yz'}, dimensions={0} | all-to-all | bytes 16384 | tf_op jit(solution)/shard_map/all_to_all | solution.py:1148
  124.6 20.8 %all_to_all.33 = f32[32,1,128]{2,1,0:T(1,128)} all-to-all(f32[32,1,128]{2,1,0:T(1,128)S(1)} %bitcast.60), channel_id=1, replica_groups=mesh['gx'=16,'yz'=16,'lvl'=2] {'gx','lvl'}, dimensions={0} | all-to-all | bytes 32768 | tf_op jit(solution)/shard_map/all_to_all | solution.py:1150
  145.4 14.1 %post.1 = f32[16,64,128]{2,1,0:T(8,128)} custom-call(f32[144]{0:T(256)} %copy-done.15, f32[32,128]{1,0:T(8,128)} %bitcast.68, f32[8,16,768]{2,1,0:T(8,128)} %copy-done.7, f32[128,1024]{1,0:T(8,128)} %copy-done, f32[2,8,16,768]{3,2,1,0:T(8,128)} %copy-done.4, f32[8,64,128]{2,1,0:T(8,128)} %copy-done.10, f32[16,64,128]{2,1,0:T(8,128)} %copy-done.6, ...), custom_call_target="tpu_custom_call" | custom-call | flops 1000000 | bytes 1000000 | tf_op jit(solution)/shard_map/post/pallas_call | solution.py:1151
  159.5 20.1 %all_to_all.34.got = f32[16,64,128]{2,1,0:T(8,128)S(1)} all-to-all(f32[16,64,128]{2,1,0:T(8,128)} %post.1), channel_id=1, replica_groups=mesh['gx'=16,'yz'=16,'lvl'=2] {'gx'}, dimensions={0} | all-to-all | bytes 1048576 | tf_op jit(solution)/shard_map/all_to_all | solution.py:1174
  179.7 1.4 unpack.1
  (108 shorter events, 20.3 us)
Async XLA Ops:
  3.2 9.4 %copy-start.17 = (f32[64,64]{1,0:T(8,128)S(1)}, f32[64,64]{1,0:T(8,128)}, u32[]{:S(2)}) copy-start(f32[64,64]{1,0:T(8,128)} %param.25) | copy-start | bytes 49156
  3.2 9.4 %copy-start.21 = (f32[64,64]{1,0:T(8,128)S(1)}, f32[64,64]{1,0:T(8,128)}, u32[]{:S(2)}) copy-start(f32[64,64]{1,0:T(8,128)} %constant.73.clone) | copy-start | bytes 49156
  3.2 20.7 %all-to-all-start = ((f32[16,40,128]{2,1,0:T(8,128)}), f32[16,40,128]{2,1,0:T(8,128)S(1)}, u32[]{:S(2)}, u32[]{:S(2)}) async-start(f32[16,40,128]{2,1,0:T(8,128)} %slots.1), calls=%async_computation | async-start | bytes 655360 | tf_op jit(solution)/shard_map/all_to_all | solution.py:1060
  22.8 72.4 %copy-start.15 = (f32[144]{0:T(256)}, f32[144]{0:T(256)S(1)}, u32[]{:S(2)}) copy-start(f32[144]{0:T(256)S(1)} %concatenate.22.scal) | copy-start | bytes 1732
  23.0 19.5 %copy-start.1 = (bf16[448,192]{1,0:T(8,128)(2,1)}, bf16[448,192]{1,0:T(8,128)(2,1)S(1)}, u32[]{:S(2)}) copy-start(bf16[448,192]{1,0:T(8,128)(2,1)S(1)} %pad_maximum_fusion.1.wide) | copy-start | bytes 516100
  23.0 11.3 %copy-start.5 = (bf16[512,512]{1,0:T(8,128)(2,1)S(1)}, bf16[512,512]{1,0:T(8,128)(2,1)}, u32[]{:S(2)}) copy-start(bf16[512,512]{1,0:T(8,128)(2,1)} %constant.80.clone.place_values) | copy-start | bytes 1572868
  23.1 19.4 %copy-start.11 = (bf16[64,80]{1,0:T(8,128)(2,1)}, bf16[64,80]{1,0:T(8,128)(2,1)S(1)}, u32[]{:S(2)}) copy-start(bf16[64,80]{1,0:T(8,128)(2,1)S(1)} %maximum_maximum_fusion.diag_w) | copy-start | bytes 30724
  24.0 10.4 %copy-start.8 = (bf16[384,512]{1,0:T(8,128)(2,1)S(1)}, bf16[384,512]{1,0:T(8,128)(2,1)}, u32[]{:S(2)}) copy-start(bf16[384,512]{1,0:T(8,128)(2,1)} %constant.81.clone.place_kinds) | copy-start | bytes 1179652
  24.0 7.7 %collective-permute-start.1 = (f32[16,24,128]{2,1,0:T(8,128)S(1)}, f32[16,24,128]{2,1,0:T(8,128)S(1)}, u32[]{:S(2)}, u32[]{:S(2)}) collective-permute-start(f32[16,24,128]{2,1,0:T(8,128)S(1)} %get-tuple-element.80), channel_id=1, source_target_pairs={{64,0},{128,64},{192,128},{256,192},{320,256},{384,320},{448,384},... | collective-permute-start | bytes 589832 | tf_op jit(solution)/shard_map/ppermute | solution.py:1065
  26.7 7.6 %collective-permute-start = (f32[16,24,128]{2,1,0:T(8,128)S(1)}, f32[16,24,128]{2,1,0:T(8,128)S(1)}, u32[]{:S(2)}, u32[]{:S(2)}) collective-permute-start(f32[16,24,128]{2,1,0:T(8,128)S(1)} %get-tuple-element.81), channel_id=1, source_target_pairs={{0,64},{64,128},{128,192},{192,256},{256,320},{320,384},{384,448},... | collective-permute-start | bytes 589832 | tf_op jit(solution)/shard_map/ppermute | solution.py:1064
  34.3 8.2 %copy-start.14 = (bf16[256,128]{1,0:T(8,128)(2,1)S(1)}, bf16[256,128]{1,0:T(8,128)(2,1)}, u32[]{:S(2)}) copy-start(bf16[256,128]{1,0:T(8,128)(2,1)} %constant.82.clone.pack) | copy-start | bytes 196612
  35.2 6.2 %collective-permute-start.3 = (f32[768,128]{1,0:T(8,128)S(1)}, f32[768,128]{1,0:T(8,128)S(1)}, u32[]{:S(2)}, u32[]{:S(2)}) collective-permute-start(f32[768,128]{1,0:T(8,128)S(1)} %get-tuple-element.45), channel_id=1, source_target_pairs={{2,4},{4,2},{6,8},{8,6},{10,12},{12,10},{14,16},{16,14},{18,20},{2... | collective-permute-start | bytes 1179656 | tf_op jit(solution)/shard_map/ppermute | solution.py:1074
  35.9 6.6 %collective-permute-start.2 = (f32[768,128]{1,0:T(8,128)S(1)}, f32[768,128]{1,0:T(8,128)S(1)}, u32[]{:S(2)}, u32[]{:S(2)}) collective-permute-start(f32[768,128]{1,0:T(8,128)S(1)} %get-tuple-element.44.own), channel_id=1, source_target_pairs={{0,2},{2,0},{4,6},{6,4},{8,10},{10,8},{12,14},{14,12},{16,18},{18,... | collective-permute-start | bytes 1179656 | tf_op jit(solution)/shard_map/ppermute | solution.py:1073
  41.3 7.7 %copy-start.9 = (f32[64,1]{1,0:T(8,128)}, f32[64,1]{1,0:T(8,128)S(1)}, u32[]{:S(2)}) copy-start(f32[64,1]{1,0:T(8,128)S(1)} %copy.69.diag_e) | copy-start | bytes 772
  49.7 13.2 %copy-start.10 = (f32[8,64,128]{2,1,0:T(8,128)}, f32[8,64,128]{2,1,0:T(8,128)S(1)}, u32[]{:S(2)}) copy-start(f32[8,64,128]{2,1,0:T(8,128)S(1)} %get-tuple-element.67.keep) | copy-start | bytes 786436
  49.7 18.4 %copy-start = (f32[128,1024]{1,0:T(8,128)}, f32[128,1024]{1,0:T(8,128)S(1)}, u32[]{:S(2)}) copy-start(f32[128,1024]{1,0:T(8,128)S(1)} %get-tuple-element.57.cfm) | copy-start | bytes 1572868
  49.7 8.4 %collective-permute-start.5 = (f32[384,128]{1,0:T(8,128)S(1)}, f32[384,128]{1,0:T(8,128)S(1)}, u32[]{:S(2)}, u32[]{:S(2)}) collective-permute-start(f32[384,128]{1,0:T(8,128)S(1)} %get-tuple-element.52), channel_id=1, source_target_pairs={{64,0},{128,64},{192,128},{256,192},{320,256},{384,320},{448,384},... | collective-permute-start | bytes 589832 | tf_op jit(solution)/shard_map/ppermute | solution.py:1103
  52.8 8.8 %collective-permute-start.4 = (f32[384,128]{1,0:T(8,128)S(1)}, f32[384,128]{1,0:T(8,128)S(1)}, u32[]{:S(2)}, u32[]{:S(2)}) collective-permute-start(f32[384,128]{1,0:T(8,128)S(1)} %get-tuple-element.51.own), channel_id=1, source_target_pairs={{0,64},{64,128},{128,192},{192,256},{256,320},{320,384},{384,448},... | collective-permute-start | bytes 589832 | tf_op jit(solution)/shard_map/ppermute | solution.py:1102
  63.7 4.4 %collective-permute-start.6 = (f32[896,128]{1,0:T(8,128)S(1)}, f32[896,128]{1,0:T(8,128)S(1)}, u32[]{:S(2)}, u32[]{:S(2)}) collective-permute-start(f32[896,128]{1,0:T(8,128)S(1)} %get-tuple-element.55), channel_id=1, source_target_pairs={{0,2},{2,0},{4,6},{6,4},{8,10},{10,8},{12,14},{14,12},{16,18},{18,... | collective-permute-start | bytes 1376264 | tf_op jit(solution)/shard_map/ppermute | solution.py:1110
  66.7 1.4 collective-permute-start.7
  72.6 7.4 %collective-permute-start.8 = (f32[2,16,768]{2,1,0:T(8,128)S(1)}, f32[2,16,768]{2,1,0:T(8,128)S(1)}, u32[]{:S(2)}, u32[]{:S(2)}) collective-permute-start(f32[2,16,768]{2,1,0:T(8,128)S(1)} %get-tuple-element.59), channel_id=1, source_target_pairs={{0,64},{64,128},{128,192},{192,256},{256,320},{320,384},{384,448},... | collective-permute-start | bytes 294920 | tf_op jit(solution)/shard_map/ppermute | solution.py:1128
  74.9 6.7 %collective-permute-start.9 = (f32[2,16,768]{2,1,0:T(8,128)S(1)}, f32[2,16,768]{2,1,0:T(8,128)S(1)}, u32[]{:S(2)}, u32[]{:S(2)}) collective-permute-start(f32[2,16,768]{2,1,0:T(8,128)S(1)} %get-tuple-element.60), channel_id=1, source_target_pairs={{64,0},{128,64},{192,128},{256,192},{320,256},{384,320},{448,384},... | collective-permute-start | bytes 294920 | tf_op jit(solution)/shard_map/ppermute | solution.py:1129
  82.3 12.9 %collective-permute-start.10 = (f32[5,16,512]{2,1,0:T(8,128)S(1)}, f32[5,16,512]{2,1,0:T(8,128)S(1)}, u32[]{:S(2)}, u32[]{:S(2)}) collective-permute-start(f32[5,16,512]{2,1,0:T(8,128)S(1)} %get-tuple-element.62), channel_id=1, source_target_pairs={{0,2},{2,0},{4,6},{6,4},{8,10},{10,8},{12,14},{14,12},{16,18},{18,... | collective-permute-start | bytes 491528 | tf_op jit(solution)/shard_map/ppermute | solution.py:1136
  94.2 1.0 collective-permute-start.11
  (18 other events, 20.4 us)

commit v9 on v8

--- a/solution.py
+++ b/solution.py
@@ -676,13 +676,14 @@
 PAIRS = sum(9 - i for i in range(BASIS))
 
 
-def krylov_body(scal, own, got_first, got_second, basis, gram, field, hold):
+def krylov_body(interval, own, got_first, got_second, basis, gram, field, hold):
     pos = position()
     for f in range(5):
         field[f, :, 0:512] = from_below(pos, got_first, got_second, f)
         field[f, :, 512:1792] = own[f]
         field[f, :, 1792:2304] = from_above(pos, got_first, got_second, f)
-    center, half = scal[133], scal[134]
+    center = jnp.concatenate([interval[0:1, :]] * 18, axis=1)
+    half = jnp.concatenate([interval[8:9, :]] * 18, axis=1)
     lane8 = lanes((8, 128))
 
     def apply(v):
@@ -1056,10 +1057,11 @@
     )(res, coefficient.reshape(8, 128), kind.reshape(48, 128), flag.reshape(48, 128))[0]
     element, faces, slots = lax.optimization_barrier((element, faces, slots))
     wide, spread, diag_w, diag_e, down, mid_diag_w, mid_diag_e, lift, scal = tables(element, faces)
+    interval = jnp.repeat(jnp.broadcast_to(scal[133:135, None], (2, 128)), 8, axis=0)
     parity = jnp.broadcast_to((lax.axis_index("yz") % 2).astype(F32), (8, 128))
     own = lax.all_to_all(slots, "gx", 0, 0, tiled=True)
-    own, wide, diag_w, diag_e, mid_diag_w, mid_diag_e, scal, parity = lax.optimization_barrier(
-        (own, wide, diag_w, diag_e, mid_diag_w, mid_diag_e, scal, parity)
+    own, wide, diag_w, diag_e, mid_diag_w, mid_diag_e, scal, parity, interval = lax.optimization_barrier(
+        (own, wide, diag_w, diag_e, mid_diag_w, mid_diag_e, scal, parity, interval)
     )
     dn = lax.ppermute(own[:, 16:40], z_axes, z_up)
     up = lax.ppermute(own[:, 0:24], z_axes, z_dn)
@@ -1139,12 +1141,12 @@
         krylov_body,
         "krylov",
         [f32s(BASIS, 16, 768), f32s(16, 128)],
-        (1, 0, 0, 0),
+        (0, 0, 0, 0),
         [
             pltpu.VMEM((5, 16, 2304), F32),
             pltpu.VMEM((2 * BASIS, 8, 128), F32),
         ],
-    )(scal, coarse_slab, coarse_first, coarse_second)
+    )(interval, coarse_slab, coarse_first, coarse_second)
     gram = lax.all_to_all(gram, "yz", 0, 0, tiled=True)
     gram = call(gram_body, "gram", [f32s(32, 128)], (0,))(gram)[0]
     gram = lax.all_to_all(gram, z_axes, 0, 0, tiled=True)

time: 182 us -> 181 us (level)
  no operation moved by 1% of the time
where the time goes in v9:
time: 181 us; the launch traced here: 180 us
  blocking collectives  66 us (36%)
  starting transfers between devices  49.5 us (27%)
  Pallas kernels  34.1 us (19%)
  waiting for transfers between devices  16.3 us (9%)
  local copies, waits for them, and re-layouts  7.47 us (4%)
  between operations  3.13 us (2%)
  other arithmetic  1.97 us (1%)
    all_to_all x1, blocking collectives, local(): gram = lax.all_to_all(gram, 'yz', 0, 0, tiled=True)  25.6 us
    all_to_all x1, blocking collectives, local(): gram = lax.all_to_all(gram, z_axes, 0, 0, tiled=True)  20.3 us
    all_to_all x1, blocking collectives, local(): got = lax.all_to_all(packed, 'gx', 0, 0, tiled=True)  20.1 us
    pallas_call x1, Pallas kernels, local(): call(post_body, 'post', [f32s(16, 64, 128)], (1,) + (0,) * 14, mid_scratc...  14.1 us
    ppermute x1, starting transfers between devices, local(): coarse_first = lax.ppermute(first, 'yz', y_first)  11.3 us
    all_to_all x1, starting transfers between devices, local(): own = lax.all_to_all(slots, 'gx', 0, 0, tiled=True)  9.37 us
    ppermute x2, starting transfers between devices, local(): up = lax.ppermute(send_down, z_axes, z_dn)  6.65 us
    pallas_call x1, Pallas kernels, local(): call(fine_pre_body, 'fine_pre', [f32s(8, 64, 128), f32s(*plane), f32s(8,...  6.52 us
  transfers between devices with their start and end apart: 13, of which 10 were waited for; matrix products, arithmetic and copies ran while one was open for 3% of the time, Pallas kernels for 0%

profile of v9, /device:TPU:2, one launch (start us, length us, event | category | flops | bytes accessed | tf_op | source)
XLA Modules:
  0.0 179.9 jit_solution(15660912262058394979)
XLA Ops:
  0.6 2.6 %slots.1 = f32[16,40,128]{2,1,0:T(8,128)} custom-call(f32[512,128]{1,0:T(8,128)} %bitcast.64, f32[8,128]{1,0:T(8,128)} %bitcast.73, s32[48,128]{1,0:T(8,128)} %bitcast.71, s32[48,128]{1,0:T(8,128)} %bitcast.72), custom_call_target="tpu_custom_call" | custom-call | flops 1000000 | bytes 1000000 | tf_op jit(solution)/shard_map/slots/pallas_call | solution.py:1050
  3.2 9.4 %all-to-all-start = ((f32[16,40,128]{2,1,0:T(8,128)}), f32[16,40,128]{2,1,0:T(8,128)S(1)}, u32[]{:S(2)}, u32[]{:S(2)}) async-start(f32[16,40,128]{2,1,0:T(8,128)} %slots.1), calls=%async_computation | async-start | bytes 655360 | tf_op jit(solution)/shard_map/all_to_all | solution.py:1062
  22.4 1.6 all-to-all-done.own
  24.1 2.5 %collective-permute-start.1 = (f32[16,24,128]{2,1,0:T(8,128)S(1)}, f32[16,24,128]{2,1,0:T(8,128)S(1)}, u32[]{:S(2)}, u32[]{:S(2)}) collective-permute-start(f32[16,24,128]{2,1,0:T(8,128)S(1)} %get-tuple-element.82), channel_id=1, source_target_pairs={{64,0},{128,64},{192,128},{256,192},{320,256},{384,320},{448,384},... | collective-permute-start | bytes 589832 | tf_op jit(solution)/shard_map/ppermute | solution.py:1067
  26.6 3.5 %collective-permute-start = (f32[16,24,128]{2,1,0:T(8,128)S(1)}, f32[16,24,128]{2,1,0:T(8,128)S(1)}, u32[]{:S(2)}, u32[]{:S(2)}) collective-permute-start(f32[16,24,128]{2,1,0:T(8,128)S(1)} %get-tuple-element.83), channel_id=1, source_target_pairs={{0,64},{64,128},{128,192},{192,256},{256,320},{320,384},{384,448},... | collective-permute-start | bytes 589832 | tf_op jit(solution)/shard_map/ppermute | solution.py:1066
  30.1 1.7 collective-permute-done.1.up
  31.8 2.4 %collective-permute-done.dn = f32[16,24,128]{2,1,0:T(8,128)S(1)} collective-permute-done((f32[16,24,128]{2,1,0:T(8,128)S(1)}, f32[16,24,128]{2,1,0:T(8,128)S(1)}, u32[]{:S(2)}, u32[]{:S(2)}) %collective-permute-start) | collective-permute-done | bytes 196640 | tf_op jit(solution)/shard_map/ppermute | solution.py:1066
  35.7 5.5 %collective-permute-start.2 = (f32[768,128]{1,0:T(8,128)S(1)}, f32[768,128]{1,0:T(8,128)S(1)}, u32[]{:S(2)}, u32[]{:S(2)}) collective-permute-start(f32[768,128]{1,0:T(8,128)S(1)} %get-tuple-element.46.own), channel_id=1, source_target_pairs={{0,2},{2,0},{4,6},{6,4},{8,10},{10,8},{12,14},{14,12},{16,18},{18,... | collective-permute-start | bytes 1179656 | tf_op jit(solution)/shard_map/ppermute | solution.py:1075
  42.6 6.5 %fine_pre.1 = (f32[8,64,128]{2,1,0:T(8,128)S(1)}, f32[64,4096]{1,0:T(8,128)S(1)}, f32[8,4096]{1,0:T(8,128)S(1)}, f32[128,1024]{1,0:T(8,128)S(1)}, f32[384,128]{1,0:T(8,128)S(1)}, /*index=5*/f32[384,128]{1,0:T(8,128)S(1)}) custom-call(f32[16,64,128]{2,1,0:T(8,128)S(1)} %get-tuple-element.45.rows_in, f32[768,128]{1,0:T(8,128)S(1)} %get-tuple-element.46.own, ...), custom_call_target="tpu_custom_call" | custom-call | flops 1000000 | bytes 1000000 | tf_op jit(solution)/shard_map/fine_pre/pallas_call | solution.py:1079
  49.8 3.0 %collective-permute-start.5 = (f32[384,128]{1,0:T(8,128)S(1)}, f32[384,128]{1,0:T(8,128)S(1)}, u32[]{:S(2)}, u32[]{:S(2)}) collective-permute-start(f32[384,128]{1,0:T(8,128)S(1)} %get-tuple-element.54), channel_id=1, source_target_pairs={{64,0},{128,64},{192,128},{256,192},{320,256},{384,320},{448,384},... | collective-permute-start | bytes 589832 | tf_op jit(solution)/shard_map/ppermute | solution.py:1105
  52.7 2.9 %collective-permute-start.4 = (f32[384,128]{1,0:T(8,128)S(1)}, f32[384,128]{1,0:T(8,128)S(1)}, u32[]{:S(2)}, u32[]{:S(2)}) collective-permute-start(f32[384,128]{1,0:T(8,128)S(1)} %get-tuple-element.53.own), channel_id=1, source_target_pairs={{0,64},{64,128},{128,192},{192,256},{256,320},{320,384},{384,448},... | collective-permute-start | bytes 589832 | tf_op jit(solution)/shard_map/ppermute | solution.py:1104
  55.6 2.5 %collective-permute-done.5.up = f32[384,128]{1,0:T(8,128)S(1)} collective-permute-done((f32[384,128]{1,0:T(8,128)S(1)}, f32[384,128]{1,0:T(8,128)S(1)}, u32[]{:S(2)}, u32[]{:S(2)}) %collective-permute-start.5) | collective-permute-done | bytes 196640 | tf_op jit(solution)/shard_map/ppermute | solution.py:1105
  58.1 3.3 %collective-permute-done.4.dn = f32[384,128]{1,0:T(8,128)S(1)} collective-permute-done((f32[384,128]{1,0:T(8,128)S(1)}, f32[384,128]{1,0:T(8,128)S(1)}, u32[]{:S(2)}, u32[]{:S(2)}) %collective-permute-start.4) | collective-permute-done | bytes 196640 | tf_op jit(solution)/shard_map/ppermute | solution.py:1104
  63.4 2.7 %collective-permute-start.6 = (f32[896,128]{1,0:T(8,128)S(1)}, f32[896,128]{1,0:T(8,128)S(1)}, u32[]{:S(2)}, u32[]{:S(2)}) collective-permute-start(f32[896,128]{1,0:T(8,128)S(1)} %get-tuple-element.57), channel_id=1, source_target_pairs={{0,2},{2,0},{4,6},{6,4},{8,10},{10,8},{12,14},{14,12},{16,18},{18,... | collective-permute-start | bytes 1376264 | tf_op jit(solution)/shard_map/ppermute | solution.py:1112
  67.6 3.6 %mid_pre.1 = (f32[2,8,16,768]{3,2,1,0:T(8,128)S(1)}, f32[5,16,1024]{2,1,0:T(8,128)S(1)}, f32[2,16,768]{2,1,0:T(8,128)S(1)}, f32[2,16,768]{2,1,0:T(8,128)S(1)}) custom-call(f32[144]{0:T(256)S(1)} %concatenate.25.scal, f32[128,256]{1,0:T(8,128)S(1)} %get-tuple-element.56.slab, f32[896,128]{1,0:T(8,128)S(1)} %collective-permute-done.6.got_first, ...), custom_call_target="tpu_custom_call" | custom-call | flops 1000000 | bytes 1000000 | tf_op jit(solution)/shard_map/mid_pre/pallas_call | solution.py:1121
  72.1 2.9 %collective-permute-start.8 = (f32[2,16,768]{2,1,0:T(8,128)S(1)}, f32[2,16,768]{2,1,0:T(8,128)S(1)}, u32[]{:S(2)}, u32[]{:S(2)}) collective-permute-start(f32[2,16,768]{2,1,0:T(8,128)S(1)} %get-tuple-element.61), channel_id=1, source_target_pairs={{0,64},{64,128},{128,192},{192,256},{256,320},{320,384},{384,448},... | collective-permute-start | bytes 294920 | tf_op jit(solution)/shard_map/ppermute | solution.py:1130
  75.0 3.7 %collective-permute-start.9 = (f32[2,16,768]{2,1,0:T(8,128)S(1)}, f32[2,16,768]{2,1,0:T(8,128)S(1)}, u32[]{:S(2)}, u32[]{:S(2)}) collective-permute-start(f32[2,16,768]{2,1,0:T(8,128)S(1)} %get-tuple-element.62), channel_id=1, source_target_pairs={{64,0},{128,64},{192,128},{256,192},{320,256},{384,320},{448,384},... | collective-permute-start | bytes 294920 | tf_op jit(solution)/shard_map/ppermute | solution.py:1131
  79.3 2.2 %collective-permute-done.9.up = f32[2,16,768]{2,1,0:T(8,128)S(1)} collective-permute-done((f32[2,16,768]{2,1,0:T(8,128)S(1)}, f32[2,16,768]{2,1,0:T(8,128)S(1)}, u32[]{:S(2)}, u32[]{:S(2)}) %collective-permute-start.9) | collective-permute-done | bytes 98336 | tf_op jit(solution)/shard_map/ppermute | solution.py:1131
  82.2 11.3 %collective-permute-start.10 = (f32[5,16,512]{2,1,0:T(8,128)S(1)}, f32[5,16,512]{2,1,0:T(8,128)S(1)}, u32[]{:S(2)}, u32[]{:S(2)}) collective-permute-start(f32[5,16,512]{2,1,0:T(8,128)S(1)} %get-tuple-element.64), channel_id=1, source_target_pairs={{0,2},{2,0},{4,6},{6,4},{8,10},{10,8},{12,14},{14,12},{16,18},{18,... | collective-permute-start | bytes 491528 | tf_op jit(solution)/shard_map/ppermute | solution.py:1138
  94.5 2.9 %krylov.1 = (f32[8,16,768]{2,1,0:T(8,128)S(1)}, f32[16,128]{1,0:T(8,128)S(1)}) custom-call(f32[16,128]{1,0:T(8,128)S(1)} %broadcast_in_dim_broadcast_in_dim.11.interval, f32[5,16,1280]{2,1,0:T(8,128)S(1)} %get-tuple-element.63.own, f32[5,16,512]{2,1,0:T(8,128)S(1)} %collective-permute-done.10.got_first, f32[5,16,512]{2,1,0:T(8,128)S(1)} %collective-permute-done.11.got_second), custom_call_target="tpu_custom_call" | custom-call | flops 1000000 | bytes 1000000 | tf_op jit(solution)/shard_map/krylov/pallas_call | solution.py:1140
  98.2 25.6 %all_to_all.32 = f32[16,1,128]{2,1,0:T(1,128)S(1)} all-to-all(f32[16,1,128]{2,1,0:T(1,128)S(1)} %bitcast.62), channel_id=1, replica_groups=mesh['gx'=16,'yz'=16,'lvl'=2] {'yz'}, dimensions={0} | all-to-all | bytes 16384 | tf_op jit(solution)/shard_map/all_to_all | solution.py:1150
  123.9 20.3 %all_to_all.33 = f32[32,1,128]{2,1,0:T(1,128)} all-to-all(f32[32,1,128]{2,1,0:T(1,128)S(1)} %bitcast.60), channel_id=1, replica_groups=mesh['gx'=16,'yz'=16,'lvl'=2] {'gx','lvl'}, dimensions={0} | all-to-all | bytes 32768 | tf_op jit(solution)/shard_map/all_to_all | solution.py:1152
  144.2 14.1 %post.1 = f32[16,64,128]{2,1,0:T(8,128)} custom-call(f32[144]{0:T(256)} %copy-done.15, f32[32,128]{1,0:T(8,128)} %bitcast.68, f32[8,16,768]{2,1,0:T(8,128)} %copy-done.7, f32[128,1024]{1,0:T(8,128)} %copy-done, f32[2,8,16,768]{3,2,1,0:T(8,128)} %copy-done.4, f32[8,64,128]{2,1,0:T(8,128)} %copy-done.10, f32[16,64,128]{2,1,0:T(8,128)} %copy-done.6, ...), custom_call_target="tpu_custom_call" | custom-call | flops 1000000 | bytes 1000000 | tf_op jit(solution)/shard_map/post/pallas_call | solution.py:1153
  158.3 20.1 %all_to_all.34.got = f32[16,64,128]{2,1,0:T(8,128)S(1)} all-to-all(f32[16,64,128]{2,1,0:T(8,128)} %post.1), channel_id=1, replica_groups=mesh['gx'=16,'yz'=16,'lvl'=2] {'gx'}, dimensions={0} | all-to-all | bytes 1048576 | tf_op jit(solution)/shard_map/all_to_all | solution.py:1176
  (112 shorter events, 20.1 us)
Async XLA Ops:
  3.2 9.4 %copy-start.17 = (f32[64,64]{1,0:T(8,128)S(1)}, f32[64,64]{1,0:T(8,128)}, u32[]{:S(2)}) copy-start(f32[64,64]{1,0:T(8,128)} %param.25) | copy-start | bytes 49156
  3.2 9.4 %copy-start.22 = (f32[64,8]{1,0:T(8,128)S(1)}, f32[64,8]{1,0:T(8,128)}, u32[]{:S(2)}) copy-start(f32[64,8]{1,0:T(8,128)} %constant.68.clone) | copy-start | bytes 6148
  3.2 20.7 %all-to-all-start = ((f32[16,40,128]{2,1,0:T(8,128)}), f32[16,40,128]{2,1,0:T(8,128)S(1)}, u32[]{:S(2)}, u32[]{:S(2)}) async-start(f32[16,40,128]{2,1,0:T(8,128)} %slots.1), calls=%async_computation | async-start | bytes 655360 | tf_op jit(solution)/shard_map/all_to_all | solution.py:1062
  22.1 45.6 %copy-start.15 = (f32[144]{0:T(256)}, f32[144]{0:T(256)S(1)}, u32[]{:S(2)}) copy-start(f32[144]{0:T(256)S(1)} %concatenate.25.scal) | copy-start | bytes 1732
  22.2 20.4 %copy-start.1 = (bf16[448,192]{1,0:T(8,128)(2,1)}, bf16[448,192]{1,0:T(8,128)(2,1)S(1)}, u32[]{:S(2)}) copy-start(bf16[448,192]{1,0:T(8,128)(2,1)S(1)} %pad_maximum_fusion.1.wide) | copy-start | bytes 516100
  22.2 11.9 %copy-start.5 = (bf16[512,512]{1,0:T(8,128)(2,1)S(1)}, bf16[512,512]{1,0:T(8,128)(2,1)}, u32[]{:S(2)}) copy-start(bf16[512,512]{1,0:T(8,128)(2,1)} %constant.80.clone.place_values) | copy-start | bytes 1572868
  22.3 20.2 %copy-start.11 = (bf16[64,80]{1,0:T(8,128)(2,1)}, bf16[64,80]{1,0:T(8,128)(2,1)S(1)}, u32[]{:S(2)}) copy-start(bf16[64,80]{1,0:T(8,128)(2,1)S(1)} %maximum_maximum_fusion.diag_w) | copy-start | bytes 30724
  24.0 10.1 %copy-start.8 = (bf16[384,512]{1,0:T(8,128)(2,1)S(1)}, bf16[384,512]{1,0:T(8,128)(2,1)}, u32[]{:S(2)}) copy-start(bf16[384,512]{1,0:T(8,128)(2,1)} %constant.81.clone.place_kinds) | copy-start | bytes 1179652
  24.1 7.7 %collective-permute-start.1 = (f32[16,24,128]{2,1,0:T(8,128)S(1)}, f32[16,24,128]{2,1,0:T(8,128)S(1)}, u32[]{:S(2)}, u32[]{:S(2)}) collective-permute-start(f32[16,24,128]{2,1,0:T(8,128)S(1)} %get-tuple-element.82), channel_id=1, source_target_pairs={{64,0},{128,64},{192,128},{256,192},{320,256},{384,320},{448,384},... | collective-permute-start | bytes 589832 | tf_op jit(solution)/shard_map/ppermute | solution.py:1067
  26.6 7.6 %collective-permute-start = (f32[16,24,128]{2,1,0:T(8,128)S(1)}, f32[16,24,128]{2,1,0:T(8,128)S(1)}, u32[]{:S(2)}, u32[]{:S(2)}) collective-permute-start(f32[16,24,128]{2,1,0:T(8,128)S(1)} %get-tuple-element.83), channel_id=1, source_target_pairs={{0,64},{64,128},{128,192},{192,256},{256,320},{320,384},{384,448},... | collective-permute-start | bytes 589832 | tf_op jit(solution)/shard_map/ppermute | solution.py:1066
  34.1 8.4 %copy-start.14 = (bf16[256,128]{1,0:T(8,128)(2,1)S(1)}, bf16[256,128]{1,0:T(8,128)(2,1)}, u32[]{:S(2)}) copy-start(bf16[256,128]{1,0:T(8,128)(2,1)} %constant.82.clone.pack) | copy-start | bytes 196612
  35.0 6.4 %collective-permute-start.3 = (f32[768,128]{1,0:T(8,128)S(1)}, f32[768,128]{1,0:T(8,128)S(1)}, u32[]{:S(2)}, u32[]{:S(2)}) collective-permute-start(f32[768,128]{1,0:T(8,128)S(1)} %get-tuple-element.47), channel_id=1, source_target_pairs={{2,4},{4,2},{6,8},{8,6},{10,12},{12,10},{14,16},{16,14},{18,20},{2... | collective-permute-start | bytes 1179656 | tf_op jit(solution)/shard_map/ppermute | solution.py:1076
  35.7 6.9 %collective-permute-start.2 = (f32[768,128]{1,0:T(8,128)S(1)}, f32[768,128]{1,0:T(8,128)S(1)}, u32[]{:S(2)}, u32[]{:S(2)}) collective-permute-start(f32[768,128]{1,0:T(8,128)S(1)} %get-tuple-element.46.own), channel_id=1, source_target_pairs={{0,2},{2,0},{4,6},{6,4},{8,10},{10,8},{12,14},{14,12},{16,18},{18,... | collective-permute-start | bytes 1179656 | tf_op jit(solution)/shard_map/ppermute | solution.py:1075
  41.4 7.7 %copy-start.9 = (f32[64,1]{1,0:T(8,128)}, f32[64,1]{1,0:T(8,128)S(1)}, u32[]{:S(2)}) copy-start(f32[64,1]{1,0:T(8,128)S(1)} %copy.69.diag_e) | copy-start | bytes 772
  49.8 12.8 %copy-start.10 = (f32[8,64,128]{2,1,0:T(8,128)}, f32[8,64,128]{2,1,0:T(8,128)S(1)}, u32[]{:S(2)}) copy-start(f32[8,64,128]{2,1,0:T(8,128)S(1)} %get-tuple-element.69.keep) | copy-start | bytes 786436
  49.8 17.9 %copy-start = (f32[128,1024]{1,0:T(8,128)}, f32[128,1024]{1,0:T(8,128)S(1)}, u32[]{:S(2)}) copy-start(f32[128,1024]{1,0:T(8,128)S(1)} %get-tuple-element.59.cfm) | copy-start | bytes 1572868
  49.8 8.4 %collective-permute-start.5 = (f32[384,128]{1,0:T(8,128)S(1)}, f32[384,128]{1,0:T(8,128)S(1)}, u32[]{:S(2)}, u32[]{:S(2)}) collective-permute-start(f32[384,128]{1,0:T(8,128)S(1)} %get-tuple-element.54), channel_id=1, source_target_pairs={{64,0},{128,64},{192,128},{256,192},{320,256},{384,320},{448,384},... | collective-permute-start | bytes 589832 | tf_op jit(solution)/shard_map/ppermute | solution.py:1105
  52.7 8.7 %collective-permute-start.4 = (f32[384,128]{1,0:T(8,128)S(1)}, f32[384,128]{1,0:T(8,128)S(1)}, u32[]{:S(2)}, u32[]{:S(2)}) collective-permute-start(f32[384,128]{1,0:T(8,128)S(1)} %get-tuple-element.53.own), channel_id=1, source_target_pairs={{0,64},{64,128},{128,192},{192,256},{256,320},{320,384},{384,448},... | collective-permute-start | bytes 589832 | tf_op jit(solution)/shard_map/ppermute | solution.py:1104
  63.4 4.2 %collective-permute-start.6 = (f32[896,128]{1,0:T(8,128)S(1)}, f32[896,128]{1,0:T(8,128)S(1)}, u32[]{:S(2)}, u32[]{:S(2)}) collective-permute-start(f32[896,128]{1,0:T(8,128)S(1)} %get-tuple-element.57), channel_id=1, source_target_pairs={{0,2},{2,0},{4,6},{6,4},{8,10},{10,8},{12,14},{14,12},{16,18},{18,... | collective-permute-start | bytes 1376264 | tf_op jit(solution)/shard_map/ppermute | solution.py:1112
  66.2 1.4 collective-permute-start.7
  72.1 7.2 %collective-permute-start.8 = (f32[2,16,768]{2,1,0:T(8,128)S(1)}, f32[2,16,768]{2,1,0:T(8,128)S(1)}, u32[]{:S(2)}, u32[]{:S(2)}) collective-permute-start(f32[2,16,768]{2,1,0:T(8,128)S(1)} %get-tuple-element.61), channel_id=1, source_target_pairs={{0,64},{64,128},{128,192},{192,256},{256,320},{320,384},{384,448},... | collective-permute-start | bytes 294920 | tf_op jit(solution)/shard_map/ppermute | solution.py:1130
  75.0 6.5 %collective-permute-start.9 = (f32[2,16,768]{2,1,0:T(8,128)S(1)}, f32[2,16,768]{2,1,0:T(8,128)S(1)}, u32[]{:S(2)}, u32[]{:S(2)}) collective-permute-start(f32[2,16,768]{2,1,0:T(8,128)S(1)} %get-tuple-element.62), channel_id=1, source_target_pairs={{64,0},{128,64},{192,128},{256,192},{320,256},{384,320},{448,384},... | collective-permute-start | bytes 294920 | tf_op jit(solution)/shard_map/ppermute | solution.py:1131
  82.2 12.3 %collective-permute-start.10 = (f32[5,16,512]{2,1,0:T(8,128)S(1)}, f32[5,16,512]{2,1,0:T(8,128)S(1)}, u32[]{:S(2)}, u32[]{:S(2)}) collective-permute-start(f32[5,16,512]{2,1,0:T(8,128)S(1)} %get-tuple-element.64), channel_id=1, source_target_pairs={{0,2},{2,0},{4,6},{6,4},{8,10},{10,8},{12,14},{14,12},{16,18},{18,... | collective-permute-start | bytes 491528 | tf_op jit(solution)/shard_map/ppermute | solution.py:1138
  93.5 1.0 collective-permute-start.11
  (18 other events, 24.4 us)
